TPU v7x, 256 devices: a whole 4x4x8 slice. The times are simulated.
256 devices in a mesh: gx: 16 (over y, x), gy: 8 (over z_hi, core), gz: 2 (over z_lo).
Axes of the slice: x: 4, y: 4, z: 8 (z_hi: 4, z_lo: 2; z = z_hi * 2 + z_lo), core: 2. Of those that a mesh axis runs over, the one named last changes fastest.
Arguments:
- checkpoint: float32 [5, 32, 128, 1024], P(None, 'gz', 'gx', 'gy'), may hold values from -0.6 to 0.6
- gruneisen: float32 [32, 128, 1024], P('gz', 'gx', 'gy'), may hold values from 1 to 3
- switch: int32 [2, 32, 128, 1024], P(None, 'gz', 'gx', 'gy'), may hold values 0 or 1
- probes: int32 [65536], P(('gx', 'gy', 'gz')), may hold values from 0 to 16383
- observed: float32 [65536], P(('gx', 'gy', 'gz')), may hold values from -1 to 1
Outputs:
- direction: float32 [32, 128, 1024], P('gz', 'gx', 'gy')
- misfit: float32 [], replicated
Inputs may be any that keep to these rules, and one draw needn't show every extreme that they name: `probes`: entry k names a cell of the block of the device that holds entry k, as the flat index (z * 8 + x) * 128 + y within that block; cells may repeat.
All inputs are finite; a program needn't handle non-finite values. No bound on the sum of `switch` on one device may be relied on, other than what follows from the above.
Results may differ from a plain program's by a relative error of at most 0.0001.
Values sent between devices are 32-bit elements; how exact they have to be, the bound alone decides.
No kernel may reach another device: no remote copies, remote signals or barrier semaphores. Data moves between devices by JAX's collectives and lax.ppermute only.
A program may use at most 64 MiB of HBM per device.

v0:
```python
import jax
import jax.numpy as jnp
from jax import lax
from jax.sharding import Mesh
from jax.sharding import PartitionSpec as P

STEPS = 2
GX = ("gx_0", "gx_1")
GY = ("gy_0", "gy_1")
GX_GY_GZ = ("gx_0", "gx_1", "gy_0", "gy_1", "gz")


bulk_modulus = 2.0
slope_coeff = 1.5
signal_speed = 2.5
time_ratio = 0.1
quad_viscosity = 4.0
small_eps = 1e-12


def extended_2(array, sides, width):
    edges = {}
    for axis, dim in sides:
        peers, length = (lax.axis_size(axis), array.shape[dim])
        up = [(i, (i + 1) % peers) for i in range(peers - 1)]
        last = lax.slice_in_dim(array, length - width, length, axis=dim)
        first = lax.slice_in_dim(array, 0, width, axis=dim)
        edges[dim] = (
            lax.ppermute(last, axis, up),
            lax.ppermute(first, axis, [(b, a) for a, b in up]),
        )
    done = []
    for _, dim in sides:
        low, high = edges[dim]
        around = [(width, width) if d in done else (0, 0) for d in range(array.ndim)]
        array = jnp.concatenate([jnp.pad(low, around), array, jnp.pad(high, around)], axis=dim)
        done.append(dim)
    return array


def over_axes(array, axes):
    for axis in axes:
        array = lax.psum(array, axis)
    return array


def trim_others(values, keep_dim, first_dim):
    for spatial in range(3):
        if spatial != keep_dim:
            where_dim = first_dim + spatial
            values = lax.slice_in_dim(values, 2, values.shape[where_dim] - 2, axis=where_dim)
    return values


def inner_cells(values, where_dim):
    return lax.slice_in_dim(values, 1, values.shape[where_dim] - 1, axis=where_dim)


def pair_slices(values, where_dim):
    length = values.shape[where_dim]
    return (
        lax.slice_in_dim(values, 1, length, axis=where_dim),
        lax.slice_in_dim(values, 0, length - 1, axis=where_dim),
    )


def advance(pad_state, pad_gamma, pad_switch):
    density = 1.0 + pad_state[0]
    velocity = pad_state[1:4] / density
    internal = pad_state[4] / density - 0.5 * jnp.sum(velocity * velocity, axis=0)
    pressure = (
        bulk_modulus * (pad_state[0] + slope_coeff * pad_state[0] * pad_state[0])
        + pad_gamma * density * internal
    )
    change = jnp.zeros_like(pad_state[:, 2:-2, 2:-2, 2:-2])
    for component, spatial in ((0, 1), (1, 2), (2, 0)):
        state_line = trim_others(pad_state, spatial, 1)
        speed_line = trim_others(velocity[component], spatial, 0)
        length = speed_line.shape[spatial]
        slope_cells = 0.5 * (
            lax.slice_in_dim(speed_line, 2, length, axis=spatial)
            - lax.slice_in_dim(speed_line, 0, length - 2, axis=spatial)
        )
        squeeze = jnp.minimum(slope_cells, 0.0)
        dens_mid = inner_cells(trim_others(density, spatial, 0), spatial)
        press_mid = inner_cells(trim_others(pressure, spatial, 0), spatial)
        switch_mid = inner_cells(trim_others(pad_switch, spatial, 0), spatial)
        total_press = press_mid + switch_mid * quad_viscosity * dens_mid * squeeze * squeeze
        speed_mid = inner_cells(speed_line, spatial)
        state_mid = inner_cells(state_line, spatial + 1)
        momentum_rows = [state_mid[1 + member] * speed_mid for member in range(3)]
        momentum_rows[component] = momentum_rows[component] + total_press
        flux_rows = jnp.stack(
            [state_mid[1 + component]] + momentum_rows + [(state_mid[4] + total_press) * speed_mid]
        )
        flux_upper, flux_lower = pair_slices(flux_rows, spatial + 1)
        state_upper, state_lower = pair_slices(state_mid, spatial + 1)
        face_flux = 0.5 * (flux_lower + flux_upper) - 0.5 * signal_speed * (
            state_upper - state_lower
        )
        face_upper, face_lower = pair_slices(face_flux, spatial + 1)
        change = change + face_upper - face_lower
    return pad_state[:, 2:-2, 2:-2, 2:-2] - time_ratio * change


def spread_faces(packed):
    return extended_2(packed, (("gz", 1), (GX, 2), (GY, 3)), 2)


def rim_pack(padded, spatial):
    where_dim = spatial + 1
    core_part = trim_others(padded, spatial, 1)
    length = core_part.shape[where_dim]
    lower_ghost = lax.slice_in_dim(core_part, 0, 2, axis=where_dim)
    upper_ghost = lax.slice_in_dim(core_part, length - 2, length, axis=where_dim)
    middle_zero = jnp.zeros_like(lax.slice_in_dim(core_part, 4, length - 4, axis=where_dim))
    return jnp.concatenate([lower_ghost, middle_zero, upper_ghost], axis=where_dim)


def rim_take(extended, spatial):
    where_dim = spatial + 1
    length = extended.shape[where_dim]
    from_lower = lax.slice_in_dim(extended, 0, 2, axis=where_dim)
    from_upper = lax.slice_in_dim(extended, length - 2, length, axis=where_dim)
    middle_zero = jnp.zeros_like(lax.slice_in_dim(extended, 4, length - 4, axis=where_dim))
    return jnp.concatenate([from_lower, middle_zero, from_upper], axis=where_dim)


def fold_ghosts(padded):
    interior = padded[:, 2:-2, 2:-2, 2:-2]
    channels = padded.shape[0]
    packed = jnp.concatenate(
        [rim_pack(padded, 0), rim_pack(padded, 1), rim_pack(padded, 2)], axis=0
    )
    arrived = extended_2(packed, (("gz", 1), (GX, 2), (GY, 3)), 2)
    for spatial in range(3):
        member_part = arrived[spatial * channels : (spatial + 1) * channels]
        interior = interior + rim_take(trim_others(member_part, spatial, 1), spatial)
    return interior


def local(checkpoint, gruneisen, switch, probes, observed):
    switch_f = switch.astype(jnp.float32)
    stored = []
    current = checkpoint
    for step_index in range(STEPS):
        packed = jnp.concatenate(
            [current, gruneisen[None], switch_f[step_index : step_index + 1]], axis=0
        )
        padded = spread_faces(packed)
        stored.append(padded)
        current = advance(padded[:5], padded[5], padded[6])
    probe_density = 1.0 + current[0].reshape(-1)[probes]
    probe_speed = current[1].reshape(-1)[probes] / probe_density
    residual = probe_speed - observed
    total_probes = probes.shape[0] * lax.axis_size(GX) * lax.axis_size(GY) * lax.axis_size("gz")
    weight_probe = 2.0 * residual
    seed_flat = jnp.zeros((5, current[0].size), jnp.float32)
    seed_flat = seed_flat.at[1, probes].add(weight_probe / probe_density)
    seed_flat = seed_flat.at[0, probes].add(-weight_probe * probe_speed / probe_density)
    cotangent = seed_flat.reshape(current.shape)
    gamma_total = jnp.zeros_like(stored[0][5])
    for step_index in reversed(range(STEPS)):
        padded = stored[step_index]
        if step_index > 0:
            _, pullback = jax.vjp(
                lambda state_pad, gamma_pad: advance(state_pad, gamma_pad, padded[6]),
                padded[:5],
                padded[5],
            )
            state_cot, gamma_cot = pullback(cotangent)
            cotangent = fold_ghosts(state_cot)
        else:
            _, pullback = jax.vjp(
                lambda gamma_pad: advance(padded[:5], gamma_pad, padded[6]), padded[5]
            )
            (gamma_cot,) = pullback(cotangent)
        gamma_total = gamma_total + gamma_cot
    gradient_field = fold_ghosts(gamma_total[None])[0]
    grad_total, miss_total = (
        over_axes(jnp.sum(gradient_field * gradient_field), GX_GY_GZ),
        over_axes(jnp.sum(residual * residual), GX_GY_GZ),
    )
    total_cells = gradient_field.size * lax.axis_size(GX) * lax.axis_size(GY) * lax.axis_size("gz")
    direction = gradient_field / jnp.sqrt(grad_total / total_cells + small_eps)
    misfit = miss_total / total_probes
    return (direction, misfit)


def solution(mesh):
    torus = Mesh(
        mesh.devices.reshape(4, 4, 4, 2, mesh.shape["gz"]), ("gx_0", "gx_1", "gy_0", "gy_1", "gz")
    )
    placed = (
        P(None, "gz", GX, GY),
        P("gz", GX, GY),
        P(None, "gz", GX, GY),
        P(GX_GY_GZ),
        P(GX_GY_GZ),
    )
    return jax.shard_map(
        local, mesh=torus, in_specs=placed, out_specs=(P("gz", GX, GY), P()), check_vma=False
    )
```

profile of v0, /device:TPU:1, one launch (start us, length us, event | category | flops | bytes accessed | tf_op | source)
XLA Modules:
  0.0 233.7 jit_solution(10751930779800642281)
XLA Ops:
  2.6 4.4 %collective-permute-start.1 = (f32[7,2,8,128]{3,2,1,0:T(8,128)S(1)}, f32[7,2,8,128]{3,2,1,0:T(8,128)S(1)}, u32[]{:S(2)}, u32[]{:S(2)}) collective-permute-start(f32[7,2,8,128]{3,2,1,0:T(8,128)S(1)} %get-tuple-element.114), channel_id=1, source_target_pairs={{0,1},{2,3},{4,5},{6,7},{8,9},{10,11},{12,13},{14,15},{16,17},{18,... | collective-permute-start | bytes 172040 | tf_op jit(solution)/shard_map/ppermute | solution.py:29
  8.5 2.9 %collective-permute-start.5 = (f32[7,16,8,2]{3,2,1,0:T(8,128)S(1)}, f32[7,16,8,2]{3,2,1,0:T(8,128)S(1)}, u32[]{:S(2)}, u32[]{:S(2)}) collective-permute-start(f32[7,16,8,2]{3,2,1,0:T(8,128)S(1)} %get-tuple-element.110), channel_id=1, source_target_pairs={{2,0},{4,2},{6,4},{8,6},{10,8},{12,10},{14,12},{3,1},{5,3},{7,5},{... | collective-permute-start | bytes 21512 | tf_op jit(solution)/shard_map/ppermute | solution.py:30
  12.9 4.8 %collective-permute-start.4 = (f32[7,16,8,2]{3,2,1,0:T(8,128)S(1)}, f32[7,16,8,2]{3,2,1,0:T(8,128)S(1)}, u32[]{:S(2)}, u32[]{:S(2)}) collective-permute-start(f32[7,16,8,2]{3,2,1,0:T(8,128)S(1)} %get-tuple-element.109), channel_id=1, source_target_pairs={{0,2},{2,4},{4,6},{6,8},{8,10},{10,12},{12,14},{1,3},{3,5},{5,7},{... | collective-permute-start | bytes 21512 | tf_op jit(solution)/shard_map/ppermute | solution.py:29
  17.8 3.7 %collective-permute-done.5 = f32[7,16,8,2]{3,2,1,0:T(8,128)S(1)} collective-permute-done((f32[7,16,8,2]{3,2,1,0:T(8,128)S(1)}, f32[7,16,8,2]{3,2,1,0:T(8,128)S(1)}, u32[]{:S(2)}, u32[]{:S(2)}) %collective-permute-start.5) | collective-permute-done | bytes 7200 | tf_op jit(solution)/shard_map/ppermute | solution.py:30
  21.5 3.1 %collective-permute-start = (f32[7,16,2,128]{3,2,1,0:T(2,128)S(1)}, f32[7,16,2,128]{3,2,1,0:T(2,128)S(1)}, u32[]{:S(2)}, u32[]{:S(2)}) collective-permute-start(f32[7,16,2,128]{3,2,1,0:T(2,128)S(1)} %get-tuple-element.111), channel_id=1, source_target_pairs={{0,16},{16,32},{32,48},{48,64},{64,80},{80,96},{96,112},{112,128},... | collective-permute-start | bytes 344072 | tf_op jit(solution)/shard_map/ppermute | solution.py:29
  36.0 6.6 %collective-permute-start.7 = (f32[7,2,8,128]{3,2,1,0:T(8,128)S(1)}, f32[7,2,8,128]{3,2,1,0:T(8,128)S(1)}, u32[]{:S(2)}, u32[]{:S(2)}) collective-permute-start(f32[7,2,8,128]{3,2,1,0:T(8,128)S(1)} %get-tuple-element.107), channel_id=1, source_target_pairs={{0,1},{2,3},{4,5},{6,7},{8,9},{10,11},{12,13},{14,15},{16,17},{18,... | collective-permute-start | bytes 172040 | tf_op jit(solution)/shard_map/ppermute | solution.py:29
  42.6 4.8 %collective-permute-start.10 = (f32[7,16,8,2]{3,2,1,0:T(8,128)S(1)}, f32[7,16,8,2]{3,2,1,0:T(8,128)S(1)}, u32[]{:S(2)}, u32[]{:S(2)}) collective-permute-start(f32[7,16,8,2]{3,2,1,0:T(8,128)S(1)} %get-tuple-element.103), channel_id=1, source_target_pairs={{0,2},{2,4},{4,6},{6,8},{8,10},{10,12},{12,14},{1,3},{3,5},{5,7},{... | collective-permute-start | bytes 21512 | tf_op jit(solution)/shard_map/ppermute | solution.py:29
  48.9 4.6 %collective-permute-start.6 = (f32[7,16,2,128]{3,2,1,0:T(2,128)S(1)}, f32[7,16,2,128]{3,2,1,0:T(2,128)S(1)}, u32[]{:S(2)}, u32[]{:S(2)}) collective-permute-start(f32[7,16,2,128]{3,2,1,0:T(2,128)S(1)} %get-tuple-element.105), channel_id=1, source_target_pairs={{0,16},{16,32},{32,48},{48,64},{64,80},{80,96},{96,112},{112,128},... | collective-permute-start | bytes 344072 | tf_op jit(solution)/shard_map/ppermute | solution.py:29
  67.5 11.8 %scatter_fusion = f32[5,16384]{1,0:T(8,128)S(1)} fusion(f32[5,16384]{1,0:T(8,128)S(1)} %broadcast_in_dim.95, s32[256]{0:T(256)S(1)} %bitcast.521, f32[256]{0:T(256)S(1)} %get-tuple-element.140), kind=kCustom, calls=%fused_computation.2 | custom fusion | flops 256 | bytes 5120 | tf_op jit(solution)/shard_map/scatter-add | solution.py:159
  79.3 11.8 %scatter_fusion.1 = f32[5,16384]{1,0:T(8,128)S(1)} fusion(f32[5,16384]{1,0:T(8,128)S(1)} %scatter_fusion, s32[256]{0:T(256)S(1)} %bitcast.520, f32[256]{0:T(256)S(1)} %get-tuple-element.139), kind=kCustom, calls=%fused_computation.3 | custom fusion | flops 256 | bytes 5120 | tf_op jit(solution)/shard_map/scatter-add | solution.py:160
  107.2 5.1 %collective-permute-start.14 = (f32[15,16,2,128]{3,2,1,0:T(2,128)}, f32[15,16,2,128]{3,2,1,0:T(2,128)}, u32[]{:S(2)}, u32[]{:S(2)}) collective-permute-start(f32[15,16,2,128]{3,2,1,0:T(2,128)} %get-tuple-element.79), channel_id=1, source_target_pairs={{0,16},{16,32},{32,48},{48,64},{64,80},{80,96},{96,112},{112,128},... | collective-permute-start | bytes 737288 | tf_op jit(solution)/shard_map/ppermute | solution.py:29
  113.5 5.5 %collective-permute-start.12 = (f32[15,2,8,128]{3,2,1,0:T(8,128)}, f32[15,2,8,128]{3,2,1,0:T(8,128)}, u32[]{:S(2)}, u32[]{:S(2)}) collective-permute-start(f32[15,2,8,128]{3,2,1,0:T(8,128)} %get-tuple-element.71), channel_id=1, source_target_pairs={{0,1},{2,3},{4,5},{6,7},{8,9},{10,11},{12,13},{14,15},{16,17},{18,... | collective-permute-start | bytes 368648 | tf_op jit(solution)/shard_map/ppermute | solution.py:29
  120.6 2.6 %copy.15 = f32[15,16,8,2]{1,2,3,0:T(8,128)} copy(f32[15,16,8,2]{3,2,1,0:T(8,128)} %get-tuple-element.82) | data formatting | bytes 30720 | tf_op jit(solution)/shard_map/slice | solution.py:27
  125.1 2.6 %copy.14 = f32[15,16,8,2]{1,2,3,0:T(8,128)} copy(f32[15,16,8,2]{3,2,1,0:T(8,128)} %get-tuple-element.81) | data formatting | bytes 30720 | tf_op jit(solution)/shard_map/slice | solution.py:26
  127.7 4.2 %collective-permute-done.17 = f32[15,16,8,2]{1,2,3,0:T(8,128)} collective-permute-done((f32[15,16,8,2]{1,2,3,0:T(8,128)}, f32[15,16,8,2]{1,2,3,0:T(8,128)}, u32[]{:S(2)}, u32[]{:S(2)}) %collective-permute-start.17) | collective-permute-done | bytes 15392 | tf_op jit(solution)/shard_map/ppermute | solution.py:30
  131.9 3.8 %collective-permute-start.16 = (f32[15,16,8,2]{1,2,3,0:T(8,128)}, f32[15,16,8,2]{1,2,3,0:T(8,128)}, u32[]{:S(2)}, u32[]{:S(2)}) collective-permute-start(f32[15,16,8,2]{1,2,3,0:T(8,128)} %copy.14), channel_id=1, source_target_pairs={{0,2},{2,4},{4,6},{6,8},{8,10},{10,12},{12,14},{1,3},{3,5},{5,7},{... | collective-permute-start | bytes 46088 | tf_op jit(solution)/shard_map/ppermute | solution.py:29
  153.1 4.0 %collective-permute-start.20 = (f32[3,16,2,128]{3,2,1,0:T(2,128)S(1)}, f32[3,16,2,128]{3,2,1,0:T(2,128)S(1)}, u32[]{:S(2)}, u32[]{:S(2)}) collective-permute-start(f32[3,16,2,128]{3,2,1,0:T(2,128)S(1)} %get-tuple-element.133), channel_id=1, source_target_pairs={{0,16},{16,32},{32,48},{48,64},{64,80},{80,96},{96,112},{112,128},... | collective-permute-start | bytes 147464 | tf_op jit(solution)/shard_map/ppermute | solution.py:29
  158.4 4.0 %collective-permute-start.18 = (f32[3,2,8,128]{3,2,1,0:T(8,128)S(1)}, f32[3,2,8,128]{3,2,1,0:T(8,128)S(1)}, u32[]{:S(2)}, u32[]{:S(2)}) collective-permute-start(f32[3,2,8,128]{3,2,1,0:T(8,128)S(1)} %get-tuple-element.117), channel_id=1, source_target_pairs={{0,1},{2,3},{4,5},{6,7},{8,9},{10,11},{12,13},{14,15},{16,17},{18,... | collective-permute-start | bytes 73736 | tf_op jit(solution)/shard_map/ppermute | solution.py:29
  164.9 12.1 %collective-permute-done.23 = f32[3,16,8,2]{3,2,1,0:T(8,128)S(1)} collective-permute-done((f32[3,16,8,2]{3,2,1,0:T(8,128)S(1)}, f32[3,16,8,2]{3,2,1,0:T(8,128)S(1)}, u32[]{:S(2)}, u32[]{:S(2)}) %collective-permute-start.23) | collective-permute-done | bytes 3104 | tf_op jit(solution)/shard_map/ppermute | solution.py:30
  182.3 12.2 %all-reduce.118 = (f32[]{:T(128)}, f32[]{:T(128)}) all-reduce(f32[]{:T(128)} %get-tuple-element.16, f32[]{:T(128)} %get-tuple-element.14), channel_id=1, replica_groups=mesh['gx_0'=4,'gx_1'=4,'gy_0'=4,'gy_1'=2,'gz'=2] {'gx_0'}, use_global_device_ids=true, to_apply=%region_6.7 | all-reduce | flops 2 | bytes 16 | tf_op jit(solution)/shard_map/psum | solution.py:43
  194.5 8.9 %all-reduce.117 = (f32[]{:T(128)}, f32[]{:T(128)}) all-reduce(f32[]{:T(128)} %get-tuple-element.8, f32[]{:T(128)} %get-tuple-element.9), channel_id=1, replica_groups=mesh['gx_0'=4,'gx_1'=4,'gy_0'=4,'gy_1'=2,'gz'=2] {'gx_1'}, use_global_device_ids=true, to_apply=%region_7.8 | all-reduce | flops 2 | bytes 16 | tf_op jit(solution)/shard_map/psum | solution.py:43
  203.4 10.5 %all-reduce.116 = (f32[]{:T(128)}, f32[]{:T(128)}) all-reduce(f32[]{:T(128)} %get-tuple-element.6, f32[]{:T(128)} %get-tuple-element.7), channel_id=1, replica_groups=mesh['gx_0'=4,'gx_1'=4,'gy_0'=4,'gy_1'=2,'gz'=2] {'gy_0'}, use_global_device_ids=true, to_apply=%region_8.9 | all-reduce | flops 2 | bytes 16 | tf_op jit(solution)/shard_map/psum | solution.py:43
  213.9 12.3 %all-reduce.120 = (f32[]{:T(128)}, f32[]{:T(128)}) all-reduce(f32[]{:T(128)} %get-tuple-element.4, f32[]{:T(128)} %get-tuple-element.5), channel_id=1, replica_groups=mesh['gx_0'=4,'gx_1'=4,'gy_0'=4,'gy_1'=2,'gz'=2] {'gy_1'}, use_global_device_ids=true, to_apply=%region_9.10 | all-reduce | flops 2 | bytes 16 | tf_op jit(solution)/shard_map/psum | solution.py:43
  226.2 4.4 %all-reduce.119 = (f32[]{:T(128)}, f32[]{:T(128)}) all-reduce(f32[]{:T(128)} %get-tuple-element.12, f32[]{:T(128)} %get-tuple-element.13), channel_id=1, replica_groups=mesh['gx_0'=4,'gx_1'=4,'gy_0'=4,'gy_1'=2,'gz'=2] {'gz'}, use_global_device_ids=true, to_apply=%region_10.11 | all-reduce | flops 2 | bytes 16 | tf_op jit(solution)/shard_map/psum | solution.py:43
  (257 shorter events, 78.5 us)
Async XLA Ops:
  2.6 22.2 %collective-permute-start.1 = (f32[7,2,8,128]{3,2,1,0:T(8,128)S(1)}, f32[7,2,8,128]{3,2,1,0:T(8,128)S(1)}, u32[]{:S(2)}, u32[]{:S(2)}) collective-permute-start(f32[7,2,8,128]{3,2,1,0:T(8,128)S(1)} %get-tuple-element.114), channel_id=1, source_target_pairs={{0,1},{2,3},{4,5},{6,7},{8,9},{10,11},{12,13},{14,15},{16,17},{18,... | collective-permute-start | bytes 172040 | tf_op jit(solution)/shard_map/ppermute | solution.py:29
  7.0 17.8 %collective-permute-start.2 = (f32[7,2,8,128]{3,2,1,0:T(8,128)S(1)}, f32[7,2,8,128]{3,2,1,0:T(8,128)S(1)}, u32[]{:S(2)}, u32[]{:S(2)}) collective-permute-start(f32[7,2,8,128]{3,2,1,0:T(8,128)S(1)} %get-tuple-element.113), channel_id=1, source_target_pairs={{1,0},{3,2},{5,4},{7,6},{9,8},{11,10},{13,12},{15,14},{17,16},{19,... | collective-permute-start | bytes 172040 | tf_op jit(solution)/shard_map/ppermute | solution.py:30
  8.5 12.9 %collective-permute-start.5 = (f32[7,16,8,2]{3,2,1,0:T(8,128)S(1)}, f32[7,16,8,2]{3,2,1,0:T(8,128)S(1)}, u32[]{:S(2)}, u32[]{:S(2)}) collective-permute-start(f32[7,16,8,2]{3,2,1,0:T(8,128)S(1)} %get-tuple-element.110), channel_id=1, source_target_pairs={{2,0},{4,2},{6,4},{8,6},{10,8},{12,10},{14,12},{3,1},{5,3},{7,5},{... | collective-permute-start | bytes 21512 | tf_op jit(solution)/shard_map/ppermute | solution.py:30
  11.5 13.4 %collective-permute-start.3 = (f32[7,16,2,128]{3,2,1,0:T(2,128)S(1)}, f32[7,16,2,128]{3,2,1,0:T(2,128)S(1)}, u32[]{:S(2)}, u32[]{:S(2)}) collective-permute-start(f32[7,16,2,128]{3,2,1,0:T(2,128)S(1)} %get-tuple-element.112), channel_id=1, source_target_pairs={{16,0},{32,16},{48,32},{64,48},{80,64},{96,80},{112,96},{128,112},... | collective-permute-start | bytes 344072 | tf_op jit(solution)/shard_map/ppermute | solution.py:30
  12.9 11.8 %collective-permute-start.4 = (f32[7,16,8,2]{3,2,1,0:T(8,128)S(1)}, f32[7,16,8,2]{3,2,1,0:T(8,128)S(1)}, u32[]{:S(2)}, u32[]{:S(2)}) collective-permute-start(f32[7,16,8,2]{3,2,1,0:T(8,128)S(1)} %get-tuple-element.109), channel_id=1, source_target_pairs={{0,2},{2,4},{4,6},{6,8},{8,10},{10,12},{12,14},{1,3},{3,5},{5,7},{... | collective-permute-start | bytes 21512 | tf_op jit(solution)/shard_map/ppermute | solution.py:29
  21.5 4.9 %collective-permute-start = (f32[7,16,2,128]{3,2,1,0:T(2,128)S(1)}, f32[7,16,2,128]{3,2,1,0:T(2,128)S(1)}, u32[]{:S(2)}, u32[]{:S(2)}) collective-permute-start(f32[7,16,2,128]{3,2,1,0:T(2,128)S(1)} %get-tuple-element.111), channel_id=1, source_target_pairs={{0,16},{16,32},{32,48},{48,64},{64,80},{80,96},{96,112},{112,128},... | collective-permute-start | bytes 344072 | tf_op jit(solution)/shard_map/ppermute | solution.py:29
  32.8 16.0 %collective-permute-start.11 = (f32[7,16,8,2]{3,2,1,0:T(8,128)S(1)}, f32[7,16,8,2]{3,2,1,0:T(8,128)S(1)}, u32[]{:S(2)}, u32[]{:S(2)}) collective-permute-start(f32[7,16,8,2]{3,2,1,0:T(8,128)S(1)} %get-tuple-element.104), channel_id=1, source_target_pairs={{2,0},{4,2},{6,4},{8,6},{10,8},{12,10},{14,12},{3,1},{5,3},{7,5},{... | collective-permute-start | bytes 21512 | tf_op jit(solution)/shard_map/ppermute | solution.py:30
  34.7 18.9 %collective-permute-start.8 = (f32[7,2,8,128]{3,2,1,0:T(8,128)S(1)}, f32[7,2,8,128]{3,2,1,0:T(8,128)S(1)}, u32[]{:S(2)}, u32[]{:S(2)}) collective-permute-start(f32[7,2,8,128]{3,2,1,0:T(8,128)S(1)} %get-tuple-element.108), channel_id=1, source_target_pairs={{1,0},{3,2},{5,4},{7,6},{9,8},{11,10},{13,12},{15,14},{17,16},{19,... | collective-permute-start | bytes 172040 | tf_op jit(solution)/shard_map/ppermute | solution.py:30
  36.0 17.7 %collective-permute-start.7 = (f32[7,2,8,128]{3,2,1,0:T(8,128)S(1)}, f32[7,2,8,128]{3,2,1,0:T(8,128)S(1)}, u32[]{:S(2)}, u32[]{:S(2)}) collective-permute-start(f32[7,2,8,128]{3,2,1,0:T(8,128)S(1)} %get-tuple-element.107), channel_id=1, source_target_pairs={{0,1},{2,3},{4,5},{6,7},{8,9},{10,11},{12,13},{14,15},{16,17},{18,... | collective-permute-start | bytes 172040 | tf_op jit(solution)/shard_map/ppermute | solution.py:29
  42.6 10.9 %collective-permute-start.10 = (f32[7,16,8,2]{3,2,1,0:T(8,128)S(1)}, f32[7,16,8,2]{3,2,1,0:T(8,128)S(1)}, u32[]{:S(2)}, u32[]{:S(2)}) collective-permute-start(f32[7,16,8,2]{3,2,1,0:T(8,128)S(1)} %get-tuple-element.103), channel_id=1, source_target_pairs={{0,2},{2,4},{4,6},{6,8},{8,10},{10,12},{12,14},{1,3},{3,5},{5,7},{... | collective-permute-start | bytes 21512 | tf_op jit(solution)/shard_map/ppermute | solution.py:29
  47.5 6.2 %collective-permute-start.9 = (f32[7,16,2,128]{3,2,1,0:T(2,128)S(1)}, f32[7,16,2,128]{3,2,1,0:T(2,128)S(1)}, u32[]{:S(2)}, u32[]{:S(2)}) collective-permute-start(f32[7,16,2,128]{3,2,1,0:T(2,128)S(1)} %get-tuple-element.106), channel_id=1, source_target_pairs={{16,0},{32,16},{48,32},{64,48},{80,64},{96,80},{112,96},{128,112},... | collective-permute-start | bytes 344072 | tf_op jit(solution)/shard_map/ppermute | solution.py:30
  48.9 6.2 %collective-permute-start.6 = (f32[7,16,2,128]{3,2,1,0:T(2,128)S(1)}, f32[7,16,2,128]{3,2,1,0:T(2,128)S(1)}, u32[]{:S(2)}, u32[]{:S(2)}) collective-permute-start(f32[7,16,2,128]{3,2,1,0:T(2,128)S(1)} %get-tuple-element.105), channel_id=1, source_target_pairs={{0,16},{16,32},{32,48},{48,64},{64,80},{80,96},{96,112},{112,128},... | collective-permute-start | bytes 344072 | tf_op jit(solution)/shard_map/ppermute | solution.py:29
  105.9 37.8 %collective-permute-start.15 = (f32[15,16,2,128]{3,2,1,0:T(2,128)}, f32[15,16,2,128]{3,2,1,0:T(2,128)}, u32[]{:S(2)}, u32[]{:S(2)}) collective-permute-start(f32[15,16,2,128]{3,2,1,0:T(2,128)} %get-tuple-element.80), channel_id=1, source_target_pairs={{16,0},{32,16},{48,32},{64,48},{80,64},{96,80},{112,96},{128,112},... | collective-permute-start | bytes 737288 | tf_op jit(solution)/shard_map/ppermute | solution.py:30
  107.2 37.4 %collective-permute-start.14 = (f32[15,16,2,128]{3,2,1,0:T(2,128)}, f32[15,16,2,128]{3,2,1,0:T(2,128)}, u32[]{:S(2)}, u32[]{:S(2)}) collective-permute-start(f32[15,16,2,128]{3,2,1,0:T(2,128)} %get-tuple-element.79), channel_id=1, source_target_pairs={{0,16},{16,32},{32,48},{48,64},{64,80},{80,96},{96,112},{112,128},... | collective-permute-start | bytes 737288 | tf_op jit(solution)/shard_map/ppermute | solution.py:29
  112.2 29.9 %collective-permute-start.13 = (f32[15,2,8,128]{3,2,1,0:T(8,128)}, f32[15,2,8,128]{3,2,1,0:T(8,128)}, u32[]{:S(2)}, u32[]{:S(2)}) collective-permute-start(f32[15,2,8,128]{3,2,1,0:T(8,128)} %get-tuple-element.72), channel_id=1, source_target_pairs={{1,0},{3,2},{5,4},{7,6},{9,8},{11,10},{13,12},{15,14},{17,16},{19,... | collective-permute-start | bytes 368648 | tf_op jit(solution)/shard_map/ppermute | solution.py:30
  113.5 29.4 %collective-permute-start.12 = (f32[15,2,8,128]{3,2,1,0:T(8,128)}, f32[15,2,8,128]{3,2,1,0:T(8,128)}, u32[]{:S(2)}, u32[]{:S(2)}) collective-permute-start(f32[15,2,8,128]{3,2,1,0:T(8,128)} %get-tuple-element.71), channel_id=1, source_target_pairs={{0,1},{2,3},{4,5},{6,7},{8,9},{10,11},{12,13},{14,15},{16,17},{18,... | collective-permute-start | bytes 368648 | tf_op jit(solution)/shard_map/ppermute | solution.py:29
  123.2 8.7 %collective-permute-start.17 = (f32[15,16,8,2]{1,2,3,0:T(8,128)}, f32[15,16,8,2]{1,2,3,0:T(8,128)}, u32[]{:S(2)}, u32[]{:S(2)}) collective-permute-start(f32[15,16,8,2]{1,2,3,0:T(8,128)} %copy.15), channel_id=1, source_target_pairs={{2,0},{4,2},{6,4},{8,6},{10,8},{12,10},{14,12},{3,1},{5,3},{7,5},{... | collective-permute-start | bytes 46088 | tf_op jit(solution)/shard_map/ppermute | solution.py:30
  131.9 7.0 %collective-permute-start.16 = (f32[15,16,8,2]{1,2,3,0:T(8,128)}, f32[15,16,8,2]{1,2,3,0:T(8,128)}, u32[]{:S(2)}, u32[]{:S(2)}) collective-permute-start(f32[15,16,8,2]{1,2,3,0:T(8,128)} %copy.14), channel_id=1, source_target_pairs={{0,2},{2,4},{4,6},{6,8},{8,10},{10,12},{12,14},{1,3},{3,5},{5,7},{... | collective-permute-start | bytes 46088 | tf_op jit(solution)/shard_map/ppermute | solution.py:29
  151.8 29.7 %collective-permute-start.21 = (f32[3,16,2,128]{3,2,1,0:T(2,128)S(1)}, f32[3,16,2,128]{3,2,1,0:T(2,128)S(1)}, u32[]{:S(2)}, u32[]{:S(2)}) collective-permute-start(f32[3,16,2,128]{3,2,1,0:T(2,128)S(1)} %get-tuple-element.134), channel_id=1, source_target_pairs={{16,0},{32,16},{48,32},{64,48},{80,64},{96,80},{112,96},{128,112},... | collective-permute-start | bytes 147464 | tf_op jit(solution)/shard_map/ppermute | solution.py:30
  153.1 28.5 %collective-permute-start.20 = (f32[3,16,2,128]{3,2,1,0:T(2,128)S(1)}, f32[3,16,2,128]{3,2,1,0:T(2,128)S(1)}, u32[]{:S(2)}, u32[]{:S(2)}) collective-permute-start(f32[3,16,2,128]{3,2,1,0:T(2,128)S(1)} %get-tuple-element.133), channel_id=1, source_target_pairs={{0,16},{16,32},{32,48},{48,64},{64,80},{80,96},{96,112},{112,128},... | collective-permute-start | bytes 147464 | tf_op jit(solution)/shard_map/ppermute | solution.py:29
  157.1 24.4 %collective-permute-start.19 = (f32[3,2,8,128]{3,2,1,0:T(8,128)S(1)}, f32[3,2,8,128]{3,2,1,0:T(8,128)S(1)}, u32[]{:S(2)}, u32[]{:S(2)}) collective-permute-start(f32[3,2,8,128]{3,2,1,0:T(8,128)S(1)} %get-tuple-element.118), channel_id=1, source_target_pairs={{1,0},{3,2},{5,4},{7,6},{9,8},{11,10},{13,12},{15,14},{17,16},{19,... | collective-permute-start | bytes 73736 | tf_op jit(solution)/shard_map/ppermute | solution.py:30
  158.4 23.1 %collective-permute-start.18 = (f32[3,2,8,128]{3,2,1,0:T(8,128)S(1)}, f32[3,2,8,128]{3,2,1,0:T(8,128)S(1)}, u32[]{:S(2)}, u32[]{:S(2)}) collective-permute-start(f32[3,2,8,128]{3,2,1,0:T(8,128)S(1)} %get-tuple-element.117), channel_id=1, source_target_pairs={{0,1},{2,3},{4,5},{6,7},{8,9},{10,11},{12,13},{14,15},{16,17},{18,... | collective-permute-start | bytes 73736 | tf_op jit(solution)/shard_map/ppermute | solution.py:29
  162.5 14.5 %collective-permute-start.23 = (f32[3,16,8,2]{3,2,1,0:T(8,128)S(1)}, f32[3,16,8,2]{3,2,1,0:T(8,128)S(1)}, u32[]{:S(2)}, u32[]{:S(2)}) collective-permute-start(f32[3,16,8,2]{3,2,1,0:T(8,128)S(1)} %get-tuple-element.136), channel_id=1, source_target_pairs={{2,0},{4,2},{6,4},{8,6},{10,8},{12,10},{14,12},{3,1},{5,3},{7,5},{... | collective-permute-start | bytes 9224 | tf_op jit(solution)/shard_map/ppermute | solution.py:30
  177.0 4.5 %collective-permute-start.22 = (f32[3,16,8,2]{3,2,1,0:T(8,128)S(1)}, f32[3,16,8,2]{3,2,1,0:T(8,128)S(1)}, u32[]{:S(2)}, u32[]{:S(2)}) collective-permute-start(f32[3,16,8,2]{3,2,1,0:T(8,128)S(1)} %get-tuple-element.135), channel_id=1, source_target_pairs={{0,2},{2,4},{4,6},{6,8},{8,10},{10,12},{12,14},{1,3},{3,5},{5,7},{... | collective-permute-start | bytes 9224 | tf_op jit(solution)/shard_map/ppermute | solution.py:29
  (34 other events, 118.0 us)
where the time goes:
time: 235 us; the launch traced here: 234 us
  starting transfers between devices  71.9 us (31%)
  other arithmetic  55.5 us (24%)
  blocking collectives  48.2 us (21%)
  local copies, waits for them, and re-layouts  28.2 us (12%)
  waiting for transfers between devices  25.2 us (11%)
  between operations  4.7 us (2%)
    ppermute x12, starting transfers between devices, extended_2(): lax.ppermute(last, axis, up)  52.4 us
    psum x5, blocking collectives, over_axes(): array = lax.psum(array, axis)  48.2 us
    ppermute x12, waiting for transfers between devices, extended_2(): lax.ppermute(first, axis, [(b, a) for a, b in up])  20 us
    ppermute x12, starting transfers between devices, extended_2(): lax.ppermute(first, axis, [(b, a) for a, b in up])  19.5 us
    scatter-add x1, other arithmetic, local(): seed_flat.at[0, probes].add(-weight_probe * probe_speed / probe_density)  11.8 us
    scatter-add x1, other arithmetic, local(): seed_flat = seed_flat.at[1, probes].add(weight_probe / probe_density)  11.8 us
    slice x10, local copies, waits for them, and re-layouts, extended_2(): last = lax.slice_in_dim(array, length - width, length, axis=dim)  5.95 us
    ppermute x12, waiting for transfers between devices, extended_2(): lax.ppermute(last, axis, up)  5.15 us
  transfers between devices with their start and end apart: 24, of which 6 were waited for; matrix products, arithmetic and copies ran while one was open for 7% of the time, Pallas kernels for 0%

commit v1 on v0

v1 whole, which is shorter than its diff:
```python
import functools
import jax
import jax.numpy as jnp
from jax import lax
from jax.experimental import pallas as pl
from jax.experimental.pallas import tpu as pltpu
from jax.sharding import PartitionSpec as P

NZ, NX, NY = 16, 8, 128
CELLS = NZ * NX
bulk_modulus = 2.0
slope_coeff = 1.5
signal_speed = 2.5
time_ratio = 0.1
quad_viscosity = 4.0
small_eps = 1e-12
HALF_C = 0.5 * signal_speed
HALF_T = 0.5 * time_ratio
F32 = jnp.float32


def primitives(r, mx, my, mz, en, gamma):
    inv = 1.0 / (1.0 + r)
    ux, uy, uz = mx * inv, my * inv, mz * inv
    heat = en - 0.5 * (mx * ux + my * uy + mz * uz)
    press = bulk_modulus * (r + slope_coeff * r * r) + gamma * heat
    return ux, uy, uz, heat, press


def total_pressure(press, sw, r, slope):
    squeeze = jnp.minimum(slope, 0.0)
    return press + sw * quad_viscosity * (1.0 + r) * squeeze * squeeze


def flux(state, axis, speed, total):
    rows = [state[1 + axis]] + [state[1 + k] * speed for k in range(3)]
    rows[1 + axis] = rows[1 + axis] + total
    return rows + [(state[4] + total) * speed]


def upper_part(f, u):
    return 0.5 * f - HALF_C * u


def lower_part(f, u):
    return 0.5 * f + HALF_C * u


def layer(z):
    return pl.ds(NX * z, NX)


def x_row(x):
    return pl.ds(x, NZ, stride=NX)


def lanes():
    return lax.broadcasted_iota(jnp.int32, (NX, NY), 1)


def y_next(value, column, lane):
    return jnp.where(lane == NY - 1, column, pltpu.roll(value, NY - 1, 1))


def y_prev(value, column, lane):
    return jnp.where(lane == 0, column, pltpu.roll(value, 1, 1))


def inside(flag):
    return jnp.where(flag, 1.0, 0.0).astype(F32)


def masks(mesh):
    ix, iy, iz = lax.axis_index("gx"), lax.axis_index("gy"), lax.axis_index("gz")
    return (
        (inside(ix > 0), inside(ix < mesh["gx"] - 1)),
        (inside(iy > 0), inside(iy < mesh["gy"] - 1)),
        (inside(iz > 0), inside(iz < mesh["gz"] - 1)),
        iz == 0,
    )


def face_layer(is_first, depth):
    return jnp.where(is_first, NZ - 1 - depth, depth)


def dyn_layer(z):
    return pl.ds(pl.multiple_of(NX * z, NX), NX)


def pack_columns(values, lane):
    out = pltpu.roll(values[0], 1, 1)
    for i in range(1, len(values)):
        out = jnp.where(lane < 2 * i, out, pltpu.roll(values[i], 2 * i + 1, 1))
    return out


def prep_kernel(mesh, u_ref, g_ref, s_ref, xlo, xhi, ylo, yhi, zs, yown, yp):
    _, _, _, first = masks(mesh)
    for out, edge, second in ((xlo, 0, 1), (xhi, NX - 1, NX - 2)):
        st = [u_ref[k, x_row(edge), :] for k in range(5)]
        press = primitives(*st, g_ref[x_row(edge), :])[4]
        for k in range(5):
            out[k] = st[k]
        out[5] = press
        out[6] = s_ref[0, x_row(edge), :].astype(F32)
        out[7] = u_ref[1, x_row(second), :] / (1.0 + u_ref[0, x_row(second), :])
    za, zb = face_layer(first, 0), face_layer(first, 1)
    st = [u_ref[k, dyn_layer(za), :] for k in range(5)]
    for k in range(5):
        zs[k] = st[k]
    zs[5] = primitives(*st, g_ref[dyn_layer(za), :])[4]
    zs[6] = s_ref[0, dyn_layer(za), :].astype(F32)
    zs[7] = u_ref[3, dyn_layer(zb), :] / (1.0 + u_ref[0, dyn_layer(zb), :])
    lane = lanes()
    for z in range(NZ):
        vals = [u_ref[k, layer(z), :] for k in range(5)]
        vals += [g_ref[layer(z), :], s_ref[0, layer(z), :].astype(F32)]
        out = pltpu.roll(vals[0], 2, 1)
        for i in range(1, 7):
            out = jnp.where(lane < 4 * i, out, pltpu.roll(vals[i], 4 * i + 2, 1))
        yp[layer(z), :] = out
    rows = yp[...].T
    for out, edge, second, own in ((yhi, 1, 0, 1), (ylo, 2, 3, 0)):
        st = [rows[4 * k + edge : 4 * k + edge + 1] for k in range(7)]
        prim = primitives(*st[:6])
        for k in range(5):
            out[k : k + 1] = st[k]
        out[5:6] = prim[4]
        out[6:7] = st[6]
        out[7:8] = rows[8 + second : 9 + second] / (1.0 + rows[second : second + 1])
        yown[own : own + 1] = prim[1]


def step_kernel(
    mesh, u_ref, g_ref, s_ref, xl, xh, yl, yh, zr, yown,
    o_ref, xlo, xhi, ylo, yhi, zs,
    vx, vy, vz, pr, ax, bx, az, bz, ch, yr, yc, yp,
):
    (mxl, mxh), (myl, myh), (mzl, mzh), first = masks(mesh)
    lane = lanes()
    for z in range(NZ):
        ux, uy, uz, _, press = primitives(*[u_ref[k, layer(z), :] for k in range(5)], g_ref[layer(z), :])
        vx[pl.ds(24 * z + 8, 8), :] = ux
        vy[layer(z), :] = uy
        vz[layer(z + 1), :] = uz
        pr[layer(z), :] = press
    low = [xl[k] * mxl for k in range(8)]
    high = [xh[k] * mxh for k in range(8)]
    speed = low[1] / (1.0 + low[0])
    vx[pl.ds(7, NZ, stride=24), :] = speed
    slope = 0.5 * (vx[pl.ds(8, NZ, stride=24), :] - low[7])
    fl = flux(low[:5], 0, speed, total_pressure(low[5], low[6], low[0], slope))
    for k in range(5):
        bx[k, pl.ds(7, NZ, stride=16), :] = lower_part(fl[k], low[k])
    speed = high[1] / (1.0 + high[0])
    vx[pl.ds(16, NZ, stride=24), :] = speed
    slope = 0.5 * (high[7] - vx[pl.ds(15, NZ, stride=24), :])
    fl = flux(high[:5], 0, speed, total_pressure(high[5], high[6], high[0], slope))
    for k in range(5):
        ax[k, pl.ds(8, NZ, stride=16), :] = upper_part(fl[k], high[k])
    far = [zr[k] for k in range(8)]
    speed = far[3] / (1.0 + far[0])
    own = vz[dyn_layer(face_layer(first, 0) + 1), :]
    slope = (far[7] - own) * jnp.where(first, 0.5, -0.5)
    fl = flux(far[:5], 2, speed, total_pressure(far[5], far[6], far[0], slope))
    for k in range(5):
        bz[k, layer(0), :] = lower_part(fl[k], far[k]) * mzl
        az[k, layer(NZ), :] = upper_part(fl[k], far[k]) * mzh
    vz[layer(0), :] = speed * mzl
    vz[layer(NZ + 1), :] = speed * mzh
    low = [yl[k : k + 1] * myl for k in range(8)]
    high = [yh[k : k + 1] * myh for k in range(8)]
    speed = low[2] / (1.0 + low[0])
    yr[10:11, :] = speed
    slope = 0.5 * (yown[0:1] - low[7])
    fl = flux(low[:5], 1, speed, total_pressure(low[5], low[6], low[0], slope))
    for k in range(5):
        yr[k : k + 1, :] = lower_part(fl[k], low[k])
    speed = high[2] / (1.0 + high[0])
    yr[11:12, :] = speed
    slope = 0.5 * (high[7] - yown[1:2])
    fl = flux(high[:5], 1, speed, total_pressure(high[5], high[6], high[0], slope))
    for k in range(5):
        yr[5 + k : 6 + k, :] = upper_part(fl[k], high[k])
    yr[12:16, :] = jnp.zeros((4, NY), F32)
    yc[...] = yr[...].T
    for z in range(NZ):
        st = [u_ref[k, layer(z), :] for k in range(5)]
        sw = s_ref[0, layer(z), :].astype(F32)
        press = pr[layer(z), :]
        visc = sw * quad_viscosity * (1.0 + st[0])
        uy = vy[layer(z), :]
        ux = vx[pl.ds(24 * z + 8, 8), :]
        uz = vz[layer(z + 1), :]

        def col(i):
            return yc[layer(z), i : i + 1]

        def total(up, down):
            squeeze = jnp.minimum(0.5 * (up - down), 0.0)
            return press + visc * squeeze * squeeze

        fx = flux(st, 0, ux, total(vx[pl.ds(24 * z + 9, 8), :], vx[pl.ds(24 * z + 7, 8), :]))
        fy = flux(st, 1, uy, total(y_next(uy, col(11), lane), y_prev(uy, col(10), lane)))
        fz = flux(st, 2, uz, total(vz[layer(z + 2), :], vz[layer(z), :]))
        for k in range(5):
            ax[k, pl.ds(16 * z, 8), :] = upper_part(fx[k], st[k])
            bx[k, pl.ds(16 * z + 8, 8), :] = lower_part(fx[k], st[k])
            az[k, layer(z), :] = upper_part(fz[k], st[k])
            bz[k, layer(z + 1), :] = lower_part(fz[k], st[k])
            ch[k, layer(z), :] = (
                3.0 * signal_speed * st[k]
                + y_next(upper_part(fy[k], st[k]), col(5 + k), lane)
                - y_prev(lower_part(fy[k], st[k]), col(k), lane)
            )
    for z in range(NZ):
        new = []
        for k in range(5):
            change = (
                ch[k, layer(z), :]
                + (ax[k, pl.ds(16 * z + 1, 8), :] - bx[k, pl.ds(16 * z + 7, 8), :])
                + (az[k, layer(z + 1), :] - bz[k, layer(z), :])
            )
            new.append(u_ref[k, layer(z), :] - time_ratio * change)
            o_ref[k, layer(z), :] = new[k]
        yp[layer(z), :] = pack_columns(new[:3], lane)
    for out, edge, second in ((xlo, 0, 1), (xhi, NX - 1, NX - 2)):
        st = [o_ref[k, x_row(edge), :] for k in range(5)]
        out[0] = st[0]
        out[1] = st[1]
        out[2] = primitives(*st, g_ref[x_row(edge), :])[4]
        out[3] = s_ref[1, x_row(edge), :].astype(F32)
        out[4] = o_ref[1, x_row(second), :] / (1.0 + o_ref[0, x_row(second), :])
    za = face_layer(first, 0)
    r, mx, mz = [o_ref[k, dyn_layer(za), :] for k in (0, 1, 3)]
    sign = jnp.where(first, HALF_C, -HALF_C)
    zs[0] = 0.5 * mz + sign * r
    zs[1] = 0.5 * mx * (mz / (1.0 + r)) + sign * mx
    rows = yp[...].T
    r, mx, my = rows[0:1], rows[2:3], rows[4:5]
    yhi[...] = jnp.zeros((8, NY), F32)
    yhi[0:1] = lower_part(my, r)
    yhi[1:2] = lower_part(mx * (my / (1.0 + r)), mx)
    r, mx, my = rows[1:2], rows[3:4], rows[5:6]
    ylo[...] = jnp.zeros((8, NY), F32)
    ylo[0:1] = upper_part(my, r)
    ylo[1:2] = upper_part(mx * (my / (1.0 + r)), mx)


def columns_of(low, high, count, low_mask, high_mask):
    rows = [low[k : k + 1] * low_mask for k in range(count)]
    rows += [high[k : k + 1] * high_mask for k in range(count)]
    rows.append(jnp.zeros((8 - 2 * count, NY), F32))
    return jnp.concatenate(rows, axis=0).T


def speed_kernel(
    mesh, u_ref, g_ref, s_ref, xl, xh, yl, yh, zr, n_ref, m_ref,
    lam_ref, cf_ref, cfh_ref, mis_ref, xlo, xhi, ylo, yhi, zs,
    vx, ax, bx, az, bz, ch, yc, yp,
):
    (mxl, mxh), (myl, myh), (mzl, mzh), first = masks(mesh)
    lane = lanes()
    for z in range(NZ):
        vx[pl.ds(24 * z + 8, 8), :] = u_ref[1, layer(z), :] / (1.0 + u_ref[0, layer(z), :])
    for side, ref, mask in ((0, xl, mxl), (1, xh, mxh)):
        r, mx, press, sw, second = [ref[k] * mask for k in range(5)]
        speed = mx / (1.0 + r)
        vx[pl.ds(16 if side else 7, NZ, stride=24), :] = speed
        own = vx[pl.ds(15 if side else 8, NZ, stride=24), :]
        slope = 0.5 * (second - own if side else own - second)
        squeeze = jnp.minimum(slope, 0.0)
        visc = sw * quad_viscosity * (1.0 + r) * squeeze
        cfh_ref[side] = 2.0 * visc
        f1 = mx * speed + press + visc * squeeze
        if side:
            ax[0, pl.ds(8, NZ, stride=16), :] = upper_part(mx, r)
            ax[1, pl.ds(8, NZ, stride=16), :] = upper_part(f1, mx)
        else:
            bx[0, pl.ds(7, NZ, stride=16), :] = lower_part(mx, r)
            bx[1, pl.ds(7, NZ, stride=16), :] = lower_part(f1, mx)
    for k in range(2):
        bz[k, layer(0), :] = zr[k] * mzl
        az[k, layer(NZ), :] = zr[k] * mzh
    yc[...] = columns_of(yl, yh, 2, myl, myh)
    for z in range(NZ):
        r, mx, my, mz, en = [u_ref[k, layer(z), :] for k in range(5)]
        ux, uy, uz, _, press = primitives(r, mx, my, mz, en, g_ref[layer(z), :])
        squeeze = jnp.minimum(0.5 * (vx[pl.ds(24 * z + 9, 8), :] - vx[pl.ds(24 * z + 7, 8), :]), 0.0)
        visc = s_ref[1, layer(z), :].astype(F32) * quad_viscosity * (1.0 + r) * squeeze
        cf_ref[layer(z), :] = 2.0 * visc
        f1 = mx * ux + press + visc * squeeze
        for k, st, fx, fy, fz in ((0, r, mx, my, mz), (1, mx, f1, mx * uy, mx * uz)):
            ax[k, pl.ds(16 * z, 8), :] = upper_part(fx, st)
            bx[k, pl.ds(16 * z + 8, 8), :] = lower_part(fx, st)
            az[k, layer(z), :] = upper_part(fz, st)
            bz[k, layer(z + 1), :] = lower_part(fz, st)
            ch[k, layer(z), :] = (
                3.0 * signal_speed * st
                + y_next(upper_part(fy, st), yc[layer(z), 2 + k : 3 + k], lane)
                - y_prev(lower_part(fy, st), yc[layer(z), k : k + 1], lane)
            )
    mis = jnp.zeros((NX, NY), F32)
    for z in range(NZ):
        new = []
        for k in range(2):
            change = (
                ch[k, layer(z), :]
                + (ax[k, pl.ds(16 * z + 1, 8), :] - bx[k, pl.ds(16 * z + 7, 8), :])
                + (az[k, layer(z + 1), :] - bz[k, layer(z), :])
            )
            new.append(u_ref[k, layer(z), :] - time_ratio * change)
        inv = 1.0 / (1.0 + new[0])
        speed = new[1] * inv
        off = speed - m_ref[layer(z), :]
        weight = n_ref[layer(z), :] * off
        mis = mis + weight * off
        lam_m = 2.0 * weight * inv
        lam_r = -lam_m * speed
        lam_ref[0, layer(z), :] = lam_r
        lam_ref[1, layer(z), :] = lam_m
        yp[layer(z), :] = pack_columns([lam_r, lam_m], lane)
    mis_ref[...] = mis
    for out, edge, second in ((xlo, 0, 1), (xhi, NX - 1, NX - 2)):
        out[0] = lam_ref[0, x_row(edge), :]
        out[1] = lam_ref[1, x_row(edge), :]
        out[2] = lam_ref[1, x_row(second), :]
    za = face_layer(first, 0)
    for k in range(2):
        zs[k] = lam_ref[k, dyn_layer(za), :]
    rows = yp[...].T
    for k in range(2):
        yhi[k : k + 1] = rows[2 * k : 2 * k + 1]
        ylo[k : k + 1] = rows[2 * k + 1 : 2 * k + 2]
    yhi[2:8] = jnp.zeros((6, NY), F32)
    ylo[2:8] = jnp.zeros((6, NY), F32)


def adjoint_kernel(
    mesh, u_ref, g_ref, lam_ref, cf_ref, cfh_ref, xl, xh, yl, yh, zr,
    out_ref, dg_ref, xlo, xhi, ylo, yhi, zs,
    lx, lz, px, dx, yc, yp,
):
    (mxl, mxh), (myl, myh), (mzl, mzh), first = masks(mesh)
    lane = lanes()
    for k in range(2):
        for z in range(NZ):
            lx[k, pl.ds(24 * z + 8, 8), :] = lam_ref[k, layer(z), :]
            lz[k, layer(z + 1), :] = lam_ref[k, layer(z), :]
        lx[k, pl.ds(7, NZ, stride=24), :] = xl[k] * mxl
        lx[k, pl.ds(16, NZ, stride=24), :] = xh[k] * mxh
        lz[k, layer(0), :] = zr[k] * mzl
        lz[k, layer(NZ + 1), :] = zr[k] * mzh
    dx[pl.ds(7, NZ, stride=24), :] = HALF_T * (lam_ref[1, x_row(0), :] - xl[2] * mxl) * cfh_ref[0]
    dx[pl.ds(16, NZ, stride=24), :] = HALF_T * (xh[2] * mxh - lam_ref[1, x_row(NX - 1), :]) * cfh_ref[1]
    for z in range(NZ):
        phi = HALF_T * (lx[1, pl.ds(24 * z + 9, 8), :] - lx[1, pl.ds(24 * z + 7, 8), :])
        px[layer(z), :] = phi
        dx[pl.ds(24 * z + 8, 8), :] = phi * cf_ref[layer(z), :]
    yc[...] = columns_of(yl, yh, 2, myl, myh)
    for z in range(NZ):
        r, mx, my, mz, en = [u_ref[k, layer(z), :] for k in range(5)]
        gamma = g_ref[layer(z), :]
        inv = 1.0 / (1.0 + r)
        ux, uy, uz = mx * inv, my * inv, mz * inv
        heat = en - 0.5 * (mx * ux + my * uy + mz * uz)
        lr, lm = lam_ref[0, layer(z), :], lam_ref[1, layer(z), :]
        lr_x = [lx[0, pl.ds(24 * z + s, 8), :] for s in (7, 9)]
        lm_x = [lx[1, pl.ds(24 * z + s, 8), :] for s in (7, 9)]
        lr_z = [lz[0, layer(z + s), :] for s in (0, 2)]
        lm_z = [lz[1, layer(z + s), :] for s in (0, 2)]
        lr_y = [y_prev(lr, yc[layer(z), 0:1], lane), y_next(lr, yc[layer(z), 2:3], lane)]
        lm_y = [y_prev(lm, yc[layer(z), 1:2], lane), y_next(lm, yc[layer(z), 3:4], lane)]
        phi_x0 = HALF_T * (lr_x[1] - lr_x[0])
        phi_y0 = HALF_T * (lr_y[1] - lr_y[0])
        phi_z0 = HALF_T * (lr_z[1] - lr_z[0])
        phi_x1 = px[layer(z), :]
        phi_y1 = HALF_T * (lm_y[1] - lm_y[0])
        phi_z1 = HALF_T * (lm_z[1] - lm_z[0])
        near = (lm_x[0] + lm_x[1]) + (lm_y[0] + lm_y[1]) + (lm_z[0] + lm_z[1])
        d_speed = phi_x1 * mx + 0.5 * (dx[pl.ds(24 * z + 7, 8), :] - dx[pl.ds(24 * z + 9, 8), :])
        d_en = phi_x1 * gamma
        out_mx = (
            lm * (1.0 - 3.0 * time_ratio * signal_speed)
            + (time_ratio * HALF_C) * near
            + phi_x0
            + (phi_x1 - d_en) * ux
            + phi_y1 * uy
            + phi_z1 * uz
            + d_speed * inv
        )
        out_my = phi_y0 - d_en * uy + phi_y1 * ux
        out_mz = phi_z0 - d_en * uz + phi_z1 * ux
        out_ref[0, layer(z), :] = out_mx
        out_ref[1, layer(z), :] = out_my
        out_ref[2, layer(z), :] = out_mz
        out_ref[3, layer(z), :] = d_en
        dg_ref[layer(z), :] = phi_x1 * heat
        yp[layer(z), :] = pack_columns([out_my, d_en], lane)
    for out, edge in ((xlo, 0), (xhi, NX - 1)):
        out[0] = out_ref[0, x_row(edge), :]
        out[1] = out_ref[3, x_row(edge), :]
    za = face_layer(first, 0)
    zs[0] = out_ref[2, dyn_layer(za), :]
    zs[1] = out_ref[3, dyn_layer(za), :]
    rows = yp[...].T
    for k in range(2):
        yhi[k : k + 1] = rows[2 * k : 2 * k + 1]
        ylo[k : k + 1] = rows[2 * k + 1 : 2 * k + 2]
    yhi[2:8] = jnp.zeros((6, NY), F32)
    ylo[2:8] = jnp.zeros((6, NY), F32)


def gradient_kernel(
    mesh, u_ref, lam_ref, dg_ref, mis_ref, v_ref, xl, xh, yl, yh, zr,
    grad_ref, row_ref,
    lx, lz, yc,
):
    (mxl, mxh), (myl, myh), (mzl, mzh), first = masks(mesh)
    lane = lanes()
    for k in range(2):
        for z in range(NZ):
            lx[k, pl.ds(24 * z + 8, 8), :] = lam_ref[3 * k, layer(z), :]
            lz[k, layer(z + 1), :] = lam_ref[2 + k, layer(z), :]
        lx[k, pl.ds(7, NZ, stride=24), :] = xl[k] * mxl
        lx[k, pl.ds(16, NZ, stride=24), :] = xh[k] * mxh
        lz[k, layer(0), :] = zr[k] * mzl
        lz[k, layer(NZ + 1), :] = zr[k] * mzh
    yc[...] = columns_of(yl, yh, 2, myl, myh)
    acc = jnp.zeros((NX, NY), F32)
    for z in range(NZ):
        r, mx, my, mz, en = [u_ref[k, layer(z), :] for k in range(5)]
        inv = 1.0 / (1.0 + r)
        ux, uy, uz = mx * inv, my * inv, mz * inv
        heat = en - 0.5 * (mx * ux + my * uy + mz * uz)
        dif_x = [lx[k, pl.ds(24 * z + 9, 8), :] - lx[k, pl.ds(24 * z + 7, 8), :] for k in range(2)]
        dif_z = [lz[k, layer(z + 2), :] - lz[k, layer(z), :] for k in range(2)]
        dif_y = []
        for k in range(2):
            own = lam_ref[1 + 2 * k, layer(z), :]
            dif_y.append(
                y_next(own, yc[layer(z), 2 + k : 3 + k], lane) - y_prev(own, yc[layer(z), k : k + 1], lane)
            )
        d_press = HALF_T * (
            (dif_x[0] + ux * dif_x[1]) + (dif_y[0] + uy * dif_y[1]) + (dif_z[0] + uz * dif_z[1])
        )
        grad = dg_ref[layer(z), :] + d_press * heat
        grad_ref[layer(z), :] = grad
        acc = acc + grad * grad
    total = jnp.sum(jnp.sum(acc, axis=0, keepdims=True), axis=1, keepdims=True)
    miss = jnp.sum(jnp.sum(mis_ref[...], axis=0, keepdims=True), axis=1, keepdims=True)
    miss = miss + jnp.sum(v_ref[...], axis=1, keepdims=True)
    row_ref[...] = jnp.where(lane == 0, total, jnp.where(lane == 1, miss, 0.0))


def split3(value):
    hi = value.astype(jnp.bfloat16)
    rest = value - hi.astype(F32)
    mid = rest.astype(jnp.bfloat16)
    low = (rest - mid.astype(F32)).astype(jnp.bfloat16)
    return hi, mid, low


def probe_kernel(p_ref, o_ref, n_ref, m_ref, v_ref):
    count = p_ref.shape[1]
    probes, obs = p_ref[...], o_ref[...]
    row = lax.broadcasted_iota(jnp.int32, (CELLS, count), 0)
    on_a = row == lax.shift_right_logical(probes, 7)
    on_b = row == lax.bitwise_and(probes, NY - 1)
    one_a = jnp.where(on_a, 1.0, 0.0).astype(jnp.bfloat16)
    one_b = jnp.where(on_b, 1.0, 0.0).astype(jnp.bfloat16)

    def nt(a, b):
        return lax.dot_general(a, b, (((1,), (1,)), ((), ())), preferred_element_type=F32)

    parts = [jnp.where(on_a, part.astype(F32), 0.0).astype(jnp.bfloat16) for part in split3(obs)]
    hits = nt(one_a, one_b)
    sums = nt(parts[0], one_b) + (nt(parts[1], one_b) + nt(parts[2], one_b))
    n_ref[...] = hits
    mean = sums / jnp.maximum(hits, 1.0)
    m_ref[...] = mean
    mean_t = split3(mean.T)
    picked = sum(jnp.dot(part, one_a, preferred_element_type=F32) for part in reversed(mean_t))
    at_probe = jnp.sum(jnp.where(on_b, picked, 0.0), axis=0, keepdims=True)
    off = obs - at_probe
    v_ref[...] = off * off


def rows_of(*shape):
    return jax.ShapeDtypeStruct(shape, F32)


def vmem(*shape):
    return pltpu.VMEM(shape, F32)


def call(kernel, outs, scratch, flops=100000):
    return pl.pallas_call(
        kernel,
        out_shape=outs,
        scratch_shapes=scratch,
        cost_estimate=pl.CostEstimate(flops=flops, bytes_accessed=100000, transcendentals=0),
    )


def exchange(sizes, xlo, xhi, ylo, yhi, zs):
    def ring(axis, step):
        n = sizes[axis]
        return [(i, (i + step) % n) for i in range(n)]

    zr = lax.ppermute(zs, "gz", ring("gz", 1))
    xl = lax.ppermute(xhi, "gx", ring("gx", 1))
    xh = lax.ppermute(xlo, "gx", ring("gx", -1))
    yl = lax.ppermute(yhi, "gy", ring("gy", 1))
    yh = lax.ppermute(ylo, "gy", ring("gy", -1))
    return xl, xh, yl, yh, zr


def local(sizes, checkpoint, gruneisen, switch, probes, observed):
    bind = functools.partial
    state = checkpoint.reshape(5, CELLS, NY)
    gamma = gruneisen.reshape(CELLS, NY)
    sw = switch.reshape(2, CELLS, NY)
    plane = rows_of(8, NY)

    def slabs(x_items, z_items):
        x = rows_of(x_items, NZ, NY)
        return [x, x, plane, plane, rows_of(z_items, NX, NY)]

    *sent, yown = call(bind(prep_kernel, sizes), slabs(8, 8) + [plane], [vmem(CELLS, NY)])(state, gamma, sw)
    got = exchange(sizes, *sent)
    hits, mean, spread = call(
        probe_kernel,
        [rows_of(CELLS, NY), rows_of(CELLS, NY), rows_of(1, probes.shape[0])],
        [],
    )(probes.reshape(1, -1), observed.reshape(1, -1))
    tall = (NZ + 2) * NX
    state_1, *sent = call(
        bind(step_kernel, sizes),
        [rows_of(5, CELLS, NY)] + slabs(5, 2),
        [
            vmem(NZ * 24, NY), vmem(CELLS, NY), vmem(tall, NY), vmem(CELLS, NY),
            vmem(5, NZ * 16, NY), vmem(5, NZ * 16, NY), vmem(5, tall, NY), vmem(5, tall, NY),
            vmem(5, CELLS, NY), vmem(16, NY), vmem(CELLS, 16), vmem(CELLS, NY),
        ],
    )(state, gamma, sw, *got, yown)
    got = exchange(sizes, *sent)
    lam_2, coef, coef_halo, mis, *sent = call(
        bind(speed_kernel, sizes),
        [rows_of(2, CELLS, NY), rows_of(CELLS, NY), rows_of(2, NZ, NY), plane] + slabs(3, 2),
        [
            vmem(NZ * 24, NY), vmem(2, NZ * 16, NY), vmem(2, NZ * 16, NY), vmem(2, tall, NY), vmem(2, tall, NY),
            vmem(2, CELLS, NY), vmem(CELLS, 8), vmem(CELLS, NY),
        ],
    )(state_1, gamma, sw, *got, hits, mean)
    got = exchange(sizes, *sent)
    lam_1, d_gamma, *sent = call(
        bind(adjoint_kernel, sizes),
        [rows_of(4, CELLS, NY), rows_of(CELLS, NY)] + slabs(2, 2),
        [
            vmem(2, NZ * 24, NY), vmem(2, tall, NY), vmem(CELLS, NY), vmem(NZ * 24, NY),
            vmem(CELLS, 8), vmem(CELLS, NY),
        ],
    )(state_1, gamma, lam_2, coef, coef_halo, *got)
    got = exchange(sizes, *sent)
    gradient, row = call(
        bind(gradient_kernel, sizes),
        [rows_of(CELLS, NY), plane],
        [vmem(2, NZ * 24, NY), vmem(2, tall, NY), vmem(CELLS, 8)],
    )(state, lam_1, d_gamma, mis, spread, *got)
    for axes in (("gy",), ("gx", "gz")):
        group = 1
        for axis in axes:
            group *= sizes[axis]
        row = jnp.broadcast_to(row[:1], (group, NY))
        row = jnp.sum(lax.all_to_all(row, axes, 0, 0, tiled=True), axis=0, keepdims=True)
    devices = sizes["gx"] * sizes["gy"] * sizes["gz"]
    direction = gradient / jnp.sqrt(row[0, 0] / (devices * CELLS * NY) + small_eps)
    misfit = row[0, 1] / (devices * probes.shape[0])
    return direction.reshape(NZ, NX, NY), misfit


def solution(mesh):
    block = P("gz", "gx", "gy")
    parted = P(None, "gz", "gx", "gy")
    listed = P(("gx", "gy", "gz"))
    return jax.shard_map(
        functools.partial(local, dict(mesh.shape)),
        mesh=mesh,
        in_specs=(parted, block, parted, listed, listed),
        out_specs=(block, P()),
        check_vma=False,
    )
```

time: 235 us -> 94 us (0.40)
  other arithmetic: 55.5 us -> 0.68 us
  starting transfers between devices: 71.9 us -> 32.8 us
  blocking collectives: 48.2 us -> 22.8 us
  local copies, waits for them, and re-layouts: 28.2 us -> 3.79 us
  Pallas kernels: 0 us -> 13.6 us
  waiting for transfers between devices: 25.2 us -> 16.6 us
    psum x5 -> x0, blocking collectives: 48.2 us -> none  [over_axes(): array = lax.psum(array, axis)]
    ppermute x24 -> x20, starting transfers between devices: 71.9 us -> 32.8 us  [the longest x4 18.1 us: exchange(): xh = lax.ppermute(xlo, 'gx', ring('gx', -1))]
    scatter-add x2 -> x0, other arithmetic: 23.7 us -> none  [the longest x1 11.8 us: local(): seed_flat.at[0, probes].add(-weight_probe * probe_speed / probe_density)]
    all_to_all x0 -> x2, blocking collectives: none -> 22.8 us  [local(): lax.all_to_all(row, axes, 0, 0, tiled=True)]
    slice x36 -> x2, local copies, waits for them, and re-layouts: 19.2 us -> 1.29 us  [the longest x1 0.7 us: local(): row = jnp.broadcast_to(row[:1], (group, NY))]
    pallas_call x0 -> x6, Pallas kernels: none -> 13.6 us  [the longest x1 3.28 us: local(): call(bind(step_kernel, sizes), [rows_of(5, CELLS, NY)] + slabs(5, 2), [vm...]
    ppermute x24 -> x20, waiting for transfers between devices: 25.2 us -> 16.6 us  [the longest x4 14.3 us: exchange(): yh = lax.ppermute(ylo, 'gy', ring('gy', -1))]
    add_any x16 -> x0, other arithmetic: 5.37 us -> none  [the longest x6 2.17 us: advance(): momentum_rows = [state_mid[1 + member] * speed_mid for member in range(3)]]
  transfers between devices with their start and end apart: 24 -> 20, of which waited for: 6 -> 7; matrix products, arithmetic and copies ran while one was open for 7% -> 0% of each run, Pallas kernels for 0% -> 2%
where the time goes in v1:
time: 94 us; the launch traced here: 93.6 us
  starting transfers between devices  32.8 us (35%)
  blocking collectives  22.8 us (24%)
  waiting for transfers between devices  16.6 us (18%)
  Pallas kernels  13.6 us (14%)
  local copies, waits for them, and re-layouts  3.79 us (4%)
  between operations  3.35 us (4%)
    all_to_all x2, blocking collectives, local(): lax.all_to_all(row, axes, 0, 0, tiled=True)  22.8 us
    ppermute x4, starting transfers between devices, exchange(): xh = lax.ppermute(xlo, 'gx', ring('gx', -1))  18.1 us
    ppermute x4, waiting for transfers between devices, exchange(): yh = lax.ppermute(ylo, 'gy', ring('gy', -1))  14.3 us
    ppermute x4, starting transfers between devices, exchange(): yl = lax.ppermute(yhi, 'gy', ring('gy', 1))  9.16 us
    pallas_call x1, Pallas kernels, local(): call(bind(step_kernel, sizes), [rows_of(5, CELLS, NY)] + slabs(5, 2), [vm...  3.28 us
    ppermute x4, starting transfers between devices, exchange(): zr = lax.ppermute(zs, 'gz', ring('gz', 1))  3.11 us
    unnamed x58, local copies, waits for them, and re-layouts  2.48 us
    ppermute x4, starting transfers between devices, exchange(): xl = lax.ppermute(xhi, 'gx', ring('gx', 1))  2.36 us
  transfers between devices with their start and end apart: 20, of which 7 were waited for; matrix products, arithmetic and copies ran while one was open for 0% of the time, Pallas kernels for 2%

profile of v1, /device:TPU:1, one launch (start us, length us, event | category | flops | bytes accessed | tf_op | source)
XLA Modules:
  0.0 93.6 jit_solution(8977882485801374695)
XLA Ops:
  0.6 1.9 %shard_map.68 = (f32[8,16,128]{2,1,0:T(8,128)}, f32[8,16,128]{2,1,0:T(8,128)}, f32[8,128]{1,0:T(8,128)}, f32[8,128]{1,0:T(8,128)}, f32[8,8,128]{2,1,0:T(8,128)}, /*index=5*/f32[8,128]{1,0:T(8,128)}) custom-call(f32[5,128,128]{2,1,0:T(8,128)} %bitcast.14, f32[128,128]{1,0:T(8,128)} %bitcast.20, s32[2,128,128]{2,1,0:T(8,128)} %bitcast.17), custom_call_target="tpu_custom_call" | custom-call | flops 100000 | bytes 100000 | tf_op jit(solution)/shard_map/pallas_call | solution.py:531
  2.5 2.1 %collective-permute-start = (f32[8,16,128]{2,1,0:T(8,128)}, f32[8,16,128]{2,1,0:T(8,128)S(1)}, u32[]{:S(2)}, u32[]{:S(2)}) collective-permute-start(f32[8,16,128]{2,1,0:T(8,128)} %get-tuple-element.35), channel_id=1, source_target_pairs={{0,16},{16,32},{32,48},{48,64},{64,80},{80,96},{96,112},{112,128},... | collective-permute-start | bytes 196616 | tf_op jit(solution)/shard_map/ppermute | solution.py:513
  4.7 3.8 %collective-permute-start.1 = (f32[8,16,128]{2,1,0:T(8,128)}, f32[8,16,128]{2,1,0:T(8,128)S(1)}, u32[]{:S(2)}, u32[]{:S(2)}) collective-permute-start(f32[8,16,128]{2,1,0:T(8,128)} %get-tuple-element.36), channel_id=1, source_target_pairs={{0,240},{16,0},{32,16},{48,32},{64,48},{80,64},{96,80},{112,96},{1... | collective-permute-start | bytes 196616 | tf_op jit(solution)/shard_map/ppermute | solution.py:514
  8.5 1.6 %collective-permute-start.4 = (f32[8,8,128]{2,1,0:T(8,128)}, f32[8,8,128]{2,1,0:T(8,128)S(1)}, u32[]{:S(2)}, u32[]{:S(2)}) collective-permute-start(f32[8,8,128]{2,1,0:T(8,128)} %get-tuple-element.39), channel_id=1, source_target_pairs={{0,1},{1,0},{2,3},{3,2},{4,5},{5,4},{6,7},{7,6},{8,9},{9,8},{10,11... | collective-permute-start | bytes 98312 | tf_op jit(solution)/shard_map/ppermute | solution.py:512
  10.1 4.2 %collective-permute-start.2 = (f32[8,128]{1,0:T(8,128)S(1)}, f32[8,128]{1,0:T(8,128)S(1)}, u32[]{:S(2)}, u32[]{:S(2)}) collective-permute-start(f32[8,128]{1,0:T(8,128)S(1)} %copy-done.28), channel_id=1, source_target_pairs={{0,2},{2,4},{4,6},{6,8},{8,10},{10,12},{12,14},{14,0},{1,3},{3,5},... | collective-permute-start | bytes 12296 | tf_op jit(solution)/shard_map/ppermute | solution.py:515
  14.3 0.7 collective-permute-done.2.yl
  15.0 3.2 %collective-permute-done.3.yh = f32[8,128]{1,0:T(8,128)S(1)} collective-permute-done((f32[8,128]{1,0:T(8,128)S(1)}, f32[8,128]{1,0:T(8,128)S(1)}, u32[]{:S(2)}, u32[]{:S(2)}) %collective-permute-start.3) | collective-permute-done | bytes 4128 | tf_op jit(solution)/shard_map/ppermute | solution.py:516
  18.9 3.3 %shard_map.69 = (f32[5,128,128]{2,1,0:T(8,128)}, f32[5,16,128]{2,1,0:T(8,128)}, f32[5,16,128]{2,1,0:T(8,128)}, f32[8,128]{1,0:T(8,128)}, f32[8,128]{1,0:T(8,128)}, /*index=5*/f32[2,8,128]{2,1,0:T(8,128)}) custom-call(f32[5,128,128]{2,1,0:T(8,128)} %bitcast.15, f32[128,128]{1,0:T(8,128)} %bitcast.21, s32[2,128,128]{2,1,0:T(8,128)} %bitcast.18, ...), custom_call_target="tpu_custom_call" | custom-call | flops 100000 | bytes 100000 | tf_op jit(solution)/shard_map/pallas_call | solution.py:539
  22.2 4.8 %collective-permute-start.6 = (f32[5,16,128]{2,1,0:T(8,128)}, f32[5,16,128]{2,1,0:T(8,128)S(1)}, u32[]{:S(2)}, u32[]{:S(2)}) collective-permute-start(f32[5,16,128]{2,1,0:T(8,128)} %get-tuple-element.43), channel_id=1, source_target_pairs={{0,240},{16,0},{32,16},{48,32},{64,48},{80,64},{96,80},{112,96},{1... | collective-permute-start | bytes 122888 | tf_op jit(solution)/shard_map/ppermute | solution.py:514
  27.0 2.0 %collective-permute-start.7 = (f32[8,128]{1,0:T(8,128)S(1)}, f32[8,128]{1,0:T(8,128)S(1)}, u32[]{:S(2)}, u32[]{:S(2)}) collective-permute-start(f32[8,128]{1,0:T(8,128)S(1)} %copy-done.24), channel_id=1, source_target_pairs={{0,2},{2,4},{4,6},{6,8},{8,10},{10,12},{12,14},{14,0},{1,3},{3,5},... | collective-permute-start | bytes 12296 | tf_op jit(solution)/shard_map/ppermute | solution.py:515
  29.0 1.8 %shard_map.70 = (f32[128,128]{1,0:T(8,128)}, f32[128,128]{1,0:T(8,128)}, f32[1,256]{1,0:T(1,128)}) custom-call(s32[1,256]{1,0:T(1,128)} %bitcast.27, f32[1,256]{1,0:T(1,128)} %bitcast.28), custom_call_target="tpu_custom_call" | custom-call | flops 100000 | bytes 100000 | tf_op jit(solution)/shard_map/pallas_call | solution.py:533
  30.8 3.1 %collective-permute-done.8.yh = f32[8,128]{1,0:T(8,128)S(1)} collective-permute-done((f32[8,128]{1,0:T(8,128)S(1)}, f32[8,128]{1,0:T(8,128)S(1)}, u32[]{:S(2)}, u32[]{:S(2)}) %collective-permute-start.8) | collective-permute-done | bytes 4128 | tf_op jit(solution)/shard_map/ppermute | solution.py:516
  34.6 2.2 %shard_map.71 = (f32[2,128,128]{2,1,0:T(8,128)}, f32[128,128]{1,0:T(8,128)}, f32[2,16,128]{2,1,0:T(8,128)}, f32[8,128]{1,0:T(8,128)}, f32[3,16,128]{2,1,0:T(8,12...) custom-call(f32[5,128,128]{2,1,0:T(8,128)} %get-tuple-element.41.u_ref, ...), custom_call_target="tpu_custom_call" | custom-call | flops 100000 | bytes 100000 | tf_op jit(solution)/shard_map/pallas_call | solution.py:549
  36.9 4.8 %collective-permute-start.11 = (f32[3,16,128]{2,1,0:T(8,128)}, f32[3,16,128]{2,1,0:T(8,128)S(1)}, u32[]{:S(2)}, u32[]{:S(2)}) collective-permute-start(f32[3,16,128]{2,1,0:T(8,128)} %get-tuple-element.53), channel_id=1, source_target_pairs={{0,240},{16,0},{32,16},{48,32},{64,48},{80,64},{96,80},{112,96},{1... | collective-permute-start | bytes 73736 | tf_op jit(solution)/shard_map/ppermute | solution.py:514
  42.4 1.4 %collective-permute-start.12 = (f32[8,128]{1,0:T(8,128)S(1)}, f32[8,128]{1,0:T(8,128)S(1)}, u32[]{:S(2)}, u32[]{:S(2)}) collective-permute-start(f32[8,128]{1,0:T(8,128)S(1)} %copy-done.25), channel_id=1, source_target_pairs={{0,2},{2,4},{4,6},{6,8},{8,10},{10,12},{12,14},{14,0},{1,3},{3,5},... | collective-permute-start | bytes 12296 | tf_op jit(solution)/shard_map/ppermute | solution.py:515
  44.6 3.9 %collective-permute-done.13.yh = f32[8,128]{1,0:T(8,128)S(1)} collective-permute-done((f32[8,128]{1,0:T(8,128)S(1)}, f32[8,128]{1,0:T(8,128)S(1)}, u32[]{:S(2)}, u32[]{:S(2)}) %collective-permute-start.13) | collective-permute-done | bytes 4128 | tf_op jit(solution)/shard_map/ppermute | solution.py:516
  49.1 2.3 %shard_map.72 = (f32[4,128,128]{2,1,0:T(8,128)}, f32[128,128]{1,0:T(8,128)}, f32[2,16,128]{2,1,0:T(8,128)}, f32[2,16,128]{2,1,0:T(8,128)}, f32[8,128]{1,0:T(8,12...) custom-call(f32[5,128,128]{2,1,0:T(8,128)} %get-tuple-element.41.u_ref, f32[128,128]{1,0:T(8,128)} %bitcast.23, ...), custom_call_target="tpu_custom_call" | custom-call | flops 100000 | bytes 100000 | tf_op jit(solution)/shard_map/pallas_call | solution.py:558
  51.5 4.8 %collective-permute-start.16 = (f32[2,16,128]{2,1,0:T(8,128)}, f32[2,16,128]{2,1,0:T(8,128)S(1)}, u32[]{:S(2)}, u32[]{:S(2)}) collective-permute-start(f32[2,16,128]{2,1,0:T(8,128)} %get-tuple-element.62), channel_id=1, source_target_pairs={{0,240},{16,0},{32,16},{48,32},{64,48},{80,64},{96,80},{112,96},{1... | collective-permute-start | bytes 49160 | tf_op jit(solution)/shard_map/ppermute | solution.py:514
  57.0 1.6 %collective-permute-start.17 = (f32[8,128]{1,0:T(8,128)S(1)}, f32[8,128]{1,0:T(8,128)S(1)}, u32[]{:S(2)}, u32[]{:S(2)}) collective-permute-start(f32[8,128]{1,0:T(8,128)S(1)} %copy-done.26), channel_id=1, source_target_pairs={{0,2},{2,4},{4,6},{6,8},{8,10},{10,12},{12,14},{14,0},{1,3},{3,5},... | collective-permute-start | bytes 12296 | tf_op jit(solution)/shard_map/ppermute | solution.py:515
  58.7 0.7 collective-permute-done.17.yl
  59.4 4.2 %collective-permute-done.18.yh = f32[8,128]{1,0:T(8,128)S(1)} collective-permute-done((f32[8,128]{1,0:T(8,128)S(1)}, f32[8,128]{1,0:T(8,128)S(1)}, u32[]{:S(2)}, u32[]{:S(2)}) %collective-permute-start.18) | collective-permute-done | bytes 4128 | tf_op jit(solution)/shard_map/ppermute | solution.py:516
  64.2 2.1 %shard_map.73 = (f32[128,128]{1,0:T(8,128)}, f32[8,128]{1,0:T(8,128)}) custom-call(f32[5,128,128]{2,1,0:T(8,128)} %bitcast.16, f32[4,128,128]{2,1,0:T(8,128)} %get-tuple-element.57.lam_ref, f32[128,128]{1,0:T(8,128)} %get-tuple-element.58.dg_ref, f32[8,128]{1,0:T(8,128)} %get-tuple-element.59.mis_ref, f32[1,256]{1,0:T(1,128)} %get-tuple-element.60.v_ref, ...), custom_call_target="tpu_custom_call" | custom-call | flops 100000 | bytes 100000 | tf_op jit(solution)/shard_map/pallas_call | solution.py:567
  67.0 12.8 %all_to_all.12 = f32[8,1,128]{2,1,0:T(1,128)S(1)} all-to-all(f32[8,1,128]{2,1,0:T(1,128)S(1)} %broadcast_in_dim.6), channel_id=1, replica_groups=mesh['gx'=16,'gy'=8,'gz'=2] {'gy'}, dimensions={0} | all-to-all | bytes 8192 | tf_op jit(solution)/shard_map/all_to_all | solution.py:577
  79.8 10.1 %all_to_all.13 = f32[32,1,128]{2,1,0:T(1,128)S(1)} all-to-all(f32[32,1,128]{2,1,0:T(1,128)S(1)} %broadcast_in_dim.7), channel_id=1, replica_groups=mesh['gx'=16,'gy'=8,'gz'=2] {'gx','gz'}, dimensions={0} | all-to-all | bytes 32768 | tf_op jit(solution)/shard_map/all_to_all | solution.py:577
  (89 shorter events, 7.0 us)
Async XLA Ops:
  2.5 7.6 %copy-start.28 = (f32[8,128]{1,0:T(8,128)S(1)}, f32[8,128]{1,0:T(8,128)}, u32[]{:S(2)}) copy-start(f32[8,128]{1,0:T(8,128)} %get-tuple-element.37) | copy-start | bytes 12292
  2.5 11.7 %copy-start.27 = (f32[8,128]{1,0:T(8,128)S(1)}, f32[8,128]{1,0:T(8,128)}, u32[]{:S(2)}) copy-start(f32[8,128]{1,0:T(8,128)} %get-tuple-element.38) | copy-start | bytes 12292
  2.5 15.7 %collective-permute-start = (f32[8,16,128]{2,1,0:T(8,128)}, f32[8,16,128]{2,1,0:T(8,128)S(1)}, u32[]{:S(2)}, u32[]{:S(2)}) collective-permute-start(f32[8,16,128]{2,1,0:T(8,128)} %get-tuple-element.35), channel_id=1, source_target_pairs={{0,16},{16,32},{32,48},{48,64},{64,80},{80,96},{96,112},{112,128},... | collective-permute-start | bytes 196616 | tf_op jit(solution)/shard_map/ppermute | solution.py:513
  4.7 13.6 %collective-permute-start.1 = (f32[8,16,128]{2,1,0:T(8,128)}, f32[8,16,128]{2,1,0:T(8,128)S(1)}, u32[]{:S(2)}, u32[]{:S(2)}) collective-permute-start(f32[8,16,128]{2,1,0:T(8,128)} %get-tuple-element.36), channel_id=1, source_target_pairs={{0,240},{16,0},{32,16},{48,32},{64,48},{80,64},{96,80},{112,96},{1... | collective-permute-start | bytes 196616 | tf_op jit(solution)/shard_map/ppermute | solution.py:514
  8.5 9.7 %collective-permute-start.4 = (f32[8,8,128]{2,1,0:T(8,128)}, f32[8,8,128]{2,1,0:T(8,128)S(1)}, u32[]{:S(2)}, u32[]{:S(2)}) collective-permute-start(f32[8,8,128]{2,1,0:T(8,128)} %get-tuple-element.39), channel_id=1, source_target_pairs={{0,1},{1,0},{2,3},{3,2},{4,5},{5,4},{6,7},{7,6},{8,9},{9,8},{10,11... | collective-permute-start | bytes 98312 | tf_op jit(solution)/shard_map/ppermute | solution.py:512
  10.1 4.9 %collective-permute-start.2 = (f32[8,128]{1,0:T(8,128)S(1)}, f32[8,128]{1,0:T(8,128)S(1)}, u32[]{:S(2)}, u32[]{:S(2)}) collective-permute-start(f32[8,128]{1,0:T(8,128)S(1)} %copy-done.28), channel_id=1, source_target_pairs={{0,2},{2,4},{4,6},{6,8},{8,10},{10,12},{12,14},{14,0},{1,3},{3,5},... | collective-permute-start | bytes 12296 | tf_op jit(solution)/shard_map/ppermute | solution.py:515
  14.3 3.9 %collective-permute-start.3 = (f32[8,128]{1,0:T(8,128)S(1)}, f32[8,128]{1,0:T(8,128)S(1)}, u32[]{:S(2)}, u32[]{:S(2)}) collective-permute-start(f32[8,128]{1,0:T(8,128)S(1)} %copy-done.27), channel_id=1, source_target_pairs={{0,14},{2,0},{4,2},{6,4},{8,6},{10,8},{12,10},{14,12},{1,15},{3,1}... | collective-permute-start | bytes 12296 | tf_op jit(solution)/shard_map/ppermute | solution.py:516
  22.2 11.8 %collective-permute-start.5 = (f32[5,16,128]{2,1,0:T(8,128)}, f32[5,16,128]{2,1,0:T(8,128)S(1)}, u32[]{:S(2)}, u32[]{:S(2)}) collective-permute-start(f32[5,16,128]{2,1,0:T(8,128)} %get-tuple-element.42), channel_id=1, source_target_pairs={{0,16},{16,32},{32,48},{48,64},{64,80},{80,96},{96,112},{112,128},... | collective-permute-start | bytes 122888 | tf_op jit(solution)/shard_map/ppermute | solution.py:513
  22.2 11.7 %collective-permute-start.6 = (f32[5,16,128]{2,1,0:T(8,128)}, f32[5,16,128]{2,1,0:T(8,128)S(1)}, u32[]{:S(2)}, u32[]{:S(2)}) collective-permute-start(f32[5,16,128]{2,1,0:T(8,128)} %get-tuple-element.43), channel_id=1, source_target_pairs={{0,240},{16,0},{32,16},{48,32},{64,48},{80,64},{96,80},{112,96},{1... | collective-permute-start | bytes 122888 | tf_op jit(solution)/shard_map/ppermute | solution.py:514
  27.0 6.9 %collective-permute-start.9 = (f32[2,8,128]{2,1,0:T(8,128)}, f32[2,8,128]{2,1,0:T(8,128)S(1)}, u32[]{:S(2)}, u32[]{:S(2)}) collective-permute-start(f32[2,8,128]{2,1,0:T(8,128)} %get-tuple-element.46), channel_id=1, source_target_pairs={{0,1},{1,0},{2,3},{3,2},{4,5},{5,4},{6,7},{7,6},{8,9},{9,8},{10,11... | collective-permute-start | bytes 24584 | tf_op jit(solution)/shard_map/ppermute | solution.py:512
  27.0 3.8 %collective-permute-start.7 = (f32[8,128]{1,0:T(8,128)S(1)}, f32[8,128]{1,0:T(8,128)S(1)}, u32[]{:S(2)}, u32[]{:S(2)}) collective-permute-start(f32[8,128]{1,0:T(8,128)S(1)} %copy-done.24), channel_id=1, source_target_pairs={{0,2},{2,4},{4,6},{6,8},{8,10},{10,12},{12,14},{14,0},{1,3},{3,5},... | collective-permute-start | bytes 12296 | tf_op jit(solution)/shard_map/ppermute | solution.py:515
  29.0 4.9 %collective-permute-start.8 = (f32[8,128]{1,0:T(8,128)S(1)}, f32[8,128]{1,0:T(8,128)S(1)}, u32[]{:S(2)}, u32[]{:S(2)}) collective-permute-start(f32[8,128]{1,0:T(8,128)S(1)} %copy-done.21), channel_id=1, source_target_pairs={{0,14},{2,0},{4,2},{6,4},{8,6},{10,8},{12,10},{14,12},{1,15},{3,1}... | collective-permute-start | bytes 12296 | tf_op jit(solution)/shard_map/ppermute | solution.py:516
  36.8 11.6 %collective-permute-start.10 = (f32[3,16,128]{2,1,0:T(8,128)}, f32[3,16,128]{2,1,0:T(8,128)S(1)}, u32[]{:S(2)}, u32[]{:S(2)}) collective-permute-start(f32[3,16,128]{2,1,0:T(8,128)} %get-tuple-element.52), channel_id=1, source_target_pairs={{0,16},{16,32},{32,48},{48,64},{64,80},{80,96},{96,112},{112,128},... | collective-permute-start | bytes 73736 | tf_op jit(solution)/shard_map/ppermute | solution.py:513
  36.9 11.6 %collective-permute-start.11 = (f32[3,16,128]{2,1,0:T(8,128)}, f32[3,16,128]{2,1,0:T(8,128)S(1)}, u32[]{:S(2)}, u32[]{:S(2)}) collective-permute-start(f32[3,16,128]{2,1,0:T(8,128)} %get-tuple-element.53), channel_id=1, source_target_pairs={{0,240},{16,0},{32,16},{48,32},{64,48},{80,64},{96,80},{112,96},{1... | collective-permute-start | bytes 73736 | tf_op jit(solution)/shard_map/ppermute | solution.py:514
  41.7 6.8 %collective-permute-start.14 = (f32[2,8,128]{2,1,0:T(8,128)}, f32[2,8,128]{2,1,0:T(8,128)S(1)}, u32[]{:S(2)}, u32[]{:S(2)}) collective-permute-start(f32[2,8,128]{2,1,0:T(8,128)} %get-tuple-element.56), channel_id=1, source_target_pairs={{0,1},{1,0},{2,3},{3,2},{4,5},{5,4},{6,7},{7,6},{8,9},{9,8},{10,11... | collective-permute-start | bytes 24584 | tf_op jit(solution)/shard_map/ppermute | solution.py:512
  42.4 2.2 %collective-permute-start.12 = (f32[8,128]{1,0:T(8,128)S(1)}, f32[8,128]{1,0:T(8,128)S(1)}, u32[]{:S(2)}, u32[]{:S(2)}) collective-permute-start(f32[8,128]{1,0:T(8,128)S(1)} %copy-done.25), channel_id=1, source_target_pairs={{0,2},{2,4},{4,6},{6,8},{8,10},{10,12},{12,14},{14,0},{1,3},{3,5},... | collective-permute-start | bytes 12296 | tf_op jit(solution)/shard_map/ppermute | solution.py:515
  43.9 4.6 %collective-permute-start.13 = (f32[8,128]{1,0:T(8,128)S(1)}, f32[8,128]{1,0:T(8,128)S(1)}, u32[]{:S(2)}, u32[]{:S(2)}) collective-permute-start(f32[8,128]{1,0:T(8,128)S(1)} %copy-done.22), channel_id=1, source_target_pairs={{0,14},{2,0},{4,2},{6,4},{8,6},{10,8},{12,10},{14,12},{1,15},{3,1}... | collective-permute-start | bytes 12296 | tf_op jit(solution)/shard_map/ppermute | solution.py:516
  51.4 7.2 %copy-start.23 = (f32[8,128]{1,0:T(8,128)S(1)}, f32[8,128]{1,0:T(8,128)}, u32[]{:S(2)}) copy-start(f32[8,128]{1,0:T(8,128)} %get-tuple-element.64) | copy-start | bytes 12292
  51.5 12.2 %collective-permute-start.15 = (f32[2,16,128]{2,1,0:T(8,128)}, f32[2,16,128]{2,1,0:T(8,128)S(1)}, u32[]{:S(2)}, u32[]{:S(2)}) collective-permute-start(f32[2,16,128]{2,1,0:T(8,128)} %get-tuple-element.61), channel_id=1, source_target_pairs={{0,16},{16,32},{32,48},{48,64},{64,80},{80,96},{96,112},{112,128},... | collective-permute-start | bytes 49160 | tf_op jit(solution)/shard_map/ppermute | solution.py:513
  51.5 12.1 %collective-permute-start.16 = (f32[2,16,128]{2,1,0:T(8,128)}, f32[2,16,128]{2,1,0:T(8,128)S(1)}, u32[]{:S(2)}, u32[]{:S(2)}) collective-permute-start(f32[2,16,128]{2,1,0:T(8,128)} %get-tuple-element.62), channel_id=1, source_target_pairs={{0,240},{16,0},{32,16},{48,32},{64,48},{80,64},{96,80},{112,96},{1... | collective-permute-start | bytes 49160 | tf_op jit(solution)/shard_map/ppermute | solution.py:514
  56.3 7.3 %collective-permute-start.19 = (f32[2,8,128]{2,1,0:T(8,128)}, f32[2,8,128]{2,1,0:T(8,128)S(1)}, u32[]{:S(2)}, u32[]{:S(2)}) collective-permute-start(f32[2,8,128]{2,1,0:T(8,128)} %get-tuple-element.65), channel_id=1, source_target_pairs={{0,1},{1,0},{2,3},{3,2},{4,5},{5,4},{6,7},{7,6},{8,9},{9,8},{10,11... | collective-permute-start | bytes 24584 | tf_op jit(solution)/shard_map/ppermute | solution.py:512
  57.0 2.4 %collective-permute-start.17 = (f32[8,128]{1,0:T(8,128)S(1)}, f32[8,128]{1,0:T(8,128)S(1)}, u32[]{:S(2)}, u32[]{:S(2)}) collective-permute-start(f32[8,128]{1,0:T(8,128)S(1)} %copy-done.26), channel_id=1, source_target_pairs={{0,2},{2,4},{4,6},{6,8},{8,10},{10,12},{12,14},{14,0},{1,3},{3,5},... | collective-permute-start | bytes 12296 | tf_op jit(solution)/shard_map/ppermute | solution.py:515
  58.7 4.9 %collective-permute-start.18 = (f32[8,128]{1,0:T(8,128)S(1)}, f32[8,128]{1,0:T(8,128)S(1)}, u32[]{:S(2)}, u32[]{:S(2)}) collective-permute-start(f32[8,128]{1,0:T(8,128)S(1)} %copy-done.23), channel_id=1, source_target_pairs={{0,14},{2,0},{4,2},{6,4},{8,6},{10,8},{12,10},{14,12},{1,15},{3,1}... | collective-permute-start | bytes 12296 | tf_op jit(solution)/shard_map/ppermute | solution.py:516
  66.3 25.5 %copy-start = (f32[128,128]{1,0:T(8,128)S(1)}, f32[128,128]{1,0:T(8,128)}, u32[]{:S(2)}) copy-start(f32[128,128]{1,0:T(8,128)} %get-tuple-element.66) | copy-start | bytes 196612
  (25 other events, 54.2 us)

commit v2 on v1

--- a/solution.py
+++ b/solution.py
@@ -451,7 +451,19 @@
     total = jnp.sum(jnp.sum(acc, axis=0, keepdims=True), axis=1, keepdims=True)
     miss = jnp.sum(jnp.sum(mis_ref[...], axis=0, keepdims=True), axis=1, keepdims=True)
     miss = miss + jnp.sum(v_ref[...], axis=1, keepdims=True)
-    row_ref[...] = jnp.where(lane == 0, total, jnp.where(lane == 1, miss, 0.0))
+    row = jnp.where(lane == 0, total, jnp.where(lane == 1, miss, 0.0))
+    for i in range(row_ref.shape[0] // NX):
+        row_ref[layer(i), :] = row
+
+
+def scale_kernel(devices, count, grad_ref, rows_ref, out_ref, misfit_ref):
+    acc = rows_ref[layer(0), :]
+    for i in range(1, devices // NX):
+        acc = acc + rows_ref[layer(i), :]
+    row = jnp.sum(acc, axis=0, keepdims=True)
+    misfit_ref[0, 0] = row[0, 1] / (devices * count)
+    scale = 1.0 / jnp.sqrt(row[0:1, 0:1] / (devices * CELLS * NY) + small_eps)
+    out_ref[...] = grad_ref[...] * scale
 
 
 def split3(value):
@@ -487,6 +499,9 @@
     v_ref[...] = off * off
 
 
+SMALL = pltpu.CompilerParams(vmem_limit_bytes=12 * 1024 * 1024)
+
+
 def rows_of(*shape):
     return jax.ShapeDtypeStruct(shape, F32)
 
@@ -501,6 +516,7 @@
         out_shape=outs,
         scratch_shapes=scratch,
         cost_estimate=pl.CostEstimate(flops=flops, bytes_accessed=100000, transcendentals=0),
+        compiler_params=SMALL,
     )
 
 
@@ -564,21 +580,20 @@
         ],
     )(state_1, gamma, lam_2, coef, coef_halo, *got)
     got = exchange(sizes, *sent)
-    gradient, row = call(
+    devices = sizes["gx"] * sizes["gy"] * sizes["gz"]
+    gradient, rows = call(
         bind(gradient_kernel, sizes),
-        [rows_of(CELLS, NY), plane],
+        [rows_of(CELLS, NY), rows_of(devices, NY)],
         [vmem(2, NZ * 24, NY), vmem(2, tall, NY), vmem(CELLS, 8)],
     )(state, lam_1, d_gamma, mis, spread, *got)
-    for axes in (("gy",), ("gx", "gz")):
-        group = 1
-        for axis in axes:
-            group *= sizes[axis]
-        row = jnp.broadcast_to(row[:1], (group, NY))
-        row = jnp.sum(lax.all_to_all(row, axes, 0, 0, tiled=True), axis=0, keepdims=True)
-    devices = sizes["gx"] * sizes["gy"] * sizes["gz"]
-    direction = gradient / jnp.sqrt(row[0, 0] / (devices * CELLS * NY) + small_eps)
-    misfit = row[0, 1] / (devices * probes.shape[0])
-    return direction.reshape(NZ, NX, NY), misfit
+    rows = lax.all_to_all(rows, ("gx", "gy", "gz"), 0, 0, tiled=True)
+    direction, misfit = pl.pallas_call(
+        bind(scale_kernel, devices, probes.shape[0]),
+        out_shape=[rows_of(CELLS, NY), rows_of(1, 1)],
+        out_specs=[pl.BlockSpec(memory_space=pltpu.VMEM), pl.BlockSpec(memory_space=pltpu.SMEM)],
+        compiler_params=SMALL,
+    )(gradient, rows)
+    return direction.reshape(NZ, NX, NY), misfit.reshape(())
 
 
 def solution(mesh):

time: 94 us -> 77.9 us (0.83)
  Pallas kernels: 13.6 us -> 4.31 us
  blocking collectives: 22.8 us -> 19.6 us
  between operations: 3.35 us -> 0.9 us
    all_to_all x2 -> x1, blocking collectives: 22.8 us -> 19.6 us  [local(): rows = lax.all_to_all(rows, ('gx', 'gy', 'gz'), 0, 0, tiled=True)]
    pallas_call x1, Pallas kernels: 3.28 us -> 1.41 us  [local(): call(bind(step_kernel, sizes), [rows_of(5, CELLS, NY)] + slabs(5, 2), [vm...]
    pallas_call x1, Pallas kernels: 2.32 us -> 0.48 us  [local(): call(bind(adjoint_kernel, sizes), [rows_of(4, CELLS, NY), rows_of(CELLS,...]
    pallas_call x1, Pallas kernels: 2.2 us -> 0.43 us  [local(): call(bind(speed_kernel, sizes), [rows_of(2, CELLS, NY), rows_of(CELLS, NY...]
    pallas_call x1, Pallas kernels: 1.91 us -> 0.25 us  [local(): call(bind(prep_kernel, sizes), slabs(8, 8) + [plane], [vmem(CELLS, NY)])]
    slice x2 -> x0, local copies, waits for them, and re-layouts: 1.29 us -> none  [the longest x1 0.7 us: local(): row = jnp.broadcast_to(row[:1], (group, NY))]
    pallas_call x1, Pallas kernels: 1.81 us -> 0.53 us  [local(): call(probe_kernel, [rows_of(CELLS, NY), rows_of(CELLS, NY), rows_of(1, pr...]
    unnamed x58 -> x12, local copies, waits for them, and re-layouts: 2.48 us -> 3.4 us
  transfers between devices with their start and end apart: 20 -> 20, of which waited for: 7 -> 7; matrix products, arithmetic and copies ran while one was open for 0% -> 0% of each run, Pallas kernels for 2% -> 1%
where the time goes in v2:
time: 77.9 us; the launch traced here: 77.7 us
  starting transfers between devices  31.9 us (41%)
  blocking collectives  19.6 us (25%)
  waiting for transfers between devices  17.5 us (22%)
  Pallas kernels  4.31 us (6%)
  local copies, waits for them, and re-layouts  3.4 us (4%)
  between operations  0.9 us (1%)
    all_to_all x1, blocking collectives, local(): rows = lax.all_to_all(rows, ('gx', 'gy', 'gz'), 0, 0, tiled=True)  19.6 us
    ppermute x4, starting transfers between devices, exchange(): xh = lax.ppermute(xlo, 'gx', ring('gx', -1))  18.1 us
    ppermute x4, waiting for transfers between devices, exchange(): yh = lax.ppermute(ylo, 'gy', ring('gy', -1))  15.2 us
    ppermute x4, starting transfers between devices, exchange(): yl = lax.ppermute(yhi, 'gy', ring('gy', 1))  8.33 us
    unnamed x12, local copies, waits for them, and re-layouts  3.4 us
    ppermute x4, starting transfers between devices, exchange(): zr = lax.ppermute(zs, 'gz', ring('gz', 1))  3.1 us
    ppermute x4, starting transfers between devices, exchange(): xl = lax.ppermute(xhi, 'gx', ring('gx', 1))  2.35 us
    ppermute x4, waiting for transfers between devices, exchange(): yl = lax.ppermute(yhi, 'gy', ring('gy', 1))  2.26 us
  transfers between devices with their start and end apart: 20, of which 7 were waited for; matrix products, arithmetic and copies ran while one was open for 0% of the time, Pallas kernels for 1%

profile of v2, /device:TPU:1, one launch (start us, length us, event | category | flops | bytes accessed | tf_op | source)
XLA Modules:
  0.0 77.7 jit_solution(1092109942080674645)
XLA Ops:
  0.6 1.0 %copy-done = f32[5,16,8,128]{3,2,1,0:T(8,128)S(1)} copy-done((f32[5,16,8,128]{3,2,1,0:T(8,128)S(1)}, f32[5,16,8,128]{3,2,1,0:T(8,128)}, u32[]{:S(2)}) %copy-start) | copy-done | bytes 327704
  1.6 0.9 %copy-done.2 = s32[2,16,8,128]{3,2,1,0:T(8,128)S(1)} copy-done((s32[2,16,8,128]{3,2,1,0:T(8,128)S(1)}, s32[2,16,8,128]{3,2,1,0:T(8,128)}, u32[]{:S(2)}) %copy-start.2) | copy-done | bytes 131096
  2.5 0.8 %copy-done.3 = f32[16,8,128]{2,1,0:T(8,128)S(1)} copy-done((f32[16,8,128]{2,1,0:T(8,128)S(1)}, f32[16,8,128]{2,1,0:T(8,128)}, u32[]{:S(2)}) %copy-start.3) | copy-done | bytes 65560
  3.6 2.1 %collective-permute-start = (f32[8,16,128]{2,1,0:T(8,128)S(1)}, f32[8,16,128]{2,1,0:T(8,128)S(1)}, u32[]{:S(2)}, u32[]{:S(2)}) collective-permute-start(f32[8,16,128]{2,1,0:T(8,128)S(1)} %get-tuple-element.37), channel_id=1, source_target_pairs={{0,16},{16,32},{32,48},{48,64},{64,80},{80,96},{96,112},{112,128},... | collective-permute-start | bytes 196616 | tf_op jit(solution)/shard_map/ppermute | solution.py:529
  5.7 3.8 %collective-permute-start.1 = (f32[8,16,128]{2,1,0:T(8,128)S(1)}, f32[8,16,128]{2,1,0:T(8,128)S(1)}, u32[]{:S(2)}, u32[]{:S(2)}) collective-permute-start(f32[8,16,128]{2,1,0:T(8,128)S(1)} %get-tuple-element.38), channel_id=1, source_target_pairs={{0,240},{16,0},{32,16},{48,32},{64,48},{80,64},{96,80},{112,96},{1... | collective-permute-start | bytes 196616 | tf_op jit(solution)/shard_map/ppermute | solution.py:530
  9.5 1.6 %collective-permute-start.4 = (f32[8,8,128]{2,1,0:T(8,128)S(1)}, f32[8,8,128]{2,1,0:T(8,128)S(1)}, u32[]{:S(2)}, u32[]{:S(2)}) collective-permute-start(f32[8,8,128]{2,1,0:T(8,128)S(1)} %get-tuple-element.41), channel_id=1, source_target_pairs={{0,1},{1,0},{2,3},{3,2},{4,5},{5,4},{6,7},{7,6},{8,9},{9,8},{10,11... | collective-permute-start | bytes 98312 | tf_op jit(solution)/shard_map/ppermute | solution.py:528
  11.2 4.2 %collective-permute-start.2 = (f32[8,128]{1,0:T(8,128)S(1)}, f32[8,128]{1,0:T(8,128)S(1)}, u32[]{:S(2)}, u32[]{:S(2)}) collective-permute-start(f32[8,128]{1,0:T(8,128)S(1)} %get-tuple-element.39), channel_id=1, source_target_pairs={{0,2},{2,4},{4,6},{6,8},{8,10},{10,12},{12,14},{14,0},{1,3},{3,5},... | collective-permute-start | bytes 12296 | tf_op jit(solution)/shard_map/ppermute | solution.py:531
  15.3 0.8 collective-permute-done.2.yl
  16.1 3.2 %collective-permute-done.3.yh = f32[8,128]{1,0:T(8,128)S(1)} collective-permute-done((f32[8,128]{1,0:T(8,128)S(1)}, f32[8,128]{1,0:T(8,128)S(1)}, u32[]{:S(2)}, u32[]{:S(2)}) %collective-permute-start.3) | collective-permute-done | bytes 4128 | tf_op jit(solution)/shard_map/ppermute | solution.py:532
  19.3 1.4 %shard_map.69 = (f32[5,128,128]{2,1,0:T(8,128)S(1)}, f32[5,16,128]{2,1,0:T(8,128)S(1)}, f32[5,16,128]{2,1,0:T(8,128)S(1)}, f32[8,128]{1,0:T(8,128)S(1)}, f32[8,128]{1,0:T(8,128)S(1)}, /*index=5*/f32[2,8,128]{2,1,0:T(8,128)S(1)}) custom-call(f32[5,128,128]{2,1,0:T(8,128)S(1)} %bitcast.12, f32[128,128]{1,0:T(8,128)S(1)} %bitcast.18, ...), custom_call_target="tpu_custom_call" | custom-call | flops 100000 | bytes 100000 | tf_op jit(solution)/shard_map/pallas_call | solution.py:555
  20.8 4.8 %collective-permute-start.6 = (f32[5,16,128]{2,1,0:T(8,128)S(1)}, f32[5,16,128]{2,1,0:T(8,128)S(1)}, u32[]{:S(2)}, u32[]{:S(2)}) collective-permute-start(f32[5,16,128]{2,1,0:T(8,128)S(1)} %get-tuple-element.45), channel_id=1, source_target_pairs={{0,240},{16,0},{32,16},{48,32},{64,48},{80,64},{96,80},{112,96},{1... | collective-permute-start | bytes 122888 | tf_op jit(solution)/shard_map/ppermute | solution.py:530
  25.6 2.0 %collective-permute-start.7 = (f32[8,128]{1,0:T(8,128)S(1)}, f32[8,128]{1,0:T(8,128)S(1)}, u32[]{:S(2)}, u32[]{:S(2)}) collective-permute-start(f32[8,128]{1,0:T(8,128)S(1)} %get-tuple-element.46), channel_id=1, source_target_pairs={{0,2},{2,4},{4,6},{6,8},{8,10},{10,12},{12,14},{14,0},{1,3},{3,5},... | collective-permute-start | bytes 12296 | tf_op jit(solution)/shard_map/ppermute | solution.py:531
  28.8 3.7 %collective-permute-done.8.yh = f32[8,128]{1,0:T(8,128)S(1)} collective-permute-done((f32[8,128]{1,0:T(8,128)S(1)}, f32[8,128]{1,0:T(8,128)S(1)}, u32[]{:S(2)}, u32[]{:S(2)}) %collective-permute-start.8) | collective-permute-done | bytes 4128 | tf_op jit(solution)/shard_map/ppermute | solution.py:532
  33.0 4.8 %collective-permute-start.11 = (f32[3,16,128]{2,1,0:T(8,128)S(1)}, f32[3,16,128]{2,1,0:T(8,128)S(1)}, u32[]{:S(2)}, u32[]{:S(2)}) collective-permute-start(f32[3,16,128]{2,1,0:T(8,128)S(1)} %get-tuple-element.55), channel_id=1, source_target_pairs={{0,240},{16,0},{32,16},{48,32},{64,48},{80,64},{96,80},{112,96},{1... | collective-permute-start | bytes 73736 | tf_op jit(solution)/shard_map/ppermute | solution.py:530
  37.8 0.7 collective-permute-start.14
  38.5 1.1 %collective-permute-start.12 = (f32[8,128]{1,0:T(8,128)S(1)}, f32[8,128]{1,0:T(8,128)S(1)}, u32[]{:S(2)}, u32[]{:S(2)}) collective-permute-start(f32[8,128]{1,0:T(8,128)S(1)} %get-tuple-element.56), channel_id=1, source_target_pairs={{0,2},{2,4},{4,6},{6,8},{8,10},{10,12},{12,14},{14,0},{1,3},{3,5},... | collective-permute-start | bytes 12296 | tf_op jit(solution)/shard_map/ppermute | solution.py:531
  39.6 0.8 collective-permute-done.12.yl
  40.4 4.2 %collective-permute-done.13.yh = f32[8,128]{1,0:T(8,128)S(1)} collective-permute-done((f32[8,128]{1,0:T(8,128)S(1)}, f32[8,128]{1,0:T(8,128)S(1)}, u32[]{:S(2)}, u32[]{:S(2)}) %collective-permute-start.13) | collective-permute-done | bytes 4128 | tf_op jit(solution)/shard_map/ppermute | solution.py:532
  45.1 4.8 %collective-permute-start.16 = (f32[2,16,128]{2,1,0:T(8,128)S(1)}, f32[2,16,128]{2,1,0:T(8,128)S(1)}, u32[]{:S(2)}, u32[]{:S(2)}) collective-permute-start(f32[2,16,128]{2,1,0:T(8,128)S(1)} %get-tuple-element.64), channel_id=1, source_target_pairs={{0,240},{16,0},{32,16},{48,32},{64,48},{80,64},{96,80},{112,96},{1... | collective-permute-start | bytes 49160 | tf_op jit(solution)/shard_map/ppermute | solution.py:530
  50.6 1.1 %collective-permute-start.17 = (f32[8,128]{1,0:T(8,128)S(1)}, f32[8,128]{1,0:T(8,128)S(1)}, u32[]{:S(2)}, u32[]{:S(2)}) collective-permute-start(f32[8,128]{1,0:T(8,128)S(1)} %get-tuple-element.65), channel_id=1, source_target_pairs={{0,2},{2,4},{4,6},{6,8},{8,10},{10,12},{12,14},{14,0},{1,3},{3,5},... | collective-permute-start | bytes 12296 | tf_op jit(solution)/shard_map/ppermute | solution.py:531
  51.7 0.8 collective-permute-done.17.yl
  52.5 4.2 %collective-permute-done.18.yh = f32[8,128]{1,0:T(8,128)S(1)} collective-permute-done((f32[8,128]{1,0:T(8,128)S(1)}, f32[8,128]{1,0:T(8,128)S(1)}, u32[]{:S(2)}, u32[]{:S(2)}) %collective-permute-start.18) | collective-permute-done | bytes 4128 | tf_op jit(solution)/shard_map/ppermute | solution.py:532
  57.1 19.6 %all_to_all.11 = f32[256,1,128]{2,1,0:T(1,128)S(1)} all-to-all(f32[256,1,128]{2,1,0:T(1,128)S(1)} %bitcast.22), channel_id=1, replica_groups=mesh['gx'=16,'gy'=8,'gz'=2] {'gx','gy','gz'}, dimensions={0} | all-to-all | bytes 262144 | tf_op jit(solution)/shard_map/all_to_all | solution.py:589
  76.7 0.8 shard_map.74
  (36 shorter events, 3.8 us)
Async XLA Ops:
  0.6 1.0 %copy-start = (f32[5,16,8,128]{3,2,1,0:T(8,128)S(1)}, f32[5,16,8,128]{3,2,1,0:T(8,128)}, u32[]{:S(2)}) copy-start(f32[5,16,8,128]{3,2,1,0:T(8,128)} %param.5) | copy-start | bytes 983044
  1.6 0.9 %copy-start.2 = (s32[2,16,8,128]{3,2,1,0:T(8,128)S(1)}, s32[2,16,8,128]{3,2,1,0:T(8,128)}, u32[]{:S(2)}) copy-start(s32[2,16,8,128]{3,2,1,0:T(8,128)} %param.7) | copy-start | bytes 393220
  3.6 15.7 %collective-permute-start = (f32[8,16,128]{2,1,0:T(8,128)S(1)}, f32[8,16,128]{2,1,0:T(8,128)S(1)}, u32[]{:S(2)}, u32[]{:S(2)}) collective-permute-start(f32[8,16,128]{2,1,0:T(8,128)S(1)} %get-tuple-element.37), channel_id=1, source_target_pairs={{0,16},{16,32},{32,48},{48,64},{64,80},{80,96},{96,112},{112,128},... | collective-permute-start | bytes 196616 | tf_op jit(solution)/shard_map/ppermute | solution.py:529
  5.7 13.5 %collective-permute-start.1 = (f32[8,16,128]{2,1,0:T(8,128)S(1)}, f32[8,16,128]{2,1,0:T(8,128)S(1)}, u32[]{:S(2)}, u32[]{:S(2)}) collective-permute-start(f32[8,16,128]{2,1,0:T(8,128)S(1)} %get-tuple-element.38), channel_id=1, source_target_pairs={{0,240},{16,0},{32,16},{48,32},{64,48},{80,64},{96,80},{112,96},{1... | collective-permute-start | bytes 196616 | tf_op jit(solution)/shard_map/ppermute | solution.py:530
  9.5 9.7 %collective-permute-start.4 = (f32[8,8,128]{2,1,0:T(8,128)S(1)}, f32[8,8,128]{2,1,0:T(8,128)S(1)}, u32[]{:S(2)}, u32[]{:S(2)}) collective-permute-start(f32[8,8,128]{2,1,0:T(8,128)S(1)} %get-tuple-element.41), channel_id=1, source_target_pairs={{0,1},{1,0},{2,3},{3,2},{4,5},{5,4},{6,7},{7,6},{8,9},{9,8},{10,11... | collective-permute-start | bytes 98312 | tf_op jit(solution)/shard_map/ppermute | solution.py:528
  11.2 4.9 %collective-permute-start.2 = (f32[8,128]{1,0:T(8,128)S(1)}, f32[8,128]{1,0:T(8,128)S(1)}, u32[]{:S(2)}, u32[]{:S(2)}) collective-permute-start(f32[8,128]{1,0:T(8,128)S(1)} %get-tuple-element.39), channel_id=1, source_target_pairs={{0,2},{2,4},{4,6},{6,8},{8,10},{10,12},{12,14},{14,0},{1,3},{3,5},... | collective-permute-start | bytes 12296 | tf_op jit(solution)/shard_map/ppermute | solution.py:531
  15.3 3.9 %collective-permute-start.3 = (f32[8,128]{1,0:T(8,128)S(1)}, f32[8,128]{1,0:T(8,128)S(1)}, u32[]{:S(2)}, u32[]{:S(2)}) collective-permute-start(f32[8,128]{1,0:T(8,128)S(1)} %get-tuple-element.40), channel_id=1, source_target_pairs={{0,14},{2,0},{4,2},{6,4},{8,6},{10,8},{12,10},{14,12},{1,15},{3,1}... | collective-permute-start | bytes 12296 | tf_op jit(solution)/shard_map/ppermute | solution.py:532
  19.3 8.3 %copy-start.5 = (f32[256]{0:T(256)S(1)}, f32[256]{0:T(256)}, u32[]{:S(2)}) copy-start(f32[256]{0:T(256)} %param.9) | copy-start | bytes 3076
  20.7 11.8 %collective-permute-start.5 = (f32[5,16,128]{2,1,0:T(8,128)S(1)}, f32[5,16,128]{2,1,0:T(8,128)S(1)}, u32[]{:S(2)}, u32[]{:S(2)}) collective-permute-start(f32[5,16,128]{2,1,0:T(8,128)S(1)} %get-tuple-element.44), channel_id=1, source_target_pairs={{0,16},{16,32},{32,48},{48,64},{64,80},{80,96},{96,112},{112,128},... | collective-permute-start | bytes 122888 | tf_op jit(solution)/shard_map/ppermute | solution.py:529
  20.8 11.7 %collective-permute-start.6 = (f32[5,16,128]{2,1,0:T(8,128)S(1)}, f32[5,16,128]{2,1,0:T(8,128)S(1)}, u32[]{:S(2)}, u32[]{:S(2)}) collective-permute-start(f32[5,16,128]{2,1,0:T(8,128)S(1)} %get-tuple-element.45), channel_id=1, source_target_pairs={{0,240},{16,0},{32,16},{48,32},{64,48},{80,64},{96,80},{112,96},{1... | collective-permute-start | bytes 122888 | tf_op jit(solution)/shard_map/ppermute | solution.py:530
  25.6 6.9 %collective-permute-start.9 = (f32[2,8,128]{2,1,0:T(8,128)S(1)}, f32[2,8,128]{2,1,0:T(8,128)S(1)}, u32[]{:S(2)}, u32[]{:S(2)}) collective-permute-start(f32[2,8,128]{2,1,0:T(8,128)S(1)} %get-tuple-element.48), channel_id=1, source_target_pairs={{0,1},{1,0},{2,3},{3,2},{4,5},{5,4},{6,7},{7,6},{8,9},{9,8},{10,11... | collective-permute-start | bytes 24584 | tf_op jit(solution)/shard_map/ppermute | solution.py:528
  25.6 3.2 %collective-permute-start.7 = (f32[8,128]{1,0:T(8,128)S(1)}, f32[8,128]{1,0:T(8,128)S(1)}, u32[]{:S(2)}, u32[]{:S(2)}) collective-permute-start(f32[8,128]{1,0:T(8,128)S(1)} %get-tuple-element.46), channel_id=1, source_target_pairs={{0,2},{2,4},{4,6},{6,8},{8,10},{10,12},{12,14},{14,0},{1,3},{3,5},... | collective-permute-start | bytes 12296 | tf_op jit(solution)/shard_map/ppermute | solution.py:531
  27.6 4.9 %collective-permute-start.8 = (f32[8,128]{1,0:T(8,128)S(1)}, f32[8,128]{1,0:T(8,128)S(1)}, u32[]{:S(2)}, u32[]{:S(2)}) collective-permute-start(f32[8,128]{1,0:T(8,128)S(1)} %get-tuple-element.47), channel_id=1, source_target_pairs={{0,14},{2,0},{4,2},{6,4},{8,6},{10,8},{12,10},{14,12},{1,15},{3,1}... | collective-permute-start | bytes 12296 | tf_op jit(solution)/shard_map/ppermute | solution.py:532
  32.9 11.6 %collective-permute-start.10 = (f32[3,16,128]{2,1,0:T(8,128)S(1)}, f32[3,16,128]{2,1,0:T(8,128)S(1)}, u32[]{:S(2)}, u32[]{:S(2)}) collective-permute-start(f32[3,16,128]{2,1,0:T(8,128)S(1)} %get-tuple-element.54), channel_id=1, source_target_pairs={{0,16},{16,32},{32,48},{48,64},{64,80},{80,96},{96,112},{112,128},... | collective-permute-start | bytes 73736 | tf_op jit(solution)/shard_map/ppermute | solution.py:529
  33.0 11.5 %collective-permute-start.11 = (f32[3,16,128]{2,1,0:T(8,128)S(1)}, f32[3,16,128]{2,1,0:T(8,128)S(1)}, u32[]{:S(2)}, u32[]{:S(2)}) collective-permute-start(f32[3,16,128]{2,1,0:T(8,128)S(1)} %get-tuple-element.55), channel_id=1, source_target_pairs={{0,240},{16,0},{32,16},{48,32},{64,48},{80,64},{96,80},{112,96},{1... | collective-permute-start | bytes 73736 | tf_op jit(solution)/shard_map/ppermute | solution.py:530
  37.8 6.8 %collective-permute-start.14 = (f32[2,8,128]{2,1,0:T(8,128)S(1)}, f32[2,8,128]{2,1,0:T(8,128)S(1)}, u32[]{:S(2)}, u32[]{:S(2)}) collective-permute-start(f32[2,8,128]{2,1,0:T(8,128)S(1)} %get-tuple-element.58), channel_id=1, source_target_pairs={{0,1},{1,0},{2,3},{3,2},{4,5},{5,4},{6,7},{7,6},{8,9},{9,8},{10,11... | collective-permute-start | bytes 24584 | tf_op jit(solution)/shard_map/ppermute | solution.py:528
  38.5 1.8 %collective-permute-start.12 = (f32[8,128]{1,0:T(8,128)S(1)}, f32[8,128]{1,0:T(8,128)S(1)}, u32[]{:S(2)}, u32[]{:S(2)}) collective-permute-start(f32[8,128]{1,0:T(8,128)S(1)} %get-tuple-element.56), channel_id=1, source_target_pairs={{0,2},{2,4},{4,6},{6,8},{8,10},{10,12},{12,14},{14,0},{1,3},{3,5},... | collective-permute-start | bytes 12296 | tf_op jit(solution)/shard_map/ppermute | solution.py:531
  39.6 4.9 %collective-permute-start.13 = (f32[8,128]{1,0:T(8,128)S(1)}, f32[8,128]{1,0:T(8,128)S(1)}, u32[]{:S(2)}, u32[]{:S(2)}) collective-permute-start(f32[8,128]{1,0:T(8,128)S(1)} %get-tuple-element.57), channel_id=1, source_target_pairs={{0,14},{2,0},{4,2},{6,4},{8,6},{10,8},{12,10},{14,12},{1,15},{3,1}... | collective-permute-start | bytes 12296 | tf_op jit(solution)/shard_map/ppermute | solution.py:532
  44.6 12.1 %copy-start.1 = (f32[5,16,8,128]{3,2,1,0:T(8,128)S(1)}, f32[5,16,8,128]{3,2,1,0:T(8,128)}, u32[]{:S(2)}) copy-start(f32[5,16,8,128]{3,2,1,0:T(8,128)} %param.5) | copy-start | bytes 983044
  45.1 11.6 %collective-permute-start.15 = (f32[2,16,128]{2,1,0:T(8,128)S(1)}, f32[2,16,128]{2,1,0:T(8,128)S(1)}, u32[]{:S(2)}, u32[]{:S(2)}) collective-permute-start(f32[2,16,128]{2,1,0:T(8,128)S(1)} %get-tuple-element.63), channel_id=1, source_target_pairs={{0,16},{16,32},{32,48},{48,64},{64,80},{80,96},{96,112},{112,128},... | collective-permute-start | bytes 49160 | tf_op jit(solution)/shard_map/ppermute | solution.py:529
  45.1 11.5 %collective-permute-start.16 = (f32[2,16,128]{2,1,0:T(8,128)S(1)}, f32[2,16,128]{2,1,0:T(8,128)S(1)}, u32[]{:S(2)}, u32[]{:S(2)}) collective-permute-start(f32[2,16,128]{2,1,0:T(8,128)S(1)} %get-tuple-element.64), channel_id=1, source_target_pairs={{0,240},{16,0},{32,16},{48,32},{64,48},{80,64},{96,80},{112,96},{1... | collective-permute-start | bytes 49160 | tf_op jit(solution)/shard_map/ppermute | solution.py:530
  49.9 6.8 %collective-permute-start.19 = (f32[2,8,128]{2,1,0:T(8,128)S(1)}, f32[2,8,128]{2,1,0:T(8,128)S(1)}, u32[]{:S(2)}, u32[]{:S(2)}) collective-permute-start(f32[2,8,128]{2,1,0:T(8,128)S(1)} %get-tuple-element.67), channel_id=1, source_target_pairs={{0,1},{1,0},{2,3},{3,2},{4,5},{5,4},{6,7},{7,6},{8,9},{9,8},{10,11... | collective-permute-start | bytes 24584 | tf_op jit(solution)/shard_map/ppermute | solution.py:528
  50.6 1.8 %collective-permute-start.17 = (f32[8,128]{1,0:T(8,128)S(1)}, f32[8,128]{1,0:T(8,128)S(1)}, u32[]{:S(2)}, u32[]{:S(2)}) collective-permute-start(f32[8,128]{1,0:T(8,128)S(1)} %get-tuple-element.65), channel_id=1, source_target_pairs={{0,2},{2,4},{4,6},{6,8},{8,10},{10,12},{12,14},{14,0},{1,3},{3,5},... | collective-permute-start | bytes 12296 | tf_op jit(solution)/shard_map/ppermute | solution.py:531
  51.7 4.9 %collective-permute-start.18 = (f32[8,128]{1,0:T(8,128)S(1)}, f32[8,128]{1,0:T(8,128)S(1)}, u32[]{:S(2)}, u32[]{:S(2)}) collective-permute-start(f32[8,128]{1,0:T(8,128)S(1)} %get-tuple-element.66), channel_id=1, source_target_pairs={{0,14},{2,0},{4,2},{6,4},{8,6},{10,8},{12,10},{14,12},{1,15},{3,1}... | collective-permute-start | bytes 12296 | tf_op jit(solution)/shard_map/ppermute | solution.py:532
  (2 other events, 1.5 us)

commit v3 on v2

--- a/solution.py
+++ b/solution.py
@@ -92,6 +92,13 @@
     out = pltpu.roll(values[0], 1, 1)
     for i in range(1, len(values)):
         out = jnp.where(lane < 2 * i, out, pltpu.roll(values[i], 2 * i + 1, 1))
+    return out
+
+
+def pack_edges(values, lane):
+    out = pltpu.roll(values[0], 2, 1)
+    for i in range(1, len(values)):
+        out = jnp.where(lane < 4 * i, out, pltpu.roll(values[i], 4 * i + 2, 1))
     return out
 
 
@@ -116,10 +123,7 @@
     for z in range(NZ):
         vals = [u_ref[k, layer(z), :] for k in range(5)]
         vals += [g_ref[layer(z), :], s_ref[0, layer(z), :].astype(F32)]
-        out = pltpu.roll(vals[0], 2, 1)
-        for i in range(1, 7):
-            out = jnp.where(lane < 4 * i, out, pltpu.roll(vals[i], 4 * i + 2, 1))
-        yp[layer(z), :] = out
+        yp[layer(z), :] = pack_edges(vals, lane)
     rows = yp[...].T
     for out, edge, second, own in ((yhi, 1, 0, 1), (ylo, 2, 3, 0)):
         st = [rows[4 * k + edge : 4 * k + edge + 1] for k in range(7)]
@@ -257,7 +261,7 @@
 
 def speed_kernel(
     mesh, u_ref, g_ref, s_ref, xl, xh, yl, yh, zr, n_ref, m_ref,
-    lam_ref, cf_ref, cfh_ref, mis_ref, xlo, xhi, ylo, yhi, zs,
+    lam_ref, cf_ref, cfh_ref, mis_ref, ylo, yhi, zs, yown,
     vx, ax, bx, az, bz, ch, yc, yp,
 ):
     (mxl, mxh), (myl, myh), (mzl, mzh), first = masks(mesh)
@@ -320,27 +324,76 @@
         lam_r = -lam_m * speed
         lam_ref[0, layer(z), :] = lam_r
         lam_ref[1, layer(z), :] = lam_m
-        yp[layer(z), :] = pack_columns([lam_r, lam_m], lane)
+        inv = 1.0 / (1.0 + u_ref[0, layer(z), :])
+        extra = [u_ref[1, layer(z), :] * inv, u_ref[2, layer(z), :] * inv, g_ref[layer(z), :]]
+        yp[layer(z), :] = pack_edges([lam_r, lam_m] + extra, lane)
     mis_ref[...] = mis
-    for out, edge, second in ((xlo, 0, 1), (xhi, NX - 1, NX - 2)):
-        out[0] = lam_ref[0, x_row(edge), :]
-        out[1] = lam_ref[1, x_row(edge), :]
-        out[2] = lam_ref[1, x_row(second), :]
-    za = face_layer(first, 0)
-    for k in range(2):
-        zs[k] = lam_ref[k, dyn_layer(za), :]
+    za, zb = dyn_layer(face_layer(first, 0)), dyn_layer(face_layer(first, 1))
+    inv = 1.0 / (1.0 + u_ref[0, za, :])
+    ux = u_ref[1, za, :] * inv
+    zs[0] = lam_ref[0, za, :]
+    zs[1] = lam_ref[1, za, :]
+    zs[2] = jnp.where(first, -HALF_T, HALF_T) * (lam_ref[0, zb, :] + lam_ref[1, zb, :] * ux)
+    zs[3] = ux
+    zs[4] = u_ref[3, za, :] * inv
+    zs[5] = g_ref[za, :]
     rows = yp[...].T
-    for k in range(2):
-        yhi[k : k + 1] = rows[2 * k : 2 * k + 1]
-        ylo[k : k + 1] = rows[2 * k + 1 : 2 * k + 2]
-    yhi[2:8] = jnp.zeros((6, NY), F32)
-    ylo[2:8] = jnp.zeros((6, NY), F32)
-
-
-def adjoint_kernel(
-    mesh, u_ref, g_ref, lam_ref, cf_ref, cfh_ref, xl, xh, yl, yh, zr,
-    out_ref, dg_ref, xlo, xhi, ylo, yhi, zs,
-    lx, lz, px, dx, yc, yp,
+    for out, edge, second, own, sign in ((yhi, 1, 0, 2, -HALF_T), (ylo, 2, 3, 0, HALF_T)):
+        lam_r, lam_m, ux, uy, gamma = [rows[4 * i + edge : 4 * i + edge + 1] for i in range(5)]
+        out[0:1] = lam_r
+        out[1:2] = lam_m
+        out[2:3] = sign * (rows[second : second + 1] + rows[4 + second : 5 + second] * ux)
+        out[3:4] = ux
+        out[4:5] = uy
+        out[5:6] = gamma
+        out[6:8] = jnp.zeros((2, NY), F32)
+        yown[own : own + 1] = lam_r
+        yown[own + 1 : own + 2] = lam_m
+    yown[4:8] = jnp.zeros((4, NY), F32)
+
+
+NEAR = time_ratio * HALF_C
+STAY = 1.0 - 3.0 * time_ratio * signal_speed
+
+
+def edge_kernel(mesh, u_ref, g_ref, lam_ref, cf_ref, yl, yh, zr, xlo, xhi, yc):
+    _, (myl, myh), (mzl, mzh), _ = masks(mesh)
+    low_y, high_y = yl[1:2] * myl, yh[1:2] * myh
+    yc[:, 0:8] = jnp.concatenate([low_y, high_y, jnp.zeros((6, NY), F32)], axis=0).T
+    lane = lax.broadcasted_iota(jnp.int32, (NZ, NY), 1)
+    deep = lax.broadcasted_iota(jnp.int32, (NZ, NY), 0)
+    for out, e, i, i2, sign in ((xhi, NX - 1, NX - 2, NX - 3, 1.0), (xlo, 0, 1, 2, -1.0)):
+        r, mx, my, mz = [u_ref[k, x_row(e), :] for k in range(4)]
+        inv = 1.0 / (1.0 + r)
+        lm, lm_i = lam_ref[1, x_row(e), :], lam_ref[1, x_row(i), :]
+        col = yc[x_row(e), :]
+        side = zr[1, e : e + 1, :]
+        up_y = jnp.where(lane == NY - 1, col[:, 1:2], pltpu.roll(lm, NY - 1, 1))
+        down_y = jnp.where(lane == 0, col[:, 0:1], pltpu.roll(lm, 1, 1))
+        up_z = jnp.where(deep == NZ - 1, side * mzh, pltpu.roll(lm, NZ - 1, 0))
+        down_z = jnp.where(deep == 0, side * mzl, pltpu.roll(lm, 1, 0))
+        slope = (sign * HALF_T) * (lm - lam_ref[1, x_row(i2), :]) * cf_ref[x_row(i), :]
+        out[0] = lam_ref[0, x_row(e), :]
+        out[1] = lm
+        out[2] = lm_i
+        out[3] = (
+            STAY * lm
+            + NEAR * (lm_i + (up_y + down_y) + (up_z + down_z))
+            - (sign * HALF_T) * lam_ref[0, x_row(i), :]
+            + HALF_T * ((up_y - down_y) * (my * inv) + (up_z - down_z) * (mz * inv))
+            + (sign * 0.5) * slope * inv
+        )
+        gamma = g_ref[x_row(e), :]
+        out[4] = (2.0 - gamma) * (mx * inv)
+        out[5] = inv
+        out[6] = gamma
+        out[7] = jnp.where(deep == 0, low_y, jnp.where(deep == 1, high_y, jnp.where(deep == 2, side, 0.0)))
+
+
+def gradient_kernel(
+    mesh, u0_ref, u_ref, g_ref, lam_ref, cf_ref, cfh_ref, yown, yl, yh, zr, xl, xh, mis_ref, v_ref,
+    grad_ref, row_ref,
+    lx, lz, px, dx, dg, yc, gx, gy, gz,
 ):
     (mxl, mxh), (myl, myh), (mzl, mzh), first = masks(mesh)
     lane = lanes()
@@ -352,13 +405,55 @@
         lx[k, pl.ds(16, NZ, stride=24), :] = xh[k] * mxh
         lz[k, layer(0), :] = zr[k] * mzl
         lz[k, layer(NZ + 1), :] = zr[k] * mzh
-    dx[pl.ds(7, NZ, stride=24), :] = HALF_T * (lam_ref[1, x_row(0), :] - xl[2] * mxl) * cfh_ref[0]
-    dx[pl.ds(16, NZ, stride=24), :] = HALF_T * (xh[2] * mxh - lam_ref[1, x_row(NX - 1), :]) * cfh_ref[1]
+    phi_low = HALF_T * (lam_ref[1, x_row(0), :] - xl[2] * mxl)
+    phi_high = HALF_T * (xh[2] * mxh - lam_ref[1, x_row(NX - 1), :])
+    dx[pl.ds(7, NZ, stride=24), :] = phi_low * cfh_ref[0]
+    dx[pl.ds(16, NZ, stride=24), :] = phi_high * cfh_ref[1]
     for z in range(NZ):
         phi = HALF_T * (lx[1, pl.ds(24 * z + 9, 8), :] - lx[1, pl.ds(24 * z + 7, 8), :])
         px[layer(z), :] = phi
         dx[pl.ds(24 * z + 8, 8), :] = phi * cf_ref[layer(z), :]
-    yc[...] = columns_of(yl, yh, 2, myl, myh)
+    gx[1, pl.ds(7, NZ, stride=24), :] = mxl * phi_low * xl[6]
+    gx[1, pl.ds(16, NZ, stride=24), :] = mxh * phi_high * xh[6]
+    gx[0, pl.ds(7, NZ, stride=24), :] = mxl * (
+        xl[3]
+        + HALF_T * lam_ref[0, x_row(0), :]
+        + NEAR * lam_ref[1, x_row(0), :]
+        + phi_low * xl[4]
+        - 0.5 * dx[pl.ds(8, NZ, stride=24), :] * xl[5]
+    )
+    gx[0, pl.ds(16, NZ, stride=24), :] = mxh * (
+        xh[3]
+        - HALF_T * lam_ref[0, x_row(NX - 1), :]
+        + NEAR * lam_ref[1, x_row(NX - 1), :]
+        + phi_high * xh[4]
+        + 0.5 * dx[pl.ds(15, NZ, stride=24), :] * xh[5]
+    )
+    at_x = lax.bitwise_and(lax.broadcasted_iota(jnp.int32, (1, NY), 1), NX - 1)
+    from_high, from_low = pltpu.roll(xh[7], NX - 1, 1) * mxh, pltpu.roll(xl[7], NY - NX + 1, 1) * mxl
+    halo = []
+    for side, ref, mask, sign in ((0, yl, myl, HALF_T), (1, yh, myh, -HALF_T)):
+        items = ref[...]
+        up = jnp.where(at_x == NX - 1, from_high[side : side + 1], pltpu.roll(items, NY - 1, 1)[1:2])
+        down = jnp.where(at_x == 0, from_low[side : side + 1], pltpu.roll(items, 1, 1)[1:2])
+        d_en = HALF_T * (up - down) * items[5:6]
+        own_r, own_m = yown[2 * side : 2 * side + 1], yown[2 * side + 1 : 2 * side + 2]
+        d_my = items[2:3] + sign * (own_r + own_m * items[3:4]) - d_en * items[4:5]
+        halo += [items[0:1] * mask, items[1:2] * mask, d_my * mask, d_en * mask]
+    yc[...] = jnp.concatenate(halo, axis=0).T
+    deep = lax.broadcasted_iota(jnp.int32, (NX, NY), 0)
+    up = jnp.where(deep == NX - 1, xh[7, 2:3, :] * mxh, pltpu.roll(zr[1], NX - 1, 0))
+    down = jnp.where(deep == 0, xl[7, 2:3, :] * mxl, pltpu.roll(zr[1], 1, 0))
+    d_en = HALF_T * (up - down) * zr[5]
+    za = dyn_layer(face_layer(first, 0))
+    d_mz = (
+        zr[2]
+        + jnp.where(first, -HALF_T, HALF_T) * (lam_ref[0, za, :] + lam_ref[1, za, :] * zr[3])
+        - d_en * zr[4]
+    )
+    for k, value in ((0, d_mz), (1, d_en)):
+        gz[k, layer(0), :] = value * mzl
+        gz[k, layer(NZ + 1), :] = value * mzh
     for z in range(NZ):
         r, mx, my, mz, en = [u_ref[k, layer(z), :] for k in range(5)]
         gamma = g_ref[layer(z), :]
@@ -370,8 +465,8 @@
         lm_x = [lx[1, pl.ds(24 * z + s, 8), :] for s in (7, 9)]
         lr_z = [lz[0, layer(z + s), :] for s in (0, 2)]
         lm_z = [lz[1, layer(z + s), :] for s in (0, 2)]
-        lr_y = [y_prev(lr, yc[layer(z), 0:1], lane), y_next(lr, yc[layer(z), 2:3], lane)]
-        lm_y = [y_prev(lm, yc[layer(z), 1:2], lane), y_next(lm, yc[layer(z), 3:4], lane)]
+        lr_y = [y_prev(lr, yc[layer(z), 0:1], lane), y_next(lr, yc[layer(z), 4:5], lane)]
+        lm_y = [y_prev(lm, yc[layer(z), 1:2], lane), y_next(lm, yc[layer(z), 5:6], lane)]
         phi_x0 = HALF_T * (lr_x[1] - lr_x[0])
         phi_y0 = HALF_T * (lr_y[1] - lr_y[0])
         phi_z0 = HALF_T * (lr_z[1] - lr_z[0])
@@ -381,71 +476,37 @@
         near = (lm_x[0] + lm_x[1]) + (lm_y[0] + lm_y[1]) + (lm_z[0] + lm_z[1])
         d_speed = phi_x1 * mx + 0.5 * (dx[pl.ds(24 * z + 7, 8), :] - dx[pl.ds(24 * z + 9, 8), :])
         d_en = phi_x1 * gamma
-        out_mx = (
-            lm * (1.0 - 3.0 * time_ratio * signal_speed)
-            + (time_ratio * HALF_C) * near
+        gx[0, pl.ds(24 * z + 8, 8), :] = (
+            STAY * lm
+            + NEAR * near
             + phi_x0
             + (phi_x1 - d_en) * ux
             + phi_y1 * uy
             + phi_z1 * uz
             + d_speed * inv
         )
-        out_my = phi_y0 - d_en * uy + phi_y1 * ux
-        out_mz = phi_z0 - d_en * uz + phi_z1 * ux
-        out_ref[0, layer(z), :] = out_mx
-        out_ref[1, layer(z), :] = out_my
-        out_ref[2, layer(z), :] = out_mz
-        out_ref[3, layer(z), :] = d_en
-        dg_ref[layer(z), :] = phi_x1 * heat
-        yp[layer(z), :] = pack_columns([out_my, d_en], lane)
-    for out, edge in ((xlo, 0), (xhi, NX - 1)):
-        out[0] = out_ref[0, x_row(edge), :]
-        out[1] = out_ref[3, x_row(edge), :]
-    za = face_layer(first, 0)
-    zs[0] = out_ref[2, dyn_layer(za), :]
-    zs[1] = out_ref[3, dyn_layer(za), :]
-    rows = yp[...].T
-    for k in range(2):
-        yhi[k : k + 1] = rows[2 * k : 2 * k + 1]
-        ylo[k : k + 1] = rows[2 * k + 1 : 2 * k + 2]
-    yhi[2:8] = jnp.zeros((6, NY), F32)
-    ylo[2:8] = jnp.zeros((6, NY), F32)
-
-
-def gradient_kernel(
-    mesh, u_ref, lam_ref, dg_ref, mis_ref, v_ref, xl, xh, yl, yh, zr,
-    grad_ref, row_ref,
-    lx, lz, yc,
-):
-    (mxl, mxh), (myl, myh), (mzl, mzh), first = masks(mesh)
-    lane = lanes()
-    for k in range(2):
-        for z in range(NZ):
-            lx[k, pl.ds(24 * z + 8, 8), :] = lam_ref[3 * k, layer(z), :]
-            lz[k, layer(z + 1), :] = lam_ref[2 + k, layer(z), :]
-        lx[k, pl.ds(7, NZ, stride=24), :] = xl[k] * mxl
-        lx[k, pl.ds(16, NZ, stride=24), :] = xh[k] * mxh
-        lz[k, layer(0), :] = zr[k] * mzl
-        lz[k, layer(NZ + 1), :] = zr[k] * mzh
-    yc[...] = columns_of(yl, yh, 2, myl, myh)
+        gx[1, pl.ds(24 * z + 8, 8), :] = d_en
+        gy[layer(z), :] = phi_y0 - d_en * uy + phi_y1 * ux
+        gz[0, layer(z + 1), :] = phi_z0 - d_en * uz + phi_z1 * ux
+        gz[1, layer(z + 1), :] = d_en
+        dg[layer(z), :] = phi_x1 * heat
     acc = jnp.zeros((NX, NY), F32)
     for z in range(NZ):
-        r, mx, my, mz, en = [u_ref[k, layer(z), :] for k in range(5)]
+        r, mx, my, mz, en = [u0_ref[k, layer(z), :] for k in range(5)]
         inv = 1.0 / (1.0 + r)
         ux, uy, uz = mx * inv, my * inv, mz * inv
         heat = en - 0.5 * (mx * ux + my * uy + mz * uz)
-        dif_x = [lx[k, pl.ds(24 * z + 9, 8), :] - lx[k, pl.ds(24 * z + 7, 8), :] for k in range(2)]
-        dif_z = [lz[k, layer(z + 2), :] - lz[k, layer(z), :] for k in range(2)]
+        dif_x = [gx[k, pl.ds(24 * z + 9, 8), :] - gx[k, pl.ds(24 * z + 7, 8), :] for k in range(2)]
+        dif_z = [gz[k, layer(z + 2), :] - gz[k, layer(z), :] for k in range(2)]
         dif_y = []
-        for k in range(2):
-            own = lam_ref[1 + 2 * k, layer(z), :]
+        for k, own in ((0, gy[layer(z), :]), (1, gz[1, layer(z + 1), :])):
             dif_y.append(
-                y_next(own, yc[layer(z), 2 + k : 3 + k], lane) - y_prev(own, yc[layer(z), k : k + 1], lane)
+                y_next(own, yc[layer(z), 6 + k : 7 + k], lane) - y_prev(own, yc[layer(z), 2 + k : 3 + k], lane)
             )
         d_press = HALF_T * (
             (dif_x[0] + ux * dif_x[1]) + (dif_y[0] + uy * dif_y[1]) + (dif_z[0] + uz * dif_z[1])
         )
-        grad = dg_ref[layer(z), :] + d_press * heat
+        grad = dg[layer(z), :] + d_press * heat
         grad_ref[layer(z), :] = grad
         acc = acc + grad * grad
     total = jnp.sum(jnp.sum(acc, axis=0, keepdims=True), axis=1, keepdims=True)
@@ -510,27 +571,38 @@
     return pltpu.VMEM(shape, F32)
 
 
-def call(kernel, outs, scratch, flops=100000):
+def call(kernel, outs, scratch, params=SMALL):
     return pl.pallas_call(
         kernel,
         out_shape=outs,
         scratch_shapes=scratch,
-        cost_estimate=pl.CostEstimate(flops=flops, bytes_accessed=100000, transcendentals=0),
-        compiler_params=SMALL,
+        cost_estimate=pl.CostEstimate(flops=100000, bytes_accessed=100000, transcendentals=0),
+        compiler_params=params,
     )
 
 
+def ring(sizes, axis, step):
+    n = sizes[axis]
+    return [(i, (i + step) % n) for i in range(n)]
+
+
+def exchange_x(sizes, xlo, xhi):
+    return (
+        lax.ppermute(xhi, "gx", ring(sizes, "gx", 1)),
+        lax.ppermute(xlo, "gx", ring(sizes, "gx", -1)),
+    )
+
+
+def exchange_yz(sizes, ylo, yhi, zs):
+    zr = lax.ppermute(zs, "gz", ring(sizes, "gz", 1))
+    yl = lax.ppermute(yhi, "gy", ring(sizes, "gy", 1))
+    yh = lax.ppermute(ylo, "gy", ring(sizes, "gy", -1))
+    return yl, yh, zr
+
+
 def exchange(sizes, xlo, xhi, ylo, yhi, zs):
-    def ring(axis, step):
-        n = sizes[axis]
-        return [(i, (i + step) % n) for i in range(n)]
-
-    zr = lax.ppermute(zs, "gz", ring("gz", 1))
-    xl = lax.ppermute(xhi, "gx", ring("gx", 1))
-    xh = lax.ppermute(xlo, "gx", ring("gx", -1))
-    yl = lax.ppermute(yhi, "gy", ring("gy", 1))
-    yh = lax.ppermute(ylo, "gy", ring("gy", -1))
-    return xl, xh, yl, yh, zr
+    xl, xh = exchange_x(sizes, xlo, xhi)
+    return xl, xh, *exchange_yz(sizes, ylo, yhi, zs)
 
 
 def local(sizes, checkpoint, gruneisen, switch, probes, observed):
@@ -544,7 +616,7 @@
         x = rows_of(x_items, NZ, NY)
         return [x, x, plane, plane, rows_of(z_items, NX, NY)]
 
-    *sent, yown = call(bind(prep_kernel, sizes), slabs(8, 8) + [plane], [vmem(CELLS, NY)])(state, gamma, sw)
+    *sent, yown = call(bind(prep_kernel, sizes), slabs(8, 8) + [plane], [vmem(CELLS, NY)], None)(state, gamma, sw)
     got = exchange(sizes, *sent)
     hits, mean, spread = call(
         probe_kernel,
@@ -562,30 +634,27 @@
         ],
     )(state, gamma, sw, *got, yown)
     got = exchange(sizes, *sent)
-    lam_2, coef, coef_halo, mis, *sent = call(
+    lam_2, coef, coef_halo, mis, *sent, yown = call(
         bind(speed_kernel, sizes),
-        [rows_of(2, CELLS, NY), rows_of(CELLS, NY), rows_of(2, NZ, NY), plane] + slabs(3, 2),
+        [rows_of(2, CELLS, NY), rows_of(CELLS, NY), rows_of(2, NZ, NY), plane]
+        + [plane, plane, rows_of(6, NX, NY), plane],
         [
             vmem(NZ * 24, NY), vmem(2, NZ * 16, NY), vmem(2, NZ * 16, NY), vmem(2, tall, NY), vmem(2, tall, NY),
             vmem(2, CELLS, NY), vmem(CELLS, 8), vmem(CELLS, NY),
         ],
     )(state_1, gamma, sw, *got, hits, mean)
-    got = exchange(sizes, *sent)
-    lam_1, d_gamma, *sent = call(
-        bind(adjoint_kernel, sizes),
-        [rows_of(4, CELLS, NY), rows_of(CELLS, NY)] + slabs(2, 2),
-        [
-            vmem(2, NZ * 24, NY), vmem(2, tall, NY), vmem(CELLS, NY), vmem(NZ * 24, NY),
-            vmem(CELLS, 8), vmem(CELLS, NY),
-        ],
-    )(state_1, gamma, lam_2, coef, coef_halo, *got)
-    got = exchange(sizes, *sent)
+    got_yz = exchange_yz(sizes, *sent)
+    sent = call(bind(edge_kernel, sizes), slabs(8, 1)[:2], [vmem(CELLS, NY)])(state_1, gamma, lam_2, coef, *got_yz)
+    got_x = exchange_x(sizes, *sent)
     devices = sizes["gx"] * sizes["gy"] * sizes["gz"]
     gradient, rows = call(
         bind(gradient_kernel, sizes),
         [rows_of(CELLS, NY), rows_of(devices, NY)],
-        [vmem(2, NZ * 24, NY), vmem(2, tall, NY), vmem(CELLS, 8)],
-    )(state, lam_1, d_gamma, mis, spread, *got)
+        [
+            vmem(2, NZ * 24, NY), vmem(2, tall, NY), vmem(CELLS, NY), vmem(NZ * 24, NY), vmem(CELLS, NY),
+            vmem(CELLS, 8), vmem(2, NZ * 24, NY), vmem(CELLS, NY), vmem(2, tall, NY),
+        ],
+    )(state, state_1, gamma, lam_2, coef, coef_halo, yown, *got_yz, *got_x, mis, spread)
     rows = lax.all_to_all(rows, ("gx", "gy", "gz"), 0, 0, tiled=True)
     direction, misfit = pl.pallas_call(
         bind(scale_kernel, devices, probes.shape[0]),

time: 77.9 us -> 71.6 us (0.919)
  starting transfers between devices: 31.9 us -> 24.9 us
  blocking collectives: 19.6 us -> 24.3 us
  local copies, waits for them, and re-layouts: 3.4 us -> 0.7 us
  waiting for transfers between devices: 17.5 us -> 14.8 us
  Pallas kernels: 4.31 us -> 6.01 us
    ppermute x20 -> x15, starting transfers between devices: 31.9 us -> 24.9 us  [the longest x3 13.4 us: exchange_x(): lax.ppermute(xlo, 'gx', ring(sizes, 'gx', -1))]
    all_to_all x1, blocking collectives: 19.6 us -> 24.3 us  [local(): rows = lax.all_to_all(rows, ('gx', 'gy', 'gz'), 0, 0, tiled=True)]
    ppermute x20 -> x15, waiting for transfers between devices: 17.5 us -> 14.8 us  [the longest x3 11.4 us: exchange_yz(): yh = lax.ppermute(ylo, 'gy', ring(sizes, 'gy', -1))]
    unnamed x12 -> x14, local copies, waits for them, and re-layouts: 3.4 us -> 0.7 us
    pallas_call x2, Pallas kernels: 0.74 us -> 2.16 us  [the longest x1 1.95 us: local(): call(bind(prep_kernel, sizes), slabs(8, 8) + [plane], [vmem(CELLS, NY)],...]
  transfers between devices with their start and end apart: 20 -> 15, of which waited for: 7 -> 6; matrix products, arithmetic and copies ran while one was open for 0% -> 0% of each run, Pallas kernels for 1% -> 1%
where the time goes in v3:
time: 71.6 us; the launch traced here: 71.5 us
  starting transfers between devices  24.9 us (35%)
  blocking collectives  24.3 us (34%)
  waiting for transfers between devices  14.8 us (21%)
  Pallas kernels  6.01 us (8%)
  between operations  0.76 us (1%)
    all_to_all x1, blocking collectives, local(): rows = lax.all_to_all(rows, ('gx', 'gy', 'gz'), 0, 0, tiled=True)  24.3 us
    ppermute x3, starting transfers between devices, exchange_x(): lax.ppermute(xlo, 'gx', ring(sizes, 'gx', -1))  13.4 us
    ppermute x3, waiting for transfers between devices, exchange_yz(): yh = lax.ppermute(ylo, 'gy', ring(sizes, 'gy', -1))  11.4 us
    ppermute x3, starting transfers between devices, exchange_yz(): yl = lax.ppermute(yhi, 'gy', ring(sizes, 'gy', 1))  6.85 us
    ppermute x3, starting transfers between devices, exchange_yz(): zr = lax.ppermute(zs, 'gz', ring(sizes, 'gz', 1))  2.46 us
    ppermute x3, starting transfers between devices, exchange_x(): lax.ppermute(xhi, 'gx', ring(sizes, 'gx', 1))  2.24 us
    pallas_call x1, Pallas kernels, local(): call(bind(prep_kernel, sizes), slabs(8, 8) + [plane], [vmem(CELLS, NY)],...  1.95 us
    ppermute x3, waiting for transfers between devices, exchange_yz(): yl = lax.ppermute(yhi, 'gy', ring(sizes, 'gy', 1))  1.71 us
  transfers between devices with their start and end apart: 15, of which 6 were waited for; matrix products, arithmetic and copies ran while one was open for 0% of the time, Pallas kernels for 1%

profile of v3, /device:TPU:1, one launch (start us, length us, event | category | flops | bytes accessed | tf_op | source)
XLA Modules:
  0.0 71.5 jit_solution(12775169942414600449)
XLA Ops:
  0.7 2.0 %shard_map.68 = (f32[8,16,128]{2,1,0:T(8,128)}, f32[8,16,128]{2,1,0:T(8,128)}, f32[8,128]{1,0:T(8,128)}, f32[8,128]{1,0:T(8,128)}, f32[8,8,128]{2,1,0:T(8,128)}, /*index=5*/f32[8,128]{1,0:T(8,128)}) custom-call(f32[5,128,128]{2,1,0:T(8,128)} %bitcast.11, f32[128,128]{1,0:T(8,128)} %bitcast.14, s32[2,128,128]{2,1,0:T(8,128)} %bitcast.19), custom_call_target="tpu_custom_call" | custom-call | flops 100000 | bytes 100000 | tf_op jit(solution)/shard_map/pallas_call | solution.py:619
  2.6 2.1 %collective-permute-start = (f32[8,16,128]{2,1,0:T(8,128)}, f32[8,16,128]{2,1,0:T(8,128)S(1)}, u32[]{:S(2)}, u32[]{:S(2)}) collective-permute-start(f32[8,16,128]{2,1,0:T(8,128)} %get-tuple-element.31), channel_id=1, source_target_pairs={{0,16},{16,32},{32,48},{48,64},{64,80},{80,96},{96,112},{112,128},... | collective-permute-start | bytes 196616 | tf_op jit(solution)/shard_map/ppermute | solution.py:591
  4.7 3.8 %collective-permute-start.1 = (f32[8,16,128]{2,1,0:T(8,128)}, f32[8,16,128]{2,1,0:T(8,128)S(1)}, u32[]{:S(2)}, u32[]{:S(2)}) collective-permute-start(f32[8,16,128]{2,1,0:T(8,128)} %get-tuple-element.32), channel_id=1, source_target_pairs={{0,240},{16,0},{32,16},{48,32},{64,48},{80,64},{96,80},{112,96},{1... | collective-permute-start | bytes 196616 | tf_op jit(solution)/shard_map/ppermute | solution.py:592
  8.5 1.6 %collective-permute-start.4 = (f32[8,8,128]{2,1,0:T(8,128)}, f32[8,8,128]{2,1,0:T(8,128)S(1)}, u32[]{:S(2)}, u32[]{:S(2)}) collective-permute-start(f32[8,8,128]{2,1,0:T(8,128)} %get-tuple-element.35), channel_id=1, source_target_pairs={{0,1},{1,0},{2,3},{3,2},{4,5},{5,4},{6,7},{7,6},{8,9},{9,8},{10,11... | collective-permute-start | bytes 98312 | tf_op jit(solution)/shard_map/ppermute | solution.py:597
  10.2 4.2 %collective-permute-start.2 = (f32[8,128]{1,0:T(8,128)}, f32[8,128]{1,0:T(8,128)S(1)}, u32[]{:S(2)}, u32[]{:S(2)}) collective-permute-start(f32[8,128]{1,0:T(8,128)} %get-tuple-element.33), channel_id=1, source_target_pairs={{0,2},{2,4},{4,6},{6,8},{8,10},{10,12},{12,14},{14,0},{1,3},{3,5},... | collective-permute-start | bytes 12296 | tf_op jit(solution)/shard_map/ppermute | solution.py:598
  14.3 1.0 %collective-permute-done.2.yl = f32[8,128]{1,0:T(8,128)S(1)} collective-permute-done((f32[8,128]{1,0:T(8,128)}, f32[8,128]{1,0:T(8,128)S(1)}, u32[]{:S(2)}, u32[]{:S(2)}) %collective-permute-start.2) | collective-permute-done | bytes 4128 | tf_op jit(solution)/shard_map/ppermute | solution.py:598
  15.3 3.0 %collective-permute-done.3.yh = f32[8,128]{1,0:T(8,128)S(1)} collective-permute-done((f32[8,128]{1,0:T(8,128)S(1)}, f32[8,128]{1,0:T(8,128)S(1)}, u32[]{:S(2)}, u32[]{:S(2)}) %collective-permute-start.3) | collective-permute-done | bytes 4128 | tf_op jit(solution)/shard_map/ppermute | solution.py:599
  18.3 1.4 %shard_map.69 = (f32[5,128,128]{2,1,0:T(8,128)S(1)}, f32[5,16,128]{2,1,0:T(8,128)S(1)}, f32[5,16,128]{2,1,0:T(8,128)S(1)}, f32[8,128]{1,0:T(8,128)S(1)}, f32[8,128]{1,0:T(8,128)S(1)}, /*index=5*/f32[2,8,128]{2,1,0:T(8,128)S(1)}) custom-call(f32[5,128,128]{2,1,0:T(8,128)S(1)} %bitcast.12, f32[128,128]{1,0:T(8,128)S(1)} %bitcast.15, ...), custom_call_target="tpu_custom_call" | custom-call | flops 100000 | bytes 100000 | tf_op jit(solution)/shard_map/pallas_call | solution.py:627
  19.8 4.8 %collective-permute-start.6 = (f32[5,16,128]{2,1,0:T(8,128)S(1)}, f32[5,16,128]{2,1,0:T(8,128)S(1)}, u32[]{:S(2)}, u32[]{:S(2)}) collective-permute-start(f32[5,16,128]{2,1,0:T(8,128)S(1)} %get-tuple-element.39), channel_id=1, source_target_pairs={{0,240},{16,0},{32,16},{48,32},{64,48},{80,64},{96,80},{112,96},{1... | collective-permute-start | bytes 122888 | tf_op jit(solution)/shard_map/ppermute | solution.py:592
  24.6 2.0 %collective-permute-start.7 = (f32[8,128]{1,0:T(8,128)S(1)}, f32[8,128]{1,0:T(8,128)S(1)}, u32[]{:S(2)}, u32[]{:S(2)}) collective-permute-start(f32[8,128]{1,0:T(8,128)S(1)} %get-tuple-element.40), channel_id=1, source_target_pairs={{0,2},{2,4},{4,6},{6,8},{8,10},{10,12},{12,14},{14,0},{1,3},{3,5},... | collective-permute-start | bytes 12296 | tf_op jit(solution)/shard_map/ppermute | solution.py:598
  26.6 0.7 copy-done.4
  27.3 0.5 shard_map.70
  27.8 3.7 %collective-permute-done.8.yh = f32[8,128]{1,0:T(8,128)S(1)} collective-permute-done((f32[8,128]{1,0:T(8,128)S(1)}, f32[8,128]{1,0:T(8,128)S(1)}, u32[]{:S(2)}, u32[]{:S(2)}) %collective-permute-start.8) | collective-permute-done | bytes 4128 | tf_op jit(solution)/shard_map/ppermute | solution.py:599
  31.5 0.5 shard_map.71
  32.0 0.8 %collective-permute-start.12 = (f32[6,8,128]{2,1,0:T(8,128)S(1)}, f32[6,8,128]{2,1,0:T(8,128)S(1)}, u32[]{:S(2)}, u32[]{:S(2)}) collective-permute-start(f32[6,8,128]{2,1,0:T(8,128)S(1)} %get-tuple-element.51), channel_id=1, source_target_pairs={{0,1},{1,0},{2,3},{3,2},{4,5},{5,4},{6,7},{7,6},{8,9},{9,8},{10,11... | collective-permute-start | bytes 73736 | tf_op jit(solution)/shard_map/ppermute | solution.py:597
  32.8 0.7 collective-permute-start.10
  33.5 0.8 %collective-permute-done.10.yl = f32[8,128]{1,0:T(8,128)S(1)} collective-permute-done((f32[8,128]{1,0:T(8,128)S(1)}, f32[8,128]{1,0:T(8,128)S(1)}, u32[]{:S(2)}, u32[]{:S(2)}) %collective-permute-start.10) | collective-permute-done | bytes 4128 | tf_op jit(solution)/shard_map/ppermute | solution.py:598
  34.3 4.7 %collective-permute-done.11.yh = f32[8,128]{1,0:T(8,128)S(1)} collective-permute-done((f32[8,128]{1,0:T(8,128)S(1)}, f32[8,128]{1,0:T(8,128)S(1)}, u32[]{:S(2)}, u32[]{:S(2)}) %collective-permute-start.11) | collective-permute-done | bytes 4128 | tf_op jit(solution)/shard_map/ppermute | solution.py:599
  39.0 0.2 shard_map.72
  39.3 4.8 %collective-permute-start.14 = (f32[8,16,128]{2,1,0:T(8,128)S(1)}, f32[8,16,128]{2,1,0:T(8,128)S(1)}, u32[]{:S(2)}, u32[]{:S(2)}) collective-permute-start(f32[8,16,128]{2,1,0:T(8,128)S(1)} %get-tuple-element.53), channel_id=1, source_target_pairs={{0,240},{16,0},{32,16},{48,32},{64,48},{80,64},{96,80},{112,96},{1... | collective-permute-start | bytes 196616 | tf_op jit(solution)/shard_map/ppermute | solution.py:592
  44.1 1.6 %collective-permute-done.13.xl = f32[8,16,128]{2,1,0:T(8,128)S(1)} collective-permute-done((f32[8,16,128]{2,1,0:T(8,128)S(1)}, f32[8,16,128]{2,1,0:T(8,128)S(1)}, u32[]{:S(2)}, u32[]{:S(2)}) %collective-permute-start.13) | collective-permute-done | bytes 65568 | tf_op jit(solution)/shard_map/ppermute | solution.py:591
  45.7 0.7 shard_map.73
  46.4 24.3 %all_to_all.11 = f32[256,1,128]{2,1,0:T(1,128)S(1)} all-to-all(f32[256,1,128]{2,1,0:T(1,128)S(1)} %bitcast.23), channel_id=1, replica_groups=mesh['gx'=16,'gy'=8,'gz'=2] {'gx','gy','gz'}, dimensions={0} | all-to-all | bytes 262144 | tf_op jit(solution)/shard_map/all_to_all | solution.py:658
  70.7 0.8 %shard_map.74 = (f32[128,128]{1,0:T(8,128)}, f32[1,1]{1,0:T(1,128)}) custom-call(f32[128,128]{1,0:T(8,128)S(1)} %get-tuple-element.56.grad_ref, f32[256,128]{1,0:T(8,128)S(1)} %bitcast.22), custom_call_target="tpu_custom_call" | custom-call | tf_op jit(solution)/shard_map/pallas_call | solution.py:659
  (28 shorter events, 0.2 us)
Async XLA Ops:
  0.6 17.6 %copy-start = (f32[5,16,8,128]{3,2,1,0:T(8,128)S(1)}, f32[5,16,8,128]{3,2,1,0:T(8,128)}, u32[]{:S(2)}) copy-start(f32[5,16,8,128]{3,2,1,0:T(8,128)} %param.5) | copy-start | bytes 983044
  0.6 17.6 %copy-start.1 = (f32[16,8,128]{2,1,0:T(8,128)S(1)}, f32[16,8,128]{2,1,0:T(8,128)}, u32[]{:S(2)}) copy-start(f32[16,8,128]{2,1,0:T(8,128)} %param.6) | copy-start | bytes 196612
  0.6 17.6 %copy-start.2 = (s32[2,16,8,128]{3,2,1,0:T(8,128)S(1)}, s32[2,16,8,128]{3,2,1,0:T(8,128)}, u32[]{:S(2)}) copy-start(s32[2,16,8,128]{3,2,1,0:T(8,128)} %param.7) | copy-start | bytes 393220
  2.6 11.7 %copy-start.6 = (f32[8,128]{1,0:T(8,128)S(1)}, f32[8,128]{1,0:T(8,128)}, u32[]{:S(2)}) copy-start(f32[8,128]{1,0:T(8,128)} %get-tuple-element.34) | copy-start | bytes 12292
  2.6 15.6 %collective-permute-start = (f32[8,16,128]{2,1,0:T(8,128)}, f32[8,16,128]{2,1,0:T(8,128)S(1)}, u32[]{:S(2)}, u32[]{:S(2)}) collective-permute-start(f32[8,16,128]{2,1,0:T(8,128)} %get-tuple-element.31), channel_id=1, source_target_pairs={{0,16},{16,32},{32,48},{48,64},{64,80},{80,96},{96,112},{112,128},... | collective-permute-start | bytes 196616 | tf_op jit(solution)/shard_map/ppermute | solution.py:591
  4.7 13.6 %copy-start.3 = (f32[8,128]{1,0:T(8,128)S(1)}, f32[8,128]{1,0:T(8,128)}, u32[]{:S(2)}) copy-start(f32[8,128]{1,0:T(8,128)} %get-tuple-element.36.yown) | copy-start | bytes 12292
  4.7 13.5 %collective-permute-start.1 = (f32[8,16,128]{2,1,0:T(8,128)}, f32[8,16,128]{2,1,0:T(8,128)S(1)}, u32[]{:S(2)}, u32[]{:S(2)}) collective-permute-start(f32[8,16,128]{2,1,0:T(8,128)} %get-tuple-element.32), channel_id=1, source_target_pairs={{0,240},{16,0},{32,16},{48,32},{64,48},{80,64},{96,80},{112,96},{1... | collective-permute-start | bytes 196616 | tf_op jit(solution)/shard_map/ppermute | solution.py:592
  8.5 9.7 %collective-permute-start.4 = (f32[8,8,128]{2,1,0:T(8,128)}, f32[8,8,128]{2,1,0:T(8,128)S(1)}, u32[]{:S(2)}, u32[]{:S(2)}) collective-permute-start(f32[8,8,128]{2,1,0:T(8,128)} %get-tuple-element.35), channel_id=1, source_target_pairs={{0,1},{1,0},{2,3},{3,2},{4,5},{5,4},{6,7},{7,6},{8,9},{9,8},{10,11... | collective-permute-start | bytes 98312 | tf_op jit(solution)/shard_map/ppermute | solution.py:597
  10.2 5.1 %collective-permute-start.2 = (f32[8,128]{1,0:T(8,128)}, f32[8,128]{1,0:T(8,128)S(1)}, u32[]{:S(2)}, u32[]{:S(2)}) collective-permute-start(f32[8,128]{1,0:T(8,128)} %get-tuple-element.33), channel_id=1, source_target_pairs={{0,2},{2,4},{4,6},{6,8},{8,10},{10,12},{12,14},{14,0},{1,3},{3,5},... | collective-permute-start | bytes 12296 | tf_op jit(solution)/shard_map/ppermute | solution.py:598
  14.3 3.9 %collective-permute-start.3 = (f32[8,128]{1,0:T(8,128)S(1)}, f32[8,128]{1,0:T(8,128)S(1)}, u32[]{:S(2)}, u32[]{:S(2)}) collective-permute-start(f32[8,128]{1,0:T(8,128)S(1)} %copy-done.6), channel_id=1, source_target_pairs={{0,14},{2,0},{4,2},{6,4},{8,6},{10,8},{12,10},{14,12},{1,15},{3,1}... | collective-permute-start | bytes 12296 | tf_op jit(solution)/shard_map/ppermute | solution.py:599
  18.3 8.3 %copy-start.5 = (f32[256]{0:T(256)S(1)}, f32[256]{0:T(256)}, u32[]{:S(2)}) copy-start(f32[256]{0:T(256)} %param.9) | copy-start | bytes 3076
  19.7 11.8 %collective-permute-start.5 = (f32[5,16,128]{2,1,0:T(8,128)S(1)}, f32[5,16,128]{2,1,0:T(8,128)S(1)}, u32[]{:S(2)}, u32[]{:S(2)}) collective-permute-start(f32[5,16,128]{2,1,0:T(8,128)S(1)} %get-tuple-element.38), channel_id=1, source_target_pairs={{0,16},{16,32},{32,48},{48,64},{64,80},{80,96},{96,112},{112,128},... | collective-permute-start | bytes 122888 | tf_op jit(solution)/shard_map/ppermute | solution.py:591
  19.8 11.7 %collective-permute-start.6 = (f32[5,16,128]{2,1,0:T(8,128)S(1)}, f32[5,16,128]{2,1,0:T(8,128)S(1)}, u32[]{:S(2)}, u32[]{:S(2)}) collective-permute-start(f32[5,16,128]{2,1,0:T(8,128)S(1)} %get-tuple-element.39), channel_id=1, source_target_pairs={{0,240},{16,0},{32,16},{48,32},{64,48},{80,64},{96,80},{112,96},{1... | collective-permute-start | bytes 122888 | tf_op jit(solution)/shard_map/ppermute | solution.py:592
  24.6 6.9 %collective-permute-start.9 = (f32[2,8,128]{2,1,0:T(8,128)S(1)}, f32[2,8,128]{2,1,0:T(8,128)S(1)}, u32[]{:S(2)}, u32[]{:S(2)}) collective-permute-start(f32[2,8,128]{2,1,0:T(8,128)S(1)} %get-tuple-element.42), channel_id=1, source_target_pairs={{0,1},{1,0},{2,3},{3,2},{4,5},{5,4},{6,7},{7,6},{8,9},{9,8},{10,11... | collective-permute-start | bytes 24584 | tf_op jit(solution)/shard_map/ppermute | solution.py:597
  24.6 3.2 %collective-permute-start.7 = (f32[8,128]{1,0:T(8,128)S(1)}, f32[8,128]{1,0:T(8,128)S(1)}, u32[]{:S(2)}, u32[]{:S(2)}) collective-permute-start(f32[8,128]{1,0:T(8,128)S(1)} %get-tuple-element.40), channel_id=1, source_target_pairs={{0,2},{2,4},{4,6},{6,8},{8,10},{10,12},{12,14},{14,0},{1,3},{3,5},... | collective-permute-start | bytes 12296 | tf_op jit(solution)/shard_map/ppermute | solution.py:598
  26.6 4.9 %collective-permute-start.8 = (f32[8,128]{1,0:T(8,128)S(1)}, f32[8,128]{1,0:T(8,128)S(1)}, u32[]{:S(2)}, u32[]{:S(2)}) collective-permute-start(f32[8,128]{1,0:T(8,128)S(1)} %get-tuple-element.41), channel_id=1, source_target_pairs={{0,14},{2,0},{4,2},{6,4},{8,6},{10,8},{12,10},{14,12},{1,15},{3,1}... | collective-permute-start | bytes 12296 | tf_op jit(solution)/shard_map/ppermute | solution.py:599
  26.6 0.7 copy-start.4
  32.0 7.0 %collective-permute-start.12 = (f32[6,8,128]{2,1,0:T(8,128)S(1)}, f32[6,8,128]{2,1,0:T(8,128)S(1)}, u32[]{:S(2)}, u32[]{:S(2)}) collective-permute-start(f32[6,8,128]{2,1,0:T(8,128)S(1)} %get-tuple-element.51), channel_id=1, source_target_pairs={{0,1},{1,0},{2,3},{3,2},{4,5},{5,4},{6,7},{7,6},{8,9},{9,8},{10,11... | collective-permute-start | bytes 73736 | tf_op jit(solution)/shard_map/ppermute | solution.py:597
  32.8 1.5 %collective-permute-start.10 = (f32[8,128]{1,0:T(8,128)S(1)}, f32[8,128]{1,0:T(8,128)S(1)}, u32[]{:S(2)}, u32[]{:S(2)}) collective-permute-start(f32[8,128]{1,0:T(8,128)S(1)} %get-tuple-element.49), channel_id=1, source_target_pairs={{0,2},{2,4},{4,6},{6,8},{8,10},{10,12},{12,14},{14,0},{1,3},{3,5},... | collective-permute-start | bytes 12296 | tf_op jit(solution)/shard_map/ppermute | solution.py:598
  33.5 5.5 %collective-permute-start.11 = (f32[8,128]{1,0:T(8,128)S(1)}, f32[8,128]{1,0:T(8,128)S(1)}, u32[]{:S(2)}, u32[]{:S(2)}) collective-permute-start(f32[8,128]{1,0:T(8,128)S(1)} %get-tuple-element.50), channel_id=1, source_target_pairs={{0,14},{2,0},{4,2},{6,4},{8,6},{10,8},{12,10},{14,12},{1,15},{3,1}... | collective-permute-start | bytes 12296 | tf_op jit(solution)/shard_map/ppermute | solution.py:599
  39.2 6.5 %collective-permute-start.13 = (f32[8,16,128]{2,1,0:T(8,128)S(1)}, f32[8,16,128]{2,1,0:T(8,128)S(1)}, u32[]{:S(2)}, u32[]{:S(2)}) collective-permute-start(f32[8,16,128]{2,1,0:T(8,128)S(1)} %get-tuple-element.52), channel_id=1, source_target_pairs={{0,16},{16,32},{32,48},{48,64},{64,80},{80,96},{96,112},{112,128},... | collective-permute-start | bytes 196616 | tf_op jit(solution)/shard_map/ppermute | solution.py:591
  39.3 6.4 %collective-permute-start.14 = (f32[8,16,128]{2,1,0:T(8,128)S(1)}, f32[8,16,128]{2,1,0:T(8,128)S(1)}, u32[]{:S(2)}, u32[]{:S(2)}) collective-permute-start(f32[8,16,128]{2,1,0:T(8,128)S(1)} %get-tuple-element.53), channel_id=1, source_target_pairs={{0,240},{16,0},{32,16},{48,32},{64,48},{80,64},{96,80},{112,96},{1... | collective-permute-start | bytes 196616 | tf_op jit(solution)/shard_map/ppermute | solution.py:592

commit v4 on v3

--- a/solution.py
+++ b/solution.py
@@ -16,6 +16,8 @@
 small_eps = 1e-12
 HALF_C = 0.5 * signal_speed
 HALF_T = 0.5 * time_ratio
+NEAR = time_ratio * HALF_C
+STAY = 1.0 - 3.0 * time_ratio * signal_speed
 F32 = jnp.float32
 
 
@@ -88,81 +90,58 @@
     return pl.ds(pl.multiple_of(NX * z, NX), NX)
 
 
-def pack_columns(values, lane):
-    out = pltpu.roll(values[0], 1, 1)
+def pack_edges(values, lane, depth=2):
+    out = pltpu.roll(values[0], depth, 1)
     for i in range(1, len(values)):
-        out = jnp.where(lane < 2 * i, out, pltpu.roll(values[i], 2 * i + 1, 1))
+        out = jnp.where(lane < 2 * depth * i, out, pltpu.roll(values[i], depth * (2 * i + 1), 1))
     return out
 
 
-def pack_edges(values, lane):
-    out = pltpu.roll(values[0], 2, 1)
-    for i in range(1, len(values)):
-        out = jnp.where(lane < 4 * i, out, pltpu.roll(values[i], 4 * i + 2, 1))
-    return out
-
-
-def prep_kernel(mesh, u_ref, g_ref, s_ref, xlo, xhi, ylo, yhi, zs, yown, yp):
+def begun(u, f, far, sign):
+    return STAY * u + time_ratio * (sign * 0.5 * f + HALF_C * far)
+
+
+def prep_kernel(mesh, u_ref, g_ref, s_ref, ylo, yhi, zs, yp):
     _, _, _, first = masks(mesh)
-    for out, edge, second in ((xlo, 0, 1), (xhi, NX - 1, NX - 2)):
-        st = [u_ref[k, x_row(edge), :] for k in range(5)]
-        press = primitives(*st, g_ref[x_row(edge), :])[4]
-        for k in range(5):
-            out[k] = st[k]
-        out[5] = press
-        out[6] = s_ref[0, x_row(edge), :].astype(F32)
-        out[7] = u_ref[1, x_row(second), :] / (1.0 + u_ref[0, x_row(second), :])
-    za, zb = face_layer(first, 0), face_layer(first, 1)
-    st = [u_ref[k, dyn_layer(za), :] for k in range(5)]
-    for k in range(5):
-        zs[k] = st[k]
-    zs[5] = primitives(*st, g_ref[dyn_layer(za), :])[4]
-    zs[6] = s_ref[0, dyn_layer(za), :].astype(F32)
-    zs[7] = u_ref[3, dyn_layer(zb), :] / (1.0 + u_ref[0, dyn_layer(zb), :])
     lane = lanes()
     for z in range(NZ):
         vals = [u_ref[k, layer(z), :] for k in range(5)]
         vals += [g_ref[layer(z), :], s_ref[0, layer(z), :].astype(F32)]
-        yp[layer(z), :] = pack_edges(vals, lane)
+        yp[layer(z), :] = pack_edges(vals, lane, 3)
     rows = yp[...].T
-    for out, edge, second, own in ((yhi, 1, 0, 1), (ylo, 2, 3, 0)):
-        st = [rows[4 * k + edge : 4 * k + edge + 1] for k in range(7)]
-        prim = primitives(*st[:6])
-        for k in range(5):
-            out[k : k + 1] = st[k]
-        out[5:6] = prim[4]
-        out[6:7] = st[6]
-        out[7:8] = rows[8 + second : 9 + second] / (1.0 + rows[second : second + 1])
-        yown[own : own + 1] = prim[1]
-
-
-def step_kernel(
-    mesh, u_ref, g_ref, s_ref, xl, xh, yl, yh, zr, yown,
-    o_ref, xlo, xhi, ylo, yhi, zs,
-    vx, vy, vz, pr, ax, bx, az, bz, ch, yr, yc, yp,
+    for out, c1, c2, c3, sign in ((yhi, 2, 1, 0, 1.0), (ylo, 3, 4, 5, -1.0)):
+        st, st2, st3 = [[rows[6 * k + c : 6 * k + c + 1] for k in range(7)] for c in (c1, c2, c3)]
+        prim, prim2 = primitives(*st[:6]), primitives(*st2[:6])
+        slope = (sign * 0.5) * (prim[1] - st3[2] / (1.0 + st3[0]))
+        fl = flux(st2[:5], 1, prim2[1], total_pressure(prim2[4], st2[6], st2[0], slope))
+        items = st[:5] + [prim[4], st[6], prim2[1]] + [begun(st[k], fl[k], st2[k], sign) for k in range(3)]
+        for k in range(11):
+            out[k : k + 1] = items[k]
+        out[11:16] = jnp.zeros((5, NY), F32)
+    za, zb, zc = [dyn_layer(face_layer(first, d)) for d in range(3)]
+    sign = jnp.where(first, 1.0, -1.0)
+    st, st2 = [[u_ref[k, at, :] for k in range(5)] for at in (za, zb)]
+    prim, prim2 = primitives(*st, g_ref[za, :]), primitives(*st2, g_ref[zb, :])
+    slope = (sign * 0.5) * (prim[2] - u_ref[3, zc, :] / (1.0 + u_ref[0, zc, :]))
+    fl = flux(st2, 2, prim2[2], total_pressure(prim2[4], s_ref[0, zb, :].astype(F32), st2[0], slope))
+    items = st + [prim[4], s_ref[0, za, :].astype(F32), prim2[2]]
+    items += [begun(st[k], fl[k], st2[k], sign) for k in (0, 1, 3)]
+    for k in range(11):
+        zs[k] = items[k]
+
+
+def side_kernel(
+    mesh, u_ref, g_ref, s_ref, ylo, yhi, yl, yh, zr,
+    part, xlo, xhi, zz,
+    vy, vz, pr, az, bz, yr, yc,
 ):
-    (mxl, mxh), (myl, myh), (mzl, mzh), first = masks(mesh)
+    _, (myl, myh), (mzl, mzh), first = masks(mesh)
     lane = lanes()
     for z in range(NZ):
-        ux, uy, uz, _, press = primitives(*[u_ref[k, layer(z), :] for k in range(5)], g_ref[layer(z), :])
-        vx[pl.ds(24 * z + 8, 8), :] = ux
+        _, uy, uz, _, press = primitives(*[u_ref[k, layer(z), :] for k in range(5)], g_ref[layer(z), :])
         vy[layer(z), :] = uy
         vz[layer(z + 1), :] = uz
         pr[layer(z), :] = press
-    low = [xl[k] * mxl for k in range(8)]
-    high = [xh[k] * mxh for k in range(8)]
-    speed = low[1] / (1.0 + low[0])
-    vx[pl.ds(7, NZ, stride=24), :] = speed
-    slope = 0.5 * (vx[pl.ds(8, NZ, stride=24), :] - low[7])
-    fl = flux(low[:5], 0, speed, total_pressure(low[5], low[6], low[0], slope))
-    for k in range(5):
-        bx[k, pl.ds(7, NZ, stride=16), :] = lower_part(fl[k], low[k])
-    speed = high[1] / (1.0 + high[0])
-    vx[pl.ds(16, NZ, stride=24), :] = speed
-    slope = 0.5 * (high[7] - vx[pl.ds(15, NZ, stride=24), :])
-    fl = flux(high[:5], 0, speed, total_pressure(high[5], high[6], high[0], slope))
-    for k in range(5):
-        ax[k, pl.ds(8, NZ, stride=16), :] = upper_part(fl[k], high[k])
     far = [zr[k] for k in range(8)]
     speed = far[3] / (1.0 + far[0])
     own = vz[dyn_layer(face_layer(first, 0) + 1), :]
@@ -177,13 +156,13 @@
     high = [yh[k : k + 1] * myh for k in range(8)]
     speed = low[2] / (1.0 + low[0])
     yr[10:11, :] = speed
-    slope = 0.5 * (yown[0:1] - low[7])
+    slope = 0.5 * (ylo[2:3] / (1.0 + ylo[0:1]) - low[7])
     fl = flux(low[:5], 1, speed, total_pressure(low[5], low[6], low[0], slope))
     for k in range(5):
         yr[k : k + 1, :] = lower_part(fl[k], low[k])
     speed = high[2] / (1.0 + high[0])
     yr[11:12, :] = speed
-    slope = 0.5 * (high[7] - yown[1:2])
+    slope = 0.5 * (high[7] - yhi[2:3] / (1.0 + yhi[0:1]))
     fl = flux(high[:5], 1, speed, total_pressure(high[5], high[6], high[0], slope))
     for k in range(5):
         yr[5 + k : 6 + k, :] = upper_part(fl[k], high[k])
@@ -191,12 +170,9 @@
     yc[...] = yr[...].T
     for z in range(NZ):
         st = [u_ref[k, layer(z), :] for k in range(5)]
-        sw = s_ref[0, layer(z), :].astype(F32)
         press = pr[layer(z), :]
-        visc = sw * quad_viscosity * (1.0 + st[0])
-        uy = vy[layer(z), :]
-        ux = vx[pl.ds(24 * z + 8, 8), :]
-        uz = vz[layer(z + 1), :]
+        visc = s_ref[0, layer(z), :].astype(F32) * quad_viscosity * (1.0 + st[0])
+        uy, uz = vy[layer(z), :], vz[layer(z + 1), :]
 
         def col(i):
             return yc[layer(z), i : i + 1]
@@ -205,51 +181,217 @@
             squeeze = jnp.minimum(0.5 * (up - down), 0.0)
             return press + visc * squeeze * squeeze
 
-        fx = flux(st, 0, ux, total(vx[pl.ds(24 * z + 9, 8), :], vx[pl.ds(24 * z + 7, 8), :]))
         fy = flux(st, 1, uy, total(y_next(uy, col(11), lane), y_prev(uy, col(10), lane)))
         fz = flux(st, 2, uz, total(vz[layer(z + 2), :], vz[layer(z), :]))
         for k in range(5):
+            az[k, layer(z), :] = upper_part(fz[k], st[k])
+            bz[k, layer(z + 1), :] = lower_part(fz[k], st[k])
+            part[k, layer(z), :] = STAY * st[k] - time_ratio * (
+                y_next(upper_part(fy[k], st[k]), col(5 + k), lane)
+                - y_prev(lower_part(fy[k], st[k]), col(k), lane)
+            )
+    for z in range(NZ):
+        for k in range(5):
+            part[k, layer(z), :] = part[k, layer(z), :] - time_ratio * (
+                az[k, layer(z + 1), :] - bz[k, layer(z), :]
+            )
+    for k in range(8):
+        zz[k : k + 1, :] = low[k]
+        zz[8 + k : 9 + k, :] = high[k]
+    for out, e, i, j, sign in ((xhi, NX - 1, NX - 2, NX - 3, 1.0), (xlo, 0, 1, 2, -1.0)):
+        st, st1, st2 = [[u_ref[k, x_row(at), :] for k in range(5)] for at in (e, i, j)]
+        ux = st[1] / (1.0 + st[0])
+        prim1, prim2 = primitives(*st1, g_ref[x_row(i), :]), primitives(*st2, g_ref[x_row(j), :])
+        last = j - 1 if sign > 0 else j + 1
+        ux3 = u_ref[1, x_row(last), :] / (1.0 + u_ref[0, x_row(last), :])
+        slope1, slope2 = (sign * 0.5) * (ux - prim2[0]), (sign * 0.5) * (prim1[0] - ux3)
+        f1 = flux(st1, 0, prim1[0], total_pressure(prim1[4], s_ref[0, x_row(i), :].astype(F32), st1[0], slope1))
+        f2 = flux(st2, 0, prim2[0], total_pressure(prim2[4], s_ref[0, x_row(j), :].astype(F32), st2[0], slope2))
+        for k in range(5):
+            out[k] = st[k]
+        out[5] = g_ref[x_row(e), :]
+        out[6] = s_ref[0, x_row(e), :].astype(F32)
+        out[7] = prim1[0]
+        out[8] = s_ref[1, x_row(e), :].astype(F32)
+        for k in range(5):
+            out[9 + k] = part[k, x_row(e), :] + time_ratio * (sign * 0.5 * f1[k] + HALF_C * st1[k])
+        for k in range(2):
+            out[14 + k] = part[k, x_row(i), :] + time_ratio * (sign * 0.5 * f2[k] + HALF_C * st2[k])
+        out[16] = zz[...]
+        for k in range(8):
+            out[17, k : k + 1, :] = zr[k, e : e + 1, :]
+        out[17, 8:9, :] = zr[1, i : i + 1, :] / (1.0 + zr[0, i : i + 1, :])
+        out[17, 9:16, :] = jnp.zeros((7, NY), F32)
+
+
+def shifted_x(own, low, high, at_x):
+    up = jnp.where(at_x == NX - 1, pltpu.roll(high, NX - 1, 1), pltpu.roll(own, NY - 1, 1))
+    down = jnp.where(at_x == 0, pltpu.roll(low, NY - NX + 1, 1), pltpu.roll(own, 1, 1))
+    return up, down
+
+
+def halo_step(
+    mesh, u_ref, g_ref, s_ref, part, ylo, yhi, yl, yh, zr, xl, xh, zz,
+    o_ref, hxl, hxh, hyl, hyh, hz, vx, ax, bx, zc,
+):
+    (mxl, mxh), (myl, myh), (mzl, mzh), first = masks(mesh)
+    for z in range(NZ):
+        vx[pl.ds(24 * z + 8, 8), :] = u_ref[1, layer(z), :] / (1.0 + u_ref[0, layer(z), :])
+    low = [xl[k] * mxl for k in range(8)]
+    high = [xh[k] * mxh for k in range(8)]
+    prim = primitives(*low[:6])
+    vx[pl.ds(7, NZ, stride=24), :] = prim[0]
+    slope = 0.5 * (vx[pl.ds(8, NZ, stride=24), :] - low[7])
+    f_low = flux(low[:5], 0, prim[0], total_pressure(prim[4], low[6], low[0], slope))
+    prim = primitives(*high[:6])
+    vx[pl.ds(16, NZ, stride=24), :] = prim[0]
+    slope = 0.5 * (high[7] - vx[pl.ds(15, NZ, stride=24), :])
+    f_high = flux(high[:5], 0, prim[0], total_pressure(prim[4], high[6], high[0], slope))
+    for k in range(5):
+        bx[k, pl.ds(7, NZ, stride=16), :] = lower_part(f_low[k], low[k])
+        ax[k, pl.ds(8, NZ, stride=16), :] = upper_part(f_high[k], high[k])
+    for z in range(NZ):
+        st = [u_ref[k, layer(z), :] for k in range(5)]
+        ux, _, _, _, press = primitives(*st, g_ref[layer(z), :])
+        slope = 0.5 * (vx[pl.ds(24 * z + 9, 8), :] - vx[pl.ds(24 * z + 7, 8), :])
+        fx = flux(st, 0, ux, total_pressure(press, s_ref[0, layer(z), :].astype(F32), st[0], slope))
+        for k in range(5):
             ax[k, pl.ds(16 * z, 8), :] = upper_part(fx[k], st[k])
             bx[k, pl.ds(16 * z + 8, 8), :] = lower_part(fx[k], st[k])
-            az[k, layer(z), :] = upper_part(fz[k], st[k])
-            bz[k, layer(z + 1), :] = lower_part(fz[k], st[k])
-            ch[k, layer(z), :] = (
-                3.0 * signal_speed * st[k]
-                + y_next(upper_part(fy[k], st[k]), col(5 + k), lane)
-                - y_prev(lower_part(fy[k], st[k]), col(k), lane)
+    for z in range(NZ):
+        for k in range(5):
+            o_ref[k, layer(z), :] = part[k, layer(z), :] - time_ratio * (
+                ax[k, pl.ds(16 * z + 1, 8), :] - bx[k, pl.ds(16 * z + 7, 8), :]
             )
-    for z in range(NZ):
-        new = []
-        for k in range(5):
-            change = (
-                ch[k, layer(z), :]
-                + (ax[k, pl.ds(16 * z + 1, 8), :] - bx[k, pl.ds(16 * z + 7, 8), :])
-                + (az[k, layer(z + 1), :] - bz[k, layer(z), :])
-            )
-            new.append(u_ref[k, layer(z), :] - time_ratio * change)
-            o_ref[k, layer(z), :] = new[k]
-        yp[layer(z), :] = pack_columns(new[:3], lane)
-    for out, edge, second in ((xlo, 0, 1), (xhi, NX - 1, NX - 2)):
-        st = [o_ref[k, x_row(edge), :] for k in range(5)]
+    for out, ref, mask in ((hxl, xl, mxl), (hxh, xh, mxh)):
+        if ref is xl:
+            near = [-ax[k, pl.ds(0, NZ, stride=16), :] for k in range(5)]
+            next_ = [-upper_part(f_low[k], low[k]) for k in range(2)]
+        else:
+            near = [bx[k, pl.ds(15, NZ, stride=16), :] for k in range(5)]
+            next_ = [lower_part(f_high[k], high[k]) for k in range(2)]
+        st = [(ref[9 + k] + time_ratio * near[k]) * mask for k in range(5)]
+        st2 = [(ref[14 + k] + time_ratio * next_[k]) * mask for k in range(2)]
         out[0] = st[0]
         out[1] = st[1]
-        out[2] = primitives(*st, g_ref[x_row(edge), :])[4]
-        out[3] = s_ref[1, x_row(edge), :].astype(F32)
-        out[4] = o_ref[1, x_row(second), :] / (1.0 + o_ref[0, x_row(second), :])
-    za = face_layer(first, 0)
-    r, mx, mz = [o_ref[k, dyn_layer(za), :] for k in (0, 1, 3)]
-    sign = jnp.where(first, HALF_C, -HALF_C)
-    zs[0] = 0.5 * mz + sign * r
-    zs[1] = 0.5 * mx * (mz / (1.0 + r)) + sign * mx
-    rows = yp[...].T
-    r, mx, my = rows[0:1], rows[2:3], rows[4:5]
-    yhi[...] = jnp.zeros((8, NY), F32)
-    yhi[0:1] = lower_part(my, r)
-    yhi[1:2] = lower_part(mx * (my / (1.0 + r)), mx)
-    r, mx, my = rows[1:2], rows[3:4], rows[5:6]
-    ylo[...] = jnp.zeros((8, NY), F32)
-    ylo[0:1] = upper_part(my, r)
-    ylo[1:2] = upper_part(mx * (my / (1.0 + r)), mx)
+        out[2] = primitives(*st, ref[5] * mask)[4]
+        out[3] = ref[8] * mask
+        out[4] = st2[1] / (1.0 + st2[0])
+    lane = lax.broadcasted_iota(jnp.int32, (1, NY), 1)
+    at_x = lax.bitwise_and(lane, NX - 1)
+    for side, ref, mask, own, out, sign in ((0, yl, myl, ylo, hyl, -1.0), (1, yh, myh, yhi, hyh, 1.0)):
+
+        def items(values, m):
+            return [values[k : k + 1] * m for k in range(8)]
+
+        here = items(ref, mask)
+        near_l, near_h = items(xl[16, 8 * side : 8 * side + 8, :], mxl), items(xh[16, 8 * side : 8 * side + 8, :], mxh)
+        ux, ux_l, ux_h = [v[1] / (1.0 + v[0]) for v in (here, near_l, near_h)]
+        up, down = shifted_x(ux, ux_l, ux_h, at_x)
+        slope = 0.5 * (up - down)
+        slope_h = 0.5 * (pltpu.roll(ux_h, NY - 1, 1) - pltpu.roll(ux, NY - NX + 1, 1))
+        slope_l = 0.5 * (pltpu.roll(ux, NX - 1, 1) - pltpu.roll(ux_l, 1, 1))
+
+        def fx_of(v, speed, slope):
+            return [v[1], v[1] * speed + total_pressure(v[5], v[6], v[0], slope), v[2] * speed]
+
+        f_here, f_l, f_h = fx_of(here, ux, slope), fx_of(near_l, ux_l, slope_l), fx_of(near_h, ux_h, slope_h)
+        uz = here[3] / (1.0 + here[0])
+        near_z = items(zz[8 * side : 8 * side + 8, :], 1.0)
+        uz_z = near_z[3] / (1.0 + near_z[0])
+        fz, fz_z = [[v[3], v[1] * w, v[2] * w] for v, w in ((here, uz), (near_z, uz_z))]
+        self_ = items(own, 1.0)
+        uy = self_[2] / (1.0 + self_[0])
+        uy_here = here[2] / (1.0 + here[0])
+        slope = 0.5 * (self_[7] - uy_here if side == 0 else uy_here - self_[7])
+        fy = [self_[2], self_[1] * uy, self_[2] * uy + total_pressure(self_[5], self_[6], self_[0], slope)]
+        new = []
+        for k in range(3):
+            a_x, _ = shifted_x(upper_part(f_here[k], here[k]), ux_l, upper_part(f_h[k], near_h[k]), at_x)
+            _, b_x = shifted_x(lower_part(f_here[k], here[k]), lower_part(f_l[k], near_l[k]), ux_h, at_x)
+            a_z = jnp.where(
+                lane >= NY - NX,
+                pltpu.roll(upper_part(fz_z[k], near_z[k]), NY - NX, 1) * mzh,
+                pltpu.roll(upper_part(fz[k], here[k]), NY - NX, 1),
+            )
+            b_z = jnp.where(
+                lane < NX,
+                pltpu.roll(lower_part(fz_z[k], near_z[k]), NX, 1) * mzl,
+                pltpu.roll(lower_part(fz[k], here[k]), NX, 1),
+            )
+            facing = sign * 0.5 * fy[k] + HALF_C * self_[k]
+            new.append(mask * (ref[8 + k : 9 + k] + time_ratio * (facing - (a_x - b_x) - (a_z - b_z))))
+        r, mx, my = new
+        combine = lower_part if side == 0 else upper_part
+        out[0:1, :] = combine(my, r)
+        out[1:2, :] = combine(mx * (my / (1.0 + r)), mx)
+        out[2:8, :] = jnp.zeros((6, NY), F32)
+    rows = []
+    for side in range(2):
+        v = [zz[8 * side + k : 8 * side + k + 1, :] for k in range(8)]
+        speed = v[2] / (1.0 + v[0])
+        fy = [v[2], v[1] * speed, v[3] * speed]
+        combine = upper_part if side else lower_part
+        rows += [combine(f, v[k]) for f, k in zip(fy, (0, 1, 3))]
+    zc[...] = jnp.concatenate(rows + [jnp.zeros((2, NY), F32)], axis=0).T
+    cols = zc[dyn_layer(jnp.where(first, 0, NZ - 1)), :]
+    full = lanes()
+    deep = lax.broadcasted_iota(jnp.int32, (NX, NY), 0)
+    here = [zr[k] for k in range(8)]
+    near_l = [xl[17, k : k + 1, :] * mxl for k in range(9)]
+    near_h = [xh[17, k : k + 1, :] * mxh for k in range(9)]
+    ux, ux_l, ux_h = [v[1] / (1.0 + v[0]) for v in (here, near_l, near_h)]
+
+    def next_x(value, row):
+        return jnp.where(deep == NX - 1, row, pltpu.roll(value, NX - 1, 0))
+
+    def prev_x(value, row):
+        return jnp.where(deep == 0, row, pltpu.roll(value, 1, 0))
+
+    slope = 0.5 * (next_x(ux, ux_h) - prev_x(ux, ux_l))
+    slope_h = 0.5 * (near_h[8] - ux[NX - 1 : NX])
+    slope_l = 0.5 * (ux[0:1] - near_l[8])
+
+    def fx_layer(v, speed, slope):
+        return [v[1], v[1] * speed + total_pressure(v[5], v[6], v[0], slope), v[3] * speed]
+
+    f_here, f_l, f_h = fx_layer(here, ux, slope), fx_layer(near_l, ux_l, slope_l), fx_layer(near_h, ux_h, slope_h)
+    uy = here[2] / (1.0 + here[0])
+    fy = [here[2], here[1] * uy, here[3] * uy]
+    za, zb = dyn_layer(face_layer(first, 0)), dyn_layer(face_layer(first, 1))
+    sign = jnp.where(first, 1.0, -1.0)
+    st = [u_ref[k, za, :] for k in range(5)]
+    prim = primitives(*st, g_ref[za, :])
+    uz_b = u_ref[3, zb, :] / (1.0 + u_ref[0, zb, :])
+    slope = (sign * 0.5) * (here[3] / (1.0 + here[0]) - uz_b)
+    fz = flux(st, 2, prim[2], total_pressure(prim[4], s_ref[0, za, :].astype(F32), st[0], slope))
+    new = []
+    for n, k in enumerate((0, 1, 3)):
+        a_x = next_x(upper_part(f_here[n], here[k]), upper_part(f_h[n], near_h[k]))
+        b_x = prev_x(lower_part(f_here[n], here[k]), lower_part(f_l[n], near_l[k]))
+        a_y = y_next(upper_part(fy[n], here[k]), cols[:, 3 + n : 4 + n], full)
+        b_y = y_prev(lower_part(fy[n], here[k]), cols[:, n : n + 1], full)
+        facing = sign * 0.5 * fz[k] + HALF_C * st[k]
+        new.append(zr[8 + n] + time_ratio * (facing - (a_x - b_x) - (a_y - b_y)))
+    r, mx, mz = new
+    hz[0] = 0.5 * mz - (sign * HALF_C) * r
+    hz[1] = 0.5 * mx * (mz / (1.0 + r)) - (sign * HALF_C) * mx
+
+
+def forward_kernel(
+    mesh, u0_ref, g_ref, s_ref, part, ylo_in, yhi_in, yl, yh, zr, xl, xh, zz, n_ref, m_ref,
+    u_ref, lam_ref, cf_ref, cfh_ref, mis_ref, ylo, yhi, zs, yown,
+    hxl, hxh, hyl, hyh, hz, vx, ax, bx, az, bz, ch, yc, yp, zc,
+):
+    halo_step(
+        mesh, u0_ref, g_ref, s_ref, part, ylo_in, yhi_in, yl, yh, zr, xl, xh, zz,
+        u_ref, hxl, hxh, hyl, hyh, hz, vx, ax, bx, zc,
+    )
+    speed_kernel(
+        mesh, u_ref, g_ref, s_ref, hxl, hxh, hyl, hyh, hz, n_ref, m_ref,
+        lam_ref, cf_ref, cfh_ref, mis_ref, ylo, yhi, zs, yown,
+        vx, ax, bx, az, bz, ch, yc, yp,
+    )
 
 
 def columns_of(low, high, count, low_mask, high_mask):
@@ -350,10 +492,6 @@
         yown[own : own + 1] = lam_r
         yown[own + 1 : own + 2] = lam_m
     yown[4:8] = jnp.zeros((4, NY), F32)
-
-
-NEAR = time_ratio * HALF_C
-STAY = 1.0 - 3.0 * time_ratio * signal_speed
 
 
 def edge_kernel(mesh, u_ref, g_ref, lam_ref, cf_ref, yl, yh, zr, xlo, xhi, yc):
@@ -600,11 +738,6 @@
     return yl, yh, zr
 
 
-def exchange(sizes, xlo, xhi, ylo, yhi, zs):
-    xl, xh = exchange_x(sizes, xlo, xhi)
-    return xl, xh, *exchange_yz(sizes, ylo, yhi, zs)
-
-
 def local(sizes, checkpoint, gruneisen, switch, probes, observed):
     bind = functools.partial
     state = checkpoint.reshape(5, CELLS, NY)
@@ -612,39 +745,40 @@
     sw = switch.reshape(2, CELLS, NY)
     plane = rows_of(8, NY)
 
-    def slabs(x_items, z_items):
-        x = rows_of(x_items, NZ, NY)
-        return [x, x, plane, plane, rows_of(z_items, NX, NY)]
-
-    *sent, yown = call(bind(prep_kernel, sizes), slabs(8, 8) + [plane], [vmem(CELLS, NY)], None)(state, gamma, sw)
-    got = exchange(sizes, *sent)
+    def x_slabs(items):
+        return [rows_of(items, NZ, NY)] * 2
+
+    pair = rows_of(16, NY)
+    tall = (NZ + 2) * NX
+    sent = call(bind(prep_kernel, sizes), [pair, pair, rows_of(11, NX, NY)], [vmem(CELLS, NY)], None)(state, gamma, sw)
+    got_yz = exchange_yz(sizes, *sent)
     hits, mean, spread = call(
         probe_kernel,
         [rows_of(CELLS, NY), rows_of(CELLS, NY), rows_of(1, probes.shape[0])],
         [],
     )(probes.reshape(1, -1), observed.reshape(1, -1))
-    tall = (NZ + 2) * NX
-    state_1, *sent = call(
-        bind(step_kernel, sizes),
-        [rows_of(5, CELLS, NY)] + slabs(5, 2),
+    part, xlo, xhi, zz = call(
+        bind(side_kernel, sizes),
+        [rows_of(5, CELLS, NY)] + x_slabs(18) + [pair],
         [
-            vmem(NZ * 24, NY), vmem(CELLS, NY), vmem(tall, NY), vmem(CELLS, NY),
-            vmem(5, NZ * 16, NY), vmem(5, NZ * 16, NY), vmem(5, tall, NY), vmem(5, tall, NY),
-            vmem(5, CELLS, NY), vmem(16, NY), vmem(CELLS, 16), vmem(CELLS, NY),
+            vmem(CELLS, NY), vmem(tall, NY), vmem(CELLS, NY),
+            vmem(5, tall, NY), vmem(5, tall, NY), vmem(16, NY), vmem(CELLS, 16),
         ],
-    )(state, gamma, sw, *got, yown)
-    got = exchange(sizes, *sent)
-    lam_2, coef, coef_halo, mis, *sent, yown = call(
-        bind(speed_kernel, sizes),
-        [rows_of(2, CELLS, NY), rows_of(CELLS, NY), rows_of(2, NZ, NY), plane]
+    )(state, gamma, sw, *sent[:2], *got_yz)
+    got_x = exchange_x(sizes, xlo, xhi)
+    zz = lax.ppermute(zz, "gz", ring(sizes, "gz", 1))
+    state_1, lam_2, coef, coef_halo, mis, *sent, yown = call(
+        bind(forward_kernel, sizes),
+        [rows_of(5, CELLS, NY), rows_of(2, CELLS, NY), rows_of(CELLS, NY), rows_of(2, NZ, NY), plane]
         + [plane, plane, rows_of(6, NX, NY), plane],
         [
-            vmem(NZ * 24, NY), vmem(2, NZ * 16, NY), vmem(2, NZ * 16, NY), vmem(2, tall, NY), vmem(2, tall, NY),
-            vmem(2, CELLS, NY), vmem(CELLS, 8), vmem(CELLS, NY),
+            vmem(5, NZ, NY), vmem(5, NZ, NY), vmem(8, NY), vmem(8, NY), vmem(2, NX, NY),
+            vmem(NZ * 24, NY), vmem(5, NZ * 16, NY), vmem(5, NZ * 16, NY), vmem(2, tall, NY), vmem(2, tall, NY),
+            vmem(2, CELLS, NY), vmem(CELLS, 8), vmem(CELLS, NY), vmem(CELLS, 8),
         ],
-    )(state_1, gamma, sw, *got, hits, mean)
+    )(state, gamma, sw, part, *sent[:2], *got_yz, *got_x, zz, hits, mean)
     got_yz = exchange_yz(sizes, *sent)
-    sent = call(bind(edge_kernel, sizes), slabs(8, 1)[:2], [vmem(CELLS, NY)])(state_1, gamma, lam_2, coef, *got_yz)
+    sent = call(bind(edge_kernel, sizes), x_slabs(8), [vmem(CELLS, NY)])(state_1, gamma, lam_2, coef, *got_yz)
     got_x = exchange_x(sizes, *sent)
     devices = sizes["gx"] * sizes["gy"] * sizes["gz"]
     gradient, rows = call(

time: 71.6 us -> 66.1 us (0.923)
  waiting for transfers between devices: 14.8 us -> 5.61 us
  blocking collectives: 24.3 us -> 26.5 us
  local copies, waits for them, and re-layouts: 0.7 us -> 2.08 us
    ppermute x3 -> x2, waiting for transfers between devices: 11.4 us -> 1.81 us  [exchange_yz(): yh = lax.ppermute(ylo, 'gy', ring(sizes, 'gy', -1))]
    ppermute x3 -> x2, starting transfers between devices: 13.4 us -> 9.14 us  [exchange_x(): lax.ppermute(xlo, 'gx', ring(sizes, 'gx', -1))]
    ppermute x3 -> x2, starting transfers between devices: 0.01 us -> 3.97 us  [exchange_yz(): yh = lax.ppermute(ylo, 'gy', ring(sizes, 'gy', -1))]
    all_to_all x1, blocking collectives: 24.3 us -> 26.5 us  [local(): rows = lax.all_to_all(rows, ('gx', 'gy', 'gz'), 0, 0, tiled=True)]
    unnamed x14, local copies, waits for them, and re-layouts: 0.7 us -> 2.08 us
    ppermute x3 -> x2, starting transfers between devices: 2.24 us -> 1.37 us  [exchange_x(): lax.ppermute(xhi, 'gx', ring(sizes, 'gx', 1))]
    ppermute x3 -> x2, starting transfers between devices: 2.46 us -> 3.25 us  [exchange_yz(): zr = lax.ppermute(zs, 'gz', ring(sizes, 'gz', 1))]
    ppermute x0 -> x1, starting transfers between devices: none -> 0.73 us  [local(): zz = lax.ppermute(zz, 'gz', ring(sizes, 'gz', 1))]
  transfers between devices with their start and end apart: 15 -> 11, of which waited for: 6 -> 6; matrix products, arithmetic and copies ran while one was open for 0% -> 0% of each run, Pallas kernels for 1% -> 1%
where the time goes in v4:
time: 66.1 us; the launch traced here: 65.8 us
  blocking collectives  26.5 us (40%)
  starting transfers between devices  24.6 us (37%)
  Pallas kernels  6.28 us (10%)
  waiting for transfers between devices  5.61 us (8%)
  local copies, waits for them, and re-layouts  2.08 us (3%)
  between operations  0.71 us (1%)
    all_to_all x1, blocking collectives, local(): rows = lax.all_to_all(rows, ('gx', 'gy', 'gz'), 0, 0, tiled=True)  26.5 us
    ppermute x2, starting transfers between devices, exchange_x(): lax.ppermute(xlo, 'gx', ring(sizes, 'gx', -1))  9.14 us
    ppermute x2, starting transfers between devices, exchange_yz(): yl = lax.ppermute(yhi, 'gy', ring(sizes, 'gy', 1))  6.14 us
    ppermute x2, starting transfers between devices, exchange_yz(): yh = lax.ppermute(ylo, 'gy', ring(sizes, 'gy', -1))  3.97 us
    ppermute x2, starting transfers between devices, exchange_yz(): zr = lax.ppermute(zs, 'gz', ring(sizes, 'gz', 1))  3.25 us
    unnamed x14, local copies, waits for them, and re-layouts  2.08 us
    pallas_call x1, Pallas kernels, local(): call(bind(prep_kernel, sizes), [pair, pair, rows_of(11, NX, NY)], [vmem(C...  1.97 us
    ppermute x2, waiting for transfers between devices, exchange_yz(): yh = lax.ppermute(ylo, 'gy', ring(sizes, 'gy', -1))  1.81 us
  transfers between devices with their start and end apart: 11, of which 6 were waited for; matrix products, arithmetic and copies ran while one was open for 0% of the time, Pallas kernels for 1%

profile of v4, /device:TPU:1, one launch (start us, length us, event | category | flops | bytes accessed | tf_op | source)
XLA Modules:
  0.0 65.8 jit_solution(14698344292143646961)
XLA Ops:
  0.7 2.0 %shard_map.68 = (f32[16,128]{1,0:T(8,128)}, f32[16,128]{1,0:T(8,128)}, f32[11,8,128]{2,1,0:T(8,128)}) custom-call(f32[5,128,128]{2,1,0:T(8,128)} %bitcast.11, f32[128,128]{1,0:T(8,128)} %bitcast.15, s32[2,128,128]{2,1,0:T(8,128)} %bitcast.20), custom_call_target="tpu_custom_call" | custom-call | flops 100000 | bytes 100000 | tf_op jit(solution)/shard_map/pallas_call | solution.py:753
  2.6 2.5 %collective-permute-start.2 = (f32[11,8,128]{2,1,0:T(8,128)}, f32[11,8,128]{2,1,0:T(8,128)S(1)}, u32[]{:S(2)}, u32[]{:S(2)}) collective-permute-start(f32[11,8,128]{2,1,0:T(8,128)} %get-tuple-element.29), channel_id=1, source_target_pairs={{0,1},{1,0},{2,3},{3,2},{4,5},{5,4},{6,7},{7,6},{8,9},{9,8},{10,11... | collective-permute-start | bytes 135176 | tf_op jit(solution)/shard_map/ppermute | solution.py:735
  5.1 1.0 %collective-permute-start.1 = (f32[16,128]{1,0:T(8,128)}, f32[16,128]{1,0:T(8,128)S(1)}, u32[]{:S(2)}, u32[]{:S(2)}) collective-permute-start(f32[16,128]{1,0:T(8,128)} %get-tuple-element.27.ylo.ylo_in), channel_id=1, source_target_pairs={{0,14},{2,0},{4,2},{6,4},{8,6},{10,8},{12,10},{14,12},{1,15},{3,1}... | collective-permute-start | bytes 24584 | tf_op jit(solution)/shard_map/ppermute | solution.py:737
  6.0 2.9 %collective-permute-start = (f32[16,128]{1,0:T(8,128)}, f32[16,128]{1,0:T(8,128)S(1)}, u32[]{:S(2)}, u32[]{:S(2)}) collective-permute-start(f32[16,128]{1,0:T(8,128)} %get-tuple-element.28.yhi.yhi_in), channel_id=1, source_target_pairs={{0,2},{2,4},{4,6},{6,8},{8,10},{10,12},{12,14},{14,0},{1,3},{3,5},... | collective-permute-start | bytes 24584 | tf_op jit(solution)/shard_map/ppermute | solution.py:736
  8.9 1.6 %collective-permute-done.1.yh = f32[16,128]{1,0:T(8,128)S(1)} collective-permute-done((f32[16,128]{1,0:T(8,128)}, f32[16,128]{1,0:T(8,128)S(1)}, u32[]{:S(2)}, u32[]{:S(2)}) %collective-permute-start.1) | collective-permute-done | bytes 8224 | tf_op jit(solution)/shard_map/ppermute | solution.py:737
  10.5 1.0 %collective-permute-done.yl = f32[16,128]{1,0:T(8,128)S(1)} collective-permute-done((f32[16,128]{1,0:T(8,128)}, f32[16,128]{1,0:T(8,128)S(1)}, u32[]{:S(2)}, u32[]{:S(2)}) %collective-permute-start) | collective-permute-done | bytes 8224 | tf_op jit(solution)/shard_map/ppermute | solution.py:736
  11.5 0.7 %copy-done.3 = f32[16,128]{1,0:T(8,128)S(1)} copy-done((f32[16,128]{1,0:T(8,128)S(1)}, f32[16,128]{1,0:T(8,128)}, u32[]{:S(2)}) %copy-start.3) | copy-done | bytes 8216
  12.2 0.7 %copy-done.4 = f32[16,128]{1,0:T(8,128)S(1)} copy-done((f32[16,128]{1,0:T(8,128)S(1)}, f32[16,128]{1,0:T(8,128)}, u32[]{:S(2)}) %copy-start.4) | copy-done | bytes 8216
  12.9 1.2 %shard_map.69 = (f32[5,128,128]{2,1,0:T(8,128)S(1)}, f32[18,16,128]{2,1,0:T(8,128)S(1)}, f32[18,16,128]{2,1,0:T(8,128)S(1)}, f32[16,128]{1,0:T(8,128)S(1)}) custom-call(f32[5,128,128]{2,1,0:T(8,128)S(1)} %bitcast.12, f32[128,128]{1,0:T(8,128)S(1)} %bitcast.16, s32[2,128,128]{2,1,0:T(8,128)S(1)} %bitcast.21, f32[16,128]{1,0:T(8,128)S(1)} %copy-done.3, ...), custom_call_target="tpu_custom_call" | custom-call | flops 100000 | bytes 100000 | tf_op jit(solution)/shard_map/pallas_call | solution.py:760
  14.1 1.3 %collective-permute-start.3 = (f32[18,16,128]{2,1,0:T(8,128)S(1)}, f32[18,16,128]{2,1,0:T(8,128)S(1)}, u32[]{:S(2)}, u32[]{:S(2)}) collective-permute-start(f32[18,16,128]{2,1,0:T(8,128)S(1)} %get-tuple-element.31), channel_id=1, source_target_pairs={{0,16},{16,32},{32,48},{48,64},{64,80},{80,96},{96,112},{112,128},... | collective-permute-start | bytes 442376 | tf_op jit(solution)/shard_map/ppermute | solution.py:729
  15.4 3.8 %collective-permute-start.4 = (f32[18,16,128]{2,1,0:T(8,128)S(1)}, f32[18,16,128]{2,1,0:T(8,128)S(1)}, u32[]{:S(2)}, u32[]{:S(2)}) collective-permute-start(f32[18,16,128]{2,1,0:T(8,128)S(1)} %get-tuple-element.32), channel_id=1, source_target_pairs={{0,240},{16,0},{32,16},{48,32},{64,48},{80,64},{96,80},{112,96},{1... | collective-permute-start | bytes 442376 | tf_op jit(solution)/shard_map/ppermute | solution.py:730
  19.2 0.7 %collective-permute-start.5 = (f32[16,128]{1,0:T(8,128)S(1)}, f32[16,128]{1,0:T(8,128)S(1)}, u32[]{:S(2)}, u32[]{:S(2)}) collective-permute-start(f32[16,128]{1,0:T(8,128)S(1)} %get-tuple-element.33), channel_id=1, source_target_pairs={{0,1},{1,0},{2,3},{3,2},{4,5},{5,4},{6,7},{7,6},{8,9},{9,8},{10,11... | collective-permute-start | bytes 24584 | tf_op jit(solution)/shard_map/ppermute | solution.py:769
  20.0 0.7 %copy-done.5 = s32[256]{0:T(256)S(1)} copy-done((s32[256]{0:T(256)S(1)}, s32[256]{0:T(256)}, u32[]{:S(2)}) %copy-start.5) | copy-done | bytes 1048
  21.2 0.6 collective-permute-done.5.zz
  21.8 0.9 %shard_map.71 = (f32[5,128,128]{2,1,0:T(8,128)S(1)}, f32[2,128,128]{2,1,0:T(8,128)S(1)}, f32[128,128]{1,0:T(8,128)S(1)}, f32[2,16,128]{2,1,0:T(8,128)S(1)}, f32[...) custom-call(f32[5,128,128]{2,1,0:T(8,128)S(1)} %bitcast.13, ...), custom_call_target="tpu_custom_call" | custom-call | flops 100000 | bytes 100000 | tf_op jit(solution)/shard_map/pallas_call | solution.py:770
  22.7 0.8 %collective-permute-start.8 = (f32[6,8,128]{2,1,0:T(8,128)S(1)}, f32[6,8,128]{2,1,0:T(8,128)S(1)}, u32[]{:S(2)}, u32[]{:S(2)}) collective-permute-start(f32[6,8,128]{2,1,0:T(8,128)S(1)} %get-tuple-element.43), channel_id=1, source_target_pairs={{0,1},{1,0},{2,3},{3,2},{4,5},{5,4},{6,7},{7,6},{8,9},{9,8},{10,11... | collective-permute-start | bytes 73736 | tf_op jit(solution)/shard_map/ppermute | solution.py:735
  23.4 3.3 %collective-permute-start.6 = (f32[8,128]{1,0:T(8,128)S(1)}, f32[8,128]{1,0:T(8,128)S(1)}, u32[]{:S(2)}, u32[]{:S(2)}) collective-permute-start(f32[8,128]{1,0:T(8,128)S(1)} %get-tuple-element.41), channel_id=1, source_target_pairs={{0,2},{2,4},{4,6},{6,8},{8,10},{10,12},{12,14},{14,0},{1,3},{3,5},... | collective-permute-start | bytes 12296 | tf_op jit(solution)/shard_map/ppermute | solution.py:736
  26.7 3.0 %collective-permute-start.7 = (f32[8,128]{1,0:T(8,128)S(1)}, f32[8,128]{1,0:T(8,128)S(1)}, u32[]{:S(2)}, u32[]{:S(2)}) collective-permute-start(f32[8,128]{1,0:T(8,128)S(1)} %get-tuple-element.42), channel_id=1, source_target_pairs={{0,14},{2,0},{4,2},{6,4},{8,6},{10,8},{12,10},{14,12},{1,15},{3,1}... | collective-permute-start | bytes 12296 | tf_op jit(solution)/shard_map/ppermute | solution.py:737
  29.7 0.7 collective-permute-done.6.yl
  30.9 5.3 %collective-permute-start.10 = (f32[8,16,128]{2,1,0:T(8,128)S(1)}, f32[8,16,128]{2,1,0:T(8,128)S(1)}, u32[]{:S(2)}, u32[]{:S(2)}) collective-permute-start(f32[8,16,128]{2,1,0:T(8,128)S(1)} %get-tuple-element.45), channel_id=1, source_target_pairs={{0,240},{16,0},{32,16},{48,32},{64,48},{80,64},{96,80},{112,96},{1... | collective-permute-start | bytes 196616 | tf_op jit(solution)/shard_map/ppermute | solution.py:730
  36.3 1.6 %collective-permute-done.9.xl = f32[8,16,128]{2,1,0:T(8,128)S(1)} collective-permute-done((f32[8,16,128]{2,1,0:T(8,128)S(1)}, f32[8,16,128]{2,1,0:T(8,128)S(1)}, u32[]{:S(2)}, u32[]{:S(2)}) %collective-permute-start.9) | collective-permute-done | bytes 65568 | tf_op jit(solution)/shard_map/ppermute | solution.py:729
  37.8 0.7 %shard_map.73 = (f32[128,128]{1,0:T(8,128)S(1)}, f32[256,128]{1,0:T(8,128)S(1)}) custom-call(f32[5,128,128]{2,1,0:T(8,128)S(1)} %bitcast.14, f32[5,128,128]{2,1,0:T(8,128)S(1)} %get-tuple-element.36.u_ref, f32[128,128]{1,0:T(8,128)S(1)} %bitcast.19, f32[2,128,128]{2,1,0:T(8,128)S(1)} %get-tuple-element.37.lam_ref, f32[128,128]{1,0:T(8,128)S(1)} %get-tuple-element.38.cf_ref, ...), custom_call_target="tpu_custom_call" | custom-call | flops 100000 | bytes 100000 | tf_op jit(solution)/shard_map/pallas_call | solution.py:784
  38.5 26.5 %all_to_all.11 = f32[256,1,128]{2,1,0:T(1,128)S(1)} all-to-all(f32[256,1,128]{2,1,0:T(1,128)S(1)} %bitcast.24), channel_id=1, replica_groups=mesh['gx'=16,'gy'=8,'gz'=2] {'gx','gy','gz'}, dimensions={0} | all-to-all | bytes 262144 | tf_op jit(solution)/shard_map/all_to_all | solution.py:792
  65.0 0.8 %shard_map.74 = (f32[128,128]{1,0:T(8,128)}, f32[1,1]{1,0:T(1,128)}) custom-call(f32[128,128]{1,0:T(8,128)S(1)} %get-tuple-element.48.grad_ref, f32[256,128]{1,0:T(8,128)S(1)} %bitcast.23), custom_call_target="tpu_custom_call" | custom-call | tf_op jit(solution)/shard_map/pallas_call | solution.py:793
  (20 shorter events, 1.1 us)
Async XLA Ops:
  0.6 10.9 %copy-start = (f32[5,16,8,128]{3,2,1,0:T(8,128)S(1)}, f32[5,16,8,128]{3,2,1,0:T(8,128)}, u32[]{:S(2)}) copy-start(f32[5,16,8,128]{3,2,1,0:T(8,128)} %param.5) | copy-start | bytes 983044
  0.6 10.9 %copy-start.1 = (f32[16,8,128]{2,1,0:T(8,128)S(1)}, f32[16,8,128]{2,1,0:T(8,128)}, u32[]{:S(2)}) copy-start(f32[16,8,128]{2,1,0:T(8,128)} %param.6) | copy-start | bytes 196612
  0.6 10.9 %copy-start.2 = (s32[2,16,8,128]{3,2,1,0:T(8,128)S(1)}, s32[2,16,8,128]{3,2,1,0:T(8,128)}, u32[]{:S(2)}) copy-start(s32[2,16,8,128]{3,2,1,0:T(8,128)} %param.7) | copy-start | bytes 393220
  2.6 8.9 %collective-permute-start.2 = (f32[11,8,128]{2,1,0:T(8,128)}, f32[11,8,128]{2,1,0:T(8,128)S(1)}, u32[]{:S(2)}, u32[]{:S(2)}) collective-permute-start(f32[11,8,128]{2,1,0:T(8,128)} %get-tuple-element.29), channel_id=1, source_target_pairs={{0,1},{1,0},{2,3},{3,2},{4,5},{5,4},{6,7},{7,6},{8,9},{9,8},{10,11... | collective-permute-start | bytes 135176 | tf_op jit(solution)/shard_map/ppermute | solution.py:735
  5.1 5.4 %collective-permute-start.1 = (f32[16,128]{1,0:T(8,128)}, f32[16,128]{1,0:T(8,128)S(1)}, u32[]{:S(2)}, u32[]{:S(2)}) collective-permute-start(f32[16,128]{1,0:T(8,128)} %get-tuple-element.27.ylo.ylo_in), channel_id=1, source_target_pairs={{0,14},{2,0},{4,2},{6,4},{8,6},{10,8},{12,10},{14,12},{1,15},{3,1}... | collective-permute-start | bytes 24584 | tf_op jit(solution)/shard_map/ppermute | solution.py:737
  6.0 5.4 %collective-permute-start = (f32[16,128]{1,0:T(8,128)}, f32[16,128]{1,0:T(8,128)S(1)}, u32[]{:S(2)}, u32[]{:S(2)}) collective-permute-start(f32[16,128]{1,0:T(8,128)} %get-tuple-element.28.yhi.yhi_in), channel_id=1, source_target_pairs={{0,2},{2,4},{4,6},{6,8},{8,10},{10,12},{12,14},{14,0},{1,3},{3,5},... | collective-permute-start | bytes 24584 | tf_op jit(solution)/shard_map/ppermute | solution.py:736
  11.5 0.7 %copy-start.3 = (f32[16,128]{1,0:T(8,128)S(1)}, f32[16,128]{1,0:T(8,128)}, u32[]{:S(2)}) copy-start(f32[16,128]{1,0:T(8,128)} %get-tuple-element.27.ylo.ylo_in) | copy-start | bytes 24580
  12.2 0.7 %copy-start.4 = (f32[16,128]{1,0:T(8,128)S(1)}, f32[16,128]{1,0:T(8,128)}, u32[]{:S(2)}) copy-start(f32[16,128]{1,0:T(8,128)} %get-tuple-element.28.yhi.yhi_in) | copy-start | bytes 24580
  12.9 7.1 %copy-start.6 = (f32[256]{0:T(256)S(1)}, f32[256]{0:T(256)}, u32[]{:S(2)}) copy-start(f32[256]{0:T(256)} %param.9) | copy-start | bytes 3076
  14.1 7.6 %collective-permute-start.3 = (f32[18,16,128]{2,1,0:T(8,128)S(1)}, f32[18,16,128]{2,1,0:T(8,128)S(1)}, u32[]{:S(2)}, u32[]{:S(2)}) collective-permute-start(f32[18,16,128]{2,1,0:T(8,128)S(1)} %get-tuple-element.31), channel_id=1, source_target_pairs={{0,16},{16,32},{32,48},{48,64},{64,80},{80,96},{96,112},{112,128},... | collective-permute-start | bytes 442376 | tf_op jit(solution)/shard_map/ppermute | solution.py:729
  15.4 6.3 %collective-permute-start.4 = (f32[18,16,128]{2,1,0:T(8,128)S(1)}, f32[18,16,128]{2,1,0:T(8,128)S(1)}, u32[]{:S(2)}, u32[]{:S(2)}) collective-permute-start(f32[18,16,128]{2,1,0:T(8,128)S(1)} %get-tuple-element.32), channel_id=1, source_target_pairs={{0,240},{16,0},{32,16},{48,32},{64,48},{80,64},{96,80},{112,96},{1... | collective-permute-start | bytes 442376 | tf_op jit(solution)/shard_map/ppermute | solution.py:730
  19.2 2.5 %collective-permute-start.5 = (f32[16,128]{1,0:T(8,128)S(1)}, f32[16,128]{1,0:T(8,128)S(1)}, u32[]{:S(2)}, u32[]{:S(2)}) collective-permute-start(f32[16,128]{1,0:T(8,128)S(1)} %get-tuple-element.33), channel_id=1, source_target_pairs={{0,1},{1,0},{2,3},{3,2},{4,5},{5,4},{6,7},{7,6},{8,9},{9,8},{10,11... | collective-permute-start | bytes 24584 | tf_op jit(solution)/shard_map/ppermute | solution.py:769
  20.0 0.7 %copy-start.5 = (s32[256]{0:T(256)S(1)}, s32[256]{0:T(256)}, u32[]{:S(2)}) copy-start(s32[256]{0:T(256)} %param.8) | copy-start | bytes 3076
  22.7 8.0 %collective-permute-start.8 = (f32[6,8,128]{2,1,0:T(8,128)S(1)}, f32[6,8,128]{2,1,0:T(8,128)S(1)}, u32[]{:S(2)}, u32[]{:S(2)}) collective-permute-start(f32[6,8,128]{2,1,0:T(8,128)S(1)} %get-tuple-element.43), channel_id=1, source_target_pairs={{0,1},{1,0},{2,3},{3,2},{4,5},{5,4},{6,7},{7,6},{8,9},{9,8},{10,11... | collective-permute-start | bytes 73736 | tf_op jit(solution)/shard_map/ppermute | solution.py:735
  23.4 6.9 %collective-permute-start.6 = (f32[8,128]{1,0:T(8,128)S(1)}, f32[8,128]{1,0:T(8,128)S(1)}, u32[]{:S(2)}, u32[]{:S(2)}) collective-permute-start(f32[8,128]{1,0:T(8,128)S(1)} %get-tuple-element.41), channel_id=1, source_target_pairs={{0,2},{2,4},{4,6},{6,8},{8,10},{10,12},{12,14},{14,0},{1,3},{3,5},... | collective-permute-start | bytes 12296 | tf_op jit(solution)/shard_map/ppermute | solution.py:736
  26.7 3.9 %collective-permute-start.7 = (f32[8,128]{1,0:T(8,128)S(1)}, f32[8,128]{1,0:T(8,128)S(1)}, u32[]{:S(2)}, u32[]{:S(2)}) collective-permute-start(f32[8,128]{1,0:T(8,128)S(1)} %get-tuple-element.42), channel_id=1, source_target_pairs={{0,14},{2,0},{4,2},{6,4},{8,6},{10,8},{12,10},{14,12},{1,15},{3,1}... | collective-permute-start | bytes 12296 | tf_op jit(solution)/shard_map/ppermute | solution.py:737
  30.8 7.0 %collective-permute-start.9 = (f32[8,16,128]{2,1,0:T(8,128)S(1)}, f32[8,16,128]{2,1,0:T(8,128)S(1)}, u32[]{:S(2)}, u32[]{:S(2)}) collective-permute-start(f32[8,16,128]{2,1,0:T(8,128)S(1)} %get-tuple-element.44), channel_id=1, source_target_pairs={{0,16},{16,32},{32,48},{48,64},{64,80},{80,96},{96,112},{112,128},... | collective-permute-start | bytes 196616 | tf_op jit(solution)/shard_map/ppermute | solution.py:729
  30.9 6.9 %collective-permute-start.10 = (f32[8,16,128]{2,1,0:T(8,128)S(1)}, f32[8,16,128]{2,1,0:T(8,128)S(1)}, u32[]{:S(2)}, u32[]{:S(2)}) collective-permute-start(f32[8,16,128]{2,1,0:T(8,128)S(1)} %get-tuple-element.45), channel_id=1, source_target_pairs={{0,240},{16,0},{32,16},{48,32},{64,48},{80,64},{96,80},{112,96},{1... | collective-permute-start | bytes 196616 | tf_op jit(solution)/shard_map/ppermute | solution.py:730

commit v5 on v4

--- a/solution.py
+++ b/solution.py
@@ -232,7 +232,7 @@
 
 def halo_step(
     mesh, u_ref, g_ref, s_ref, part, ylo, yhi, yl, yh, zr, xl, xh, zz,
-    o_ref, hxl, hxh, hyl, hyh, hz, vx, ax, bx, zc,
+    o_ref, xc, hxl, hxh, hyl, hyh, hz, vx, ax, bx, zc,
 ):
     (mxl, mxh), (myl, myh), (mzl, mzh), first = masks(mesh)
     for z in range(NZ):
@@ -277,6 +277,11 @@
         out[2] = primitives(*st, ref[5] * mask)[4]
         out[3] = ref[8] * mask
         out[4] = st2[1] / (1.0 + st2[0])
+        base = 0 if ref is xl else 3
+        inv, gamma = 1.0 / (1.0 + st[0]), ref[5] * mask
+        xc[base] = (2.0 - gamma) * (st[1] * inv)
+        xc[base + 1] = inv
+        xc[base + 2] = gamma
     lane = lax.broadcasted_iota(jnp.int32, (1, NY), 1)
     at_x = lax.bitwise_and(lane, NX - 1)
     for side, ref, mask, own, out, sign in ((0, yl, myl, ylo, hyl, -1.0), (1, yh, myh, yhi, hyh, 1.0)):
@@ -380,12 +385,12 @@
 
 def forward_kernel(
     mesh, u0_ref, g_ref, s_ref, part, ylo_in, yhi_in, yl, yh, zr, xl, xh, zz, n_ref, m_ref,
-    u_ref, lam_ref, cf_ref, cfh_ref, mis_ref, ylo, yhi, zs, yown,
+    u_ref, lam_ref, cf_ref, cfh_ref, mis_ref, xc, ylo, yhi, zs, yown,
     hxl, hxh, hyl, hyh, hz, vx, ax, bx, az, bz, ch, yc, yp, zc,
 ):
     halo_step(
         mesh, u0_ref, g_ref, s_ref, part, ylo_in, yhi_in, yl, yh, zr, xl, xh, zz,
-        u_ref, hxl, hxh, hyl, hyh, hz, vx, ax, bx, zc,
+        u_ref, xc, hxl, hxh, hyl, hyh, hz, vx, ax, bx, zc,
     )
     speed_kernel(
         mesh, u_ref, g_ref, s_ref, hxl, hxh, hyl, hyh, hz, n_ref, m_ref,
@@ -494,14 +499,14 @@
     yown[4:8] = jnp.zeros((4, NY), F32)
 
 
-def edge_kernel(mesh, u_ref, g_ref, lam_ref, cf_ref, yl, yh, zr, xlo, xhi, yc):
+def edge_kernel(mesh, u_ref, lam_ref, cf_ref, yl, yh, zr, xlo, xhi, yc):
     _, (myl, myh), (mzl, mzh), _ = masks(mesh)
     low_y, high_y = yl[1:2] * myl, yh[1:2] * myh
     yc[:, 0:8] = jnp.concatenate([low_y, high_y, jnp.zeros((6, NY), F32)], axis=0).T
     lane = lax.broadcasted_iota(jnp.int32, (NZ, NY), 1)
     deep = lax.broadcasted_iota(jnp.int32, (NZ, NY), 0)
     for out, e, i, i2, sign in ((xhi, NX - 1, NX - 2, NX - 3, 1.0), (xlo, 0, 1, 2, -1.0)):
-        r, mx, my, mz = [u_ref[k, x_row(e), :] for k in range(4)]
+        r, my, mz = [u_ref[k, x_row(e), :] for k in (0, 2, 3)]
         inv = 1.0 / (1.0 + r)
         lm, lm_i = lam_ref[1, x_row(e), :], lam_ref[1, x_row(i), :]
         col = yc[x_row(e), :]
@@ -521,15 +526,11 @@
             + HALF_T * ((up_y - down_y) * (my * inv) + (up_z - down_z) * (mz * inv))
             + (sign * 0.5) * slope * inv
         )
-        gamma = g_ref[x_row(e), :]
-        out[4] = (2.0 - gamma) * (mx * inv)
-        out[5] = inv
-        out[6] = gamma
-        out[7] = jnp.where(deep == 0, low_y, jnp.where(deep == 1, high_y, jnp.where(deep == 2, side, 0.0)))
+        out[4] = jnp.where(deep == 0, low_y, jnp.where(deep == 1, high_y, jnp.where(deep == 2, side, 0.0)))
 
 
 def gradient_kernel(
-    mesh, u0_ref, u_ref, g_ref, lam_ref, cf_ref, cfh_ref, yown, yl, yh, zr, xl, xh, mis_ref, v_ref,
+    mesh, u0_ref, u_ref, g_ref, lam_ref, cf_ref, cfh_ref, xc, yown, yl, yh, zr, xl, xh, mis_ref, v_ref,
     grad_ref, row_ref,
     lx, lz, px, dx, dg, yc, gx, gy, gz,
 ):
@@ -551,24 +552,24 @@
         phi = HALF_T * (lx[1, pl.ds(24 * z + 9, 8), :] - lx[1, pl.ds(24 * z + 7, 8), :])
         px[layer(z), :] = phi
         dx[pl.ds(24 * z + 8, 8), :] = phi * cf_ref[layer(z), :]
-    gx[1, pl.ds(7, NZ, stride=24), :] = mxl * phi_low * xl[6]
-    gx[1, pl.ds(16, NZ, stride=24), :] = mxh * phi_high * xh[6]
+    gx[1, pl.ds(7, NZ, stride=24), :] = mxl * phi_low * xc[2]
+    gx[1, pl.ds(16, NZ, stride=24), :] = mxh * phi_high * xc[5]
     gx[0, pl.ds(7, NZ, stride=24), :] = mxl * (
         xl[3]
         + HALF_T * lam_ref[0, x_row(0), :]
         + NEAR * lam_ref[1, x_row(0), :]
-        + phi_low * xl[4]
-        - 0.5 * dx[pl.ds(8, NZ, stride=24), :] * xl[5]
+        + phi_low * xc[0]
+        - 0.5 * dx[pl.ds(8, NZ, stride=24), :] * xc[1]
     )
     gx[0, pl.ds(16, NZ, stride=24), :] = mxh * (
         xh[3]
         - HALF_T * lam_ref[0, x_row(NX - 1), :]
         + NEAR * lam_ref[1, x_row(NX - 1), :]
-        + phi_high * xh[4]
-        + 0.5 * dx[pl.ds(15, NZ, stride=24), :] * xh[5]
+        + phi_high * xc[3]
+        + 0.5 * dx[pl.ds(15, NZ, stride=24), :] * xc[4]
     )
     at_x = lax.bitwise_and(lax.broadcasted_iota(jnp.int32, (1, NY), 1), NX - 1)
-    from_high, from_low = pltpu.roll(xh[7], NX - 1, 1) * mxh, pltpu.roll(xl[7], NY - NX + 1, 1) * mxl
+    from_high, from_low = pltpu.roll(xh[4], NX - 1, 1) * mxh, pltpu.roll(xl[4], NY - NX + 1, 1) * mxl
     halo = []
     for side, ref, mask, sign in ((0, yl, myl, HALF_T), (1, yh, myh, -HALF_T)):
         items = ref[...]
@@ -580,8 +581,8 @@
         halo += [items[0:1] * mask, items[1:2] * mask, d_my * mask, d_en * mask]
     yc[...] = jnp.concatenate(halo, axis=0).T
     deep = lax.broadcasted_iota(jnp.int32, (NX, NY), 0)
-    up = jnp.where(deep == NX - 1, xh[7, 2:3, :] * mxh, pltpu.roll(zr[1], NX - 1, 0))
-    down = jnp.where(deep == 0, xl[7, 2:3, :] * mxl, pltpu.roll(zr[1], 1, 0))
+    up = jnp.where(deep == NX - 1, xh[4, 2:3, :] * mxh, pltpu.roll(zr[1], NX - 1, 0))
+    down = jnp.where(deep == 0, xl[4, 2:3, :] * mxl, pltpu.roll(zr[1], 1, 0))
     d_en = HALF_T * (up - down) * zr[5]
     za = dyn_layer(face_layer(first, 0))
     d_mz = (
@@ -700,6 +701,8 @@
 
 SMALL = pltpu.CompilerParams(vmem_limit_bytes=12 * 1024 * 1024)
 
+LARGE = pltpu.CompilerParams(vmem_limit_bytes=55168 * 1024)
+
 
 def rows_of(*shape):
     return jax.ShapeDtypeStruct(shape, F32)
@@ -731,8 +734,12 @@
     )
 
 
+def exchange_z(sizes, zs):
+    return lax.ppermute(zs, "gz", ring(sizes, "gz", 1))
+
+
 def exchange_yz(sizes, ylo, yhi, zs):
-    zr = lax.ppermute(zs, "gz", ring(sizes, "gz", 1))
+    zr = exchange_z(sizes, zs)
     yl = lax.ppermute(yhi, "gy", ring(sizes, "gy", 1))
     yh = lax.ppermute(ylo, "gy", ring(sizes, "gy", -1))
     return yl, yh, zr
@@ -750,8 +757,10 @@
 
     pair = rows_of(16, NY)
     tall = (NZ + 2) * NX
-    sent = call(bind(prep_kernel, sizes), [pair, pair, rows_of(11, NX, NY)], [vmem(CELLS, NY)], None)(state, gamma, sw)
-    got_yz = exchange_yz(sizes, *sent)
+    *sent_y, sent_z = call(
+        bind(prep_kernel, sizes), [pair, pair, rows_of(11, NX, NY)], [vmem(CELLS, NY)], LARGE
+    )(state, gamma, sw)
+    got_yz = exchange_yz(sizes, *sent_y, sent_z)
     hits, mean, spread = call(
         probe_kernel,
         [rows_of(CELLS, NY), rows_of(CELLS, NY), rows_of(1, probes.shape[0])],
@@ -764,21 +773,21 @@
             vmem(CELLS, NY), vmem(tall, NY), vmem(CELLS, NY),
             vmem(5, tall, NY), vmem(5, tall, NY), vmem(16, NY), vmem(CELLS, 16),
         ],
-    )(state, gamma, sw, *sent[:2], *got_yz)
+    )(state, gamma, sw, *sent_y, *got_yz)
     got_x = exchange_x(sizes, xlo, xhi)
-    zz = lax.ppermute(zz, "gz", ring(sizes, "gz", 1))
-    state_1, lam_2, coef, coef_halo, mis, *sent, yown = call(
+    zz = exchange_z(sizes, zz)
+    state_1, lam_2, coef, coef_halo, mis, beside, *sent, yown = call(
         bind(forward_kernel, sizes),
         [rows_of(5, CELLS, NY), rows_of(2, CELLS, NY), rows_of(CELLS, NY), rows_of(2, NZ, NY), plane]
-        + [plane, plane, rows_of(6, NX, NY), plane],
+        + [rows_of(6, NZ, NY), plane, plane, rows_of(6, NX, NY), plane],
         [
             vmem(5, NZ, NY), vmem(5, NZ, NY), vmem(8, NY), vmem(8, NY), vmem(2, NX, NY),
             vmem(NZ * 24, NY), vmem(5, NZ * 16, NY), vmem(5, NZ * 16, NY), vmem(2, tall, NY), vmem(2, tall, NY),
             vmem(2, CELLS, NY), vmem(CELLS, 8), vmem(CELLS, NY), vmem(CELLS, 8),
         ],
-    )(state, gamma, sw, part, *sent[:2], *got_yz, *got_x, zz, hits, mean)
+    )(state, gamma, sw, part, *sent_y, *got_yz, *got_x, zz, hits, mean)
     got_yz = exchange_yz(sizes, *sent)
-    sent = call(bind(edge_kernel, sizes), x_slabs(8), [vmem(CELLS, NY)])(state_1, gamma, lam_2, coef, *got_yz)
+    sent = call(bind(edge_kernel, sizes), x_slabs(5), [vmem(CELLS, NY)])(state_1, lam_2, coef, *got_yz)
     got_x = exchange_x(sizes, *sent)
     devices = sizes["gx"] * sizes["gy"] * sizes["gz"]
     gradient, rows = call(
@@ -788,7 +797,7 @@
             vmem(2, NZ * 24, NY), vmem(2, tall, NY), vmem(CELLS, NY), vmem(NZ * 24, NY), vmem(CELLS, NY),
             vmem(CELLS, 8), vmem(2, NZ * 24, NY), vmem(CELLS, NY), vmem(2, tall, NY),
         ],
-    )(state, state_1, gamma, lam_2, coef, coef_halo, yown, *got_yz, *got_x, mis, spread)
+    )(state, state_1, gamma, lam_2, coef, coef_halo, beside, yown, *got_yz, *got_x, mis, spread)
     rows = lax.all_to_all(rows, ("gx", "gy", "gz"), 0, 0, tiled=True)
     direction, misfit = pl.pallas_call(
         bind(scale_kernel, devices, probes.shape[0]),

time: 66.1 us -> 63.6 us (0.962)
  local copies, waits for them, and re-layouts: 2.08 us -> 0.69 us
    unnamed x14 -> x10, local copies, waits for them, and re-layouts: 2.08 us -> 0.69 us
where the time goes in v5:
time: 63.6 us; the launch traced here: 63.4 us
  blocking collectives  26.5 us (42%)
  starting transfers between devices  24.7 us (39%)
  Pallas kernels  5.68 us (9%)
  waiting for transfers between devices  5.13 us (8%)
  between operations  0.72 us (1%)
  local copies, waits for them, and re-layouts  0.69 us (1%)
    all_to_all x1, blocking collectives, local(): rows = lax.all_to_all(rows, ('gx', 'gy', 'gz'), 0, 0, tiled=True)  26.5 us
    ppermute x2, starting transfers between devices, exchange_x(): lax.ppermute(xlo, 'gx', ring(sizes, 'gx', -1))  9.14 us
    ppermute x2, starting transfers between devices, exchange_yz(): yl = lax.ppermute(yhi, 'gy', ring(sizes, 'gy', 1))  6.14 us
    ppermute x3, starting transfers between devices, exchange_z(): return lax.ppermute(zs, 'gz', ring(sizes, 'gz', 1))  4.07 us
    ppermute x2, starting transfers between devices, exchange_yz(): yh = lax.ppermute(ylo, 'gy', ring(sizes, 'gy', -1))  3.97 us
    ppermute x2, waiting for transfers between devices, exchange_yz(): yl = lax.ppermute(yhi, 'gy', ring(sizes, 'gy', 1))  1.66 us
    ppermute x2, waiting for transfers between devices, exchange_yz(): yh = lax.ppermute(ylo, 'gy', ring(sizes, 'gy', -1))  1.6 us
    ppermute x2, starting transfers between devices, exchange_x(): lax.ppermute(xhi, 'gx', ring(sizes, 'gx', 1))  1.37 us
  transfers between devices with their start and end apart: 11, of which 6 were waited for; matrix products, arithmetic and copies ran while one was open for 0% of the time, Pallas kernels for 1%

profile of v5, /device:TPU:1, one launch (start us, length us, event | category | flops | bytes accessed | tf_op | source)
XLA Modules:
  0.0 63.4 jit_solution(2047286754385056709)
XLA Ops:
  0.7 1.3 %shard_map.68 = (f32[16,128]{1,0:T(8,128)S(1)}, f32[16,128]{1,0:T(8,128)S(1)}, f32[11,8,128]{2,1,0:T(8,128)S(1)}) custom-call(f32[5,128,128]{2,1,0:T(8,128)} %bitcast.11, f32[128,128]{1,0:T(8,128)} %bitcast.18, s32[2,128,128]{2,1,0:T(8,128)} %bitcast.15), custom_call_target="tpu_custom_call" | custom-call | flops 100000 | bytes 100000 | tf_op jit(solution)/shard_map/pallas_call | solution.py:760
  2.0 2.6 %collective-permute-start.2 = (f32[11,8,128]{2,1,0:T(8,128)S(1)}, f32[11,8,128]{2,1,0:T(8,128)S(1)}, u32[]{:S(2)}, u32[]{:S(2)}) collective-permute-start(f32[11,8,128]{2,1,0:T(8,128)S(1)} %get-tuple-element.30), channel_id=1, source_target_pairs={{0,1},{1,0},{2,3},{3,2},{4,5},{5,4},{6,7},{7,6},{8,9},{9,8},{10,11... | collective-permute-start | bytes 135176 | tf_op jit(solution)/shard_map/ppermute | solution.py:738
  4.6 1.0 %collective-permute-start.1 = (f32[16,128]{1,0:T(8,128)S(1)}, f32[16,128]{1,0:T(8,128)S(1)}, u32[]{:S(2)}, u32[]{:S(2)}) collective-permute-start(f32[16,128]{1,0:T(8,128)S(1)} %get-tuple-element.28.ylo.ylo_in), channel_id=1, source_target_pairs={{0,14},{2,0},{4,2},{6,4},{8,6},{10,8},{12,10},{14,12},{1,15},{3,1}... | collective-permute-start | bytes 24584 | tf_op jit(solution)/shard_map/ppermute | solution.py:744
  5.5 2.9 %collective-permute-start = (f32[16,128]{1,0:T(8,128)S(1)}, f32[16,128]{1,0:T(8,128)S(1)}, u32[]{:S(2)}, u32[]{:S(2)}) collective-permute-start(f32[16,128]{1,0:T(8,128)S(1)} %get-tuple-element.29.yhi.yhi_in), channel_id=1, source_target_pairs={{0,2},{2,4},{4,6},{6,8},{8,10},{10,12},{12,14},{14,0},{1,3},{3,5},... | collective-permute-start | bytes 24584 | tf_op jit(solution)/shard_map/ppermute | solution.py:743
  8.4 1.3 %collective-permute-done.1.yh = f32[16,128]{1,0:T(8,128)S(1)} collective-permute-done((f32[16,128]{1,0:T(8,128)S(1)}, f32[16,128]{1,0:T(8,128)S(1)}, u32[]{:S(2)}, u32[]{:S(2)}) %collective-permute-start.1) | collective-permute-done | bytes 8224 | tf_op jit(solution)/shard_map/ppermute | solution.py:744
  9.7 1.0 %collective-permute-done.yl = f32[16,128]{1,0:T(8,128)S(1)} collective-permute-done((f32[16,128]{1,0:T(8,128)S(1)}, f32[16,128]{1,0:T(8,128)S(1)}, u32[]{:S(2)}, u32[]{:S(2)}) %collective-permute-start) | collective-permute-done | bytes 8224 | tf_op jit(solution)/shard_map/ppermute | solution.py:743
  10.8 1.2 %shard_map.69 = (f32[5,128,128]{2,1,0:T(8,128)S(1)}, f32[18,16,128]{2,1,0:T(8,128)S(1)}, f32[18,16,128]{2,1,0:T(8,128)S(1)}, f32[16,128]{1,0:T(8,128)S(1)}) custom-call(f32[5,128,128]{2,1,0:T(8,128)S(1)} %bitcast.12, f32[128,128]{1,0:T(8,128)S(1)} %bitcast.19, s32[2,128,128]{2,1,0:T(8,128)S(1)} %bitcast.16, f32[16,128]{1,0:T(8,128)S(1)} %get-tuple-element.28.ylo.ylo_in, ...), custom_call_target="tpu_custom_call" | custom-call | flops 100000 | bytes 100000 | tf_op jit(solution)/shard_map/pallas_call | solution.py:769
  12.0 1.3 %collective-permute-start.3 = (f32[18,16,128]{2,1,0:T(8,128)S(1)}, f32[18,16,128]{2,1,0:T(8,128)S(1)}, u32[]{:S(2)}, u32[]{:S(2)}) collective-permute-start(f32[18,16,128]{2,1,0:T(8,128)S(1)} %get-tuple-element.32), channel_id=1, source_target_pairs={{0,16},{16,32},{32,48},{48,64},{64,80},{80,96},{96,112},{112,128},... | collective-permute-start | bytes 442376 | tf_op jit(solution)/shard_map/ppermute | solution.py:732
  13.3 3.8 %collective-permute-start.4 = (f32[18,16,128]{2,1,0:T(8,128)S(1)}, f32[18,16,128]{2,1,0:T(8,128)S(1)}, u32[]{:S(2)}, u32[]{:S(2)}) collective-permute-start(f32[18,16,128]{2,1,0:T(8,128)S(1)} %get-tuple-element.33), channel_id=1, source_target_pairs={{0,240},{16,0},{32,16},{48,32},{64,48},{80,64},{96,80},{112,96},{1... | collective-permute-start | bytes 442376 | tf_op jit(solution)/shard_map/ppermute | solution.py:733
  17.1 0.7 %collective-permute-start.5 = (f32[16,128]{1,0:T(8,128)S(1)}, f32[16,128]{1,0:T(8,128)S(1)}, u32[]{:S(2)}, u32[]{:S(2)}) collective-permute-start(f32[16,128]{1,0:T(8,128)S(1)} %get-tuple-element.34), channel_id=1, source_target_pairs={{0,1},{1,0},{2,3},{3,2},{4,5},{5,4},{6,7},{7,6},{8,9},{9,8},{10,11... | collective-permute-start | bytes 24584 | tf_op jit(solution)/shard_map/ppermute | solution.py:738
  17.9 0.7 %copy-done.3 = s32[256]{0:T(256)S(1)} copy-done((s32[256]{0:T(256)S(1)}, s32[256]{0:T(256)}, u32[]{:S(2)}) %copy-start.3) | copy-done | bytes 1048
  18.5 0.5 shard_map.70
  19.1 0.6 collective-permute-done.5.zz
  19.6 0.9 %shard_map.71 = (f32[5,128,128]{2,1,0:T(8,128)S(1)}, f32[2,128,128]{2,1,0:T(8,128)S(1)}, f32[128,128]{1,0:T(8,128)S(1)}, f32[2,16,128]{2,1,0:T(8,128)S(1)}, f32[...) custom-call(f32[5,128,128]{2,1,0:T(8,128)S(1)} %bitcast.13, ...), custom_call_target="tpu_custom_call" | custom-call | flops 100000 | bytes 100000 | tf_op jit(solution)/shard_map/pallas_call | solution.py:779
  20.5 0.8 %collective-permute-start.8 = (f32[6,8,128]{2,1,0:T(8,128)S(1)}, f32[6,8,128]{2,1,0:T(8,128)S(1)}, u32[]{:S(2)}, u32[]{:S(2)}) collective-permute-start(f32[6,8,128]{2,1,0:T(8,128)S(1)} %get-tuple-element.45), channel_id=1, source_target_pairs={{0,1},{1,0},{2,3},{3,2},{4,5},{5,4},{6,7},{7,6},{8,9},{9,8},{10,11... | collective-permute-start | bytes 73736 | tf_op jit(solution)/shard_map/ppermute | solution.py:738
  21.3 3.3 %collective-permute-start.6 = (f32[8,128]{1,0:T(8,128)S(1)}, f32[8,128]{1,0:T(8,128)S(1)}, u32[]{:S(2)}, u32[]{:S(2)}) collective-permute-start(f32[8,128]{1,0:T(8,128)S(1)} %get-tuple-element.43), channel_id=1, source_target_pairs={{0,2},{2,4},{4,6},{6,8},{8,10},{10,12},{12,14},{14,0},{1,3},{3,5},... | collective-permute-start | bytes 12296 | tf_op jit(solution)/shard_map/ppermute | solution.py:743
  24.6 3.0 %collective-permute-start.7 = (f32[8,128]{1,0:T(8,128)S(1)}, f32[8,128]{1,0:T(8,128)S(1)}, u32[]{:S(2)}, u32[]{:S(2)}) collective-permute-start(f32[8,128]{1,0:T(8,128)S(1)} %get-tuple-element.44), channel_id=1, source_target_pairs={{0,14},{2,0},{4,2},{6,4},{8,6},{10,8},{12,10},{14,12},{1,15},{3,1}... | collective-permute-start | bytes 12296 | tf_op jit(solution)/shard_map/ppermute | solution.py:744
  27.6 0.7 %collective-permute-done.6.yl = f32[8,128]{1,0:T(8,128)S(1)} collective-permute-done((f32[8,128]{1,0:T(8,128)S(1)}, f32[8,128]{1,0:T(8,128)S(1)}, u32[]{:S(2)}, u32[]{:S(2)}) %collective-permute-start.6) | collective-permute-done | bytes 4128 | tf_op jit(solution)/shard_map/ppermute | solution.py:743
  28.3 0.3 collective-permute-done.7.yh
  28.8 5.3 %collective-permute-start.10 = (f32[5,16,128]{2,1,0:T(8,128)S(1)}, f32[5,16,128]{2,1,0:T(8,128)S(1)}, u32[]{:S(2)}, u32[]{:S(2)}) collective-permute-start(f32[5,16,128]{2,1,0:T(8,128)S(1)} %get-tuple-element.47), channel_id=1, source_target_pairs={{0,240},{16,0},{32,16},{48,32},{64,48},{80,64},{96,80},{112,96},{1... | collective-permute-start | bytes 122888 | tf_op jit(solution)/shard_map/ppermute | solution.py:733
  34.2 1.3 %collective-permute-done.9.xl = f32[5,16,128]{2,1,0:T(8,128)S(1)} collective-permute-done((f32[5,16,128]{2,1,0:T(8,128)S(1)}, f32[5,16,128]{2,1,0:T(8,128)S(1)}, u32[]{:S(2)}, u32[]{:S(2)}) %collective-permute-start.9) | collective-permute-done | bytes 40992 | tf_op jit(solution)/shard_map/ppermute | solution.py:732
  35.5 0.7 %shard_map.73 = (f32[128,128]{1,0:T(8,128)S(1)}, f32[256,128]{1,0:T(8,128)S(1)}) custom-call(f32[5,128,128]{2,1,0:T(8,128)S(1)} %bitcast.14, f32[5,128,128]{2,1,0:T(8,128)S(1)} %get-tuple-element.37.u_ref, f32[128,128]{1,0:T(8,128)S(1)} %bitcast.21, f32[2,128,128]{2,1,0:T(8,128)S(1)} %get-tuple-element.38.lam_ref, f32[128,128]{1,0:T(8,128)S(1)} %get-tuple-element.39.cf_ref, ...), custom_call_target="tpu_custom_call" | custom-call | flops 100000 | bytes 100000 | tf_op jit(solution)/shard_map/pallas_call | solution.py:793
  36.1 26.5 %all_to_all.11 = f32[256,1,128]{2,1,0:T(1,128)S(1)} all-to-all(f32[256,1,128]{2,1,0:T(1,128)S(1)} %bitcast.23), channel_id=1, replica_groups=mesh['gx'=16,'gy'=8,'gz'=2] {'gx','gy','gz'}, dimensions={0} | all-to-all | bytes 262144 | tf_op jit(solution)/shard_map/all_to_all | solution.py:801
  62.7 0.8 %shard_map.74 = (f32[128,128]{1,0:T(8,128)}, f32[1,1]{1,0:T(1,128)}) custom-call(f32[128,128]{1,0:T(8,128)S(1)} %get-tuple-element.50.grad_ref, f32[256,128]{1,0:T(8,128)S(1)} %bitcast.22), custom_call_target="tpu_custom_call" | custom-call | tf_op jit(solution)/shard_map/pallas_call | solution.py:802
  (16 shorter events, 0.3 us)
Async XLA Ops:
  0.6 10.1 %copy-start = (f32[5,16,8,128]{3,2,1,0:T(8,128)S(1)}, f32[5,16,8,128]{3,2,1,0:T(8,128)}, u32[]{:S(2)}) copy-start(f32[5,16,8,128]{3,2,1,0:T(8,128)} %param.5) | copy-start | bytes 983044
  0.6 10.1 %copy-start.1 = (s32[2,16,8,128]{3,2,1,0:T(8,128)S(1)}, s32[2,16,8,128]{3,2,1,0:T(8,128)}, u32[]{:S(2)}) copy-start(s32[2,16,8,128]{3,2,1,0:T(8,128)} %param.7) | copy-start | bytes 393220
  0.6 10.1 %copy-start.2 = (f32[16,8,128]{2,1,0:T(8,128)S(1)}, f32[16,8,128]{2,1,0:T(8,128)}, u32[]{:S(2)}) copy-start(f32[16,8,128]{2,1,0:T(8,128)} %param.6) | copy-start | bytes 196612
  2.0 8.7 %collective-permute-start.2 = (f32[11,8,128]{2,1,0:T(8,128)S(1)}, f32[11,8,128]{2,1,0:T(8,128)S(1)}, u32[]{:S(2)}, u32[]{:S(2)}) collective-permute-start(f32[11,8,128]{2,1,0:T(8,128)S(1)} %get-tuple-element.30), channel_id=1, source_target_pairs={{0,1},{1,0},{2,3},{3,2},{4,5},{5,4},{6,7},{7,6},{8,9},{9,8},{10,11... | collective-permute-start | bytes 135176 | tf_op jit(solution)/shard_map/ppermute | solution.py:738
  4.6 5.2 %collective-permute-start.1 = (f32[16,128]{1,0:T(8,128)S(1)}, f32[16,128]{1,0:T(8,128)S(1)}, u32[]{:S(2)}, u32[]{:S(2)}) collective-permute-start(f32[16,128]{1,0:T(8,128)S(1)} %get-tuple-element.28.ylo.ylo_in), channel_id=1, source_target_pairs={{0,14},{2,0},{4,2},{6,4},{8,6},{10,8},{12,10},{14,12},{1,15},{3,1}... | collective-permute-start | bytes 24584 | tf_op jit(solution)/shard_map/ppermute | solution.py:744
  5.5 5.2 %collective-permute-start = (f32[16,128]{1,0:T(8,128)S(1)}, f32[16,128]{1,0:T(8,128)S(1)}, u32[]{:S(2)}, u32[]{:S(2)}) collective-permute-start(f32[16,128]{1,0:T(8,128)S(1)} %get-tuple-element.29.yhi.yhi_in), channel_id=1, source_target_pairs={{0,2},{2,4},{4,6},{6,8},{8,10},{10,12},{12,14},{14,0},{1,3},{3,5},... | collective-permute-start | bytes 24584 | tf_op jit(solution)/shard_map/ppermute | solution.py:743
  10.8 7.1 %copy-start.4 = (f32[256]{0:T(256)S(1)}, f32[256]{0:T(256)}, u32[]{:S(2)}) copy-start(f32[256]{0:T(256)} %param.9) | copy-start | bytes 3076
  12.0 7.6 %collective-permute-start.3 = (f32[18,16,128]{2,1,0:T(8,128)S(1)}, f32[18,16,128]{2,1,0:T(8,128)S(1)}, u32[]{:S(2)}, u32[]{:S(2)}) collective-permute-start(f32[18,16,128]{2,1,0:T(8,128)S(1)} %get-tuple-element.32), channel_id=1, source_target_pairs={{0,16},{16,32},{32,48},{48,64},{64,80},{80,96},{96,112},{112,128},... | collective-permute-start | bytes 442376 | tf_op jit(solution)/shard_map/ppermute | solution.py:732
  13.3 6.3 %collective-permute-start.4 = (f32[18,16,128]{2,1,0:T(8,128)S(1)}, f32[18,16,128]{2,1,0:T(8,128)S(1)}, u32[]{:S(2)}, u32[]{:S(2)}) collective-permute-start(f32[18,16,128]{2,1,0:T(8,128)S(1)} %get-tuple-element.33), channel_id=1, source_target_pairs={{0,240},{16,0},{32,16},{48,32},{64,48},{80,64},{96,80},{112,96},{1... | collective-permute-start | bytes 442376 | tf_op jit(solution)/shard_map/ppermute | solution.py:733
  17.1 2.5 %collective-permute-start.5 = (f32[16,128]{1,0:T(8,128)S(1)}, f32[16,128]{1,0:T(8,128)S(1)}, u32[]{:S(2)}, u32[]{:S(2)}) collective-permute-start(f32[16,128]{1,0:T(8,128)S(1)} %get-tuple-element.34), channel_id=1, source_target_pairs={{0,1},{1,0},{2,3},{3,2},{4,5},{5,4},{6,7},{7,6},{8,9},{9,8},{10,11... | collective-permute-start | bytes 24584 | tf_op jit(solution)/shard_map/ppermute | solution.py:738
  17.8 0.7 %copy-start.3 = (s32[256]{0:T(256)S(1)}, s32[256]{0:T(256)}, u32[]{:S(2)}) copy-start(s32[256]{0:T(256)} %param.8) | copy-start | bytes 3076
  20.5 8.0 %collective-permute-start.8 = (f32[6,8,128]{2,1,0:T(8,128)S(1)}, f32[6,8,128]{2,1,0:T(8,128)S(1)}, u32[]{:S(2)}, u32[]{:S(2)}) collective-permute-start(f32[6,8,128]{2,1,0:T(8,128)S(1)} %get-tuple-element.45), channel_id=1, source_target_pairs={{0,1},{1,0},{2,3},{3,2},{4,5},{5,4},{6,7},{7,6},{8,9},{9,8},{10,11... | collective-permute-start | bytes 73736 | tf_op jit(solution)/shard_map/ppermute | solution.py:738
  21.3 6.9 %collective-permute-start.6 = (f32[8,128]{1,0:T(8,128)S(1)}, f32[8,128]{1,0:T(8,128)S(1)}, u32[]{:S(2)}, u32[]{:S(2)}) collective-permute-start(f32[8,128]{1,0:T(8,128)S(1)} %get-tuple-element.43), channel_id=1, source_target_pairs={{0,2},{2,4},{4,6},{6,8},{8,10},{10,12},{12,14},{14,0},{1,3},{3,5},... | collective-permute-start | bytes 12296 | tf_op jit(solution)/shard_map/ppermute | solution.py:743
  24.6 3.9 %collective-permute-start.7 = (f32[8,128]{1,0:T(8,128)S(1)}, f32[8,128]{1,0:T(8,128)S(1)}, u32[]{:S(2)}, u32[]{:S(2)}) collective-permute-start(f32[8,128]{1,0:T(8,128)S(1)} %get-tuple-element.44), channel_id=1, source_target_pairs={{0,14},{2,0},{4,2},{6,4},{8,6},{10,8},{12,10},{14,12},{1,15},{3,1}... | collective-permute-start | bytes 12296 | tf_op jit(solution)/shard_map/ppermute | solution.py:744
  28.7 6.7 %collective-permute-start.9 = (f32[5,16,128]{2,1,0:T(8,128)S(1)}, f32[5,16,128]{2,1,0:T(8,128)S(1)}, u32[]{:S(2)}, u32[]{:S(2)}) collective-permute-start(f32[5,16,128]{2,1,0:T(8,128)S(1)} %get-tuple-element.46), channel_id=1, source_target_pairs={{0,16},{16,32},{32,48},{48,64},{64,80},{80,96},{96,112},{112,128},... | collective-permute-start | bytes 122888 | tf_op jit(solution)/shard_map/ppermute | solution.py:732
  28.8 6.6 %collective-permute-start.10 = (f32[5,16,128]{2,1,0:T(8,128)S(1)}, f32[5,16,128]{2,1,0:T(8,128)S(1)}, u32[]{:S(2)}, u32[]{:S(2)}) collective-permute-start(f32[5,16,128]{2,1,0:T(8,128)S(1)} %get-tuple-element.47), channel_id=1, source_target_pairs={{0,240},{16,0},{32,16},{48,32},{64,48},{80,64},{96,80},{112,96},{1... | collective-permute-start | bytes 122888 | tf_op jit(solution)/shard_map/ppermute | solution.py:733

commit v6 on v5

--- a/solution.py
+++ b/solution.py
@@ -130,21 +130,41 @@
         zs[k] = items[k]
 
 
+def still_kernel(u_ref, g_ref, s_ref, vel, heat, press, slo, shi):
+    for z in range(NZ):
+        prim = primitives(*[u_ref[k, layer(z), :] for k in range(5)], g_ref[layer(z), :])
+        for k in range(3):
+            vel[k, layer(z), :] = prim[k]
+        heat[layer(z), :] = prim[3]
+        press[layer(z), :] = prim[4]
+    for out, e, i, j, last, sign in ((shi, NX - 1, NX - 2, NX - 3, NX - 4, 1.0), (slo, 0, 1, 2, 3, -1.0)):
+        for k in range(5):
+            out[k] = u_ref[k, x_row(e), :]
+        out[5] = g_ref[x_row(e), :]
+        out[6] = s_ref[0, x_row(e), :].astype(F32)
+        out[7] = vel[0, x_row(i), :]
+        out[8] = s_ref[1, x_row(e), :].astype(F32)
+        for at, before, after, base, count in ((i, e, j, 9, 5), (j, i, last, 14, 2)):
+            st = [u_ref[k, x_row(at), :] for k in range(5)]
+            slope = (sign * 0.5) * (vel[0, x_row(before), :] - vel[0, x_row(after), :])
+            total = total_pressure(press[x_row(at), :], s_ref[0, x_row(at), :].astype(F32), st[0], slope)
+            fl = flux(st, 0, vel[0, x_row(at), :], total)
+            for k in range(count):
+                out[base + k] = time_ratio * (sign * 0.5 * fl[k] + HALF_C * st[k])
+
+
 def side_kernel(
-    mesh, u_ref, g_ref, s_ref, ylo, yhi, yl, yh, zr,
+    mesh, u_ref, s_ref, vel, pr, slo, shi, ylo, yhi, yl, yh, zr,
     part, xlo, xhi, zz,
-    vy, vz, pr, az, bz, yr, yc,
+    vz, az, bz, yr, yc,
 ):
     _, (myl, myh), (mzl, mzh), first = masks(mesh)
     lane = lanes()
     for z in range(NZ):
-        _, uy, uz, _, press = primitives(*[u_ref[k, layer(z), :] for k in range(5)], g_ref[layer(z), :])
-        vy[layer(z), :] = uy
-        vz[layer(z + 1), :] = uz
-        pr[layer(z), :] = press
+        vz[layer(z + 1), :] = vel[2, layer(z), :]
     far = [zr[k] for k in range(8)]
     speed = far[3] / (1.0 + far[0])
-    own = vz[dyn_layer(face_layer(first, 0) + 1), :]
+    own = vel[2, dyn_layer(face_layer(first, 0)), :]
     slope = (far[7] - own) * jnp.where(first, 0.5, -0.5)
     fl = flux(far[:5], 2, speed, total_pressure(far[5], far[6], far[0], slope))
     for k in range(5):
@@ -172,7 +192,7 @@
         st = [u_ref[k, layer(z), :] for k in range(5)]
         press = pr[layer(z), :]
         visc = s_ref[0, layer(z), :].astype(F32) * quad_viscosity * (1.0 + st[0])
-        uy, uz = vy[layer(z), :], vz[layer(z + 1), :]
+        uy, uz = vel[1, layer(z), :], vel[2, layer(z), :]
 
         def col(i):
             return yc[layer(z), i : i + 1]
@@ -198,25 +218,13 @@
     for k in range(8):
         zz[k : k + 1, :] = low[k]
         zz[8 + k : 9 + k, :] = high[k]
-    for out, e, i, j, sign in ((xhi, NX - 1, NX - 2, NX - 3, 1.0), (xlo, 0, 1, 2, -1.0)):
-        st, st1, st2 = [[u_ref[k, x_row(at), :] for k in range(5)] for at in (e, i, j)]
-        ux = st[1] / (1.0 + st[0])
-        prim1, prim2 = primitives(*st1, g_ref[x_row(i), :]), primitives(*st2, g_ref[x_row(j), :])
-        last = j - 1 if sign > 0 else j + 1
-        ux3 = u_ref[1, x_row(last), :] / (1.0 + u_ref[0, x_row(last), :])
-        slope1, slope2 = (sign * 0.5) * (ux - prim2[0]), (sign * 0.5) * (prim1[0] - ux3)
-        f1 = flux(st1, 0, prim1[0], total_pressure(prim1[4], s_ref[0, x_row(i), :].astype(F32), st1[0], slope1))
-        f2 = flux(st2, 0, prim2[0], total_pressure(prim2[4], s_ref[0, x_row(j), :].astype(F32), st2[0], slope2))
+    for out, still, e, i in ((xhi, shi, NX - 1, NX - 2), (xlo, slo, 0, 1)):
+        for k in range(9):
+            out[k] = still[k]
         for k in range(5):
-            out[k] = st[k]
-        out[5] = g_ref[x_row(e), :]
-        out[6] = s_ref[0, x_row(e), :].astype(F32)
-        out[7] = prim1[0]
-        out[8] = s_ref[1, x_row(e), :].astype(F32)
-        for k in range(5):
-            out[9 + k] = part[k, x_row(e), :] + time_ratio * (sign * 0.5 * f1[k] + HALF_C * st1[k])
+            out[9 + k] = part[k, x_row(e), :] + still[9 + k]
         for k in range(2):
-            out[14 + k] = part[k, x_row(i), :] + time_ratio * (sign * 0.5 * f2[k] + HALF_C * st2[k])
+            out[14 + k] = part[k, x_row(i), :] + still[14 + k]
         out[16] = zz[...]
         for k in range(8):
             out[17, k : k + 1, :] = zr[k, e : e + 1, :]
@@ -231,12 +239,12 @@
 
 
 def halo_step(
-    mesh, u_ref, g_ref, s_ref, part, ylo, yhi, yl, yh, zr, xl, xh, zz,
+    mesh, u_ref, g_ref, s_ref, vel, pr, part, ylo, yhi, yl, yh, zr, xl, xh, zz,
     o_ref, xc, hxl, hxh, hyl, hyh, hz, vx, ax, bx, zc,
 ):
     (mxl, mxh), (myl, myh), (mzl, mzh), first = masks(mesh)
     for z in range(NZ):
-        vx[pl.ds(24 * z + 8, 8), :] = u_ref[1, layer(z), :] / (1.0 + u_ref[0, layer(z), :])
+        vx[pl.ds(24 * z + 8, 8), :] = vel[0, layer(z), :]
     low = [xl[k] * mxl for k in range(8)]
     high = [xh[k] * mxh for k in range(8)]
     prim = primitives(*low[:6])
@@ -252,7 +260,7 @@
         ax[k, pl.ds(8, NZ, stride=16), :] = upper_part(f_high[k], high[k])
     for z in range(NZ):
         st = [u_ref[k, layer(z), :] for k in range(5)]
-        ux, _, _, _, press = primitives(*st, g_ref[layer(z), :])
+        ux, press = vel[0, layer(z), :], pr[layer(z), :]
         slope = 0.5 * (vx[pl.ds(24 * z + 9, 8), :] - vx[pl.ds(24 * z + 7, 8), :])
         fx = flux(st, 0, ux, total_pressure(press, s_ref[0, layer(z), :].astype(F32), st[0], slope))
         for k in range(5):
@@ -366,10 +374,8 @@
     za, zb = dyn_layer(face_layer(first, 0)), dyn_layer(face_layer(first, 1))
     sign = jnp.where(first, 1.0, -1.0)
     st = [u_ref[k, za, :] for k in range(5)]
-    prim = primitives(*st, g_ref[za, :])
-    uz_b = u_ref[3, zb, :] / (1.0 + u_ref[0, zb, :])
-    slope = (sign * 0.5) * (here[3] / (1.0 + here[0]) - uz_b)
-    fz = flux(st, 2, prim[2], total_pressure(prim[4], s_ref[0, za, :].astype(F32), st[0], slope))
+    slope = (sign * 0.5) * (here[3] / (1.0 + here[0]) - vel[2, zb, :])
+    fz = flux(st, 2, vel[2, za, :], total_pressure(pr[za, :], s_ref[0, za, :].astype(F32), st[0], slope))
     new = []
     for n, k in enumerate((0, 1, 3)):
         a_x = next_x(upper_part(f_here[n], here[k]), upper_part(f_h[n], near_h[k]))
@@ -384,12 +390,12 @@
 
 
 def forward_kernel(
-    mesh, u0_ref, g_ref, s_ref, part, ylo_in, yhi_in, yl, yh, zr, xl, xh, zz, n_ref, m_ref,
+    mesh, u0_ref, g_ref, s_ref, vel, pr, part, ylo_in, yhi_in, yl, yh, zr, xl, xh, zz, n_ref, m_ref,
     u_ref, lam_ref, cf_ref, cfh_ref, mis_ref, xc, ylo, yhi, zs, yown,
     hxl, hxh, hyl, hyh, hz, vx, ax, bx, az, bz, ch, yc, yp, zc,
 ):
     halo_step(
-        mesh, u0_ref, g_ref, s_ref, part, ylo_in, yhi_in, yl, yh, zr, xl, xh, zz,
+        mesh, u0_ref, g_ref, s_ref, vel, pr, part, ylo_in, yhi_in, yl, yh, zr, xl, xh, zz,
         u_ref, xc, hxl, hxh, hyl, hyh, hz, vx, ax, bx, zc,
     )
     speed_kernel(
@@ -529,21 +535,48 @@
         out[4] = jnp.where(deep == 0, low_y, jnp.where(deep == 1, high_y, jnp.where(deep == 2, side, 0.0)))
 
 
+def lean_kernel(mesh, u_ref, lam_ref, yl, yh, zr, base, vel, inv_ref, heat, lz, yc):
+    _, (myl, myh), (mzl, mzh), _ = masks(mesh)
+    lane = lanes()
+    for k in range(2):
+        for z in range(NZ):
+            lz[k, layer(z + 1), :] = lam_ref[k, layer(z), :]
+        lz[k, layer(0), :] = zr[k] * mzl
+        lz[k, layer(NZ + 1), :] = zr[k] * mzh
+    yc[...] = columns_of(yl, yh, 2, myl, myh)
+    for z in range(NZ):
+        r, mx, my, mz, en = [u_ref[k, layer(z), :] for k in range(5)]
+        inv = 1.0 / (1.0 + r)
+        ux, uy, uz = mx * inv, my * inv, mz * inv
+        heat[layer(z), :] = en - 0.5 * (mx * ux + my * uy + mz * uz)
+        inv_ref[layer(z), :] = inv
+        for k, value in enumerate((ux, uy, uz)):
+            vel[k, layer(z), :] = value
+        lr, lm = lam_ref[0, layer(z), :], lam_ref[1, layer(z), :]
+        lr_z = [lz[0, layer(z + s), :] for s in (0, 2)]
+        lm_z = [lz[1, layer(z + s), :] for s in (0, 2)]
+        lr_y = [y_prev(lr, yc[layer(z), 0:1], lane), y_next(lr, yc[layer(z), 2:3], lane)]
+        lm_y = [y_prev(lm, yc[layer(z), 1:2], lane), y_next(lm, yc[layer(z), 3:4], lane)]
+        phi_y1 = HALF_T * (lm_y[1] - lm_y[0])
+        phi_z1 = HALF_T * (lm_z[1] - lm_z[0])
+        near = (lm_y[0] + lm_y[1]) + (lm_z[0] + lm_z[1])
+        base[0, layer(z), :] = STAY * lm + NEAR * near + phi_y1 * uy + phi_z1 * uz
+        base[1, layer(z), :] = HALF_T * (lr_y[1] - lr_y[0]) + phi_y1 * ux
+        base[2, layer(z), :] = HALF_T * (lr_z[1] - lr_z[0]) + phi_z1 * ux
+
+
 def gradient_kernel(
-    mesh, u0_ref, u_ref, g_ref, lam_ref, cf_ref, cfh_ref, xc, yown, yl, yh, zr, xl, xh, mis_ref, v_ref,
+    mesh, vel, heat_ref, u_ref, g_ref, base, vel_1, inv_1, heat_1, lam_ref, cf_ref, cfh_ref, xc, yown, yl, yh, zr, xl, xh, mis_ref, v_ref,
     grad_ref, row_ref,
-    lx, lz, px, dx, dg, yc, gx, gy, gz,
+    lx, px, dx, dg, yc, gx, gy, gz,
 ):
     (mxl, mxh), (myl, myh), (mzl, mzh), first = masks(mesh)
     lane = lanes()
     for k in range(2):
         for z in range(NZ):
             lx[k, pl.ds(24 * z + 8, 8), :] = lam_ref[k, layer(z), :]
-            lz[k, layer(z + 1), :] = lam_ref[k, layer(z), :]
         lx[k, pl.ds(7, NZ, stride=24), :] = xl[k] * mxl
         lx[k, pl.ds(16, NZ, stride=24), :] = xh[k] * mxh
-        lz[k, layer(0), :] = zr[k] * mzl
-        lz[k, layer(NZ + 1), :] = zr[k] * mzh
     phi_low = HALF_T * (lam_ref[1, x_row(0), :] - xl[2] * mxl)
     phi_high = HALF_T * (xh[2] * mxh - lam_ref[1, x_row(NX - 1), :])
     dx[pl.ds(7, NZ, stride=24), :] = phi_low * cfh_ref[0]
@@ -578,8 +611,8 @@
         d_en = HALF_T * (up - down) * items[5:6]
         own_r, own_m = yown[2 * side : 2 * side + 1], yown[2 * side + 1 : 2 * side + 2]
         d_my = items[2:3] + sign * (own_r + own_m * items[3:4]) - d_en * items[4:5]
-        halo += [items[0:1] * mask, items[1:2] * mask, d_my * mask, d_en * mask]
-    yc[...] = jnp.concatenate(halo, axis=0).T
+        halo += [d_my * mask, d_en * mask]
+    yc[...] = jnp.concatenate(halo + [jnp.zeros((4, NY), F32)], axis=0).T
     deep = lax.broadcasted_iota(jnp.int32, (NX, NY), 0)
     up = jnp.where(deep == NX - 1, xh[4, 2:3, :] * mxh, pltpu.roll(zr[1], NX - 1, 0))
     down = jnp.where(deep == 0, xl[4, 2:3, :] * mxl, pltpu.roll(zr[1], 1, 0))
@@ -594,53 +627,34 @@
         gz[k, layer(0), :] = value * mzl
         gz[k, layer(NZ + 1), :] = value * mzh
     for z in range(NZ):
-        r, mx, my, mz, en = [u_ref[k, layer(z), :] for k in range(5)]
-        gamma = g_ref[layer(z), :]
-        inv = 1.0 / (1.0 + r)
-        ux, uy, uz = mx * inv, my * inv, mz * inv
-        heat = en - 0.5 * (mx * ux + my * uy + mz * uz)
-        lr, lm = lam_ref[0, layer(z), :], lam_ref[1, layer(z), :]
+        ux, uy, uz = [vel_1[k, layer(z), :] for k in range(3)]
         lr_x = [lx[0, pl.ds(24 * z + s, 8), :] for s in (7, 9)]
         lm_x = [lx[1, pl.ds(24 * z + s, 8), :] for s in (7, 9)]
-        lr_z = [lz[0, layer(z + s), :] for s in (0, 2)]
-        lm_z = [lz[1, layer(z + s), :] for s in (0, 2)]
-        lr_y = [y_prev(lr, yc[layer(z), 0:1], lane), y_next(lr, yc[layer(z), 4:5], lane)]
-        lm_y = [y_prev(lm, yc[layer(z), 1:2], lane), y_next(lm, yc[layer(z), 5:6], lane)]
-        phi_x0 = HALF_T * (lr_x[1] - lr_x[0])
-        phi_y0 = HALF_T * (lr_y[1] - lr_y[0])
-        phi_z0 = HALF_T * (lr_z[1] - lr_z[0])
         phi_x1 = px[layer(z), :]
-        phi_y1 = HALF_T * (lm_y[1] - lm_y[0])
-        phi_z1 = HALF_T * (lm_z[1] - lm_z[0])
-        near = (lm_x[0] + lm_x[1]) + (lm_y[0] + lm_y[1]) + (lm_z[0] + lm_z[1])
-        d_speed = phi_x1 * mx + 0.5 * (dx[pl.ds(24 * z + 7, 8), :] - dx[pl.ds(24 * z + 9, 8), :])
-        d_en = phi_x1 * gamma
+        d_speed = phi_x1 * u_ref[1, layer(z), :] + 0.5 * (dx[pl.ds(24 * z + 7, 8), :] - dx[pl.ds(24 * z + 9, 8), :])
+        d_en = phi_x1 * g_ref[layer(z), :]
         gx[0, pl.ds(24 * z + 8, 8), :] = (
-            STAY * lm
-            + NEAR * near
-            + phi_x0
+            base[0, layer(z), :]
+            + NEAR * (lm_x[0] + lm_x[1])
+            + HALF_T * (lr_x[1] - lr_x[0])
             + (phi_x1 - d_en) * ux
-            + phi_y1 * uy
-            + phi_z1 * uz
-            + d_speed * inv
+            + d_speed * inv_1[layer(z), :]
         )
         gx[1, pl.ds(24 * z + 8, 8), :] = d_en
-        gy[layer(z), :] = phi_y0 - d_en * uy + phi_y1 * ux
-        gz[0, layer(z + 1), :] = phi_z0 - d_en * uz + phi_z1 * ux
+        gy[layer(z), :] = base[1, layer(z), :] - d_en * uy
+        gz[0, layer(z + 1), :] = base[2, layer(z), :] - d_en * uz
         gz[1, layer(z + 1), :] = d_en
-        dg[layer(z), :] = phi_x1 * heat
+        dg[layer(z), :] = phi_x1 * heat_1[layer(z), :]
     acc = jnp.zeros((NX, NY), F32)
     for z in range(NZ):
-        r, mx, my, mz, en = [u0_ref[k, layer(z), :] for k in range(5)]
-        inv = 1.0 / (1.0 + r)
-        ux, uy, uz = mx * inv, my * inv, mz * inv
-        heat = en - 0.5 * (mx * ux + my * uy + mz * uz)
+        ux, uy, uz = [vel[k, layer(z), :] for k in range(3)]
+        heat = heat_ref[layer(z), :]
         dif_x = [gx[k, pl.ds(24 * z + 9, 8), :] - gx[k, pl.ds(24 * z + 7, 8), :] for k in range(2)]
         dif_z = [gz[k, layer(z + 2), :] - gz[k, layer(z), :] for k in range(2)]
         dif_y = []
         for k, own in ((0, gy[layer(z), :]), (1, gz[1, layer(z + 1), :])):
             dif_y.append(
-                y_next(own, yc[layer(z), 6 + k : 7 + k], lane) - y_prev(own, yc[layer(z), 2 + k : 3 + k], lane)
+                y_next(own, yc[layer(z), 2 + k : 3 + k], lane) - y_prev(own, yc[layer(z), k : k + 1], lane)
             )
         d_press = HALF_T * (
             (dif_x[0] + ux * dif_x[1]) + (dif_y[0] + uy * dif_y[1]) + (dif_z[0] + uz * dif_z[1])
@@ -766,14 +780,17 @@
         [rows_of(CELLS, NY), rows_of(CELLS, NY), rows_of(1, probes.shape[0])],
         [],
     )(probes.reshape(1, -1), observed.reshape(1, -1))
+    grid = rows_of(CELLS, NY)
+    vel, heat, press, slo, shi = call(still_kernel, [rows_of(3, CELLS, NY), grid, grid] + x_slabs(16), [])(
+        state, gamma, sw
+    )
     part, xlo, xhi, zz = call(
         bind(side_kernel, sizes),
         [rows_of(5, CELLS, NY)] + x_slabs(18) + [pair],
         [
-            vmem(CELLS, NY), vmem(tall, NY), vmem(CELLS, NY),
-            vmem(5, tall, NY), vmem(5, tall, NY), vmem(16, NY), vmem(CELLS, 16),
+            vmem(tall, NY), vmem(5, tall, NY), vmem(5, tall, NY), vmem(16, NY), vmem(CELLS, 16),
         ],
-    )(state, gamma, sw, *sent_y, *got_yz)
+    )(state, sw, vel, press, slo, shi, *sent_y, *got_yz)
     got_x = exchange_x(sizes, xlo, xhi)
     zz = exchange_z(sizes, zz)
     state_1, lam_2, coef, coef_halo, mis, beside, *sent, yown = call(
@@ -785,19 +802,24 @@
             vmem(NZ * 24, NY), vmem(5, NZ * 16, NY), vmem(5, NZ * 16, NY), vmem(2, tall, NY), vmem(2, tall, NY),
             vmem(2, CELLS, NY), vmem(CELLS, 8), vmem(CELLS, NY), vmem(CELLS, 8),
         ],
-    )(state, gamma, sw, part, *sent_y, *got_yz, *got_x, zz, hits, mean)
+    )(state, gamma, sw, vel, press, part, *sent_y, *got_yz, *got_x, zz, hits, mean)
     got_yz = exchange_yz(sizes, *sent)
     sent = call(bind(edge_kernel, sizes), x_slabs(5), [vmem(CELLS, NY)])(state_1, lam_2, coef, *got_yz)
     got_x = exchange_x(sizes, *sent)
+    lean = call(
+        bind(lean_kernel, sizes),
+        [rows_of(3, CELLS, NY), rows_of(3, CELLS, NY), grid, grid],
+        [vmem(2, tall, NY), vmem(CELLS, 8)],
+    )(state_1, lam_2, *got_yz)
     devices = sizes["gx"] * sizes["gy"] * sizes["gz"]
     gradient, rows = call(
         bind(gradient_kernel, sizes),
         [rows_of(CELLS, NY), rows_of(devices, NY)],
         [
-            vmem(2, NZ * 24, NY), vmem(2, tall, NY), vmem(CELLS, NY), vmem(NZ * 24, NY), vmem(CELLS, NY),
+            vmem(2, NZ * 24, NY), vmem(CELLS, NY), vmem(NZ * 24, NY), vmem(CELLS, NY),
             vmem(CELLS, 8), vmem(2, NZ * 24, NY), vmem(CELLS, NY), vmem(2, tall, NY),
         ],
-    )(state, state_1, gamma, lam_2, coef, coef_halo, beside, yown, *got_yz, *got_x, mis, spread)
+    )(vel, heat, state_1, gamma, *lean, lam_2, coef, coef_halo, beside, yown, *got_yz, *got_x, mis, spread)
     rows = lax.all_to_all(rows, ("gx", "gy", "gz"), 0, 0, tiled=True)
     direction, misfit = pl.pallas_call(
         bind(scale_kernel, devices, probes.shape[0]),

time: 63.6 us -> 63.4 us (level)
  transfers between devices with their start and end apart: 11 -> 11, of which waited for: 6 -> 6; matrix products, arithmetic and copies ran while one was open for 0% -> 0% of each run, Pallas kernels for 1% -> 2%
where the time goes in v6:
time: 63.4 us; the launch traced here: 63.2 us
  blocking collectives  26.5 us (42%)
  starting transfers between devices  24.7 us (39%)
  Pallas kernels  5.95 us (9%)
  waiting for transfers between devices  4.68 us (7%)
  between operations  0.7 us (1%)
  local copies, waits for them, and re-layouts  0.69 us (1%)
    all_to_all x1, blocking collectives, local(): rows = lax.all_to_all(rows, ('gx', 'gy', 'gz'), 0, 0, tiled=True)  26.5 us
    ppermute x2, starting transfers between devices, exchange_x(): lax.ppermute(xlo, 'gx', ring(sizes, 'gx', -1))  9.14 us
    ppermute x2, starting transfers between devices, exchange_yz(): yl = lax.ppermute(yhi, 'gy', ring(sizes, 'gy', 1))  6.15 us
    ppermute x3, starting transfers between devices, exchange_z(): return lax.ppermute(zs, 'gz', ring(sizes, 'gz', 1))  4.06 us
    ppermute x2, starting transfers between devices, exchange_yz(): yh = lax.ppermute(ylo, 'gy', ring(sizes, 'gy', -1))  3.96 us
    ppermute x2, waiting for transfers between devices, exchange_yz(): yl = lax.ppermute(yhi, 'gy', ring(sizes, 'gy', 1))  1.66 us
    ppermute x2, waiting for transfers between devices, exchange_yz(): yh = lax.ppermute(ylo, 'gy', ring(sizes, 'gy', -1))  1.48 us
    ppermute x2, starting transfers between devices, exchange_x(): lax.ppermute(xhi, 'gx', ring(sizes, 'gx', 1))  1.37 us
  transfers between devices with their start and end apart: 11, of which 6 were waited for; matrix products, arithmetic and copies ran while one was open for 0% of the time, Pallas kernels for 2%

profile of v6, /device:TPU:1, one launch (start us, length us, event | category | flops | bytes accessed | tf_op | source)
XLA Modules:
  0.0 63.2 jit_solution(5464913041940732268)
XLA Ops:
  0.7 1.3 %shard_map.69 = (f32[16,128]{1,0:T(8,128)S(1)}, f32[16,128]{1,0:T(8,128)S(1)}, f32[11,8,128]{2,1,0:T(8,128)S(1)}) custom-call(f32[5,128,128]{2,1,0:T(8,128)} %bitcast.11, f32[128,128]{1,0:T(8,128)} %bitcast.19, s32[2,128,128]{2,1,0:T(8,128)} %bitcast.15), custom_call_target="tpu_custom_call" | custom-call | flops 100000 | bytes 100000 | tf_op jit(solution)/shard_map/pallas_call | solution.py:774
  2.0 2.6 %collective-permute-start.2 = (f32[11,8,128]{2,1,0:T(8,128)S(1)}, f32[11,8,128]{2,1,0:T(8,128)S(1)}, u32[]{:S(2)}, u32[]{:S(2)}) collective-permute-start(f32[11,8,128]{2,1,0:T(8,128)S(1)} %get-tuple-element.44), channel_id=1, source_target_pairs={{0,1},{1,0},{2,3},{3,2},{4,5},{5,4},{6,7},{7,6},{8,9},{9,8},{10,11... | collective-permute-start | bytes 135176 | tf_op jit(solution)/shard_map/ppermute | solution.py:752
  4.6 1.0 %collective-permute-start.1 = (f32[16,128]{1,0:T(8,128)S(1)}, f32[16,128]{1,0:T(8,128)S(1)}, u32[]{:S(2)}, u32[]{:S(2)}) collective-permute-start(f32[16,128]{1,0:T(8,128)S(1)} %get-tuple-element.42.ylo.ylo_in), channel_id=1, source_target_pairs={{0,14},{2,0},{4,2},{6,4},{8,6},{10,8},{12,10},{14,12},{1,15},{3,1}... | collective-permute-start | bytes 24584 | tf_op jit(solution)/shard_map/ppermute | solution.py:758
  5.5 2.9 %collective-permute-start = (f32[16,128]{1,0:T(8,128)S(1)}, f32[16,128]{1,0:T(8,128)S(1)}, u32[]{:S(2)}, u32[]{:S(2)}) collective-permute-start(f32[16,128]{1,0:T(8,128)S(1)} %get-tuple-element.43.yhi.yhi_in), channel_id=1, source_target_pairs={{0,2},{2,4},{4,6},{6,8},{8,10},{10,12},{12,14},{14,0},{1,3},{3,5},... | collective-permute-start | bytes 24584 | tf_op jit(solution)/shard_map/ppermute | solution.py:757
  8.5 1.2 %collective-permute-done.1.yh = f32[16,128]{1,0:T(8,128)S(1)} collective-permute-done((f32[16,128]{1,0:T(8,128)S(1)}, f32[16,128]{1,0:T(8,128)S(1)}, u32[]{:S(2)}, u32[]{:S(2)}) %collective-permute-start.1) | collective-permute-done | bytes 8224 | tf_op jit(solution)/shard_map/ppermute | solution.py:758
  9.7 1.0 %collective-permute-done.yl = f32[16,128]{1,0:T(8,128)S(1)} collective-permute-done((f32[16,128]{1,0:T(8,128)S(1)}, f32[16,128]{1,0:T(8,128)S(1)}, u32[]{:S(2)}, u32[]{:S(2)}) %collective-permute-start) | collective-permute-done | bytes 8224 | tf_op jit(solution)/shard_map/ppermute | solution.py:757
  10.7 1.2 %shard_map.70 = (f32[5,128,128]{2,1,0:T(8,128)S(1)}, f32[18,16,128]{2,1,0:T(8,128)S(1)}, f32[18,16,128]{2,1,0:T(8,128)S(1)}, f32[16,128]{1,0:T(8,128)S(1)}) custom-call(f32[5,128,128]{2,1,0:T(8,128)S(1)} %bitcast.13, s32[2,128,128]{2,1,0:T(8,128)S(1)} %bitcast.17, f32[3,128,128]{2,1,0:T(8,128)S(1)} %get-tuple-element.37.vel, ...), custom_call_target="tpu_custom_call" | custom-call | flops 100000 | bytes 100000 | tf_op jit(solution)/shard_map/pallas_call | solution.py:787
  12.0 1.3 %collective-permute-start.3 = (f32[18,16,128]{2,1,0:T(8,128)S(1)}, f32[18,16,128]{2,1,0:T(8,128)S(1)}, u32[]{:S(2)}, u32[]{:S(2)}) collective-permute-start(f32[18,16,128]{2,1,0:T(8,128)S(1)} %get-tuple-element.46), channel_id=1, source_target_pairs={{0,16},{16,32},{32,48},{48,64},{64,80},{80,96},{96,112},{112,128},... | collective-permute-start | bytes 442376 | tf_op jit(solution)/shard_map/ppermute | solution.py:746
  13.3 3.8 %collective-permute-start.4 = (f32[18,16,128]{2,1,0:T(8,128)S(1)}, f32[18,16,128]{2,1,0:T(8,128)S(1)}, u32[]{:S(2)}, u32[]{:S(2)}) collective-permute-start(f32[18,16,128]{2,1,0:T(8,128)S(1)} %get-tuple-element.47), channel_id=1, source_target_pairs={{0,240},{16,0},{32,16},{48,32},{64,48},{80,64},{96,80},{112,96},{1... | collective-permute-start | bytes 442376 | tf_op jit(solution)/shard_map/ppermute | solution.py:747
  17.1 0.7 %collective-permute-start.5 = (f32[16,128]{1,0:T(8,128)S(1)}, f32[16,128]{1,0:T(8,128)S(1)}, u32[]{:S(2)}, u32[]{:S(2)}) collective-permute-start(f32[16,128]{1,0:T(8,128)S(1)} %get-tuple-element.48), channel_id=1, source_target_pairs={{0,1},{1,0},{2,3},{3,2},{4,5},{5,4},{6,7},{7,6},{8,9},{9,8},{10,11... | collective-permute-start | bytes 24584 | tf_op jit(solution)/shard_map/ppermute | solution.py:752
  17.8 0.7 %copy-done.3 = s32[256]{0:T(256)S(1)} copy-done((s32[256]{0:T(256)S(1)}, s32[256]{0:T(256)}, u32[]{:S(2)}) %copy-start.3) | copy-done | bytes 1048
  18.5 0.5 shard_map.71
  19.0 0.6 collective-permute-done.5.zz
  19.6 0.9 %shard_map.72 = (f32[5,128,128]{2,1,0:T(8,128)S(1)}, f32[2,128,128]{2,1,0:T(8,128)S(1)}, f32[128,128]{1,0:T(8,128)S(1)}, f32[2,16,128]{2,1,0:T(8,128)S(1)}, f32[...) custom-call(f32[5,128,128]{2,1,0:T(8,128)S(1)} %bitcast.14, ...), custom_call_target="tpu_custom_call" | custom-call | flops 100000 | bytes 100000 | tf_op jit(solution)/shard_map/pallas_call | solution.py:796
  20.5 0.8 %collective-permute-start.8 = (f32[6,8,128]{2,1,0:T(8,128)S(1)}, f32[6,8,128]{2,1,0:T(8,128)S(1)}, u32[]{:S(2)}, u32[]{:S(2)}) collective-permute-start(f32[6,8,128]{2,1,0:T(8,128)S(1)} %get-tuple-element.55), channel_id=1, source_target_pairs={{0,1},{1,0},{2,3},{3,2},{4,5},{5,4},{6,7},{7,6},{8,9},{9,8},{10,11... | collective-permute-start | bytes 73736 | tf_op jit(solution)/shard_map/ppermute | solution.py:752
  21.2 3.3 %collective-permute-start.6 = (f32[8,128]{1,0:T(8,128)S(1)}, f32[8,128]{1,0:T(8,128)S(1)}, u32[]{:S(2)}, u32[]{:S(2)}) collective-permute-start(f32[8,128]{1,0:T(8,128)S(1)} %get-tuple-element.53), channel_id=1, source_target_pairs={{0,2},{2,4},{4,6},{6,8},{8,10},{10,12},{12,14},{14,0},{1,3},{3,5},... | collective-permute-start | bytes 12296 | tf_op jit(solution)/shard_map/ppermute | solution.py:757
  24.5 3.0 %collective-permute-start.7 = (f32[8,128]{1,0:T(8,128)S(1)}, f32[8,128]{1,0:T(8,128)S(1)}, u32[]{:S(2)}, u32[]{:S(2)}) collective-permute-start(f32[8,128]{1,0:T(8,128)S(1)} %get-tuple-element.54), channel_id=1, source_target_pairs={{0,14},{2,0},{4,2},{6,4},{8,6},{10,8},{12,10},{14,12},{1,15},{3,1}... | collective-permute-start | bytes 12296 | tf_op jit(solution)/shard_map/ppermute | solution.py:758
  27.5 0.7 %collective-permute-done.6.yl = f32[8,128]{1,0:T(8,128)S(1)} collective-permute-done((f32[8,128]{1,0:T(8,128)S(1)}, f32[8,128]{1,0:T(8,128)S(1)}, u32[]{:S(2)}, u32[]{:S(2)}) %collective-permute-start.6) | collective-permute-done | bytes 4128 | tf_op jit(solution)/shard_map/ppermute | solution.py:757
  28.8 5.3 %collective-permute-start.10 = (f32[5,16,128]{2,1,0:T(8,128)S(1)}, f32[5,16,128]{2,1,0:T(8,128)S(1)}, u32[]{:S(2)}, u32[]{:S(2)}) collective-permute-start(f32[5,16,128]{2,1,0:T(8,128)S(1)} %get-tuple-element.65), channel_id=1, source_target_pairs={{0,240},{16,0},{32,16},{48,32},{64,48},{80,64},{96,80},{112,96},{1... | collective-permute-start | bytes 122888 | tf_op jit(solution)/shard_map/ppermute | solution.py:747
  34.1 0.3 shard_map.73
  34.4 1.0 %collective-permute-done.9.xl = f32[5,16,128]{2,1,0:T(8,128)S(1)} collective-permute-done((f32[5,16,128]{2,1,0:T(8,128)S(1)}, f32[5,16,128]{2,1,0:T(8,128)S(1)}, u32[]{:S(2)}, u32[]{:S(2)}) %collective-permute-start.9) | collective-permute-done | bytes 40992 | tf_op jit(solution)/shard_map/ppermute | solution.py:746
  35.4 0.5 shard_map.75
  35.9 26.5 %all_to_all.11 = f32[256,1,128]{2,1,0:T(1,128)S(1)} all-to-all(f32[256,1,128]{2,1,0:T(1,128)S(1)} %bitcast.24), channel_id=1, replica_groups=mesh['gx'=16,'gy'=8,'gz'=2] {'gx','gy','gz'}, dimensions={0} | all-to-all | bytes 262144 | tf_op jit(solution)/shard_map/all_to_all | solution.py:823
  62.5 0.8 %shard_map.76 = (f32[128,128]{1,0:T(8,128)}, f32[1,1]{1,0:T(1,128)}) custom-call(f32[128,128]{1,0:T(8,128)S(1)} %get-tuple-element.68.grad_ref, f32[256,128]{1,0:T(8,128)S(1)} %bitcast.23), custom_call_target="tpu_custom_call" | custom-call | tf_op jit(solution)/shard_map/pallas_call | solution.py:824
  (18 shorter events, 0.7 us)
Async XLA Ops:
  0.6 7.8 %copy-start = (f32[5,16,8,128]{3,2,1,0:T(8,128)S(1)}, f32[5,16,8,128]{3,2,1,0:T(8,128)}, u32[]{:S(2)}) copy-start(f32[5,16,8,128]{3,2,1,0:T(8,128)} %param.5) | copy-start | bytes 983044
  0.6 7.8 %copy-start.1 = (s32[2,16,8,128]{3,2,1,0:T(8,128)S(1)}, s32[2,16,8,128]{3,2,1,0:T(8,128)}, u32[]{:S(2)}) copy-start(s32[2,16,8,128]{3,2,1,0:T(8,128)} %param.7) | copy-start | bytes 393220
  0.6 7.8 %copy-start.2 = (f32[16,8,128]{2,1,0:T(8,128)S(1)}, f32[16,8,128]{2,1,0:T(8,128)}, u32[]{:S(2)}) copy-start(f32[16,8,128]{2,1,0:T(8,128)} %param.6) | copy-start | bytes 196612
  2.0 8.7 %collective-permute-start.2 = (f32[11,8,128]{2,1,0:T(8,128)S(1)}, f32[11,8,128]{2,1,0:T(8,128)S(1)}, u32[]{:S(2)}, u32[]{:S(2)}) collective-permute-start(f32[11,8,128]{2,1,0:T(8,128)S(1)} %get-tuple-element.44), channel_id=1, source_target_pairs={{0,1},{1,0},{2,3},{3,2},{4,5},{5,4},{6,7},{7,6},{8,9},{9,8},{10,11... | collective-permute-start | bytes 135176 | tf_op jit(solution)/shard_map/ppermute | solution.py:752
  4.6 5.2 %collective-permute-start.1 = (f32[16,128]{1,0:T(8,128)S(1)}, f32[16,128]{1,0:T(8,128)S(1)}, u32[]{:S(2)}, u32[]{:S(2)}) collective-permute-start(f32[16,128]{1,0:T(8,128)S(1)} %get-tuple-element.42.ylo.ylo_in), channel_id=1, source_target_pairs={{0,14},{2,0},{4,2},{6,4},{8,6},{10,8},{12,10},{14,12},{1,15},{3,1}... | collective-permute-start | bytes 24584 | tf_op jit(solution)/shard_map/ppermute | solution.py:758
  5.5 5.2 %collective-permute-start = (f32[16,128]{1,0:T(8,128)S(1)}, f32[16,128]{1,0:T(8,128)S(1)}, u32[]{:S(2)}, u32[]{:S(2)}) collective-permute-start(f32[16,128]{1,0:T(8,128)S(1)} %get-tuple-element.43.yhi.yhi_in), channel_id=1, source_target_pairs={{0,2},{2,4},{4,6},{6,8},{8,10},{10,12},{12,14},{14,0},{1,3},{3,5},... | collective-permute-start | bytes 24584 | tf_op jit(solution)/shard_map/ppermute | solution.py:757
  10.7 7.1 %copy-start.4 = (f32[256]{0:T(256)S(1)}, f32[256]{0:T(256)}, u32[]{:S(2)}) copy-start(f32[256]{0:T(256)} %param.9) | copy-start | bytes 3076
  12.0 7.6 %collective-permute-start.3 = (f32[18,16,128]{2,1,0:T(8,128)S(1)}, f32[18,16,128]{2,1,0:T(8,128)S(1)}, u32[]{:S(2)}, u32[]{:S(2)}) collective-permute-start(f32[18,16,128]{2,1,0:T(8,128)S(1)} %get-tuple-element.46), channel_id=1, source_target_pairs={{0,16},{16,32},{32,48},{48,64},{64,80},{80,96},{96,112},{112,128},... | collective-permute-start | bytes 442376 | tf_op jit(solution)/shard_map/ppermute | solution.py:746
  13.3 6.3 %collective-permute-start.4 = (f32[18,16,128]{2,1,0:T(8,128)S(1)}, f32[18,16,128]{2,1,0:T(8,128)S(1)}, u32[]{:S(2)}, u32[]{:S(2)}) collective-permute-start(f32[18,16,128]{2,1,0:T(8,128)S(1)} %get-tuple-element.47), channel_id=1, source_target_pairs={{0,240},{16,0},{32,16},{48,32},{64,48},{80,64},{96,80},{112,96},{1... | collective-permute-start | bytes 442376 | tf_op jit(solution)/shard_map/ppermute | solution.py:747
  17.1 2.5 %collective-permute-start.5 = (f32[16,128]{1,0:T(8,128)S(1)}, f32[16,128]{1,0:T(8,128)S(1)}, u32[]{:S(2)}, u32[]{:S(2)}) collective-permute-start(f32[16,128]{1,0:T(8,128)S(1)} %get-tuple-element.48), channel_id=1, source_target_pairs={{0,1},{1,0},{2,3},{3,2},{4,5},{5,4},{6,7},{7,6},{8,9},{9,8},{10,11... | collective-permute-start | bytes 24584 | tf_op jit(solution)/shard_map/ppermute | solution.py:752
  17.8 0.7 %copy-start.3 = (s32[256]{0:T(256)S(1)}, s32[256]{0:T(256)}, u32[]{:S(2)}) copy-start(s32[256]{0:T(256)} %param.8) | copy-start | bytes 3076
  20.5 8.0 %collective-permute-start.8 = (f32[6,8,128]{2,1,0:T(8,128)S(1)}, f32[6,8,128]{2,1,0:T(8,128)S(1)}, u32[]{:S(2)}, u32[]{:S(2)}) collective-permute-start(f32[6,8,128]{2,1,0:T(8,128)S(1)} %get-tuple-element.55), channel_id=1, source_target_pairs={{0,1},{1,0},{2,3},{3,2},{4,5},{5,4},{6,7},{7,6},{8,9},{9,8},{10,11... | collective-permute-start | bytes 73736 | tf_op jit(solution)/shard_map/ppermute | solution.py:752
  21.2 6.9 %collective-permute-start.6 = (f32[8,128]{1,0:T(8,128)S(1)}, f32[8,128]{1,0:T(8,128)S(1)}, u32[]{:S(2)}, u32[]{:S(2)}) collective-permute-start(f32[8,128]{1,0:T(8,128)S(1)} %get-tuple-element.53), channel_id=1, source_target_pairs={{0,2},{2,4},{4,6},{6,8},{8,10},{10,12},{12,14},{14,0},{1,3},{3,5},... | collective-permute-start | bytes 12296 | tf_op jit(solution)/shard_map/ppermute | solution.py:757
  24.5 3.9 %collective-permute-start.7 = (f32[8,128]{1,0:T(8,128)S(1)}, f32[8,128]{1,0:T(8,128)S(1)}, u32[]{:S(2)}, u32[]{:S(2)}) collective-permute-start(f32[8,128]{1,0:T(8,128)S(1)} %get-tuple-element.54), channel_id=1, source_target_pairs={{0,14},{2,0},{4,2},{6,4},{8,6},{10,8},{12,10},{14,12},{1,15},{3,1}... | collective-permute-start | bytes 12296 | tf_op jit(solution)/shard_map/ppermute | solution.py:758
  28.7 6.7 %collective-permute-start.9 = (f32[5,16,128]{2,1,0:T(8,128)S(1)}, f32[5,16,128]{2,1,0:T(8,128)S(1)}, u32[]{:S(2)}, u32[]{:S(2)}) collective-permute-start(f32[5,16,128]{2,1,0:T(8,128)S(1)} %get-tuple-element.64), channel_id=1, source_target_pairs={{0,16},{16,32},{32,48},{48,64},{64,80},{80,96},{96,112},{112,128},... | collective-permute-start | bytes 122888 | tf_op jit(solution)/shard_map/ppermute | solution.py:746
  28.8 6.6 %collective-permute-start.10 = (f32[5,16,128]{2,1,0:T(8,128)S(1)}, f32[5,16,128]{2,1,0:T(8,128)S(1)}, u32[]{:S(2)}, u32[]{:S(2)}) collective-permute-start(f32[5,16,128]{2,1,0:T(8,128)S(1)} %get-tuple-element.65), channel_id=1, source_target_pairs={{0,240},{16,0},{32,16},{48,32},{64,48},{80,64},{96,80},{112,96},{1... | collective-permute-start | bytes 122888 | tf_op jit(solution)/shard_map/ppermute | solution.py:747

commit v7 on v6

--- a/solution.py
+++ b/solution.py
@@ -130,31 +130,34 @@
         zs[k] = items[k]
 
 
-def still_kernel(u_ref, g_ref, s_ref, vel, heat, press, slo, shi):
+def still_kernel(u_ref, g_ref, s_ref, vel, heat, press, slo, shi, addlo, addhi):
     for z in range(NZ):
         prim = primitives(*[u_ref[k, layer(z), :] for k in range(5)], g_ref[layer(z), :])
         for k in range(3):
             vel[k, layer(z), :] = prim[k]
         heat[layer(z), :] = prim[3]
         press[layer(z), :] = prim[4]
-    for out, e, i, j, last, sign in ((shi, NX - 1, NX - 2, NX - 3, NX - 4, 1.0), (slo, 0, 1, 2, 3, -1.0)):
+    for out, add, e, i, j, last, sign in (
+        (shi, addhi, NX - 1, NX - 2, NX - 3, NX - 4, 1.0),
+        (slo, addlo, 0, 1, 2, 3, -1.0),
+    ):
         for k in range(5):
             out[k] = u_ref[k, x_row(e), :]
         out[5] = g_ref[x_row(e), :]
         out[6] = s_ref[0, x_row(e), :].astype(F32)
         out[7] = vel[0, x_row(i), :]
         out[8] = s_ref[1, x_row(e), :].astype(F32)
-        for at, before, after, base, count in ((i, e, j, 9, 5), (j, i, last, 14, 2)):
+        for at, before, after, base, count in ((i, e, j, 0, 5), (j, i, last, 5, 2)):
             st = [u_ref[k, x_row(at), :] for k in range(5)]
             slope = (sign * 0.5) * (vel[0, x_row(before), :] - vel[0, x_row(after), :])
             total = total_pressure(press[x_row(at), :], s_ref[0, x_row(at), :].astype(F32), st[0], slope)
             fl = flux(st, 0, vel[0, x_row(at), :], total)
             for k in range(count):
-                out[base + k] = time_ratio * (sign * 0.5 * fl[k] + HALF_C * st[k])
+                add[base + k] = time_ratio * (sign * 0.5 * fl[k] + HALF_C * st[k])
 
 
 def side_kernel(
-    mesh, u_ref, s_ref, vel, pr, slo, shi, ylo, yhi, yl, yh, zr,
+    mesh, u_ref, s_ref, vel, pr, addlo, addhi, ylo, yhi, yl, yh, zr,
     part, xlo, xhi, zz,
     vz, az, bz, yr, yc,
 ):
@@ -218,18 +221,16 @@
     for k in range(8):
         zz[k : k + 1, :] = low[k]
         zz[8 + k : 9 + k, :] = high[k]
-    for out, still, e, i in ((xhi, shi, NX - 1, NX - 2), (xlo, slo, 0, 1)):
-        for k in range(9):
-            out[k] = still[k]
+    for out, add, e, i in ((xhi, addhi, NX - 1, NX - 2), (xlo, addlo, 0, 1)):
         for k in range(5):
-            out[9 + k] = part[k, x_row(e), :] + still[9 + k]
+            out[k] = part[k, x_row(e), :] + add[k]
         for k in range(2):
-            out[14 + k] = part[k, x_row(i), :] + still[14 + k]
-        out[16] = zz[...]
+            out[5 + k] = part[k, x_row(i), :] + add[5 + k]
+        out[7] = zz[...]
         for k in range(8):
-            out[17, k : k + 1, :] = zr[k, e : e + 1, :]
-        out[17, 8:9, :] = zr[1, i : i + 1, :] / (1.0 + zr[0, i : i + 1, :])
-        out[17, 9:16, :] = jnp.zeros((7, NY), F32)
+            out[8, k : k + 1, :] = zr[k, e : e + 1, :]
+        out[8, 8:9, :] = zr[1, i : i + 1, :] / (1.0 + zr[0, i : i + 1, :])
+        out[8, 9:16, :] = jnp.zeros((7, NY), F32)
 
 
 def shifted_x(own, low, high, at_x):
@@ -239,7 +240,7 @@
 
 
 def halo_step(
-    mesh, u_ref, g_ref, s_ref, vel, pr, part, ylo, yhi, yl, yh, zr, xl, xh, zz,
+    mesh, u_ref, g_ref, s_ref, vel, pr, part, ylo, yhi, yl, yh, zr, xl, xh, wl, wh, zz,
     o_ref, xc, hxl, hxh, hyl, hyh, hz, vx, ax, bx, zc,
 ):
     (mxl, mxh), (myl, myh), (mzl, mzh), first = masks(mesh)
@@ -271,15 +272,15 @@
             o_ref[k, layer(z), :] = part[k, layer(z), :] - time_ratio * (
                 ax[k, pl.ds(16 * z + 1, 8), :] - bx[k, pl.ds(16 * z + 7, 8), :]
             )
-    for out, ref, mask in ((hxl, xl, mxl), (hxh, xh, mxh)):
+    for out, ref, begun_ref, mask in ((hxl, xl, wl, mxl), (hxh, xh, wh, mxh)):
         if ref is xl:
             near = [-ax[k, pl.ds(0, NZ, stride=16), :] for k in range(5)]
             next_ = [-upper_part(f_low[k], low[k]) for k in range(2)]
         else:
             near = [bx[k, pl.ds(15, NZ, stride=16), :] for k in range(5)]
             next_ = [lower_part(f_high[k], high[k]) for k in range(2)]
-        st = [(ref[9 + k] + time_ratio * near[k]) * mask for k in range(5)]
-        st2 = [(ref[14 + k] + time_ratio * next_[k]) * mask for k in range(2)]
+        st = [(begun_ref[k] + time_ratio * near[k]) * mask for k in range(5)]
+        st2 = [(begun_ref[5 + k] + time_ratio * next_[k]) * mask for k in range(2)]
         out[0] = st[0]
         out[1] = st[1]
         out[2] = primitives(*st, ref[5] * mask)[4]
@@ -298,7 +299,7 @@
             return [values[k : k + 1] * m for k in range(8)]
 
         here = items(ref, mask)
-        near_l, near_h = items(xl[16, 8 * side : 8 * side + 8, :], mxl), items(xh[16, 8 * side : 8 * side + 8, :], mxh)
+        near_l, near_h = items(wl[7, 8 * side : 8 * side + 8, :], mxl), items(wh[7, 8 * side : 8 * side + 8, :], mxh)
         ux, ux_l, ux_h = [v[1] / (1.0 + v[0]) for v in (here, near_l, near_h)]
         up, down = shifted_x(ux, ux_l, ux_h, at_x)
         slope = 0.5 * (up - down)
@@ -351,8 +352,8 @@
     full = lanes()
     deep = lax.broadcasted_iota(jnp.int32, (NX, NY), 0)
     here = [zr[k] for k in range(8)]
-    near_l = [xl[17, k : k + 1, :] * mxl for k in range(9)]
-    near_h = [xh[17, k : k + 1, :] * mxh for k in range(9)]
+    near_l = [wl[8, k : k + 1, :] * mxl for k in range(9)]
+    near_h = [wh[8, k : k + 1, :] * mxh for k in range(9)]
     ux, ux_l, ux_h = [v[1] / (1.0 + v[0]) for v in (here, near_l, near_h)]
 
     def next_x(value, row):
@@ -390,12 +391,12 @@
 
 
 def forward_kernel(
-    mesh, u0_ref, g_ref, s_ref, vel, pr, part, ylo_in, yhi_in, yl, yh, zr, xl, xh, zz, n_ref, m_ref,
+    mesh, u0_ref, g_ref, s_ref, vel, pr, part, ylo_in, yhi_in, yl, yh, zr, xl, xh, wl, wh, zz, n_ref, m_ref,
     u_ref, lam_ref, cf_ref, cfh_ref, mis_ref, xc, ylo, yhi, zs, yown,
     hxl, hxh, hyl, hyh, hz, vx, ax, bx, az, bz, ch, yc, yp, zc,
 ):
     halo_step(
-        mesh, u0_ref, g_ref, s_ref, vel, pr, part, ylo_in, yhi_in, yl, yh, zr, xl, xh, zz,
+        mesh, u0_ref, g_ref, s_ref, vel, pr, part, ylo_in, yhi_in, yl, yh, zr, xl, xh, wl, wh, zz,
         u_ref, xc, hxl, hxh, hyl, hyh, hz, vx, ax, bx, zc,
     )
     speed_kernel(
@@ -781,16 +782,17 @@
         [],
     )(probes.reshape(1, -1), observed.reshape(1, -1))
     grid = rows_of(CELLS, NY)
-    vel, heat, press, slo, shi = call(still_kernel, [rows_of(3, CELLS, NY), grid, grid] + x_slabs(16), [])(
+    vel, heat, press, slo, shi, *adds = call(still_kernel, [rows_of(3, CELLS, NY), grid, grid] + x_slabs(9) + x_slabs(7), [])(
         state, gamma, sw
     )
+    got_still = exchange_x(sizes, slo, shi)
     part, xlo, xhi, zz = call(
         bind(side_kernel, sizes),
-        [rows_of(5, CELLS, NY)] + x_slabs(18) + [pair],
+        [rows_of(5, CELLS, NY)] + x_slabs(9) + [pair],
         [
             vmem(tall, NY), vmem(5, tall, NY), vmem(5, tall, NY), vmem(16, NY), vmem(CELLS, 16),
         ],
-    )(state, sw, vel, press, slo, shi, *sent_y, *got_yz)
+    )(state, sw, vel, press, *adds, *sent_y, *got_yz)
     got_x = exchange_x(sizes, xlo, xhi)
     zz = exchange_z(sizes, zz)
     state_1, lam_2, coef, coef_halo, mis, beside, *sent, yown = call(
@@ -802,7 +804,7 @@
             vmem(NZ * 24, NY), vmem(5, NZ * 16, NY), vmem(5, NZ * 16, NY), vmem(2, tall, NY), vmem(2, tall, NY),
             vmem(2, CELLS, NY), vmem(CELLS, 8), vmem(CELLS, NY), vmem(CELLS, 8),
         ],
-    )(state, gamma, sw, vel, press, part, *sent_y, *got_yz, *got_x, zz, hits, mean)
+    )(state, gamma, sw, vel, press, part, *sent_y, *got_yz, *got_still, *got_x, zz, hits, mean)
     got_yz = exchange_yz(sizes, *sent)
     sent = call(bind(edge_kernel, sizes), x_slabs(5), [vmem(CELLS, NY)])(state_1, lam_2, coef, *got_yz)
     got_x = exchange_x(sizes, *sent)

time: 63.4 us -> 63.9 us (level)
  starting transfers between devices: 24.7 us -> 26.1 us
    ppermute x2 -> x3, starting transfers between devices: 9.14 us -> 13.4 us  [exchange_x(): lax.ppermute(xlo, 'gx', ring(sizes, 'gx', -1))]
    ppermute x3, starting transfers between devices: 4.06 us -> 2.91 us  [exchange_z(): return lax.ppermute(zs, 'gz', ring(sizes, 'gz', 1))]
    ppermute x2, waiting for transfers between devices: 1.66 us -> 0.66 us  [exchange_yz(): yl = lax.ppermute(yhi, 'gy', ring(sizes, 'gy', 1))]
    ppermute x2, starting transfers between devices: 6.15 us -> 5.23 us  [exchange_yz(): yl = lax.ppermute(yhi, 'gy', ring(sizes, 'gy', 1))]
    ppermute x2, starting transfers between devices: 3.96 us -> 3.14 us  [exchange_yz(): yh = lax.ppermute(ylo, 'gy', ring(sizes, 'gy', -1))]
    ppermute x3, waiting for transfers between devices: 0.57 us -> 1.29 us  [exchange_z(): return lax.ppermute(zs, 'gz', ring(sizes, 'gz', 1))]
    ppermute x2 -> x3, starting transfers between devices: 1.37 us -> 1.45 us  [exchange_x(): lax.ppermute(xhi, 'gx', ring(sizes, 'gx', 1))]
  transfers between devices with their start and end apart: 11 -> 13, of which waited for: 6 -> 4; matrix products, arithmetic and copies ran while one was open for 0% -> 0% of each run, Pallas kernels for 2% -> 3%
where the time goes in v7:
time: 63.9 us; the launch traced here: 63.7 us
  blocking collectives  26.2 us (41%)
  starting transfers between devices  26.1 us (41%)
  Pallas kernels  5.95 us (9%)
  waiting for transfers between devices  4.11 us (6%)
  between operations  0.73 us (1%)
  local copies, waits for them, and re-layouts  0.7 us (1%)
    all_to_all x1, blocking collectives, local(): rows = lax.all_to_all(rows, ('gx', 'gy', 'gz'), 0, 0, tiled=True)  26.2 us
    ppermute x3, starting transfers between devices, exchange_x(): lax.ppermute(xlo, 'gx', ring(sizes, 'gx', -1))  13.4 us
    ppermute x2, starting transfers between devices, exchange_yz(): yl = lax.ppermute(yhi, 'gy', ring(sizes, 'gy', 1))  5.23 us
    ppermute x2, starting transfers between devices, exchange_yz(): yh = lax.ppermute(ylo, 'gy', ring(sizes, 'gy', -1))  3.14 us
    ppermute x3, starting transfers between devices, exchange_z(): return lax.ppermute(zs, 'gz', ring(sizes, 'gz', 1))  2.91 us
    ppermute x3, starting transfers between devices, exchange_x(): lax.ppermute(xhi, 'gx', ring(sizes, 'gx', 1))  1.45 us
    pallas_call x1, Pallas kernels, local(): call(bind(prep_kernel, sizes), [pair, pair, rows_of(11, NX, NY)], [vmem(C...  1.34 us
    ppermute x3, waiting for transfers between devices, exchange_z(): return lax.ppermute(zs, 'gz', ring(sizes, 'gz', 1))  1.29 us
  transfers between devices with their start and end apart: 13, of which 4 were waited for; matrix products, arithmetic and copies ran while one was open for 0% of the time, Pallas kernels for 3%

profile of v7, /device:TPU:1, one launch (start us, length us, event | category | flops | bytes accessed | tf_op | source)
XLA Modules:
  0.0 63.7 jit_solution(13451338023685703339)
XLA Ops:
  0.7 1.3 %shard_map.69 = (f32[16,128]{1,0:T(8,128)S(1)}, f32[16,128]{1,0:T(8,128)S(1)}, f32[11,8,128]{2,1,0:T(8,128)S(1)}) custom-call(f32[5,128,128]{2,1,0:T(8,128)} %bitcast.11, f32[128,128]{1,0:T(8,128)} %bitcast.19, s32[2,128,128]{2,1,0:T(8,128)} %bitcast.15), custom_call_target="tpu_custom_call" | custom-call | flops 100000 | bytes 100000 | tf_op jit(solution)/shard_map/pallas_call | solution.py:775
  2.0 2.6 %collective-permute-start.2 = (f32[11,8,128]{2,1,0:T(8,128)S(1)}, f32[11,8,128]{2,1,0:T(8,128)S(1)}, u32[]{:S(2)}, u32[]{:S(2)}) collective-permute-start(f32[11,8,128]{2,1,0:T(8,128)S(1)} %get-tuple-element.46), channel_id=1, source_target_pairs={{0,1},{1,0},{2,3},{3,2},{4,5},{5,4},{6,7},{7,6},{8,9},{9,8},{10,11... | collective-permute-start | bytes 135176 | tf_op jit(solution)/shard_map/ppermute | solution.py:753
  4.6 1.0 %collective-permute-start.1 = (f32[16,128]{1,0:T(8,128)S(1)}, f32[16,128]{1,0:T(8,128)S(1)}, u32[]{:S(2)}, u32[]{:S(2)}) collective-permute-start(f32[16,128]{1,0:T(8,128)S(1)} %get-tuple-element.44.ylo.ylo_in), channel_id=1, source_target_pairs={{0,14},{2,0},{4,2},{6,4},{8,6},{10,8},{12,10},{14,12},{1,15},{3,1}... | collective-permute-start | bytes 24584 | tf_op jit(solution)/shard_map/ppermute | solution.py:759
  5.5 2.9 %collective-permute-start = (f32[16,128]{1,0:T(8,128)S(1)}, f32[16,128]{1,0:T(8,128)S(1)}, u32[]{:S(2)}, u32[]{:S(2)}) collective-permute-start(f32[16,128]{1,0:T(8,128)S(1)} %get-tuple-element.45.yhi.yhi_in), channel_id=1, source_target_pairs={{0,2},{2,4},{4,6},{6,8},{8,10},{10,12},{12,14},{14,0},{1,3},{3,5},... | collective-permute-start | bytes 24584 | tf_op jit(solution)/shard_map/ppermute | solution.py:758
  8.5 1.3 %collective-permute-start.3 = (f32[9,16,128]{2,1,0:T(8,128)S(1)}, f32[9,16,128]{2,1,0:T(8,128)S(1)}, u32[]{:S(2)}, u32[]{:S(2)}) collective-permute-start(f32[9,16,128]{2,1,0:T(8,128)S(1)} %get-tuple-element.48), channel_id=1, source_target_pairs={{0,16},{16,32},{32,48},{48,64},{64,80},{80,96},{96,112},{112,128},... | collective-permute-start | bytes 221192 | tf_op jit(solution)/shard_map/ppermute | solution.py:747
  9.8 3.8 %collective-permute-start.4 = (f32[9,16,128]{2,1,0:T(8,128)S(1)}, f32[9,16,128]{2,1,0:T(8,128)S(1)}, u32[]{:S(2)}, u32[]{:S(2)}) collective-permute-start(f32[9,16,128]{2,1,0:T(8,128)S(1)} %get-tuple-element.49), channel_id=1, source_target_pairs={{0,240},{16,0},{32,16},{48,32},{64,48},{80,64},{96,80},{112,96},{1... | collective-permute-start | bytes 221192 | tf_op jit(solution)/shard_map/ppermute | solution.py:748
  13.6 1.2 %shard_map.70 = (f32[5,128,128]{2,1,0:T(8,128)S(1)}, f32[9,16,128]{2,1,0:T(8,128)S(1)}, f32[9,16,128]{2,1,0:T(8,128)S(1)}, f32[16,128]{1,0:T(8,128)S(1)}) custom-call(f32[5,128,128]{2,1,0:T(8,128)S(1)} %bitcast.13, s32[2,128,128]{2,1,0:T(8,128)S(1)} %bitcast.17, f32[3,128,128]{2,1,0:T(8,128)S(1)} %get-tuple-element.39.vel, ...), custom_call_target="tpu_custom_call" | custom-call | flops 100000 | bytes 100000 | tf_op jit(solution)/shard_map/pallas_call | solution.py:789
  15.0 4.8 %collective-permute-start.6 = (f32[9,16,128]{2,1,0:T(8,128)S(1)}, f32[9,16,128]{2,1,0:T(8,128)S(1)}, u32[]{:S(2)}, u32[]{:S(2)}) collective-permute-start(f32[9,16,128]{2,1,0:T(8,128)S(1)} %get-tuple-element.51), channel_id=1, source_target_pairs={{0,240},{16,0},{32,16},{48,32},{64,48},{80,64},{96,80},{112,96},{1... | collective-permute-start | bytes 221192 | tf_op jit(solution)/shard_map/ppermute | solution.py:748
  19.8 0.7 %copy-done.3 = s32[256]{0:T(256)S(1)} copy-done((s32[256]{0:T(256)S(1)}, s32[256]{0:T(256)}, u32[]{:S(2)}) %copy-start.3) | copy-done | bytes 1048
  20.4 0.5 shard_map.71
  21.0 1.3 %collective-permute-done.7.zz = f32[16,128]{1,0:T(8,128)S(1)} collective-permute-done((f32[16,128]{1,0:T(8,128)S(1)}, f32[16,128]{1,0:T(8,128)S(1)}, u32[]{:S(2)}, u32[]{:S(2)}) %collective-permute-start.7) | collective-permute-done | bytes 8224 | tf_op jit(solution)/shard_map/ppermute | solution.py:753
  22.3 0.9 %shard_map.72 = (f32[5,128,128]{2,1,0:T(8,128)S(1)}, f32[2,128,128]{2,1,0:T(8,128)S(1)}, f32[128,128]{1,0:T(8,128)S(1)}, f32[2,16,128]{2,1,0:T(8,128)S(1)}, f32[...) custom-call(f32[5,128,128]{2,1,0:T(8,128)S(1)} %bitcast.14, ...), custom_call_target="tpu_custom_call" | custom-call | flops 100000 | bytes 100000 | tf_op jit(solution)/shard_map/pallas_call | solution.py:798
  23.1 0.4 collective-permute-start.10
  23.5 2.4 %collective-permute-start.8 = (f32[8,128]{1,0:T(8,128)S(1)}, f32[8,128]{1,0:T(8,128)S(1)}, u32[]{:S(2)}, u32[]{:S(2)}) collective-permute-start(f32[8,128]{1,0:T(8,128)S(1)} %get-tuple-element.57), channel_id=1, source_target_pairs={{0,2},{2,4},{4,6},{6,8},{8,10},{10,12},{12,14},{14,0},{1,3},{3,5},... | collective-permute-start | bytes 12296 | tf_op jit(solution)/shard_map/ppermute | solution.py:758
  25.9 2.2 %collective-permute-start.9 = (f32[8,128]{1,0:T(8,128)S(1)}, f32[8,128]{1,0:T(8,128)S(1)}, u32[]{:S(2)}, u32[]{:S(2)}) collective-permute-start(f32[8,128]{1,0:T(8,128)S(1)} %get-tuple-element.58), channel_id=1, source_target_pairs={{0,14},{2,0},{4,2},{6,4},{8,6},{10,8},{12,10},{14,12},{1,15},{3,1}... | collective-permute-start | bytes 12296 | tf_op jit(solution)/shard_map/ppermute | solution.py:759
  28.0 0.7 %collective-permute-done.8.yl = f32[8,128]{1,0:T(8,128)S(1)} collective-permute-done((f32[8,128]{1,0:T(8,128)S(1)}, f32[8,128]{1,0:T(8,128)S(1)}, u32[]{:S(2)}, u32[]{:S(2)}) %collective-permute-start.8) | collective-permute-done | bytes 4128 | tf_op jit(solution)/shard_map/ppermute | solution.py:758
  28.7 1.1 %collective-permute-done.9.yh = f32[8,128]{1,0:T(8,128)S(1)} collective-permute-done((f32[8,128]{1,0:T(8,128)S(1)}, f32[8,128]{1,0:T(8,128)S(1)}, u32[]{:S(2)}, u32[]{:S(2)}) %collective-permute-start.9) | collective-permute-done | bytes 4128 | tf_op jit(solution)/shard_map/ppermute | solution.py:759
  29.8 0.2 shard_map.74
  30.1 4.8 %collective-permute-start.12 = (f32[5,16,128]{2,1,0:T(8,128)S(1)}, f32[5,16,128]{2,1,0:T(8,128)S(1)}, u32[]{:S(2)}, u32[]{:S(2)}) collective-permute-start(f32[5,16,128]{2,1,0:T(8,128)S(1)} %get-tuple-element.69), channel_id=1, source_target_pairs={{0,240},{16,0},{32,16},{48,32},{64,48},{80,64},{96,80},{112,96},{1... | collective-permute-start | bytes 122888 | tf_op jit(solution)/shard_map/ppermute | solution.py:748
  34.9 0.3 shard_map.73
  35.2 1.1 %collective-permute-done.11.xl = f32[5,16,128]{2,1,0:T(8,128)S(1)} collective-permute-done((f32[5,16,128]{2,1,0:T(8,128)S(1)}, f32[5,16,128]{2,1,0:T(8,128)S(1)}, u32[]{:S(2)}, u32[]{:S(2)}) %collective-permute-start.11) | collective-permute-done | bytes 40992 | tf_op jit(solution)/shard_map/ppermute | solution.py:747
  36.3 0.5 shard_map.75
  36.8 26.2 %all_to_all.11 = f32[256,1,128]{2,1,0:T(1,128)S(1)} all-to-all(f32[256,1,128]{2,1,0:T(1,128)S(1)} %bitcast.24), channel_id=1, replica_groups=mesh['gx'=16,'gy'=8,'gz'=2] {'gx','gy','gz'}, dimensions={0} | all-to-all | bytes 262144 | tf_op jit(solution)/shard_map/all_to_all | solution.py:825
  63.0 0.8 %shard_map.76 = (f32[128,128]{1,0:T(8,128)}, f32[1,1]{1,0:T(1,128)}) custom-call(f32[128,128]{1,0:T(8,128)S(1)} %get-tuple-element.72.grad_ref, f32[256,128]{1,0:T(8,128)S(1)} %bitcast.23), custom_call_target="tpu_custom_call" | custom-call | tf_op jit(solution)/shard_map/pallas_call | solution.py:826
  (22 shorter events, 0.3 us)
Async XLA Ops:
  0.6 7.8 %copy-start = (f32[5,16,8,128]{3,2,1,0:T(8,128)S(1)}, f32[5,16,8,128]{3,2,1,0:T(8,128)}, u32[]{:S(2)}) copy-start(f32[5,16,8,128]{3,2,1,0:T(8,128)} %param.5) | copy-start | bytes 983044
  0.6 7.8 %copy-start.1 = (s32[2,16,8,128]{3,2,1,0:T(8,128)S(1)}, s32[2,16,8,128]{3,2,1,0:T(8,128)}, u32[]{:S(2)}) copy-start(s32[2,16,8,128]{3,2,1,0:T(8,128)} %param.7) | copy-start | bytes 393220
  0.6 7.8 %copy-start.2 = (f32[16,8,128]{2,1,0:T(8,128)S(1)}, f32[16,8,128]{2,1,0:T(8,128)}, u32[]{:S(2)}) copy-start(f32[16,8,128]{2,1,0:T(8,128)} %param.6) | copy-start | bytes 196612
  2.0 11.6 %collective-permute-start.2 = (f32[11,8,128]{2,1,0:T(8,128)S(1)}, f32[11,8,128]{2,1,0:T(8,128)S(1)}, u32[]{:S(2)}, u32[]{:S(2)}) collective-permute-start(f32[11,8,128]{2,1,0:T(8,128)S(1)} %get-tuple-element.46), channel_id=1, source_target_pairs={{0,1},{1,0},{2,3},{3,2},{4,5},{5,4},{6,7},{7,6},{8,9},{9,8},{10,11... | collective-permute-start | bytes 135176 | tf_op jit(solution)/shard_map/ppermute | solution.py:753
  4.6 9.1 %collective-permute-start.1 = (f32[16,128]{1,0:T(8,128)S(1)}, f32[16,128]{1,0:T(8,128)S(1)}, u32[]{:S(2)}, u32[]{:S(2)}) collective-permute-start(f32[16,128]{1,0:T(8,128)S(1)} %get-tuple-element.44.ylo.ylo_in), channel_id=1, source_target_pairs={{0,14},{2,0},{4,2},{6,4},{8,6},{10,8},{12,10},{14,12},{1,15},{3,1}... | collective-permute-start | bytes 24584 | tf_op jit(solution)/shard_map/ppermute | solution.py:759
  5.5 8.1 %collective-permute-start = (f32[16,128]{1,0:T(8,128)S(1)}, f32[16,128]{1,0:T(8,128)S(1)}, u32[]{:S(2)}, u32[]{:S(2)}) collective-permute-start(f32[16,128]{1,0:T(8,128)S(1)} %get-tuple-element.45.yhi.yhi_in), channel_id=1, source_target_pairs={{0,2},{2,4},{4,6},{6,8},{8,10},{10,12},{12,14},{14,0},{1,3},{3,5},... | collective-permute-start | bytes 24584 | tf_op jit(solution)/shard_map/ppermute | solution.py:758
  8.5 13.7 %collective-permute-start.3 = (f32[9,16,128]{2,1,0:T(8,128)S(1)}, f32[9,16,128]{2,1,0:T(8,128)S(1)}, u32[]{:S(2)}, u32[]{:S(2)}) collective-permute-start(f32[9,16,128]{2,1,0:T(8,128)S(1)} %get-tuple-element.48), channel_id=1, source_target_pairs={{0,16},{16,32},{32,48},{48,64},{64,80},{80,96},{96,112},{112,128},... | collective-permute-start | bytes 221192 | tf_op jit(solution)/shard_map/ppermute | solution.py:747
  9.8 12.5 %collective-permute-start.4 = (f32[9,16,128]{2,1,0:T(8,128)S(1)}, f32[9,16,128]{2,1,0:T(8,128)S(1)}, u32[]{:S(2)}, u32[]{:S(2)}) collective-permute-start(f32[9,16,128]{2,1,0:T(8,128)S(1)} %get-tuple-element.49), channel_id=1, source_target_pairs={{0,240},{16,0},{32,16},{48,32},{64,48},{80,64},{96,80},{112,96},{1... | collective-permute-start | bytes 221192 | tf_op jit(solution)/shard_map/ppermute | solution.py:748
  13.6 6.1 %copy-start.4 = (f32[256]{0:T(256)S(1)}, f32[256]{0:T(256)}, u32[]{:S(2)}) copy-start(f32[256]{0:T(256)} %param.9) | copy-start | bytes 3076
  14.9 7.4 %collective-permute-start.5 = (f32[9,16,128]{2,1,0:T(8,128)S(1)}, f32[9,16,128]{2,1,0:T(8,128)S(1)}, u32[]{:S(2)}, u32[]{:S(2)}) collective-permute-start(f32[9,16,128]{2,1,0:T(8,128)S(1)} %get-tuple-element.50), channel_id=1, source_target_pairs={{0,16},{16,32},{32,48},{48,64},{64,80},{80,96},{96,112},{112,128},... | collective-permute-start | bytes 221192 | tf_op jit(solution)/shard_map/ppermute | solution.py:747
  15.0 7.3 %collective-permute-start.6 = (f32[9,16,128]{2,1,0:T(8,128)S(1)}, f32[9,16,128]{2,1,0:T(8,128)S(1)}, u32[]{:S(2)}, u32[]{:S(2)}) collective-permute-start(f32[9,16,128]{2,1,0:T(8,128)S(1)} %get-tuple-element.51), channel_id=1, source_target_pairs={{0,240},{16,0},{32,16},{48,32},{64,48},{80,64},{96,80},{112,96},{1... | collective-permute-start | bytes 221192 | tf_op jit(solution)/shard_map/ppermute | solution.py:748
  19.8 2.5 %collective-permute-start.7 = (f32[16,128]{1,0:T(8,128)S(1)}, f32[16,128]{1,0:T(8,128)S(1)}, u32[]{:S(2)}, u32[]{:S(2)}) collective-permute-start(f32[16,128]{1,0:T(8,128)S(1)} %get-tuple-element.52), channel_id=1, source_target_pairs={{0,1},{1,0},{2,3},{3,2},{4,5},{5,4},{6,7},{7,6},{8,9},{9,8},{10,11... | collective-permute-start | bytes 24584 | tf_op jit(solution)/shard_map/ppermute | solution.py:753
  19.8 0.7 %copy-start.3 = (s32[256]{0:T(256)S(1)}, s32[256]{0:T(256)}, u32[]{:S(2)}) copy-start(s32[256]{0:T(256)} %param.8) | copy-start | bytes 3076
  23.1 6.6 %collective-permute-start.10 = (f32[6,8,128]{2,1,0:T(8,128)S(1)}, f32[6,8,128]{2,1,0:T(8,128)S(1)}, u32[]{:S(2)}, u32[]{:S(2)}) collective-permute-start(f32[6,8,128]{2,1,0:T(8,128)S(1)} %get-tuple-element.59), channel_id=1, source_target_pairs={{0,1},{1,0},{2,3},{3,2},{4,5},{5,4},{6,7},{7,6},{8,9},{9,8},{10,11... | collective-permute-start | bytes 73736 | tf_op jit(solution)/shard_map/ppermute | solution.py:753
  23.5 5.2 %collective-permute-start.8 = (f32[8,128]{1,0:T(8,128)S(1)}, f32[8,128]{1,0:T(8,128)S(1)}, u32[]{:S(2)}, u32[]{:S(2)}) collective-permute-start(f32[8,128]{1,0:T(8,128)S(1)} %get-tuple-element.57), channel_id=1, source_target_pairs={{0,2},{2,4},{4,6},{6,8},{8,10},{10,12},{12,14},{14,0},{1,3},{3,5},... | collective-permute-start | bytes 12296 | tf_op jit(solution)/shard_map/ppermute | solution.py:758
  25.9 3.9 %collective-permute-start.9 = (f32[8,128]{1,0:T(8,128)S(1)}, f32[8,128]{1,0:T(8,128)S(1)}, u32[]{:S(2)}, u32[]{:S(2)}) collective-permute-start(f32[8,128]{1,0:T(8,128)S(1)} %get-tuple-element.58), channel_id=1, source_target_pairs={{0,14},{2,0},{4,2},{6,4},{8,6},{10,8},{12,10},{14,12},{1,15},{3,1}... | collective-permute-start | bytes 12296 | tf_op jit(solution)/shard_map/ppermute | solution.py:759
  30.0 6.2 %collective-permute-start.11 = (f32[5,16,128]{2,1,0:T(8,128)S(1)}, f32[5,16,128]{2,1,0:T(8,128)S(1)}, u32[]{:S(2)}, u32[]{:S(2)}) collective-permute-start(f32[5,16,128]{2,1,0:T(8,128)S(1)} %get-tuple-element.68), channel_id=1, source_target_pairs={{0,16},{16,32},{32,48},{48,64},{64,80},{80,96},{96,112},{112,128},... | collective-permute-start | bytes 122888 | tf_op jit(solution)/shard_map/ppermute | solution.py:747
  30.1 6.2 %collective-permute-start.12 = (f32[5,16,128]{2,1,0:T(8,128)S(1)}, f32[5,16,128]{2,1,0:T(8,128)S(1)}, u32[]{:S(2)}, u32[]{:S(2)}) collective-permute-start(f32[5,16,128]{2,1,0:T(8,128)S(1)} %get-tuple-element.69), channel_id=1, source_target_pairs={{0,240},{16,0},{32,16},{48,32},{64,48},{80,64},{96,80},{112,96},{1... | collective-permute-start | bytes 122888 | tf_op jit(solution)/shard_map/ppermute | solution.py:748

commit v8 on v6

--- a/solution.py
+++ b/solution.py
@@ -19,6 +19,7 @@
 NEAR = time_ratio * HALF_C
 STAY = 1.0 - 3.0 * time_ratio * signal_speed
 F32 = jnp.float32
+NARROW = 8
 
 
 def primitives(r, mx, my, mz, en, gamma):
@@ -130,13 +131,24 @@
         zs[k] = items[k]
 
 
-def still_kernel(u_ref, g_ref, s_ref, vel, heat, press, slo, shi):
+def still_kernel(u_ref, g_ref, s_ref, vel, heat, press, inner, slo, shi):
+    lane = lanes()
     for z in range(NZ):
         prim = primitives(*[u_ref[k, layer(z), :] for k in range(5)], g_ref[layer(z), :])
         for k in range(3):
             vel[k, layer(z), :] = prim[k]
         heat[layer(z), :] = prim[3]
         press[layer(z), :] = prim[4]
+        st = [u_ref[k, layer(z), :] for k in range(5)]
+        uy = prim[1]
+        squeeze = jnp.minimum(0.5 * (pltpu.roll(uy, NY - 1, 1) - pltpu.roll(uy, 1, 1)), 0.0)
+        squeeze = jnp.where((lane == 0) | (lane == NY - 1), 0.0, squeeze)
+        visc = s_ref[0, layer(z), :].astype(F32) * quad_viscosity * (1.0 + st[0])
+        fy = flux(st, 1, uy, prim[4] + visc * squeeze * squeeze)
+        for k in range(5):
+            inner[k, layer(z), :] = STAY * st[k] - time_ratio * (
+                y_next(upper_part(fy[k], st[k]), 0.0, lane) - y_prev(lower_part(fy[k], st[k]), 0.0, lane)
+            )
     for out, e, i, j, last, sign in ((shi, NX - 1, NX - 2, NX - 3, NX - 4, 1.0), (slo, 0, 1, 2, 3, -1.0)):
         for k in range(5):
             out[k] = u_ref[k, x_row(e), :]
@@ -154,12 +166,11 @@
 
 
 def side_kernel(
-    mesh, u_ref, s_ref, vel, pr, slo, shi, ylo, yhi, yl, yh, zr,
+    mesh, u_ref, s_ref, vel, pr, inner, slo, shi, ylo, yhi, yl, yh, zr,
     part, xlo, xhi, zz,
-    vz, az, bz, yr, yc,
+    vz, az, bz, yr,
 ):
     _, (myl, myh), (mzl, mzh), first = masks(mesh)
-    lane = lanes()
     for z in range(NZ):
         vz[layer(z + 1), :] = vel[2, layer(z), :]
     far = [zr[k] for k in range(8)]
@@ -172,44 +183,39 @@
         az[k, layer(NZ), :] = upper_part(fl[k], far[k]) * mzh
     vz[layer(0), :] = speed * mzl
     vz[layer(NZ + 1), :] = speed * mzh
-    low = [yl[k : k + 1] * myl for k in range(8)]
-    high = [yh[k : k + 1] * myh for k in range(8)]
-    speed = low[2] / (1.0 + low[0])
-    yr[10:11, :] = speed
-    slope = 0.5 * (ylo[2:3] / (1.0 + ylo[0:1]) - low[7])
-    fl = flux(low[:5], 1, speed, total_pressure(low[5], low[6], low[0], slope))
+    yr[...] = jnp.zeros(yr.shape, F32)
+    sides = []
+    for side, ref, mask, own, sign in ((0, yl, myl, ylo, 1.0), (1, yh, myh, yhi, -1.0)):
+        items = [ref[k : k + 1] * mask for k in range(8)]
+        sides.append(items)
+        speed = items[2] / (1.0 + items[0])
+        uy = own[2:3] / (1.0 + own[0:1])
+        slope = (sign * 0.5) * (uy - items[7])
+        fl = flux(items[:5], 1, speed, total_pressure(items[5], items[6], items[0], slope))
+        squeeze = jnp.minimum((sign * 0.5) * (own[7:8] - speed), 0.0)
+        visc = own[6:7] * quad_viscosity * (1.0 + own[0:1]) * squeeze * squeeze
+        for k in range(5):
+            at = 4 * k + side
+            yr[at : at + 1, :] = time_ratio * (sign * 0.5 * fl[k] + HALF_C * items[k])
+        yr[10 + side : 11 + side, :] = (sign * HALF_T) * visc
+        yr[18 + side : 19 + side, :] = (sign * HALF_T) * visc * uy
+    low, high = sides
+    parts = jnp.concatenate([piece.astype(F32) for piece in split3(yr[...].T)], axis=1).astype(jnp.bfloat16)
+    item = lax.bitwise_and(lax.broadcasted_iota(jnp.int32, (3 * yr.shape[0], NY), 0), yr.shape[0] - 1)
+    column = lax.broadcasted_iota(jnp.int32, (3 * yr.shape[0], NY), 1)
     for k in range(5):
-        yr[k : k + 1, :] = lower_part(fl[k], low[k])
-    speed = high[2] / (1.0 + high[0])
-    yr[11:12, :] = speed
-    slope = 0.5 * (high[7] - yhi[2:3] / (1.0 + yhi[0:1]))
-    fl = flux(high[:5], 1, speed, total_pressure(high[5], high[6], high[0], slope))
-    for k in range(5):
-        yr[5 + k : 6 + k, :] = upper_part(fl[k], high[k])
-    yr[12:16, :] = jnp.zeros((4, NY), F32)
-    yc[...] = yr[...].T
+        place = (item == 4 * k) & (column == 0) | (item == 4 * k + 1) & (column == NY - 1)
+        place = place | (item == 4 * k + 2) & (column == 1) | (item == 4 * k + 3) & (column == NY - 2)
+        spread = jnp.where(place, 1.0, 0.0).astype(jnp.bfloat16)
+        part[k] = inner[k] + jnp.dot(parts, spread, preferred_element_type=F32)
     for z in range(NZ):
         st = [u_ref[k, layer(z), :] for k in range(5)]
-        press = pr[layer(z), :]
+        squeeze = jnp.minimum(0.5 * (vz[layer(z + 2), :] - vz[layer(z), :]), 0.0)
         visc = s_ref[0, layer(z), :].astype(F32) * quad_viscosity * (1.0 + st[0])
-        uy, uz = vel[1, layer(z), :], vel[2, layer(z), :]
-
-        def col(i):
-            return yc[layer(z), i : i + 1]
-
-        def total(up, down):
-            squeeze = jnp.minimum(0.5 * (up - down), 0.0)
-            return press + visc * squeeze * squeeze
-
-        fy = flux(st, 1, uy, total(y_next(uy, col(11), lane), y_prev(uy, col(10), lane)))
-        fz = flux(st, 2, uz, total(vz[layer(z + 2), :], vz[layer(z), :]))
+        fz = flux(st, 2, vel[2, layer(z), :], pr[layer(z), :] + visc * squeeze * squeeze)
         for k in range(5):
             az[k, layer(z), :] = upper_part(fz[k], st[k])
             bz[k, layer(z + 1), :] = lower_part(fz[k], st[k])
-            part[k, layer(z), :] = STAY * st[k] - time_ratio * (
-                y_next(upper_part(fy[k], st[k]), col(5 + k), lane)
-                - y_prev(lower_part(fy[k], st[k]), col(k), lane)
-            )
     for z in range(NZ):
         for k in range(5):
             part[k, layer(z), :] = part[k, layer(z), :] - time_ratio * (
@@ -667,7 +673,7 @@
     miss = miss + jnp.sum(v_ref[...], axis=1, keepdims=True)
     row = jnp.where(lane == 0, total, jnp.where(lane == 1, miss, 0.0))
     for i in range(row_ref.shape[0] // NX):
-        row_ref[layer(i), :] = row
+        row_ref[layer(i), :] = row[:, :NARROW]
 
 
 def scale_kernel(devices, count, grad_ref, rows_ref, out_ref, misfit_ref):
@@ -781,16 +787,16 @@
         [],
     )(probes.reshape(1, -1), observed.reshape(1, -1))
     grid = rows_of(CELLS, NY)
-    vel, heat, press, slo, shi = call(still_kernel, [rows_of(3, CELLS, NY), grid, grid] + x_slabs(16), [])(
+    vel, heat, press, inner, slo, shi = call(still_kernel, [rows_of(3, CELLS, NY), grid, grid, rows_of(5, CELLS, NY)] + x_slabs(16), [])(
         state, gamma, sw
     )
     part, xlo, xhi, zz = call(
         bind(side_kernel, sizes),
         [rows_of(5, CELLS, NY)] + x_slabs(18) + [pair],
         [
-            vmem(tall, NY), vmem(5, tall, NY), vmem(5, tall, NY), vmem(16, NY), vmem(CELLS, 16),
+            vmem(tall, NY), vmem(5, tall, NY), vmem(5, tall, NY), vmem(32, NY),
         ],
-    )(state, sw, vel, press, slo, shi, *sent_y, *got_yz)
+    )(state, sw, vel, press, inner, slo, shi, *sent_y, *got_yz)
     got_x = exchange_x(sizes, xlo, xhi)
     zz = exchange_z(sizes, zz)
     state_1, lam_2, coef, coef_halo, mis, beside, *sent, yown = call(
@@ -814,7 +820,7 @@
     devices = sizes["gx"] * sizes["gy"] * sizes["gz"]
     gradient, rows = call(
         bind(gradient_kernel, sizes),
-        [rows_of(CELLS, NY), rows_of(devices, NY)],
+        [rows_of(CELLS, NY), rows_of(devices, NARROW)],
         [
             vmem(2, NZ * 24, NY), vmem(CELLS, NY), vmem(NZ * 24, NY), vmem(CELLS, NY),
             vmem(CELLS, 8), vmem(2, NZ * 24, NY), vmem(CELLS, NY), vmem(2, tall, NY),

time: 63.4 us -> 62.6 us (0.987)
    pallas_call x1, Pallas kernels: 1.24 us -> 0.44 us  [local(): call(bind(side_kernel, sizes), [rows_of(5, CELLS, NY)] + x_slabs(18) + [p...]
where the time goes in v8:
time: 62.6 us; the launch traced here: 62.4 us
  blocking collectives  26.5 us (42%)
  starting transfers between devices  24.7 us (39%)
  Pallas kernels  5.55 us (9%)
  waiting for transfers between devices  4.26 us (7%)
  between operations  0.71 us (1%)
  local copies, waits for them, and re-layouts  0.69 us (1%)
    all_to_all x1, blocking collectives, local(): rows = lax.all_to_all(rows, ('gx', 'gy', 'gz'), 0, 0, tiled=True)  26.5 us
    ppermute x2, starting transfers between devices, exchange_x(): lax.ppermute(xlo, 'gx', ring(sizes, 'gx', -1))  9.14 us
    ppermute x2, starting transfers between devices, exchange_yz(): yl = lax.ppermute(yhi, 'gy', ring(sizes, 'gy', 1))  6.15 us
    ppermute x3, starting transfers between devices, exchange_z(): return lax.ppermute(zs, 'gz', ring(sizes, 'gz', 1))  4.06 us
    ppermute x2, starting transfers between devices, exchange_yz(): yh = lax.ppermute(ylo, 'gy', ring(sizes, 'gy', -1))  3.96 us
    ppermute x2, waiting for transfers between devices, exchange_yz(): yl = lax.ppermute(yhi, 'gy', ring(sizes, 'gy', 1))  1.66 us
    ppermute x2, starting transfers between devices, exchange_x(): lax.ppermute(xhi, 'gx', ring(sizes, 'gx', 1))  1.37 us
    pallas_call x1, Pallas kernels, local(): call(bind(prep_kernel, sizes), [pair, pair, rows_of(11, NX, NY)], [vmem(C...  1.34 us
  transfers between devices with their start and end apart: 11, of which 6 were waited for; matrix products, arithmetic and copies ran while one was open for 0% of the time, Pallas kernels for 2%

profile of v8, /device:TPU:1, one launch (start us, length us, event | category | flops | bytes accessed | tf_op | source)
XLA Modules:
  0.0 62.4 jit_solution(342670446590901112)
XLA Ops:
  0.7 1.3 %shard_map.69 = (f32[16,128]{1,0:T(8,128)S(1)}, f32[16,128]{1,0:T(8,128)S(1)}, f32[11,8,128]{2,1,0:T(8,128)S(1)}) custom-call(f32[5,128,128]{2,1,0:T(8,128)} %bitcast.11, f32[128,128]{1,0:T(8,128)} %bitcast.19, s32[2,128,128]{2,1,0:T(8,128)} %bitcast.15), custom_call_target="tpu_custom_call" | custom-call | flops 100000 | bytes 100000 | tf_op jit(solution)/shard_map/pallas_call | solution.py:780
  2.0 2.6 %collective-permute-start.2 = (f32[11,8,128]{2,1,0:T(8,128)S(1)}, f32[11,8,128]{2,1,0:T(8,128)S(1)}, u32[]{:S(2)}, u32[]{:S(2)}) collective-permute-start(f32[11,8,128]{2,1,0:T(8,128)S(1)} %get-tuple-element.46), channel_id=1, source_target_pairs={{0,1},{1,0},{2,3},{3,2},{4,5},{5,4},{6,7},{7,6},{8,9},{9,8},{10,11... | collective-permute-start | bytes 135176 | tf_op jit(solution)/shard_map/ppermute | solution.py:758
  4.6 1.0 %collective-permute-start.1 = (f32[16,128]{1,0:T(8,128)S(1)}, f32[16,128]{1,0:T(8,128)S(1)}, u32[]{:S(2)}, u32[]{:S(2)}) collective-permute-start(f32[16,128]{1,0:T(8,128)S(1)} %get-tuple-element.44.ylo.ylo_in), channel_id=1, source_target_pairs={{0,14},{2,0},{4,2},{6,4},{8,6},{10,8},{12,10},{14,12},{1,15},{3,1}... | collective-permute-start | bytes 24584 | tf_op jit(solution)/shard_map/ppermute | solution.py:764
  5.5 2.9 %collective-permute-start = (f32[16,128]{1,0:T(8,128)S(1)}, f32[16,128]{1,0:T(8,128)S(1)}, u32[]{:S(2)}, u32[]{:S(2)}) collective-permute-start(f32[16,128]{1,0:T(8,128)S(1)} %get-tuple-element.45.yhi.yhi_in), channel_id=1, source_target_pairs={{0,2},{2,4},{4,6},{6,8},{8,10},{10,12},{12,14},{14,0},{1,3},{3,5},... | collective-permute-start | bytes 24584 | tf_op jit(solution)/shard_map/ppermute | solution.py:763
  8.4 0.5 shard_map.68
  8.9 0.8 %collective-permute-done.1.yh = f32[16,128]{1,0:T(8,128)S(1)} collective-permute-done((f32[16,128]{1,0:T(8,128)S(1)}, f32[16,128]{1,0:T(8,128)S(1)}, u32[]{:S(2)}, u32[]{:S(2)}) %collective-permute-start.1) | collective-permute-done | bytes 8224 | tf_op jit(solution)/shard_map/ppermute | solution.py:764
  9.7 1.0 %collective-permute-done.yl = f32[16,128]{1,0:T(8,128)S(1)} collective-permute-done((f32[16,128]{1,0:T(8,128)S(1)}, f32[16,128]{1,0:T(8,128)S(1)}, u32[]{:S(2)}, u32[]{:S(2)}) %collective-permute-start) | collective-permute-done | bytes 8224 | tf_op jit(solution)/shard_map/ppermute | solution.py:763
  10.7 0.4 shard_map.70
  11.2 1.3 %collective-permute-start.3 = (f32[18,16,128]{2,1,0:T(8,128)S(1)}, f32[18,16,128]{2,1,0:T(8,128)S(1)}, u32[]{:S(2)}, u32[]{:S(2)}) collective-permute-start(f32[18,16,128]{2,1,0:T(8,128)S(1)} %get-tuple-element.48), channel_id=1, source_target_pairs={{0,16},{16,32},{32,48},{48,64},{64,80},{80,96},{96,112},{112,128},... | collective-permute-start | bytes 442376 | tf_op jit(solution)/shard_map/ppermute | solution.py:752
  12.5 3.8 %collective-permute-start.4 = (f32[18,16,128]{2,1,0:T(8,128)S(1)}, f32[18,16,128]{2,1,0:T(8,128)S(1)}, u32[]{:S(2)}, u32[]{:S(2)}) collective-permute-start(f32[18,16,128]{2,1,0:T(8,128)S(1)} %get-tuple-element.49), channel_id=1, source_target_pairs={{0,240},{16,0},{32,16},{48,32},{64,48},{80,64},{96,80},{112,96},{1... | collective-permute-start | bytes 442376 | tf_op jit(solution)/shard_map/ppermute | solution.py:753
  16.3 0.7 %collective-permute-start.5 = (f32[16,128]{1,0:T(8,128)S(1)}, f32[16,128]{1,0:T(8,128)S(1)}, u32[]{:S(2)}, u32[]{:S(2)}) collective-permute-start(f32[16,128]{1,0:T(8,128)S(1)} %get-tuple-element.50), channel_id=1, source_target_pairs={{0,1},{1,0},{2,3},{3,2},{4,5},{5,4},{6,7},{7,6},{8,9},{9,8},{10,11... | collective-permute-start | bytes 24584 | tf_op jit(solution)/shard_map/ppermute | solution.py:758
  17.0 0.7 %copy-done.3 = s32[256]{0:T(256)S(1)} copy-done((s32[256]{0:T(256)S(1)}, s32[256]{0:T(256)}, u32[]{:S(2)}) %copy-start.3) | copy-done | bytes 1048
  17.7 0.5 shard_map.71
  18.2 0.6 collective-permute-done.5.zz
  18.8 0.9 %shard_map.72 = (f32[5,128,128]{2,1,0:T(8,128)S(1)}, f32[2,128,128]{2,1,0:T(8,128)S(1)}, f32[128,128]{1,0:T(8,128)S(1)}, f32[2,16,128]{2,1,0:T(8,128)S(1)}, f32[...) custom-call(f32[5,128,128]{2,1,0:T(8,128)S(1)} %bitcast.14, ...), custom_call_target="tpu_custom_call" | custom-call | flops 100000 | bytes 100000 | tf_op jit(solution)/shard_map/pallas_call | solution.py:802
  19.7 0.8 %collective-permute-start.8 = (f32[6,8,128]{2,1,0:T(8,128)S(1)}, f32[6,8,128]{2,1,0:T(8,128)S(1)}, u32[]{:S(2)}, u32[]{:S(2)}) collective-permute-start(f32[6,8,128]{2,1,0:T(8,128)S(1)} %get-tuple-element.57), channel_id=1, source_target_pairs={{0,1},{1,0},{2,3},{3,2},{4,5},{5,4},{6,7},{7,6},{8,9},{9,8},{10,11... | collective-permute-start | bytes 73736 | tf_op jit(solution)/shard_map/ppermute | solution.py:758
  20.4 3.3 %collective-permute-start.6 = (f32[8,128]{1,0:T(8,128)S(1)}, f32[8,128]{1,0:T(8,128)S(1)}, u32[]{:S(2)}, u32[]{:S(2)}) collective-permute-start(f32[8,128]{1,0:T(8,128)S(1)} %get-tuple-element.55), channel_id=1, source_target_pairs={{0,2},{2,4},{4,6},{6,8},{8,10},{10,12},{12,14},{14,0},{1,3},{3,5},... | collective-permute-start | bytes 12296 | tf_op jit(solution)/shard_map/ppermute | solution.py:763
  23.7 3.0 %collective-permute-start.7 = (f32[8,128]{1,0:T(8,128)S(1)}, f32[8,128]{1,0:T(8,128)S(1)}, u32[]{:S(2)}, u32[]{:S(2)}) collective-permute-start(f32[8,128]{1,0:T(8,128)S(1)} %get-tuple-element.56), channel_id=1, source_target_pairs={{0,14},{2,0},{4,2},{6,4},{8,6},{10,8},{12,10},{14,12},{1,15},{3,1}... | collective-permute-start | bytes 12296 | tf_op jit(solution)/shard_map/ppermute | solution.py:764
  26.7 0.7 %collective-permute-done.6.yl = f32[8,128]{1,0:T(8,128)S(1)} collective-permute-done((f32[8,128]{1,0:T(8,128)S(1)}, f32[8,128]{1,0:T(8,128)S(1)}, u32[]{:S(2)}, u32[]{:S(2)}) %collective-permute-start.6) | collective-permute-done | bytes 4128 | tf_op jit(solution)/shard_map/ppermute | solution.py:763
  27.9 5.3 %collective-permute-start.10 = (f32[5,16,128]{2,1,0:T(8,128)S(1)}, f32[5,16,128]{2,1,0:T(8,128)S(1)}, u32[]{:S(2)}, u32[]{:S(2)}) collective-permute-start(f32[5,16,128]{2,1,0:T(8,128)S(1)} %get-tuple-element.67), channel_id=1, source_target_pairs={{0,240},{16,0},{32,16},{48,32},{64,48},{80,64},{96,80},{112,96},{1... | collective-permute-start | bytes 122888 | tf_op jit(solution)/shard_map/ppermute | solution.py:753
  33.6 1.0 %collective-permute-done.9.xl = f32[5,16,128]{2,1,0:T(8,128)S(1)} collective-permute-done((f32[5,16,128]{2,1,0:T(8,128)S(1)}, f32[5,16,128]{2,1,0:T(8,128)S(1)}, u32[]{:S(2)}, u32[]{:S(2)}) %collective-permute-start.9) | collective-permute-done | bytes 40992 | tf_op jit(solution)/shard_map/ppermute | solution.py:752
  34.6 0.5 shard_map.75
  35.1 26.5 %all_to_all.11 = f32[256,1,8]{2,1,0:T(1,128)S(1)} all-to-all(f32[256,1,8]{2,1,0:T(1,128)S(1)} %bitcast.24), channel_id=1, replica_groups=mesh['gx'=16,'gy'=8,'gz'=2] {'gx','gy','gz'}, dimensions={0} | all-to-all | bytes 16384 | tf_op jit(solution)/shard_map/all_to_all | solution.py:829
  61.6 0.8 %shard_map.76 = (f32[128,128]{1,0:T(8,128)}, f32[1,1]{1,0:T(1,128)}) custom-call(f32[128,128]{1,0:T(8,128)S(1)} %get-tuple-element.70.grad_ref, f32[256,8]{1,0:T(8,128)S(1)} %bitcast.23), custom_call_target="tpu_custom_call" | custom-call | tf_op jit(solution)/shard_map/pallas_call | solution.py:830
  (18 shorter events, 0.9 us)
Async XLA Ops:
  0.6 7.8 %copy-start = (f32[5,16,8,128]{3,2,1,0:T(8,128)S(1)}, f32[5,16,8,128]{3,2,1,0:T(8,128)}, u32[]{:S(2)}) copy-start(f32[5,16,8,128]{3,2,1,0:T(8,128)} %param.5) | copy-start | bytes 983044
  0.6 7.8 %copy-start.1 = (s32[2,16,8,128]{3,2,1,0:T(8,128)S(1)}, s32[2,16,8,128]{3,2,1,0:T(8,128)}, u32[]{:S(2)}) copy-start(s32[2,16,8,128]{3,2,1,0:T(8,128)} %param.7) | copy-start | bytes 393220
  0.6 7.8 %copy-start.2 = (f32[16,8,128]{2,1,0:T(8,128)S(1)}, f32[16,8,128]{2,1,0:T(8,128)}, u32[]{:S(2)}) copy-start(f32[16,8,128]{2,1,0:T(8,128)} %param.6) | copy-start | bytes 196612
  2.0 8.7 %collective-permute-start.2 = (f32[11,8,128]{2,1,0:T(8,128)S(1)}, f32[11,8,128]{2,1,0:T(8,128)S(1)}, u32[]{:S(2)}, u32[]{:S(2)}) collective-permute-start(f32[11,8,128]{2,1,0:T(8,128)S(1)} %get-tuple-element.46), channel_id=1, source_target_pairs={{0,1},{1,0},{2,3},{3,2},{4,5},{5,4},{6,7},{7,6},{8,9},{9,8},{10,11... | collective-permute-start | bytes 135176 | tf_op jit(solution)/shard_map/ppermute | solution.py:758
  4.6 5.2 %collective-permute-start.1 = (f32[16,128]{1,0:T(8,128)S(1)}, f32[16,128]{1,0:T(8,128)S(1)}, u32[]{:S(2)}, u32[]{:S(2)}) collective-permute-start(f32[16,128]{1,0:T(8,128)S(1)} %get-tuple-element.44.ylo.ylo_in), channel_id=1, source_target_pairs={{0,14},{2,0},{4,2},{6,4},{8,6},{10,8},{12,10},{14,12},{1,15},{3,1}... | collective-permute-start | bytes 24584 | tf_op jit(solution)/shard_map/ppermute | solution.py:764
  5.5 5.2 %collective-permute-start = (f32[16,128]{1,0:T(8,128)S(1)}, f32[16,128]{1,0:T(8,128)S(1)}, u32[]{:S(2)}, u32[]{:S(2)}) collective-permute-start(f32[16,128]{1,0:T(8,128)S(1)} %get-tuple-element.45.yhi.yhi_in), channel_id=1, source_target_pairs={{0,2},{2,4},{4,6},{6,8},{8,10},{10,12},{12,14},{14,0},{1,3},{3,5},... | collective-permute-start | bytes 24584 | tf_op jit(solution)/shard_map/ppermute | solution.py:763
  10.7 6.3 %copy-start.4 = (f32[256]{0:T(256)S(1)}, f32[256]{0:T(256)}, u32[]{:S(2)}) copy-start(f32[256]{0:T(256)} %param.9) | copy-start | bytes 3076
  11.2 7.6 %collective-permute-start.3 = (f32[18,16,128]{2,1,0:T(8,128)S(1)}, f32[18,16,128]{2,1,0:T(8,128)S(1)}, u32[]{:S(2)}, u32[]{:S(2)}) collective-permute-start(f32[18,16,128]{2,1,0:T(8,128)S(1)} %get-tuple-element.48), channel_id=1, source_target_pairs={{0,16},{16,32},{32,48},{48,64},{64,80},{80,96},{96,112},{112,128},... | collective-permute-start | bytes 442376 | tf_op jit(solution)/shard_map/ppermute | solution.py:752
  12.5 6.3 %collective-permute-start.4 = (f32[18,16,128]{2,1,0:T(8,128)S(1)}, f32[18,16,128]{2,1,0:T(8,128)S(1)}, u32[]{:S(2)}, u32[]{:S(2)}) collective-permute-start(f32[18,16,128]{2,1,0:T(8,128)S(1)} %get-tuple-element.49), channel_id=1, source_target_pairs={{0,240},{16,0},{32,16},{48,32},{64,48},{80,64},{96,80},{112,96},{1... | collective-permute-start | bytes 442376 | tf_op jit(solution)/shard_map/ppermute | solution.py:753
  16.3 2.5 %collective-permute-start.5 = (f32[16,128]{1,0:T(8,128)S(1)}, f32[16,128]{1,0:T(8,128)S(1)}, u32[]{:S(2)}, u32[]{:S(2)}) collective-permute-start(f32[16,128]{1,0:T(8,128)S(1)} %get-tuple-element.50), channel_id=1, source_target_pairs={{0,1},{1,0},{2,3},{3,2},{4,5},{5,4},{6,7},{7,6},{8,9},{9,8},{10,11... | collective-permute-start | bytes 24584 | tf_op jit(solution)/shard_map/ppermute | solution.py:758
  17.0 0.7 %copy-start.3 = (s32[256]{0:T(256)S(1)}, s32[256]{0:T(256)}, u32[]{:S(2)}) copy-start(s32[256]{0:T(256)} %param.8) | copy-start | bytes 3076
  19.7 8.0 %collective-permute-start.8 = (f32[6,8,128]{2,1,0:T(8,128)S(1)}, f32[6,8,128]{2,1,0:T(8,128)S(1)}, u32[]{:S(2)}, u32[]{:S(2)}) collective-permute-start(f32[6,8,128]{2,1,0:T(8,128)S(1)} %get-tuple-element.57), channel_id=1, source_target_pairs={{0,1},{1,0},{2,3},{3,2},{4,5},{5,4},{6,7},{7,6},{8,9},{9,8},{10,11... | collective-permute-start | bytes 73736 | tf_op jit(solution)/shard_map/ppermute | solution.py:758
  20.4 6.9 %collective-permute-start.6 = (f32[8,128]{1,0:T(8,128)S(1)}, f32[8,128]{1,0:T(8,128)S(1)}, u32[]{:S(2)}, u32[]{:S(2)}) collective-permute-start(f32[8,128]{1,0:T(8,128)S(1)} %get-tuple-element.55), channel_id=1, source_target_pairs={{0,2},{2,4},{4,6},{6,8},{8,10},{10,12},{12,14},{14,0},{1,3},{3,5},... | collective-permute-start | bytes 12296 | tf_op jit(solution)/shard_map/ppermute | solution.py:763
  23.7 3.9 %collective-permute-start.7 = (f32[8,128]{1,0:T(8,128)S(1)}, f32[8,128]{1,0:T(8,128)S(1)}, u32[]{:S(2)}, u32[]{:S(2)}) collective-permute-start(f32[8,128]{1,0:T(8,128)S(1)} %get-tuple-element.56), channel_id=1, source_target_pairs={{0,14},{2,0},{4,2},{6,4},{8,6},{10,8},{12,10},{14,12},{1,15},{3,1}... | collective-permute-start | bytes 12296 | tf_op jit(solution)/shard_map/ppermute | solution.py:764
  27.9 6.7 %collective-permute-start.9 = (f32[5,16,128]{2,1,0:T(8,128)S(1)}, f32[5,16,128]{2,1,0:T(8,128)S(1)}, u32[]{:S(2)}, u32[]{:S(2)}) collective-permute-start(f32[5,16,128]{2,1,0:T(8,128)S(1)} %get-tuple-element.66), channel_id=1, source_target_pairs={{0,16},{16,32},{32,48},{48,64},{64,80},{80,96},{96,112},{112,128},... | collective-permute-start | bytes 122888 | tf_op jit(solution)/shard_map/ppermute | solution.py:752
  27.9 6.6 %collective-permute-start.10 = (f32[5,16,128]{2,1,0:T(8,128)S(1)}, f32[5,16,128]{2,1,0:T(8,128)S(1)}, u32[]{:S(2)}, u32[]{:S(2)}) collective-permute-start(f32[5,16,128]{2,1,0:T(8,128)S(1)} %get-tuple-element.67), channel_id=1, source_target_pairs={{0,240},{16,0},{32,16},{48,32},{64,48},{80,64},{96,80},{112,96},{1... | collective-permute-start | bytes 122888 | tf_op jit(solution)/shard_map/ppermute | solution.py:753

commit v9 on v8

--- a/solution.py
+++ b/solution.py
@@ -505,7 +505,7 @@
         out[3:4] = ux
         out[4:5] = uy
         out[5:6] = gamma
-        out[6:8] = jnp.zeros((2, NY), F32)
+        out[6:] = jnp.zeros((out.shape[0] - 6, NY), F32)
         yown[own : own + 1] = lam_r
         yown[own + 1 : own + 2] = lam_m
     yown[4:8] = jnp.zeros((4, NY), F32)
@@ -611,7 +611,7 @@
     from_high, from_low = pltpu.roll(xh[4], NX - 1, 1) * mxh, pltpu.roll(xl[4], NY - NX + 1, 1) * mxl
     halo = []
     for side, ref, mask, sign in ((0, yl, myl, HALF_T), (1, yh, myh, -HALF_T)):
-        items = ref[...]
+        items = ref[0:8]
         up = jnp.where(at_x == NX - 1, from_high[side : side + 1], pltpu.roll(items, NY - 1, 1)[1:2])
         down = jnp.where(at_x == 0, from_low[side : side + 1], pltpu.roll(items, 1, 1)[1:2])
         d_en = HALF_T * (up - down) * items[5:6]
@@ -799,10 +799,11 @@
     )(state, sw, vel, press, inner, slo, shi, *sent_y, *got_yz)
     got_x = exchange_x(sizes, xlo, xhi)
     zz = exchange_z(sizes, zz)
+    tied = rows_of(6 * NX, NY)
     state_1, lam_2, coef, coef_halo, mis, beside, *sent, yown = call(
         bind(forward_kernel, sizes),
         [rows_of(5, CELLS, NY), rows_of(2, CELLS, NY), rows_of(CELLS, NY), rows_of(2, NZ, NY), plane]
-        + [rows_of(6, NZ, NY), plane, plane, rows_of(6, NX, NY), plane],
+        + [rows_of(6, NZ, NY), tied, tied, rows_of(6, NX, NY), plane],
         [
             vmem(5, NZ, NY), vmem(5, NZ, NY), vmem(8, NY), vmem(8, NY), vmem(2, NX, NY),
             vmem(NZ * 24, NY), vmem(5, NZ * 16, NY), vmem(5, NZ * 16, NY), vmem(2, tall, NY), vmem(2, tall, NY),

time: 62.6 us -> 63.4 us (1.013)
  waiting for transfers between devices: 4.26 us -> 5.28 us
  starting transfers between devices: 24.7 us -> 24 us
    ppermute x2, waiting for transfers between devices: 1.06 us -> 2.03 us  [exchange_yz(): yh = lax.ppermute(ylo, 'gy', ring(sizes, 'gy', -1))]
    ppermute x2, starting transfers between devices: 3.96 us -> 3.14 us  [exchange_yz(): yh = lax.ppermute(ylo, 'gy', ring(sizes, 'gy', -1))]
    ppermute x3, waiting for transfers between devices: 0.57 us -> 1.27 us  [exchange_z(): return lax.ppermute(zs, 'gz', ring(sizes, 'gz', 1))]
    ppermute x2, starting transfers between devices: 6.15 us -> 6.83 us  [exchange_yz(): yl = lax.ppermute(yhi, 'gy', ring(sizes, 'gy', 1))]
    ppermute x2, waiting for transfers between devices: 1.66 us -> 1.01 us  [exchange_yz(): yl = lax.ppermute(yhi, 'gy', ring(sizes, 'gy', 1))]
where the time goes in v9:
time: 63.4 us; the launch traced here: 63.2 us
  blocking collectives  27 us (43%)
  starting transfers between devices  24 us (38%)
  Pallas kernels  5.54 us (9%)
  waiting for transfers between devices  5.28 us (8%)
  between operations  0.71 us (1%)
  local copies, waits for them, and re-layouts  0.69 us (1%)
    all_to_all x1, blocking collectives, local(): rows = lax.all_to_all(rows, ('gx', 'gy', 'gz'), 0, 0, tiled=True)  27 us
    ppermute x2, starting transfers between devices, exchange_x(): lax.ppermute(xlo, 'gx', ring(sizes, 'gx', -1))  8.67 us
    ppermute x2, starting transfers between devices, exchange_yz(): yl = lax.ppermute(yhi, 'gy', ring(sizes, 'gy', 1))  6.83 us
    ppermute x3, starting transfers between devices, exchange_z(): return lax.ppermute(zs, 'gz', ring(sizes, 'gz', 1))  4.01 us
    ppermute x2, starting transfers between devices, exchange_yz(): yh = lax.ppermute(ylo, 'gy', ring(sizes, 'gy', -1))  3.14 us
    ppermute x2, waiting for transfers between devices, exchange_yz(): yh = lax.ppermute(ylo, 'gy', ring(sizes, 'gy', -1))  2.03 us
    ppermute x2, starting transfers between devices, exchange_x(): lax.ppermute(xhi, 'gx', ring(sizes, 'gx', 1))  1.37 us
    pallas_call x1, Pallas kernels, local(): call(bind(prep_kernel, sizes), [pair, pair, rows_of(11, NX, NY)], [vmem(C...  1.34 us
  transfers between devices with their start and end apart: 11, of which 6 were waited for; matrix products, arithmetic and copies ran while one was open for 0% of the time, Pallas kernels for 2%

profile of v9, /device:TPU:1, one launch (start us, length us, event | category | flops | bytes accessed | tf_op | source)
XLA Modules:
  0.0 63.2 jit_solution(5016692245006619369)
XLA Ops:
  0.7 1.3 %shard_map.69 = (f32[16,128]{1,0:T(8,128)S(1)}, f32[16,128]{1,0:T(8,128)S(1)}, f32[11,8,128]{2,1,0:T(8,128)S(1)}) custom-call(f32[5,128,128]{2,1,0:T(8,128)} %bitcast.11, f32[128,128]{1,0:T(8,128)} %bitcast.19, s32[2,128,128]{2,1,0:T(8,128)} %bitcast.15), custom_call_target="tpu_custom_call" | custom-call | flops 100000 | bytes 100000 | tf_op jit(solution)/shard_map/pallas_call | solution.py:780
  2.0 2.6 %collective-permute-start.2 = (f32[11,8,128]{2,1,0:T(8,128)S(1)}, f32[11,8,128]{2,1,0:T(8,128)S(1)}, u32[]{:S(2)}, u32[]{:S(2)}) collective-permute-start(f32[11,8,128]{2,1,0:T(8,128)S(1)} %get-tuple-element.46), channel_id=1, source_target_pairs={{0,1},{1,0},{2,3},{3,2},{4,5},{5,4},{6,7},{7,6},{8,9},{9,8},{10,11... | collective-permute-start | bytes 135176 | tf_op jit(solution)/shard_map/ppermute | solution.py:758
  4.6 1.0 %collective-permute-start.1 = (f32[16,128]{1,0:T(8,128)S(1)}, f32[16,128]{1,0:T(8,128)S(1)}, u32[]{:S(2)}, u32[]{:S(2)}) collective-permute-start(f32[16,128]{1,0:T(8,128)S(1)} %get-tuple-element.44.ylo.ylo_in), channel_id=1, source_target_pairs={{0,14},{2,0},{4,2},{6,4},{8,6},{10,8},{12,10},{14,12},{1,15},{3,1}... | collective-permute-start | bytes 24584 | tf_op jit(solution)/shard_map/ppermute | solution.py:764
  5.5 2.9 %collective-permute-start = (f32[16,128]{1,0:T(8,128)S(1)}, f32[16,128]{1,0:T(8,128)S(1)}, u32[]{:S(2)}, u32[]{:S(2)}) collective-permute-start(f32[16,128]{1,0:T(8,128)S(1)} %get-tuple-element.45.yhi.yhi_in), channel_id=1, source_target_pairs={{0,2},{2,4},{4,6},{6,8},{8,10},{10,12},{12,14},{14,0},{1,3},{3,5},... | collective-permute-start | bytes 24584 | tf_op jit(solution)/shard_map/ppermute | solution.py:763
  8.4 0.5 shard_map.68
  8.9 0.8 %collective-permute-done.1.yh = f32[16,128]{1,0:T(8,128)S(1)} collective-permute-done((f32[16,128]{1,0:T(8,128)S(1)}, f32[16,128]{1,0:T(8,128)S(1)}, u32[]{:S(2)}, u32[]{:S(2)}) %collective-permute-start.1) | collective-permute-done | bytes 8224 | tf_op jit(solution)/shard_map/ppermute | solution.py:764
  9.7 1.0 %collective-permute-done.yl = f32[16,128]{1,0:T(8,128)S(1)} collective-permute-done((f32[16,128]{1,0:T(8,128)S(1)}, f32[16,128]{1,0:T(8,128)S(1)}, u32[]{:S(2)}, u32[]{:S(2)}) %collective-permute-start) | collective-permute-done | bytes 8224 | tf_op jit(solution)/shard_map/ppermute | solution.py:763
  11.2 1.3 %collective-permute-start.3 = (f32[18,16,128]{2,1,0:T(8,128)S(1)}, f32[18,16,128]{2,1,0:T(8,128)S(1)}, u32[]{:S(2)}, u32[]{:S(2)}) collective-permute-start(f32[18,16,128]{2,1,0:T(8,128)S(1)} %get-tuple-element.48), channel_id=1, source_target_pairs={{0,16},{16,32},{32,48},{48,64},{64,80},{80,96},{96,112},{112,128},... | collective-permute-start | bytes 442376 | tf_op jit(solution)/shard_map/ppermute | solution.py:752
  12.5 3.8 %collective-permute-start.4 = (f32[18,16,128]{2,1,0:T(8,128)S(1)}, f32[18,16,128]{2,1,0:T(8,128)S(1)}, u32[]{:S(2)}, u32[]{:S(2)}) collective-permute-start(f32[18,16,128]{2,1,0:T(8,128)S(1)} %get-tuple-element.49), channel_id=1, source_target_pairs={{0,240},{16,0},{32,16},{48,32},{64,48},{80,64},{96,80},{112,96},{1... | collective-permute-start | bytes 442376 | tf_op jit(solution)/shard_map/ppermute | solution.py:753
  16.3 0.7 %collective-permute-start.5 = (f32[16,128]{1,0:T(8,128)S(1)}, f32[16,128]{1,0:T(8,128)S(1)}, u32[]{:S(2)}, u32[]{:S(2)}) collective-permute-start(f32[16,128]{1,0:T(8,128)S(1)} %get-tuple-element.50), channel_id=1, source_target_pairs={{0,1},{1,0},{2,3},{3,2},{4,5},{5,4},{6,7},{7,6},{8,9},{9,8},{10,11... | collective-permute-start | bytes 24584 | tf_op jit(solution)/shard_map/ppermute | solution.py:758
  17.0 0.7 %copy-done.3 = s32[256]{0:T(256)S(1)} copy-done((s32[256]{0:T(256)S(1)}, s32[256]{0:T(256)}, u32[]{:S(2)}) %copy-start.3) | copy-done | bytes 1048
  17.7 0.5 shard_map.71
  18.2 0.6 collective-permute-done.5.zz
  18.8 0.9 %shard_map.72 = (f32[5,128,128]{2,1,0:T(8,128)S(1)}, f32[2,128,128]{2,1,0:T(8,128)S(1)}, f32[128,128]{1,0:T(8,128)S(1)}, f32[2,16,128]{2,1,0:T(8,128)S(1)}, f32[...) custom-call(f32[5,128,128]{2,1,0:T(8,128)S(1)} %bitcast.14, ...), custom_call_target="tpu_custom_call" | custom-call | flops 100000 | bytes 100000 | tf_op jit(solution)/shard_map/pallas_call | solution.py:803
  19.7 4.0 %collective-permute-start.6 = (f32[48,128]{1,0:T(8,128)S(1)}, f32[48,128]{1,0:T(8,128)S(1)}, u32[]{:S(2)}, u32[]{:S(2)}) collective-permute-start(f32[48,128]{1,0:T(8,128)S(1)} %get-tuple-element.55), channel_id=1, source_target_pairs={{0,2},{2,4},{4,6},{6,8},{8,10},{10,12},{12,14},{14,0},{1,3},{3,5},... | collective-permute-start | bytes 73736 | tf_op jit(solution)/shard_map/ppermute | solution.py:763
  23.6 2.2 %collective-permute-start.7 = (f32[48,128]{1,0:T(8,128)S(1)}, f32[48,128]{1,0:T(8,128)S(1)}, u32[]{:S(2)}, u32[]{:S(2)}) collective-permute-start(f32[48,128]{1,0:T(8,128)S(1)} %get-tuple-element.56), channel_id=1, source_target_pairs={{0,14},{2,0},{4,2},{6,4},{8,6},{10,8},{12,10},{14,12},{1,15},{3,1}... | collective-permute-start | bytes 73736 | tf_op jit(solution)/shard_map/ppermute | solution.py:764
  25.8 0.7 %collective-permute-start.8 = (f32[6,8,128]{2,1,0:T(8,128)S(1)}, f32[6,8,128]{2,1,0:T(8,128)S(1)}, u32[]{:S(2)}, u32[]{:S(2)}) collective-permute-start(f32[6,8,128]{2,1,0:T(8,128)S(1)} %get-tuple-element.57), channel_id=1, source_target_pairs={{0,1},{1,0},{2,3},{3,2},{4,5},{5,4},{6,7},{7,6},{8,9},{9,8},{10,11... | collective-permute-start | bytes 73736 | tf_op jit(solution)/shard_map/ppermute | solution.py:758
  26.5 1.2 %collective-permute-done.7.yh = f32[48,128]{1,0:T(8,128)S(1)} collective-permute-done((f32[48,128]{1,0:T(8,128)S(1)}, f32[48,128]{1,0:T(8,128)S(1)}, u32[]{:S(2)}, u32[]{:S(2)}) %collective-permute-start.7) | collective-permute-done | bytes 24608 | tf_op jit(solution)/shard_map/ppermute | solution.py:764
  27.8 0.7 %collective-permute-done.8.zr = f32[6,8,128]{2,1,0:T(8,128)S(1)} collective-permute-done((f32[6,8,128]{2,1,0:T(8,128)S(1)}, f32[6,8,128]{2,1,0:T(8,128)S(1)}, u32[]{:S(2)}, u32[]{:S(2)}) %collective-permute-start.8) | collective-permute-done | bytes 24608 | tf_op jit(solution)/shard_map/ppermute | solution.py:758
  28.8 4.9 %collective-permute-start.10 = (f32[5,16,128]{2,1,0:T(8,128)S(1)}, f32[5,16,128]{2,1,0:T(8,128)S(1)}, u32[]{:S(2)}, u32[]{:S(2)}) collective-permute-start(f32[5,16,128]{2,1,0:T(8,128)S(1)} %get-tuple-element.67), channel_id=1, source_target_pairs={{0,240},{16,0},{32,16},{48,32},{64,48},{80,64},{96,80},{112,96},{1... | collective-permute-start | bytes 122888 | tf_op jit(solution)/shard_map/ppermute | solution.py:753
  34.0 1.0 %collective-permute-done.9.xl = f32[5,16,128]{2,1,0:T(8,128)S(1)} collective-permute-done((f32[5,16,128]{2,1,0:T(8,128)S(1)}, f32[5,16,128]{2,1,0:T(8,128)S(1)}, u32[]{:S(2)}, u32[]{:S(2)}) %collective-permute-start.9) | collective-permute-done | bytes 40992 | tf_op jit(solution)/shard_map/ppermute | solution.py:752
  34.9 0.5 shard_map.75
  35.5 27.0 %all_to_all.11 = f32[256,1,8]{2,1,0:T(1,128)S(1)} all-to-all(f32[256,1,8]{2,1,0:T(1,128)S(1)} %bitcast.24), channel_id=1, replica_groups=mesh['gx'=16,'gy'=8,'gz'=2] {'gx','gy','gz'}, dimensions={0} | all-to-all | bytes 16384 | tf_op jit(solution)/shard_map/all_to_all | solution.py:830
  62.5 0.8 %shard_map.76 = (f32[128,128]{1,0:T(8,128)}, f32[1,1]{1,0:T(1,128)}) custom-call(f32[128,128]{1,0:T(8,128)S(1)} %get-tuple-element.70.grad_ref, f32[256,8]{1,0:T(8,128)S(1)} %bitcast.23), custom_call_target="tpu_custom_call" | custom-call | tf_op jit(solution)/shard_map/pallas_call | solution.py:831
  (18 shorter events, 1.1 us)
Async XLA Ops:
  0.6 7.8 %copy-start = (f32[5,16,8,128]{3,2,1,0:T(8,128)S(1)}, f32[5,16,8,128]{3,2,1,0:T(8,128)}, u32[]{:S(2)}) copy-start(f32[5,16,8,128]{3,2,1,0:T(8,128)} %param.5) | copy-start | bytes 983044
  0.6 7.8 %copy-start.1 = (s32[2,16,8,128]{3,2,1,0:T(8,128)S(1)}, s32[2,16,8,128]{3,2,1,0:T(8,128)}, u32[]{:S(2)}) copy-start(s32[2,16,8,128]{3,2,1,0:T(8,128)} %param.7) | copy-start | bytes 393220
  0.6 7.8 %copy-start.2 = (f32[16,8,128]{2,1,0:T(8,128)S(1)}, f32[16,8,128]{2,1,0:T(8,128)}, u32[]{:S(2)}) copy-start(f32[16,8,128]{2,1,0:T(8,128)} %param.6) | copy-start | bytes 196612
  2.0 8.7 %collective-permute-start.2 = (f32[11,8,128]{2,1,0:T(8,128)S(1)}, f32[11,8,128]{2,1,0:T(8,128)S(1)}, u32[]{:S(2)}, u32[]{:S(2)}) collective-permute-start(f32[11,8,128]{2,1,0:T(8,128)S(1)} %get-tuple-element.46), channel_id=1, source_target_pairs={{0,1},{1,0},{2,3},{3,2},{4,5},{5,4},{6,7},{7,6},{8,9},{9,8},{10,11... | collective-permute-start | bytes 135176 | tf_op jit(solution)/shard_map/ppermute | solution.py:758
  4.6 5.2 %collective-permute-start.1 = (f32[16,128]{1,0:T(8,128)S(1)}, f32[16,128]{1,0:T(8,128)S(1)}, u32[]{:S(2)}, u32[]{:S(2)}) collective-permute-start(f32[16,128]{1,0:T(8,128)S(1)} %get-tuple-element.44.ylo.ylo_in), channel_id=1, source_target_pairs={{0,14},{2,0},{4,2},{6,4},{8,6},{10,8},{12,10},{14,12},{1,15},{3,1}... | collective-permute-start | bytes 24584 | tf_op jit(solution)/shard_map/ppermute | solution.py:764
  5.5 5.2 %collective-permute-start = (f32[16,128]{1,0:T(8,128)S(1)}, f32[16,128]{1,0:T(8,128)S(1)}, u32[]{:S(2)}, u32[]{:S(2)}) collective-permute-start(f32[16,128]{1,0:T(8,128)S(1)} %get-tuple-element.45.yhi.yhi_in), channel_id=1, source_target_pairs={{0,2},{2,4},{4,6},{6,8},{8,10},{10,12},{12,14},{14,0},{1,3},{3,5},... | collective-permute-start | bytes 24584 | tf_op jit(solution)/shard_map/ppermute | solution.py:763
  10.7 6.3 %copy-start.4 = (f32[256]{0:T(256)S(1)}, f32[256]{0:T(256)}, u32[]{:S(2)}) copy-start(f32[256]{0:T(256)} %param.9) | copy-start | bytes 3076
  11.2 7.6 %collective-permute-start.3 = (f32[18,16,128]{2,1,0:T(8,128)S(1)}, f32[18,16,128]{2,1,0:T(8,128)S(1)}, u32[]{:S(2)}, u32[]{:S(2)}) collective-permute-start(f32[18,16,128]{2,1,0:T(8,128)S(1)} %get-tuple-element.48), channel_id=1, source_target_pairs={{0,16},{16,32},{32,48},{48,64},{64,80},{80,96},{96,112},{112,128},... | collective-permute-start | bytes 442376 | tf_op jit(solution)/shard_map/ppermute | solution.py:752
  12.5 6.3 %collective-permute-start.4 = (f32[18,16,128]{2,1,0:T(8,128)S(1)}, f32[18,16,128]{2,1,0:T(8,128)S(1)}, u32[]{:S(2)}, u32[]{:S(2)}) collective-permute-start(f32[18,16,128]{2,1,0:T(8,128)S(1)} %get-tuple-element.49), channel_id=1, source_target_pairs={{0,240},{16,0},{32,16},{48,32},{64,48},{80,64},{96,80},{112,96},{1... | collective-permute-start | bytes 442376 | tf_op jit(solution)/shard_map/ppermute | solution.py:753
  16.3 2.5 %collective-permute-start.5 = (f32[16,128]{1,0:T(8,128)S(1)}, f32[16,128]{1,0:T(8,128)S(1)}, u32[]{:S(2)}, u32[]{:S(2)}) collective-permute-start(f32[16,128]{1,0:T(8,128)S(1)} %get-tuple-element.50), channel_id=1, source_target_pairs={{0,1},{1,0},{2,3},{3,2},{4,5},{5,4},{6,7},{7,6},{8,9},{9,8},{10,11... | collective-permute-start | bytes 24584 | tf_op jit(solution)/shard_map/ppermute | solution.py:758
  17.0 0.7 %copy-start.3 = (s32[256]{0:T(256)S(1)}, s32[256]{0:T(256)}, u32[]{:S(2)}) copy-start(s32[256]{0:T(256)} %param.8) | copy-start | bytes 3076
  19.7 6.9 %collective-permute-start.6 = (f32[48,128]{1,0:T(8,128)S(1)}, f32[48,128]{1,0:T(8,128)S(1)}, u32[]{:S(2)}, u32[]{:S(2)}) collective-permute-start(f32[48,128]{1,0:T(8,128)S(1)} %get-tuple-element.55), channel_id=1, source_target_pairs={{0,2},{2,4},{4,6},{6,8},{8,10},{10,12},{12,14},{14,0},{1,3},{3,5},... | collective-permute-start | bytes 73736 | tf_op jit(solution)/shard_map/ppermute | solution.py:763
  23.6 4.2 %collective-permute-start.7 = (f32[48,128]{1,0:T(8,128)S(1)}, f32[48,128]{1,0:T(8,128)S(1)}, u32[]{:S(2)}, u32[]{:S(2)}) collective-permute-start(f32[48,128]{1,0:T(8,128)S(1)} %get-tuple-element.56), channel_id=1, source_target_pairs={{0,14},{2,0},{4,2},{6,4},{8,6},{10,8},{12,10},{14,12},{1,15},{3,1}... | collective-permute-start | bytes 73736 | tf_op jit(solution)/shard_map/ppermute | solution.py:764
  25.8 2.7 %collective-permute-start.8 = (f32[6,8,128]{2,1,0:T(8,128)S(1)}, f32[6,8,128]{2,1,0:T(8,128)S(1)}, u32[]{:S(2)}, u32[]{:S(2)}) collective-permute-start(f32[6,8,128]{2,1,0:T(8,128)S(1)} %get-tuple-element.57), channel_id=1, source_target_pairs={{0,1},{1,0},{2,3},{3,2},{4,5},{5,4},{6,7},{7,6},{8,9},{9,8},{10,11... | collective-permute-start | bytes 73736 | tf_op jit(solution)/shard_map/ppermute | solution.py:758
  28.7 6.3 %collective-permute-start.9 = (f32[5,16,128]{2,1,0:T(8,128)S(1)}, f32[5,16,128]{2,1,0:T(8,128)S(1)}, u32[]{:S(2)}, u32[]{:S(2)}) collective-permute-start(f32[5,16,128]{2,1,0:T(8,128)S(1)} %get-tuple-element.66), channel_id=1, source_target_pairs={{0,16},{16,32},{32,48},{48,64},{64,80},{80,96},{96,112},{112,128},... | collective-permute-start | bytes 122888 | tf_op jit(solution)/shard_map/ppermute | solution.py:752
  28.8 6.2 %collective-permute-start.10 = (f32[5,16,128]{2,1,0:T(8,128)S(1)}, f32[5,16,128]{2,1,0:T(8,128)S(1)}, u32[]{:S(2)}, u32[]{:S(2)}) collective-permute-start(f32[5,16,128]{2,1,0:T(8,128)S(1)} %get-tuple-element.67), channel_id=1, source_target_pairs={{0,240},{16,0},{32,16},{48,32},{64,48},{80,64},{96,80},{112,96},{1... | collective-permute-start | bytes 122888 | tf_op jit(solution)/shard_map/ppermute | solution.py:753

commit v10 on v8

--- a/solution.py
+++ b/solution.py
@@ -777,8 +777,17 @@
 
     pair = rows_of(16, NY)
     tall = (NZ + 2) * NX
-    *sent_y, sent_z = call(
-        bind(prep_kernel, sizes), [pair, pair, rows_of(11, NX, NY)], [vmem(CELLS, NY)], LARGE
+    *sent_y, sent_z = pl.pallas_call(
+        bind(prep_kernel, sizes),
+        out_shape=[pair, pair, rows_of(11, NX, NY)],
+        grid=(1,),
+        in_specs=[
+            pl.BlockSpec((5, CELLS, NY), lambda i: (0, 0, 0)),
+            pl.BlockSpec((CELLS, NY), lambda i: (0, 0)),
+            pl.BlockSpec((1, CELLS, NY), lambda i: (0, 0, 0)),
+        ],
+        scratch_shapes=[vmem(CELLS, NY)],
+        compiler_params=LARGE,
     )(state, gamma, sw)
     got_yz = exchange_yz(sizes, *sent_y, sent_z)
     hits, mean, spread = call(

time: 62.6 us -> 62.5 us (level)
  no operation moved by 1% of the time
where the time goes in v10:
time: 62.5 us; the launch traced here: 62.4 us
  blocking collectives  26.5 us (42%)
  starting transfers between devices  24.7 us (40%)
  Pallas kernels  5.52 us (9%)
  waiting for transfers between devices  4.26 us (7%)
  between operations  0.71 us (1%)
  local copies, waits for them, and re-layouts  0.69 us (1%)
    all_to_all x1, blocking collectives, local(): rows = lax.all_to_all(rows, ('gx', 'gy', 'gz'), 0, 0, tiled=True)  26.5 us
    ppermute x2, starting transfers between devices, exchange_x(): lax.ppermute(xlo, 'gx', ring(sizes, 'gx', -1))  9.14 us
    ppermute x2, starting transfers between devices, exchange_yz(): yl = lax.ppermute(yhi, 'gy', ring(sizes, 'gy', 1))  6.15 us
    ppermute x3, starting transfers between devices, exchange_z(): return lax.ppermute(zs, 'gz', ring(sizes, 'gz', 1))  4.06 us
    ppermute x2, starting transfers between devices, exchange_yz(): yh = lax.ppermute(ylo, 'gy', ring(sizes, 'gy', -1))  3.96 us
    ppermute x2, waiting for transfers between devices, exchange_yz(): yl = lax.ppermute(yhi, 'gy', ring(sizes, 'gy', 1))  1.66 us
    ppermute x2, starting transfers between devices, exchange_x(): lax.ppermute(xhi, 'gx', ring(sizes, 'gx', 1))  1.37 us
    pallas_call x1, Pallas kernels, local(): pl.pallas_call(bind(prep_kernel, sizes), out_shape=[pair, pair, rows_of(1...  1.31 us
  transfers between devices with their start and end apart: 11, of which 6 were waited for; matrix products, arithmetic and copies ran while one was open for 0% of the time, Pallas kernels for 2%

profile of v10, /device:TPU:1, one launch (start us, length us, event | category | flops | bytes accessed | tf_op | source)
XLA Modules:
  0.0 62.4 jit_solution(62107493614669431)
XLA Ops:
  0.7 1.3 %shard_map.69 = (f32[16,128]{1,0:T(8,128)S(1)}, f32[16,128]{1,0:T(8,128)S(1)}, f32[11,8,128]{2,1,0:T(8,128)S(1)}) custom-call(f32[5,128,128]{2,1,0:T(8,128)} %bitcast.11, f32[128,128]{1,0:T(8,128)} %bitcast.19, s32[2,128,128]{2,1,0:T(8,128)} %bitcast.15), custom_call_target="tpu_custom_call" | custom-call | tf_op jit(solution)/shard_map/pallas_call | solution.py:780
  2.0 2.6 %collective-permute-start.2 = (f32[11,8,128]{2,1,0:T(8,128)S(1)}, f32[11,8,128]{2,1,0:T(8,128)S(1)}, u32[]{:S(2)}, u32[]{:S(2)}) collective-permute-start(f32[11,8,128]{2,1,0:T(8,128)S(1)} %get-tuple-element.46), channel_id=1, source_target_pairs={{0,1},{1,0},{2,3},{3,2},{4,5},{5,4},{6,7},{7,6},{8,9},{9,8},{10,11... | collective-permute-start | bytes 135176 | tf_op jit(solution)/shard_map/ppermute | solution.py:758
  4.5 1.0 %collective-permute-start.1 = (f32[16,128]{1,0:T(8,128)S(1)}, f32[16,128]{1,0:T(8,128)S(1)}, u32[]{:S(2)}, u32[]{:S(2)}) collective-permute-start(f32[16,128]{1,0:T(8,128)S(1)} %get-tuple-element.44.ylo.ylo_in), channel_id=1, source_target_pairs={{0,14},{2,0},{4,2},{6,4},{8,6},{10,8},{12,10},{14,12},{1,15},{3,1}... | collective-permute-start | bytes 24584 | tf_op jit(solution)/shard_map/ppermute | solution.py:764
  5.5 2.9 %collective-permute-start = (f32[16,128]{1,0:T(8,128)S(1)}, f32[16,128]{1,0:T(8,128)S(1)}, u32[]{:S(2)}, u32[]{:S(2)}) collective-permute-start(f32[16,128]{1,0:T(8,128)S(1)} %get-tuple-element.45.yhi.yhi_in), channel_id=1, source_target_pairs={{0,2},{2,4},{4,6},{6,8},{8,10},{10,12},{12,14},{14,0},{1,3},{3,5},... | collective-permute-start | bytes 24584 | tf_op jit(solution)/shard_map/ppermute | solution.py:763
  8.4 0.5 shard_map.68
  8.9 0.8 %collective-permute-done.1.yh = f32[16,128]{1,0:T(8,128)S(1)} collective-permute-done((f32[16,128]{1,0:T(8,128)S(1)}, f32[16,128]{1,0:T(8,128)S(1)}, u32[]{:S(2)}, u32[]{:S(2)}) %collective-permute-start.1) | collective-permute-done | bytes 8224 | tf_op jit(solution)/shard_map/ppermute | solution.py:764
  9.7 1.0 %collective-permute-done.yl = f32[16,128]{1,0:T(8,128)S(1)} collective-permute-done((f32[16,128]{1,0:T(8,128)S(1)}, f32[16,128]{1,0:T(8,128)S(1)}, u32[]{:S(2)}, u32[]{:S(2)}) %collective-permute-start) | collective-permute-done | bytes 8224 | tf_op jit(solution)/shard_map/ppermute | solution.py:763
  10.7 0.4 shard_map.70
  11.2 1.3 %collective-permute-start.3 = (f32[18,16,128]{2,1,0:T(8,128)S(1)}, f32[18,16,128]{2,1,0:T(8,128)S(1)}, u32[]{:S(2)}, u32[]{:S(2)}) collective-permute-start(f32[18,16,128]{2,1,0:T(8,128)S(1)} %get-tuple-element.48), channel_id=1, source_target_pairs={{0,16},{16,32},{32,48},{48,64},{64,80},{80,96},{96,112},{112,128},... | collective-permute-start | bytes 442376 | tf_op jit(solution)/shard_map/ppermute | solution.py:752
  12.4 3.8 %collective-permute-start.4 = (f32[18,16,128]{2,1,0:T(8,128)S(1)}, f32[18,16,128]{2,1,0:T(8,128)S(1)}, u32[]{:S(2)}, u32[]{:S(2)}) collective-permute-start(f32[18,16,128]{2,1,0:T(8,128)S(1)} %get-tuple-element.49), channel_id=1, source_target_pairs={{0,240},{16,0},{32,16},{48,32},{64,48},{80,64},{96,80},{112,96},{1... | collective-permute-start | bytes 442376 | tf_op jit(solution)/shard_map/ppermute | solution.py:753
  16.3 0.7 %collective-permute-start.5 = (f32[16,128]{1,0:T(8,128)S(1)}, f32[16,128]{1,0:T(8,128)S(1)}, u32[]{:S(2)}, u32[]{:S(2)}) collective-permute-start(f32[16,128]{1,0:T(8,128)S(1)} %get-tuple-element.50), channel_id=1, source_target_pairs={{0,1},{1,0},{2,3},{3,2},{4,5},{5,4},{6,7},{7,6},{8,9},{9,8},{10,11... | collective-permute-start | bytes 24584 | tf_op jit(solution)/shard_map/ppermute | solution.py:758
  17.0 0.7 %copy-done.3 = s32[256]{0:T(256)S(1)} copy-done((s32[256]{0:T(256)S(1)}, s32[256]{0:T(256)}, u32[]{:S(2)}) %copy-start.3) | copy-done | bytes 1048
  17.7 0.5 shard_map.71
  18.2 0.6 collective-permute-done.5.zz
  18.8 0.9 %shard_map.72 = (f32[5,128,128]{2,1,0:T(8,128)S(1)}, f32[2,128,128]{2,1,0:T(8,128)S(1)}, f32[128,128]{1,0:T(8,128)S(1)}, f32[2,16,128]{2,1,0:T(8,128)S(1)}, f32[...) custom-call(f32[5,128,128]{2,1,0:T(8,128)S(1)} %bitcast.14, ...), custom_call_target="tpu_custom_call" | custom-call | flops 100000 | bytes 100000 | tf_op jit(solution)/shard_map/pallas_call | solution.py:811
  19.6 0.8 %collective-permute-start.8 = (f32[6,8,128]{2,1,0:T(8,128)S(1)}, f32[6,8,128]{2,1,0:T(8,128)S(1)}, u32[]{:S(2)}, u32[]{:S(2)}) collective-permute-start(f32[6,8,128]{2,1,0:T(8,128)S(1)} %get-tuple-element.57), channel_id=1, source_target_pairs={{0,1},{1,0},{2,3},{3,2},{4,5},{5,4},{6,7},{7,6},{8,9},{9,8},{10,11... | collective-permute-start | bytes 73736 | tf_op jit(solution)/shard_map/ppermute | solution.py:758
  20.4 3.3 %collective-permute-start.6 = (f32[8,128]{1,0:T(8,128)S(1)}, f32[8,128]{1,0:T(8,128)S(1)}, u32[]{:S(2)}, u32[]{:S(2)}) collective-permute-start(f32[8,128]{1,0:T(8,128)S(1)} %get-tuple-element.55), channel_id=1, source_target_pairs={{0,2},{2,4},{4,6},{6,8},{8,10},{10,12},{12,14},{14,0},{1,3},{3,5},... | collective-permute-start | bytes 12296 | tf_op jit(solution)/shard_map/ppermute | solution.py:763
  23.7 3.0 %collective-permute-start.7 = (f32[8,128]{1,0:T(8,128)S(1)}, f32[8,128]{1,0:T(8,128)S(1)}, u32[]{:S(2)}, u32[]{:S(2)}) collective-permute-start(f32[8,128]{1,0:T(8,128)S(1)} %get-tuple-element.56), channel_id=1, source_target_pairs={{0,14},{2,0},{4,2},{6,4},{8,6},{10,8},{12,10},{14,12},{1,15},{3,1}... | collective-permute-start | bytes 12296 | tf_op jit(solution)/shard_map/ppermute | solution.py:764
  26.7 0.7 %collective-permute-done.6.yl = f32[8,128]{1,0:T(8,128)S(1)} collective-permute-done((f32[8,128]{1,0:T(8,128)S(1)}, f32[8,128]{1,0:T(8,128)S(1)}, u32[]{:S(2)}, u32[]{:S(2)}) %collective-permute-start.6) | collective-permute-done | bytes 4128 | tf_op jit(solution)/shard_map/ppermute | solution.py:763
  27.9 5.3 %collective-permute-start.10 = (f32[5,16,128]{2,1,0:T(8,128)S(1)}, f32[5,16,128]{2,1,0:T(8,128)S(1)}, u32[]{:S(2)}, u32[]{:S(2)}) collective-permute-start(f32[5,16,128]{2,1,0:T(8,128)S(1)} %get-tuple-element.67), channel_id=1, source_target_pairs={{0,240},{16,0},{32,16},{48,32},{64,48},{80,64},{96,80},{112,96},{1... | collective-permute-start | bytes 122888 | tf_op jit(solution)/shard_map/ppermute | solution.py:753
  33.6 1.0 %collective-permute-done.9.xl = f32[5,16,128]{2,1,0:T(8,128)S(1)} collective-permute-done((f32[5,16,128]{2,1,0:T(8,128)S(1)}, f32[5,16,128]{2,1,0:T(8,128)S(1)}, u32[]{:S(2)}, u32[]{:S(2)}) %collective-permute-start.9) | collective-permute-done | bytes 40992 | tf_op jit(solution)/shard_map/ppermute | solution.py:752
  34.6 0.5 shard_map.75
  35.1 26.5 %all_to_all.11 = f32[256,1,8]{2,1,0:T(1,128)S(1)} all-to-all(f32[256,1,8]{2,1,0:T(1,128)S(1)} %bitcast.24), channel_id=1, replica_groups=mesh['gx'=16,'gy'=8,'gz'=2] {'gx','gy','gz'}, dimensions={0} | all-to-all | bytes 16384 | tf_op jit(solution)/shard_map/all_to_all | solution.py:838
  61.6 0.8 %shard_map.76 = (f32[128,128]{1,0:T(8,128)}, f32[1,1]{1,0:T(1,128)}) custom-call(f32[128,128]{1,0:T(8,128)S(1)} %get-tuple-element.70.grad_ref, f32[256,8]{1,0:T(8,128)S(1)} %bitcast.23), custom_call_target="tpu_custom_call" | custom-call | tf_op jit(solution)/shard_map/pallas_call | solution.py:839
  (18 shorter events, 0.9 us)
Async XLA Ops:
  0.6 7.7 %copy-start = (f32[5,16,8,128]{3,2,1,0:T(8,128)S(1)}, f32[5,16,8,128]{3,2,1,0:T(8,128)}, u32[]{:S(2)}) copy-start(f32[5,16,8,128]{3,2,1,0:T(8,128)} %param.5) | copy-start | bytes 983044
  0.6 7.7 %copy-start.1 = (s32[2,16,8,128]{3,2,1,0:T(8,128)S(1)}, s32[2,16,8,128]{3,2,1,0:T(8,128)}, u32[]{:S(2)}) copy-start(s32[2,16,8,128]{3,2,1,0:T(8,128)} %param.7) | copy-start | bytes 393220
  0.6 7.7 %copy-start.2 = (f32[16,8,128]{2,1,0:T(8,128)S(1)}, f32[16,8,128]{2,1,0:T(8,128)}, u32[]{:S(2)}) copy-start(f32[16,8,128]{2,1,0:T(8,128)} %param.6) | copy-start | bytes 196612
  2.0 8.7 %collective-permute-start.2 = (f32[11,8,128]{2,1,0:T(8,128)S(1)}, f32[11,8,128]{2,1,0:T(8,128)S(1)}, u32[]{:S(2)}, u32[]{:S(2)}) collective-permute-start(f32[11,8,128]{2,1,0:T(8,128)S(1)} %get-tuple-element.46), channel_id=1, source_target_pairs={{0,1},{1,0},{2,3},{3,2},{4,5},{5,4},{6,7},{7,6},{8,9},{9,8},{10,11... | collective-permute-start | bytes 135176 | tf_op jit(solution)/shard_map/ppermute | solution.py:758
  4.5 5.2 %collective-permute-start.1 = (f32[16,128]{1,0:T(8,128)S(1)}, f32[16,128]{1,0:T(8,128)S(1)}, u32[]{:S(2)}, u32[]{:S(2)}) collective-permute-start(f32[16,128]{1,0:T(8,128)S(1)} %get-tuple-element.44.ylo.ylo_in), channel_id=1, source_target_pairs={{0,14},{2,0},{4,2},{6,4},{8,6},{10,8},{12,10},{14,12},{1,15},{3,1}... | collective-permute-start | bytes 24584 | tf_op jit(solution)/shard_map/ppermute | solution.py:764
  5.5 5.2 %collective-permute-start = (f32[16,128]{1,0:T(8,128)S(1)}, f32[16,128]{1,0:T(8,128)S(1)}, u32[]{:S(2)}, u32[]{:S(2)}) collective-permute-start(f32[16,128]{1,0:T(8,128)S(1)} %get-tuple-element.45.yhi.yhi_in), channel_id=1, source_target_pairs={{0,2},{2,4},{4,6},{6,8},{8,10},{10,12},{12,14},{14,0},{1,3},{3,5},... | collective-permute-start | bytes 24584 | tf_op jit(solution)/shard_map/ppermute | solution.py:763
  10.7 6.3 %copy-start.4 = (f32[256]{0:T(256)S(1)}, f32[256]{0:T(256)}, u32[]{:S(2)}) copy-start(f32[256]{0:T(256)} %param.9) | copy-start | bytes 3076
  11.2 7.6 %collective-permute-start.3 = (f32[18,16,128]{2,1,0:T(8,128)S(1)}, f32[18,16,128]{2,1,0:T(8,128)S(1)}, u32[]{:S(2)}, u32[]{:S(2)}) collective-permute-start(f32[18,16,128]{2,1,0:T(8,128)S(1)} %get-tuple-element.48), channel_id=1, source_target_pairs={{0,16},{16,32},{32,48},{48,64},{64,80},{80,96},{96,112},{112,128},... | collective-permute-start | bytes 442376 | tf_op jit(solution)/shard_map/ppermute | solution.py:752
  12.4 6.3 %collective-permute-start.4 = (f32[18,16,128]{2,1,0:T(8,128)S(1)}, f32[18,16,128]{2,1,0:T(8,128)S(1)}, u32[]{:S(2)}, u32[]{:S(2)}) collective-permute-start(f32[18,16,128]{2,1,0:T(8,128)S(1)} %get-tuple-element.49), channel_id=1, source_target_pairs={{0,240},{16,0},{32,16},{48,32},{64,48},{80,64},{96,80},{112,96},{1... | collective-permute-start | bytes 442376 | tf_op jit(solution)/shard_map/ppermute | solution.py:753
  16.3 2.5 %collective-permute-start.5 = (f32[16,128]{1,0:T(8,128)S(1)}, f32[16,128]{1,0:T(8,128)S(1)}, u32[]{:S(2)}, u32[]{:S(2)}) collective-permute-start(f32[16,128]{1,0:T(8,128)S(1)} %get-tuple-element.50), channel_id=1, source_target_pairs={{0,1},{1,0},{2,3},{3,2},{4,5},{5,4},{6,7},{7,6},{8,9},{9,8},{10,11... | collective-permute-start | bytes 24584 | tf_op jit(solution)/shard_map/ppermute | solution.py:758
  17.0 0.7 %copy-start.3 = (s32[256]{0:T(256)S(1)}, s32[256]{0:T(256)}, u32[]{:S(2)}) copy-start(s32[256]{0:T(256)} %param.8) | copy-start | bytes 3076
  19.6 8.0 %collective-permute-start.8 = (f32[6,8,128]{2,1,0:T(8,128)S(1)}, f32[6,8,128]{2,1,0:T(8,128)S(1)}, u32[]{:S(2)}, u32[]{:S(2)}) collective-permute-start(f32[6,8,128]{2,1,0:T(8,128)S(1)} %get-tuple-element.57), channel_id=1, source_target_pairs={{0,1},{1,0},{2,3},{3,2},{4,5},{5,4},{6,7},{7,6},{8,9},{9,8},{10,11... | collective-permute-start | bytes 73736 | tf_op jit(solution)/shard_map/ppermute | solution.py:758
  20.4 6.9 %collective-permute-start.6 = (f32[8,128]{1,0:T(8,128)S(1)}, f32[8,128]{1,0:T(8,128)S(1)}, u32[]{:S(2)}, u32[]{:S(2)}) collective-permute-start(f32[8,128]{1,0:T(8,128)S(1)} %get-tuple-element.55), channel_id=1, source_target_pairs={{0,2},{2,4},{4,6},{6,8},{8,10},{10,12},{12,14},{14,0},{1,3},{3,5},... | collective-permute-start | bytes 12296 | tf_op jit(solution)/shard_map/ppermute | solution.py:763
  23.7 3.9 %collective-permute-start.7 = (f32[8,128]{1,0:T(8,128)S(1)}, f32[8,128]{1,0:T(8,128)S(1)}, u32[]{:S(2)}, u32[]{:S(2)}) collective-permute-start(f32[8,128]{1,0:T(8,128)S(1)} %get-tuple-element.56), channel_id=1, source_target_pairs={{0,14},{2,0},{4,2},{6,4},{8,6},{10,8},{12,10},{14,12},{1,15},{3,1}... | collective-permute-start | bytes 12296 | tf_op jit(solution)/shard_map/ppermute | solution.py:764
  27.8 6.7 %collective-permute-start.9 = (f32[5,16,128]{2,1,0:T(8,128)S(1)}, f32[5,16,128]{2,1,0:T(8,128)S(1)}, u32[]{:S(2)}, u32[]{:S(2)}) collective-permute-start(f32[5,16,128]{2,1,0:T(8,128)S(1)} %get-tuple-element.66), channel_id=1, source_target_pairs={{0,16},{16,32},{32,48},{48,64},{64,80},{80,96},{96,112},{112,128},... | collective-permute-start | bytes 122888 | tf_op jit(solution)/shard_map/ppermute | solution.py:752
  27.9 6.6 %collective-permute-start.10 = (f32[5,16,128]{2,1,0:T(8,128)S(1)}, f32[5,16,128]{2,1,0:T(8,128)S(1)}, u32[]{:S(2)}, u32[]{:S(2)}) collective-permute-start(f32[5,16,128]{2,1,0:T(8,128)S(1)} %get-tuple-element.67), channel_id=1, source_target_pairs={{0,240},{16,0},{32,16},{48,32},{64,48},{80,64},{96,80},{112,96},{1... | collective-permute-start | bytes 122888 | tf_op jit(solution)/shard_map/ppermute | solution.py:753
